TPU v7x, 32 devices: a whole 2x2x4 slice. The times are simulated.
32 devices in a mesh: ka: 4 (over x, core), tr: 2 (over y), tc: 4 (over z).
Axes of the slice: x: 2, y: 2, z: 4, core: 2. Of those that a mesh axis runs over, the one named last changes fastest.
Arguments:
- green_less: float32 [2, 4, 1024, 1024], P(None, 'ka', 'tr', 'tc'), may hold values from -6 to 6
- green_great: float32 [2, 4, 1024, 1024], P(None, 'ka', 'tr', 'tc'), may hold values from -6 to 6
- screened: float32 [2, 4, 1024, 1024], P(None, 'ka', 'tr', 'tc'), may hold values from -6 to 6
Outputs:
- collision: float32 [2, 4, 1024, 1024], P(None, 'ka', 'tr', 'tc')
- green_next: float32 [2, 4, 1024, 1024], P(None, 'ka', 'tr', 'tc')
All inputs are finite; a program needn't handle non-finite values.
Results may differ from a plain program's by a relative error of at most 0.00012.
Values sent between devices are 32-bit elements; how exact they have to be, the bound alone decides.
No kernel may reach another device: no remote copies, remote signals or barrier semaphores. Data moves between devices by JAX's collectives and lax.ppermute only.
A program may use at most 64 MiB of HBM per device.

v0:
```python
import math

import jax
import jax.numpy as jnp
from jax import lax
from jax.sharding import PartitionSpec as P

NT = 1024


def angle_tables(points):
    indices = jnp.arange(points, dtype=jnp.int32)
    phases = indices[:, None] * indices[None, :] % points
    angles = phases.astype(jnp.float32) * (2.0 * math.pi / points)
    return (jnp.cos(angles), jnp.sin(angles))


def along_momenta(matrix_in, source):
    return jnp.tensordot(matrix_in, source, axes=1, precision=lax.Precision.HIGHEST)


def to_real(source, cosine_table, sine_table):
    factor = source.shape[1] ** (-0.5)
    real_part = along_momenta(cosine_table, source[0]) - along_momenta(sine_table, source[1])
    imag_part = along_momenta(cosine_table, source[1]) + along_momenta(sine_table, source[0])
    return jnp.stack([real_part, imag_part]) * factor


def to_momentum(source, cosine_table, sine_table):
    factor = source.shape[1] ** (-0.5)
    real_part = along_momenta(cosine_table, source[0]) + along_momenta(sine_table, source[1])
    imag_part = along_momenta(cosine_table, source[1]) - along_momenta(sine_table, source[0])
    return jnp.stack([real_part, imag_part]) * factor


def self_energy(less_tiles, great_tiles, screen_tiles, cosine_table, sine_table):
    lesser = to_real(less_tiles, cosine_table, sine_table)
    greater = to_real(great_tiles, cosine_table, sine_table)
    screen_real = to_real(screen_tiles, cosine_table, sine_table)
    polar_real = lesser[0] * greater[1] - lesser[1] * greater[0]
    polar_imag = lesser[0] * greater[0] + lesser[1] * greater[1]
    inter_real = screen_real[0] + polar_real
    inter_imag = screen_real[1] + polar_imag
    sigma_re = -(lesser[0] * inter_imag + lesser[1] * inter_real)
    sigma_im = lesser[0] * inter_real - lesser[1] * inter_imag
    return to_momentum(jnp.stack([sigma_re, sigma_im]), cosine_table, sine_table)


def batch_product(left, right):
    return jnp.einsum(
        "kis,ksj->kij",
        left,
        right,
        precision=lax.Precision.HIGHEST,
        preferred_element_type=jnp.float32,
    )


def complex_product(left, right):
    first = batch_product(left[0], right[0])
    second = batch_product(left[1], right[1])
    mixed = batch_product(left[0] + left[1], right[0] + right[1])
    return jnp.stack([first - second, mixed - first - second])


def body(green_less, green_great, screened):
    momenta = green_less.shape[1] * lax.axis_size("ka")
    cosine_table, sine_table = angle_tables(momenta)
    sigma_tiles = lax.all_to_all(
        self_energy(
            lax.all_to_all(green_less, "ka", split_axis=2, concat_axis=1, tiled=True),
            lax.all_to_all(green_great, "ka", split_axis=2, concat_axis=1, tiled=True),
            lax.all_to_all(screened, "ka", split_axis=2, concat_axis=1, tiled=True),
            cosine_table,
            sine_table,
        ),
        "ka",
        split_axis=1,
        concat_axis=2,
        tiled=True,
    )
    column_panel = lax.all_gather(green_less, "tr", axis=2, tiled=True)
    summed = complex_product(lax.all_gather(sigma_tiles, "tc", axis=3, tiled=True), column_panel)
    collision = summed * NT ** (-0.5)
    return (collision, green_less + collision)


def solution(mesh):
    in_specs = (P(None, "ka", "tr", "tc"), P(None, "ka", "tr", "tc"), P(None, "ka", "tr", "tc"))
    out_specs = (P(None, "ka", "tr", "tc"), P(None, "ka", "tr", "tc"))
    return jax.shard_map(body, mesh=mesh, in_specs=in_specs, out_specs=out_specs, check_vma=False)
```

profile of v0, /device:TPU:0, one launch (start us, length us, event | category | flops | bytes accessed | tf_op | source)
XLA Modules:
  0.0 195.4 jit_solution(5462997650851783939)
XLA Ops:
  7.2 3.1 %copy.55 = f32[2,1,512,256]{3,0,1,2:T(2,128)} copy(f32[2,1,512,256]{3,2,1,0:T(8,128)} %param.4) | data formatting | bytes 2097152 | tf_op args[1]
  10.3 4.3 %all-to-all-start.2 = ((f32[2,1,512,256]{3,0,1,2:T(2,128)}), f32[2,1,512,256]{3,0,1,2:T(2,128)S(1)}, u32[]{:S(2)}, u32[]{:S(2)}) async-start(f32[2,1,512,256]{3,0,1,2:T(2,128)} %copy.55), calls=%async_computation.2 | async-start | bytes 2097152 | tf_op jit(solution)/shard_map/all_to_all | solution.py:72
  15.4 1.8 copy.41
  17.1 1.8 copy.48
  18.9 10.2 %all-to-all-done.2 = f32[2,1,512,256]{3,0,1,2:T(2,128)S(1)} async-done(((f32[2,1,512,256]{3,0,1,2:T(2,128)}), f32[2,1,512,256]{3,0,1,2:T(2,128)S(1)}, u32[]{:S(2)}, u32[]{:S(2)}) %all-to-all-start.2) | async-done | bytes 1048608 | tf_op jit(solution)/shard_map/all_to_all | solution.py:72
  29.1 3.5 %all-to-all-start.1 = ((f32[2,1,512,256]{3,0,1,2:T(2,128)}), f32[2,1,512,256]{3,0,1,2:T(2,128)S(1)}, u32[]{:S(2)}, u32[]{:S(2)}) async-start(f32[2,1,512,256]{3,0,1,2:T(2,128)} %copy.48), calls=%async_computation.1 | async-start | bytes 2097152 | tf_op jit(solution)/shard_map/all_to_all | solution.py:73
  33.5 1.2 fusion.42
  34.8 2.1 %fusion.23 = f32[1,4,128,256]{3,1,2,0:T(4,128)} fusion(f32[4,128,256]{2,0,1:T(4,128)S(1)} %fusion.42, f32[4,128,256]{2,1,0:T(8,128)S(1)} %bitcast.141), kind=kOutput, calls=%fused_computation.21 | convolution fusion | flops 6422752 | bytes 1572864 | tf_op jit(solution)/shard_map/dot_general | solution.py:19
  36.8 1.2 fusion.38
  38.1 2.1 %fusion.22 = f32[1,4,128,256]{3,1,2,0:T(4,128)} fusion(f32[4,128,256]{2,0,1:T(4,128)S(1)} %fusion.38, f32[4,128,256]{2,1,0:T(8,128)S(1)} %bitcast.136), kind=kOutput, calls=%fused_computation.19 | convolution fusion | flops 6422752 | bytes 1572864 | tf_op jit(solution)/shard_map/dot_general | solution.py:19
  40.2 6.9 %all-to-all-done.1 = f32[2,1,512,256]{3,0,1,2:T(2,128)S(1)} async-done(((f32[2,1,512,256]{3,0,1,2:T(2,128)}), f32[2,1,512,256]{3,0,1,2:T(2,128)S(1)}, u32[]{:S(2)}, u32[]{:S(2)}) %all-to-all-start.1) | async-done | bytes 1048608 | tf_op jit(solution)/shard_map/all_to_all | solution.py:73
  47.1 3.5 %all-to-all-start = ((f32[2,1,512,256]{3,0,1,2:T(2,128)}), f32[2,1,512,256]{3,0,1,2:T(2,128)S(1)}, u32[]{:S(2)}, u32[]{:S(2)}) async-start(f32[2,1,512,256]{3,0,1,2:T(2,128)} %copy.41), calls=%async_computation | async-start | bytes 2097152 | tf_op jit(solution)/shard_map/all_to_all | solution.py:71
  51.7 1.3 fusion.48
  53.0 1.3 fusion.25
  54.2 1.2 fusion.44
  55.5 1.3 fusion.24
  56.8 8.2 %all-to-all-done = f32[2,1,512,256]{3,0,1,2:T(2,128)S(1)} async-done(((f32[2,1,512,256]{3,0,1,2:T(2,128)}), f32[2,1,512,256]{3,0,1,2:T(2,128)S(1)}, u32[]{:S(2)}, u32[]{:S(2)}) %all-to-all-start) | async-done | bytes 1048608 | tf_op jit(solution)/shard_map/all_to_all | solution.py:71
  65.9 1.3 fusion.54
  67.2 1.2 fusion.50
  68.4 1.3 fusion.27
  69.7 1.5 fusion.26
  73.2 1.0 fusion.69
  74.3 1.1 fusion.21
  75.3 1.0 fusion.67
  76.4 1.1 fusion.20
  77.9 16.9 %all_to_all.19 = f32[2,4,128,256]{3,2,0,1:T(8,128)S(1)} all-to-all(f32[2,4,128,256]{3,2,0,1:T(8,128)S(1)} %copy.62), channel_id=1, replica_groups=mesh['ka'=4,'tr'=2,'tc'=4] {'ka'}, dimensions={1} | all-to-all | bytes 2097152 | tf_op jit(solution)/shard_map/all_to_all | solution.py:69
  94.8 1.0 copy.63
  95.9 81.9 %all-gather.3.cloned.1.call-done = f32[2,1,512,1024]{3,2,0,1:T(8,128)} async-done(((f32[2,1,512,256]{3,2,0,1:T(8,128)}), f32[2,1,512,1024]{3,2,0,1:T(8,128)}) %all-gather.3.cloned.1.call-update) | async-done | bytes 4194320 | tf_op jit(solution)/shard_map/all_gather | solution.py:83
  177.9 3.7 %fusion.2 = f32[512,256]{1,0:T(8,128)S(1)} fusion(f32[2,1,512,1024]{3,2,0,1:T(8,128)} %all-gather.3.cloned.1.call-done, f32[2,1,1024,256]{3,2,1,0:T(8,128)} %all-gather.5.cloned.1.call-done), kind=kOutput, calls=%fused_computation.2 | convolution fusion | flops 1610612736 | bytes 3670016 | tf_op jit(solution)/shard_map/kis,ksj->kij/dot_general | solution.py:50
  181.5 3.5 %fusion.4 = f32[512,256]{1,0:T(8,128)S(1)} fusion(f32[2,1,512,1024]{3,2,0,1:T(8,128)} %all-gather.3.cloned.1.call-done, f32[2,1,1024,256]{3,2,1,0:T(8,128)S(1)} %copy-done.2), kind=kOutput, calls=%fused_computation.4 | convolution fusion | flops 1610612736 | bytes 3670016 | tf_op jit(solution)/shard_map/kis,ksj->kij/dot_general | solution.py:50
  185.2 1.9 fusion.17
  187.1 1.5 fusion.159
  (32 shorter events, 6.1 us)
Async XLA Ops:
  7.2 8.2 %copy-start.1 = (f32[2,1,512,256]{3,2,1,0:T(8,128)S(1)}, f32[2,1,512,256]{3,2,1,0:T(8,128)}, u32[]{:S(2)}) copy-start(f32[2,1,512,256]{3,2,1,0:T(8,128)} %param.3) | copy-start | bytes 3145732
  10.3 6.9 %copy-start.5 = (f32[2,1,512,256]{3,2,1,0:T(8,128)S(1)}, f32[2,1,512,256]{3,2,1,0:T(8,128)}, u32[]{:S(2)}) copy-start(f32[2,1,512,256]{3,2,1,0:T(8,128)} %param.5) | copy-start | bytes 3145732
  10.3 18.8 %all-to-all-start.2 = ((f32[2,1,512,256]{3,0,1,2:T(2,128)}), f32[2,1,512,256]{3,0,1,2:T(2,128)S(1)}, u32[]{:S(2)}, u32[]{:S(2)}) async-start(f32[2,1,512,256]{3,0,1,2:T(2,128)} %copy.55), calls=%async_computation.2 | async-start | bytes 2097152 | tf_op jit(solution)/shard_map/all_to_all | solution.py:72
  14.6 81.3 %all-gather.5.cloned.1.call-start = ((), (), s32[]{:S(2)}) async-start(), calls=%async_computation.5 | async-start | bytes 3145728 | tf_op jit(solution)/shard_map/all_gather | solution.py:82
  29.1 18.0 %all-to-all-start.1 = ((f32[2,1,512,256]{3,0,1,2:T(2,128)}), f32[2,1,512,256]{3,0,1,2:T(2,128)S(1)}, u32[]{:S(2)}, u32[]{:S(2)}) async-start(f32[2,1,512,256]{3,0,1,2:T(2,128)} %copy.48), calls=%async_computation.1 | async-start | bytes 2097152 | tf_op jit(solution)/shard_map/all_to_all | solution.py:73
  47.1 18.0 %all-to-all-start = ((f32[2,1,512,256]{3,0,1,2:T(2,128)}), f32[2,1,512,256]{3,0,1,2:T(2,128)S(1)}, u32[]{:S(2)}, u32[]{:S(2)}) async-start(f32[2,1,512,256]{3,0,1,2:T(2,128)} %copy.41), calls=%async_computation | async-start | bytes 2097152 | tf_op jit(solution)/shard_map/all_to_all | solution.py:71
  50.6 127.3 %all-gather.3.cloned.1.call-start = ((), (), s32[]{:S(2)}) async-start(), calls=%async_computation.4 | async-start | bytes 5242880 | tf_op jit(solution)/shard_map/all_gather | solution.py:83
  71.2 1.0 copy-start.3
  71.2 1.2 copy-start.4
  95.9 85.6 %copy-start.2 = (f32[2,1,1024,256]{3,2,1,0:T(8,128)S(1)}, f32[2,1,1024,256]{3,2,1,0:T(8,128)}, u32[]{:S(2)}) copy-start(f32[2,1,1024,256]{3,2,1,0:T(8,128)} %all-gather.5.cloned.1.call-done) | copy-start | bytes 6291460
  181.5 3.6 %copy-start = (f32[2,1,512,1024]{3,2,0,1:T(8,128)S(1)}, f32[2,1,512,1024]{3,2,0,1:T(8,128)}, u32[]{:S(2)}) copy-start(f32[2,1,512,1024]{3,2,0,1:T(8,128)} %all-gather.3.cloned.1.call-done) | copy-start | bytes 12582916
Sparse Core Ops, SparseCore 0:
  17.0 35.6 all-gather.4
  96.0 81.8 all-gather.2
where the time goes:
time: 196 us; the launch traced here: 195 us
  waiting for transfers between devices  108 us (55%)
  matrix products  30.2 us (15%)
  blocking collectives  16.9 us (9%)
  between operations  14.4 us (7%)
  starting transfers between devices  11.6 us (6%)
  local copies, waits for them, and re-layouts  11.2 us (6%)
  other arithmetic  3.19 us (2%)
    all_gather x1, waiting for transfers between devices, body(): lax.all_gather(sigma_tiles, 'tc', axis=3, tiled=True)  81.9 us
    dot_general x16, matrix products, along_momenta(): jnp.tensordot(matrix_in, source, axes=1, precision=lax.Precision.HIGHEST)  21.1 us
    all_to_all x1, blocking collectives, body(): lax.all_to_all(self_energy(lax.all_to_all(green_less, 'ka', split_axis=2,...  16.9 us
    all_to_all x1, waiting for transfers between devices, body(): lax.all_to_all(green_great, 'ka', split_axis=2, concat_axis=1, tiled=True)  10.2 us
    dot_general x3, matrix products, batch_product(): jnp.einsum('kis,ksj->kij', left, right, precision=lax.Precision.HIGHEST,...  9.1 us
    all_to_all x1, waiting for transfers between devices, body(): lax.all_to_all(green_less, 'ka', split_axis=2, concat_axis=1, tiled=True)  8.24 us
    unnamed x21, local copies, waits for them, and re-layouts  7.54 us
    all_to_all x1, waiting for transfers between devices, body(): lax.all_to_all(screened, 'ka', split_axis=2, concat_axis=1, tiled=True)  6.88 us
  transfers between devices with their start and end apart: 5, of which 4 were waited for; matrix products, arithmetic and copies ran while one was open for 15% of the time, Pallas kernels for 0%

commit v1 on v0

v1 whole, which is shorter than its diff:
```python
import math

import jax
import jax.numpy as jnp
from jax import lax
from jax.sharding import PartitionSpec as P

CHUNKS = 4
SUBLANES = 8


def times_i(value, power):
    real, imag = value
    return [(real, imag), (-imag, real), (-real, -imag), (imag, -real)][power % 4]


def add(left, right):
    return (left[0] + right[0], left[1] + right[1])


def subtract(left, right):
    return (left[0] - right[0], left[1] - right[1])


def twiddle(value, index, points, sign):
    if 4 * index % points == 0:
        return times_i(value, sign * (4 * index // points))
    angle = sign * 2.0 * math.pi * index / points
    cosine, sine = math.cos(angle), math.sin(angle)
    real, imag = value
    return (real * cosine - imag * sine, imag * cosine + real * sine)


def transform(values, sign):
    points = len(values)
    if points == 1:
        return values
    if points % 2:
        return [
            sum_of([twiddle(value, at * out % points, points, sign) for at, value in enumerate(values)])
            for out in range(points)
        ]
    even, odd = transform(values[::2], sign), transform(values[1::2], sign)
    odd = [twiddle(value, at, points, sign) for at, value in enumerate(odd)]
    return [add(e, o) for e, o in zip(even, odd)] + [subtract(e, o) for e, o in zip(even, odd)]


def sum_of(values):
    total = values[0]
    for value in values[1:]:
        total = add(total, value)
    return total


def self_energy(pieces, phases, scale):
    points = len(pieces)
    lesser = transform([(x[0, 0], x[0, 1]) for x in pieces], 1)
    greater = transform([(x[1, 0], x[1, 1]) for x in pieces], 1)
    screen = transform([(x[2, 0], x[2, 1]) for x in pieces], 1)
    sigma = []
    for r in range(points):
        less, great, inter = lesser[r], greater[r], screen[r]
        cosine, sine = phases[0][r], phases[1][r]
        polar_real = less[0] * great[1] - less[1] * great[0]
        polar_imag = less[0] * great[0] + less[1] * great[1]
        inter_real = inter[0] * cosine - inter[1] * sine + polar_real * points**-0.5
        inter_imag = inter[1] * cosine + inter[0] * sine + polar_imag * points**-0.5
        sigma.append(
            (
                -(less[0] * inter_imag + less[1] * inter_real) * scale,
                (less[0] * inter_real - less[1] * inter_imag) * scale,
            )
        )
    return [jnp.stack(value) for value in transform(sigma, -1)]


def shift(value, axis, moves):
    return lax.ppermute(value, axis, moves)


def body(green_less, green_great, screened):
    momenta, row_parts, col_parts = lax.axis_size("ka"), lax.axis_size("tr"), lax.axis_size("tc")
    own, row_at, col_at = lax.axis_index("ka"), lax.axis_index("tr"), lax.axis_index("tc")
    rows, cols = green_less.shape[2], green_less.shape[3]
    group = col_parts // row_parts
    half, member = col_at // group, col_at % group
    chunks = max(1, min(CHUNKS, rows // (momenta * SUBLANES)))
    step = rows // (momenta * chunks)
    length = rows * row_parts

    less = green_less[:, 0]
    blocks = less.reshape(2, group, cols, cols)
    sides = [lax.dynamic_index_in_dim(blocks, member, 1, False)]
    for gap in range(1, group):
        moves = [
            (part * group + m, part * group + (m + gap) % group) for part in range(row_parts) for m in range(group)
        ]
        sides.append(shift(lax.dynamic_index_in_dim(blocks, (member + gap) % group, 1, False), "tc", moves))
    panel = jnp.concatenate(sides, axis=2)
    panels = [panel] + [
        shift(panel, "tr", [(i, (i + gap) % row_parts) for i in range(row_parts)]) for gap in range(1, row_parts)
    ]
    stacked = jnp.stack(panels)
    right = jnp.concatenate(
        [
            lax.dynamic_index_in_dim(stacked, (row_at - half + gap) % row_parts, 0, False)
            for gap in range(row_parts)
        ],
        axis=1,
    )
    right = jnp.concatenate(
        [jnp.concatenate([right[0], right[1]], axis=1), jnp.concatenate([-right[1], right[0]], axis=1)], axis=0
    )

    angles = (own * jnp.arange(momenta) % momenta).astype(jnp.float32) * (2.0 * math.pi / momenta)
    phases = (jnp.cos(angles), jnp.sin(angles))
    scale = momenta**-1.5 * length**-0.5
    inputs = jnp.stack([less, green_great[:, 0], screened[:, 0]]).reshape(3, 2, chunks, momenta, step, cols)

    outs = []
    for chunk in range(chunks):
        source = inputs[:, :, chunk]
        pieces = [lax.dynamic_index_in_dim(source, own, 2, False)]
        for gap in range(1, momenta):
            piece = lax.dynamic_index_in_dim(source, (own - gap) % momenta, 2, False)
            pieces.append(shift(piece, "ka", [(s, (s - gap) % momenta) for s in range(momenta)]))
        sigma = self_energy(pieces, phases, scale)
        parts = [sigma[0]] + [
            shift(sigma[gap], "ka", [(s, (s + gap) % momenta) for s in range(momenta)]) for gap in range(1, momenta)
        ]
        mine = jnp.concatenate(parts, axis=1)
        sides = [mine] + [
            shift(mine, "tc", [(j, (j + group * gap) % col_parts) for j in range(col_parts)])
            for gap in range(1, row_parts)
        ]
        left = jnp.concatenate([side[at] for at in (0, 1) for side in sides], axis=1)
        product = jnp.dot(left, right, precision=lax.Precision.HIGH, preferred_element_type=jnp.float32)
        product = product.reshape(momenta * step, 2, group, cols)
        total = product[:, :, 0]
        for gap in range(1, group):
            moves = [
                (part * group + m, part * group + (m - gap) % group) for part in range(row_parts) for m in range(group)
            ]
            total = total + shift(product[:, :, gap], "tc", moves)
        outs.append(total.reshape(momenta, step, 2, cols))
    whole = jnp.stack(outs)
    order = (own - jnp.arange(momenta)) % momenta
    whole = jnp.take(whole, order, axis=1)
    collision = jnp.moveaxis(whole.reshape(rows, 2, cols), 1, 0)[:, None]
    return collision, green_less + collision


def solution(mesh):
    spec = P(None, "ka", "tr", "tc")
    return jax.shard_map(body, mesh=mesh, in_specs=(spec,) * 3, out_specs=(spec,) * 2, check_vma=False)
```

time: 196 us -> 148 us (0.76)
  waiting for transfers between devices: 108 us -> 41.6 us
  other arithmetic: 3.19 us -> 34.9 us
  starting transfers between devices: 11.6 us -> 34.6 us
  matrix products: 30.2 us -> 12.5 us
  blocking collectives: 16.9 us -> 0 us
  between operations: 14.4 us -> 1.37 us
  local copies, waits for them, and re-layouts: 11.2 us -> 21.6 us
    all_gather x2 -> x0, waiting for transfers between devices: 82 us -> none  [the longest x1 81.9 us: body(): lax.all_gather(sigma_tiles, 'tc', axis=3, tiled=True)]
    ppermute x0 -> x34, waiting for transfers between devices: none -> 41.6 us  [shift(): return lax.ppermute(value, axis, moves)]
    ppermute x0 -> x34, starting transfers between devices: none -> 34.6 us  [shift(): return lax.ppermute(value, axis, moves)]
    add x1 -> x24, other arithmetic: 1.52 us -> 28.8 us  [the longest x20 25.8 us: add(): return (left[0] + right[0], left[1] + right[1])]
    all_to_all x3 -> x0, waiting for transfers between devices: 25.3 us -> none  [the longest x1 10.2 us: body(): lax.all_to_all(green_great, 'ka', split_axis=2, concat_axis=1, tiled=True)]
    dot_general x19 -> x4, matrix products: 30.2 us -> 12.5 us  [body(): jnp.dot(left, right, precision=lax.Precision.HIGH, preferred_element_type...]
    all_to_all x1 -> x0, blocking collectives: 16.9 us -> none  [body(): lax.all_to_all(self_energy(lax.all_to_all(green_less, 'ka', split_axis=2,...]
    all_to_all x3 -> x0, starting transfers between devices: 11.4 us -> none  [the longest x1 4.34 us: body(): lax.all_to_all(green_great, 'ka', split_axis=2, concat_axis=1, tiled=True)]
  transfers between devices with their start and end apart: 5 -> 34, of which waited for: 4 -> 8; matrix products, arithmetic and copies ran while one was open for 15% -> 38% of each run, Pallas kernels for 0% -> 0%
where the time goes in v1:
time: 148 us; the launch traced here: 147 us
  waiting for transfers between devices  41.6 us (28%)
  other arithmetic  34.9 us (24%)
  starting transfers between devices  34.6 us (23%)
  local copies, waits for them, and re-layouts  21.6 us (15%)
  matrix products  12.5 us (8%)
    ppermute x34, waiting for transfers between devices, shift(): return lax.ppermute(value, axis, moves)  41.6 us
    ppermute x34, starting transfers between devices, shift(): return lax.ppermute(value, axis, moves)  34.6 us
    add x20, other arithmetic, add(): return (left[0] + right[0], left[1] + right[1])  25.8 us
    dot_general x4, matrix products, body(): jnp.dot(left, right, precision=lax.Precision.HIGH, preferred_element_type...  12.5 us
    squeeze x8, local copies, waits for them, and re-layouts, body(): side[at]  4.32 us
    squeeze x4, local copies, waits for them, and re-layouts, body(): piece = lax.dynamic_index_in_dim(source, (own - gap) % momenta, 2, False)  3.87 us
    reshape x4, local copies, waits for them, and re-layouts, body(): product = product.reshape(momenta * step, 2, group, cols)  3.84 us
    unnamed x20, local copies, waits for them, and re-layouts  3.44 us
  transfers between devices with their start and end apart: 34, of which 8 were waited for; matrix products, arithmetic and copies ran while one was open for 38% of the time, Pallas kernels for 0%

profile of v1, /device:TPU:0, one launch (start us, length us, event | category | flops | bytes accessed | tf_op | source)
XLA Modules:
  0.0 146.6 jit_solution(7543854450831052234)
XLA Ops:
  0.7 2.2 %pad_maximum_fusion = f32[3,2,4,4,32,256]{5,4,3,2,1,0:T(8,128)S(1)} fusion(f32[1,2,4,4,32,256]{5,4,3,2,1,0:T(8,128)} %bitcast.1171, f32[1,2,4,4,32,256]{5,4,3,2,1,0:T(8,128)} %bitcast.1172, f32[1,2,4,4,32,256]{5,4,3,2,1,0:T(8,128)} %bitcast.1166), kind=kLoop, calls=%fused_computation.2 | loop fusion | flops 1572864 | bytes 6291456 | tf_op jit(solution)/shard_map/stack | solution.py:118
  2.9 1.2 fusion.331
  4.2 2.1 %dynamic-slice_bitcast_fusion.15 = (f32[3,2,32,256]{3,2,1,0:T(8,128)}, f32[3,2,32,256]{3,2,1,0:T(8,128)}, f32[3,2,32,256]{3,2,1,0:T(8,128)}, f32[3,2,32,256]{3,2,1,0:T(8,128)}) fusion(f32[3,2,1,4,32,256]{5,4,3,2,1,0:T(8,128)} %get-tuple-element.112, s32[]{:T(128)S(6)} %select_n.140, s32[]{:T(128)S(6)} %select_n.142, s32[]{:T(128)S(6)} %select_n.138, ...), kind=kLoop, calls=%fused_computation.85 | loop fusion | bytes 1572880 | tf_op jit(solution)/shard_map/jit(dynamic_index_in_dim)/squeeze | solution.py:125
  6.3 2.4 %collective-permute-start.1 = (f32[3,2,32,256]{3,2,1,0:T(8,128)}, f32[3,2,32,256]{3,2,1,0:T(8,128)}, u32[]{:S(2)}, u32[]{:S(2)}) collective-permute-start(f32[3,2,32,256]{3,2,1,0:T(8,128)} %get-tuple-element.122), channel_id=1, source_target_pairs={{0,24},{8,0},{16,8},{24,16},{1,25},{9,1},{17,9},{25,17},{2,26},{10... | collective-permute-start | bytes 589832 | tf_op jit(solution)/shard_map/ppermute | solution.py:78
  10.8 1.6 %collective-permute-start.7 = (f32[2,256,256]{2,1,0:T(8,128)}, f32[2,256,256]{2,1,0:T(8,128)}, u32[]{:S(2)}, u32[]{:S(2)}) collective-permute-start(f32[2,256,256]{2,1,0:T(8,128)} %get-tuple-element.121), channel_id=1, source_target_pairs={{0,1},{1,0},{2,3},{3,2},{4,5},{5,4},{6,7},{7,6},{8,9},{9,8},{10,11... | collective-permute-start | bytes 1572872 | tf_op jit(solution)/shard_map/ppermute | solution.py:78
  16.5 1.5 %collective-permute-start.10 = (f32[3,2,32,256]{3,2,1,0:T(8,128)S(1)}, f32[3,2,32,256]{3,2,1,0:T(8,128)S(1)}, u32[]{:S(2)}, u32[]{:S(2)}) collective-permute-start(f32[3,2,32,256]{3,2,1,0:T(8,128)S(1)} %copy-done.5), channel_id=1, source_target_pairs={{0,16},{8,24},{16,0},{24,8},{1,17},{9,25},{17,1},{25,9},{2,18},{10... | collective-permute-start | bytes 589832 | tf_op jit(solution)/shard_map/ppermute | solution.py:78
  19.0 1.7 %collective-permute-start.19 = (f32[3,2,32,256]{3,2,1,0:T(8,128)}, f32[3,2,32,256]{3,2,1,0:T(8,128)S(1)}, u32[]{:S(2)}, u32[]{:S(2)}) collective-permute-start(f32[3,2,32,256]{3,2,1,0:T(8,128)} %get-tuple-element.130), channel_id=1, source_target_pairs={{0,24},{8,0},{16,8},{24,16},{1,25},{9,1},{17,9},{25,17},{2,26},{10... | collective-permute-start | bytes 589832 | tf_op jit(solution)/shard_map/ppermute | solution.py:78
  21.6 6.2 %add_add_fusion.7 = (f32[1,32,256]{2,1,0:T(8,128)S(1)}, f32[1,32,256]{2,1,0:T(8,128)S(1)}, f32[1,32,256]{2,1,0:T(8,128)S(1)}, f32[1,32,256]{2,1,0:T(8,128)S(1)},...) fusion(f32[1,1,32,256]{3,2,1,0:T(8,128)S(1)} %get-tuple-element, ...), kind=kLoop, calls=%fused_computation.551 | loop fusion | flops 983040 | bytes 1474592 | tf_op jit(solution)/shard_map/add | solution.py:18
  28.0 1.5 %collective-permute-start.18 = (f32[3,2,32,256]{3,2,1,0:T(8,128)S(1)}, f32[3,2,32,256]{3,2,1,0:T(8,128)S(1)}, u32[]{:S(2)}, u32[]{:S(2)}) collective-permute-start(f32[3,2,32,256]{3,2,1,0:T(8,128)S(1)} %get-tuple-element.132), channel_id=1, source_target_pairs={{0,16},{8,24},{16,0},{24,8},{1,17},{9,25},{17,1},{25,9},{2,18},{10... | collective-permute-start | bytes 589832 | tf_op jit(solution)/shard_map/ppermute | solution.py:78
  30.3 1.4 collective-permute-start.27
  31.8 6.1 %add_add_fusion.5 = (f32[1,32,256]{2,1,0:T(8,128)S(1)}, f32[1,32,256]{2,1,0:T(8,128)S(1)}, f32[1,32,256]{2,1,0:T(8,128)S(1)}, f32[1,32,256]{2,1,0:T(8,128)S(1)},...) fusion(f32[1,1,32,256]{3,2,1,0:T(8,128)S(1)} %get-tuple-element, ...), kind=kLoop, calls=%fused_computation.543 | loop fusion | flops 983040 | bytes 1474592 | tf_op jit(solution)/shard_map/add | solution.py:18
  38.7 1.3 collective-permute-start.3
  40.0 5.3 %add_add_fusion.3 = (f32[1,32,256]{2,1,0:T(8,128)S(1)}, f32[1,32,256]{2,1,0:T(8,128)S(1)}, f32[1,32,256]{2,1,0:T(8,128)S(1)}, f32[1,32,256]{2,1,0:T(8,128)S(1)},...) fusion(f32[1,1,32,256]{3,2,1,0:T(8,128)S(1)} %get-tuple-element, ...), kind=kLoop, calls=%fused_computation.535 | loop fusion | flops 983040 | bytes 1474592 | tf_op jit(solution)/shard_map/add | solution.py:18
  47.3 5.3 %add_add_fusion.1 = (f32[1,32,256]{2,1,0:T(8,128)S(1)}, f32[1,32,256]{2,1,0:T(8,128)S(1)}, f32[1,32,256]{2,1,0:T(8,128)S(1)}, f32[1,32,256]{2,1,0:T(8,128)S(1)},...) fusion(f32[1,1,32,256]{3,2,1,0:T(8,128)S(1)} %get-tuple-element, ...), kind=kLoop, calls=%fused_computation.527 | loop fusion | flops 983040 | bytes 1474592 | tf_op jit(solution)/shard_map/add | solution.py:18
  54.9 1.5 %collective-permute-start.22 = (f32[2,32,256]{2,1,0:T(8,128)S(1)}, f32[2,32,256]{2,1,0:T(8,128)S(1)}, u32[]{:S(2)}, u32[]{:S(2)}) collective-permute-start(f32[2,32,256]{2,1,0:T(8,128)S(1)} %pad_maximum_fusion.15), channel_id=1, source_target_pairs={{0,16},{8,24},{16,0},{24,8},{1,17},{9,25},{17,1},{25,9},{2,18},{10... | collective-permute-start | bytes 196616 | tf_op jit(solution)/shard_map/ppermute | solution.py:78
  61.1 2.6 %collective-permute-start.6 = (f32[2,128,256]{2,1,0:T(8,128)S(1)}, f32[2,128,256]{2,1,0:T(8,128)S(1)}, u32[]{:S(2)}, u32[]{:S(2)}) collective-permute-start(f32[2,128,256]{2,1,0:T(8,128)S(1)} %pad_maximum_fusion.4), channel_id=1, source_target_pairs={{0,2},{1,3},{2,0},{3,1},{4,6},{5,7},{6,4},{7,5},{8,10},{9,11},{10,... | collective-permute-start | bytes 786440 | tf_op jit(solution)/shard_map/ppermute | solution.py:78
  64.7 2.1 %collective-permute-start.24 = (f32[2,128,256]{2,1,0:T(8,128)S(1)}, f32[2,128,256]{2,1,0:T(8,128)S(1)}, u32[]{:S(2)}, u32[]{:S(2)}) collective-permute-start(f32[2,128,256]{2,1,0:T(8,128)S(1)} %pad_maximum_fusion.6), channel_id=1, source_target_pairs={{0,2},{1,3},{2,0},{3,1},{4,6},{5,7},{6,4},{7,5},{8,10},{9,11},{10,... | collective-permute-start | bytes 786440 | tf_op jit(solution)/shard_map/ppermute | solution.py:78
  70.3 1.6 %collective-permute-start.8 = (f32[2,256,512]{2,1,0:T(8,128)S(1)}, f32[2,256,512]{2,1,0:T(8,128)S(1)}, u32[]{:S(2)}, u32[]{:S(2)}) collective-permute-start(f32[2,256,512]{2,1,0:T(8,128)S(1)} %get-tuple-element.118), channel_id=1, source_target_pairs={{0,4},{4,0},{1,5},{5,1},{2,6},{6,2},{3,7},{7,3},{8,12},{12,8},{9,1... | collective-permute-start | bytes 3145736 | tf_op jit(solution)/shard_map/ppermute | solution.py:78
  72.6 21.0 %collective-permute-done.6 = f32[2,128,256]{2,1,0:T(8,128)S(1)} collective-permute-done((f32[2,128,256]{2,1,0:T(8,128)S(1)}, f32[2,128,256]{2,1,0:T(8,128)S(1)}, u32[]{:S(2)}, u32[]{:S(2)}) %collective-permute-start.6) | collective-permute-done | bytes 262176 | tf_op jit(solution)/shard_map/ppermute | solution.py:78
  93.6 5.6 %collective-permute-done.16 = f32[2,128,256]{2,1,0:T(8,128)S(1)} collective-permute-done((f32[2,128,256]{2,1,0:T(8,128)S(1)}, f32[2,128,256]{2,1,0:T(8,128)S(1)}, u32[]{:S(2)}, u32[]{:S(2)}) %collective-permute-start.16) | collective-permute-done | bytes 262176 | tf_op jit(solution)/shard_map/ppermute | solution.py:78
  99.9 4.9 %collective-permute-done.24 = f32[2,128,256]{2,1,0:T(8,128)S(1)} collective-permute-done((f32[2,128,256]{2,1,0:T(8,128)S(1)}, f32[2,128,256]{2,1,0:T(8,128)S(1)}, u32[]{:S(2)}, u32[]{:S(2)}) %collective-permute-start.24) | collective-permute-done | bytes 262176 | tf_op jit(solution)/shard_map/ppermute | solution.py:78
  105.6 4.4 %collective-permute-done.32 = f32[2,128,256]{2,1,0:T(8,128)S(1)} collective-permute-done((f32[2,128,256]{2,1,0:T(8,128)S(1)}, f32[2,128,256]{2,1,0:T(8,128)S(1)}, u32[]{:S(2)}, u32[]{:S(2)}) %collective-permute-start.32) | collective-permute-done | bytes 262176 | tf_op jit(solution)/shard_map/ppermute | solution.py:78
  112.8 1.5 fusion.11
  116.6 4.0 %fusion.10 = f32[128,1024]{1,0:T(8,128)} fusion(f32[512,512]{1,0:T(8,128)S(1)} %fusion.1, f32[512,512]{1,0:T(8,128)} %copy-done.2, f32[512,512]{1,0:T(8,128)} %copy-done.3, f32[128,256]{1,0:T(8,128)} %get-tuple-element.217, f32[128,256]{1,0:T(8,128)} %get-tuple-element.215, f32[128,256]{1,0:T(8,128)} %get-tuple-element.216, f32[128,256]{1,0:T(8,128)} %get-tuple-element.214), kind=kOutput, calls=%fused_computation.24 | convolution fusion | flops 808845312 | bytes 4194304 | tf_op jit(solution)/shard_map/dot_general | solution.py:137
  120.6 1.5 %reshape.8429 = f32[128,2,2,256]{3,2,1,0:T(2,128)S(1)} reshape(f32[128,1024]{1,0:T(8,128)} %fusion.10) | data formatting | bytes 1048576 | tf_op jit(solution)/shard_map/reshape | solution.py:138
  123.2 1.3 collective-permute-start.17
  124.6 3.9 %fusion.9 = f32[128,1024]{1,0:T(8,128)} fusion(f32[512,512]{1,0:T(8,128)S(1)} %fusion.1, f32[512,512]{1,0:T(8,128)} %copy-done.2, f32[512,512]{1,0:T(8,128)} %copy-done.3, f32[128,256]{1,0:T(8,128)} %get-tuple-element.221, f32[128,256]{1,0:T(8,128)S(1)} %copy-done.7, f32[128,256]{1,0:T(8,128)} %get-tuple-element.220, f32[128,256]{1,0:T(8,128)S(1)} %copy-done.6), kind=kOutput, calls=%fused_computation.23 | convolution fusion | flops 808845312 | bytes 4194304 | tf_op jit(solution)/shard_map/dot_general | solution.py:137
  128.5 1.5 %reshape.8430 = f32[128,2,2,256]{3,2,1,0:T(2,128)S(1)} reshape(f32[128,1024]{1,0:T(8,128)} %fusion.9) | data formatting | bytes 1048576 | tf_op jit(solution)/shard_map/reshape | solution.py:138
  131.8 3.1 %fusion.8 = f32[128,1024]{1,0:T(8,128)S(1)} fusion(f32[512,512]{1,0:T(8,128)S(1)} %fusion.1, f32[512,512]{1,0:T(8,128)} %copy-done.2, f32[512,512]{1,0:T(8,128)} %copy-done.3, f32[128,256]{1,0:T(8,128)} %get-tuple-element.225, f32[128,256]{1,0:T(8,128)} %get-tuple-element.223, f32[128,256]{1,0:T(8,128)} %get-tuple-element.224, ...), kind=kOutput, calls=%fused_computation.22 | convolution fusion | flops 808845312 | bytes 4194304 | tf_op jit(solution)/shard_map/dot_general | solution.py:137
  135.8 1.4 collective-permute-start.33
  140.5 3.7 %collective-permute-done.33 = f32[128,2,256]{2,0,1:T(8,128)S(1)} collective-permute-done((f32[128,2,256]{2,0,1:T(8,128)S(1)}, f32[128,2,256]{2,0,1:T(8,128)S(1)}, u32[]{:S(2)}, u32[]{:S(2)}) %collective-permute-start.33) | collective-permute-done | bytes 262176 | tf_op jit(solution)/shard_map/ppermute | solution.py:78
  145.1 1.5 %fusion.7 = (f32[2,1,512,256]{3,2,1,0:T(8,128)}, f32[512,2,256]{2,0,1:T(8,128)}) fusion(f32[2,1,512,256]{3,2,1,0:T(8,128)S(1)} %copy-done, f32[4,4,32,2,256]{4,2,1,0,3:T(8,128)S(1)} %copy.25, pred[512]{0:T(512)(128)(4,1)S(1)} %broadcast_in_dim.18), kind=kLoop, calls=%fused_computation.20 | loop fusion | flops 524288 | bytes 4194816
  (140 shorter events, 38.4 us)
Async XLA Ops:
  6.3 10.1 %collective-permute-start.1 = (f32[3,2,32,256]{3,2,1,0:T(8,128)}, f32[3,2,32,256]{3,2,1,0:T(8,128)}, u32[]{:S(2)}, u32[]{:S(2)}) collective-permute-start(f32[3,2,32,256]{3,2,1,0:T(8,128)} %get-tuple-element.122), channel_id=1, source_target_pairs={{0,24},{8,0},{16,8},{24,16},{1,25},{9,1},{17,9},{25,17},{2,26},{10... | collective-permute-start | bytes 589832 | tf_op jit(solution)/shard_map/ppermute | solution.py:78
  8.7 7.8 %collective-permute-start.2 = (f32[3,2,32,256]{3,2,1,0:T(8,128)}, f32[3,2,32,256]{3,2,1,0:T(8,128)}, u32[]{:S(2)}, u32[]{:S(2)}) collective-permute-start(f32[3,2,32,256]{3,2,1,0:T(8,128)} %get-tuple-element.123), channel_id=1, source_target_pairs={{0,8},{8,16},{16,24},{24,0},{1,9},{9,17},{17,25},{25,1},{2,10},{10... | collective-permute-start | bytes 589832 | tf_op jit(solution)/shard_map/ppermute | solution.py:78
  8.7 10.3 %collective-permute-start = (f32[3,2,32,256]{3,2,1,0:T(8,128)}, f32[3,2,32,256]{3,2,1,0:T(8,128)}, u32[]{:S(2)}, u32[]{:S(2)}) collective-permute-start(f32[3,2,32,256]{3,2,1,0:T(8,128)} %get-tuple-element.124), channel_id=1, source_target_pairs={{0,16},{8,24},{16,0},{24,8},{1,17},{9,25},{17,1},{25,9},{2,18},{10... | collective-permute-start | bytes 589832 | tf_op jit(solution)/shard_map/ppermute | solution.py:78
  10.8 58.3 %collective-permute-start.7 = (f32[2,256,256]{2,1,0:T(8,128)}, f32[2,256,256]{2,1,0:T(8,128)}, u32[]{:S(2)}, u32[]{:S(2)}) collective-permute-start(f32[2,256,256]{2,1,0:T(8,128)} %get-tuple-element.121), channel_id=1, source_target_pairs={{0,1},{1,0},{2,3},{3,2},{4,5},{5,4},{6,7},{7,6},{8,9},{9,8},{10,11... | collective-permute-start | bytes 1572872 | tf_op jit(solution)/shard_map/ppermute | solution.py:78
  13.3 14.6 %collective-permute-start.11 = (f32[3,2,32,256]{3,2,1,0:T(8,128)}, f32[3,2,32,256]{3,2,1,0:T(8,128)}, u32[]{:S(2)}, u32[]{:S(2)}) collective-permute-start(f32[3,2,32,256]{3,2,1,0:T(8,128)} %get-tuple-element.126), channel_id=1, source_target_pairs={{0,24},{8,0},{16,8},{24,16},{1,25},{9,1},{17,9},{25,17},{2,26},{10... | collective-permute-start | bytes 589832 | tf_op jit(solution)/shard_map/ppermute | solution.py:78
  16.5 11.5 %collective-permute-start.12 = (f32[3,2,32,256]{3,2,1,0:T(8,128)}, f32[3,2,32,256]{3,2,1,0:T(8,128)S(1)}, u32[]{:S(2)}, u32[]{:S(2)}) collective-permute-start(f32[3,2,32,256]{3,2,1,0:T(8,128)} %get-tuple-element.127), channel_id=1, source_target_pairs={{0,8},{8,16},{16,24},{24,0},{1,9},{9,17},{17,25},{25,1},{2,10},{10... | collective-permute-start | bytes 589832 | tf_op jit(solution)/shard_map/ppermute | solution.py:78
  16.5 13.8 %collective-permute-start.10 = (f32[3,2,32,256]{3,2,1,0:T(8,128)S(1)}, f32[3,2,32,256]{3,2,1,0:T(8,128)S(1)}, u32[]{:S(2)}, u32[]{:S(2)}) collective-permute-start(f32[3,2,32,256]{3,2,1,0:T(8,128)S(1)} %copy-done.5), channel_id=1, source_target_pairs={{0,16},{8,24},{16,0},{24,8},{1,17},{9,25},{17,1},{25,9},{2,18},{10... | collective-permute-start | bytes 589832 | tf_op jit(solution)/shard_map/ppermute | solution.py:78
  19.0 19.0 %collective-permute-start.19 = (f32[3,2,32,256]{3,2,1,0:T(8,128)}, f32[3,2,32,256]{3,2,1,0:T(8,128)S(1)}, u32[]{:S(2)}, u32[]{:S(2)}) collective-permute-start(f32[3,2,32,256]{3,2,1,0:T(8,128)} %get-tuple-element.130), channel_id=1, source_target_pairs={{0,24},{8,0},{16,8},{24,16},{1,25},{9,1},{17,9},{25,17},{2,26},{10... | collective-permute-start | bytes 589832 | tf_op jit(solution)/shard_map/ppermute | solution.py:78
  27.9 10.2 %collective-permute-start.20 = (f32[3,2,32,256]{3,2,1,0:T(8,128)S(1)}, f32[3,2,32,256]{3,2,1,0:T(8,128)S(1)}, u32[]{:S(2)}, u32[]{:S(2)}) collective-permute-start(f32[3,2,32,256]{3,2,1,0:T(8,128)S(1)} %get-tuple-element.131), channel_id=1, source_target_pairs={{0,8},{8,16},{16,24},{24,0},{1,9},{9,17},{17,25},{25,1},{2,10},{10... | collective-permute-start | bytes 589832 | tf_op jit(solution)/shard_map/ppermute | solution.py:78
  28.0 10.8 %collective-permute-start.18 = (f32[3,2,32,256]{3,2,1,0:T(8,128)S(1)}, f32[3,2,32,256]{3,2,1,0:T(8,128)S(1)}, u32[]{:S(2)}, u32[]{:S(2)}) collective-permute-start(f32[3,2,32,256]{3,2,1,0:T(8,128)S(1)} %get-tuple-element.132), channel_id=1, source_target_pairs={{0,16},{8,24},{16,0},{24,8},{1,17},{9,25},{17,1},{25,9},{2,18},{10... | collective-permute-start | bytes 589832 | tf_op jit(solution)/shard_map/ppermute | solution.py:78
  30.3 15.1 %collective-permute-start.27 = (f32[3,2,32,256]{3,2,1,0:T(8,128)S(1)}, f32[3,2,32,256]{3,2,1,0:T(8,128)S(1)}, u32[]{:S(2)}, u32[]{:S(2)}) collective-permute-start(f32[3,2,32,256]{3,2,1,0:T(8,128)S(1)} %get-tuple-element.134), channel_id=1, source_target_pairs={{0,24},{8,0},{16,8},{24,16},{1,25},{9,1},{17,9},{25,17},{2,26},{10... | collective-permute-start | bytes 589832 | tf_op jit(solution)/shard_map/ppermute | solution.py:78
  38.0 8.1 %collective-permute-start.28 = (f32[3,2,32,256]{3,2,1,0:T(8,128)S(1)}, f32[3,2,32,256]{3,2,1,0:T(8,128)S(1)}, u32[]{:S(2)}, u32[]{:S(2)}) collective-permute-start(f32[3,2,32,256]{3,2,1,0:T(8,128)S(1)} %get-tuple-element.135), channel_id=1, source_target_pairs={{0,8},{8,16},{16,24},{24,0},{1,9},{9,17},{17,25},{25,1},{2,10},{10... | collective-permute-start | bytes 589832 | tf_op jit(solution)/shard_map/ppermute | solution.py:78
  38.1 9.2 %collective-permute-start.26 = (f32[3,2,32,256]{3,2,1,0:T(8,128)S(1)}, f32[3,2,32,256]{3,2,1,0:T(8,128)S(1)}, u32[]{:S(2)}, u32[]{:S(2)}) collective-permute-start(f32[3,2,32,256]{3,2,1,0:T(8,128)S(1)} %get-tuple-element.136), channel_id=1, source_target_pairs={{0,16},{8,24},{16,0},{24,8},{1,17},{9,25},{17,1},{25,9},{2,18},{10... | collective-permute-start | bytes 589832 | tf_op jit(solution)/shard_map/ppermute | solution.py:78
  38.7 14.1 %collective-permute-start.3 = (f32[2,32,256]{2,1,0:T(8,128)S(1)}, f32[2,32,256]{2,1,0:T(8,128)S(1)}, u32[]{:S(2)}, u32[]{:S(2)}) collective-permute-start(f32[2,32,256]{2,1,0:T(8,128)S(1)} %pad_maximum_fusion.8), channel_id=1, source_target_pairs={{0,8},{8,16},{16,24},{24,0},{1,9},{9,17},{17,25},{25,1},{2,10},{10... | collective-permute-start | bytes 196616 | tf_op jit(solution)/shard_map/ppermute | solution.py:78
  45.4 8.3 %collective-permute-start.4 = (f32[2,32,256]{2,1,0:T(8,128)S(1)}, f32[2,32,256]{2,1,0:T(8,128)S(1)}, u32[]{:S(2)}, u32[]{:S(2)}) collective-permute-start(f32[2,32,256]{2,1,0:T(8,128)S(1)} %pad_maximum_fusion.9), channel_id=1, source_target_pairs={{0,16},{8,24},{16,0},{24,8},{1,17},{9,25},{17,1},{25,9},{2,18},{10... | collective-permute-start | bytes 196616 | tf_op jit(solution)/shard_map/ppermute | solution.py:78
  46.1 8.8 %collective-permute-start.5 = (f32[2,32,256]{2,1,0:T(8,128)S(1)}, f32[2,32,256]{2,1,0:T(8,128)S(1)}, u32[]{:S(2)}, u32[]{:S(2)}) collective-permute-start(f32[2,32,256]{2,1,0:T(8,128)S(1)} %pad_maximum_fusion.10), channel_id=1, source_target_pairs={{0,24},{8,0},{16,8},{24,16},{1,25},{9,1},{17,9},{25,17},{2,26},{10... | collective-permute-start | bytes 196616 | tf_op jit(solution)/shard_map/ppermute | solution.py:78
  47.2 7.7 %collective-permute-start.13 = (f32[2,32,256]{2,1,0:T(8,128)S(1)}, f32[2,32,256]{2,1,0:T(8,128)S(1)}, u32[]{:S(2)}, u32[]{:S(2)}) collective-permute-start(f32[2,32,256]{2,1,0:T(8,128)S(1)} %pad_maximum_fusion.11), channel_id=1, source_target_pairs={{0,8},{8,16},{16,24},{24,0},{1,9},{9,17},{17,25},{25,1},{2,10},{10... | collective-permute-start | bytes 196616 | tf_op jit(solution)/shard_map/ppermute | solution.py:78
  52.8 4.7 %collective-permute-start.14 = (f32[2,32,256]{2,1,0:T(8,128)S(1)}, f32[2,32,256]{2,1,0:T(8,128)S(1)}, u32[]{:S(2)}, u32[]{:S(2)}) collective-permute-start(f32[2,32,256]{2,1,0:T(8,128)S(1)} %pad_maximum_fusion.12), channel_id=1, source_target_pairs={{0,16},{8,24},{16,0},{24,8},{1,17},{9,25},{17,1},{25,9},{2,18},{10... | collective-permute-start | bytes 196616 | tf_op jit(solution)/shard_map/ppermute | solution.py:78
  53.7 4.6 %collective-permute-start.15 = (f32[2,32,256]{2,1,0:T(8,128)S(1)}, f32[2,32,256]{2,1,0:T(8,128)S(1)}, u32[]{:S(2)}, u32[]{:S(2)}) collective-permute-start(f32[2,32,256]{2,1,0:T(8,128)S(1)} %pad_maximum_fusion.13), channel_id=1, source_target_pairs={{0,24},{8,0},{16,8},{24,16},{1,25},{9,1},{17,9},{25,17},{2,26},{10... | collective-permute-start | bytes 196616 | tf_op jit(solution)/shard_map/ppermute | solution.py:78
  54.9 5.7 %collective-permute-start.22 = (f32[2,32,256]{2,1,0:T(8,128)S(1)}, f32[2,32,256]{2,1,0:T(8,128)S(1)}, u32[]{:S(2)}, u32[]{:S(2)}) collective-permute-start(f32[2,32,256]{2,1,0:T(8,128)S(1)} %pad_maximum_fusion.15), channel_id=1, source_target_pairs={{0,16},{8,24},{16,0},{24,8},{1,17},{9,25},{17,1},{25,9},{2,18},{10... | collective-permute-start | bytes 196616 | tf_op jit(solution)/shard_map/ppermute | solution.py:78
  58.3 5.4 %collective-permute-start.29 = (f32[2,32,256]{2,1,0:T(8,128)S(1)}, f32[2,32,256]{2,1,0:T(8,128)S(1)}, u32[]{:S(2)}, u32[]{:S(2)}) collective-permute-start(f32[2,32,256]{2,1,0:T(8,128)S(1)} %pad_maximum_fusion.17), channel_id=1, source_target_pairs={{0,8},{8,16},{16,24},{24,0},{1,9},{9,17},{17,25},{25,1},{2,10},{10... | collective-permute-start | bytes 196616 | tf_op jit(solution)/shard_map/ppermute | solution.py:78
  59.4 5.3 %collective-permute-start.30 = (f32[2,32,256]{2,1,0:T(8,128)S(1)}, f32[2,32,256]{2,1,0:T(8,128)S(1)}, u32[]{:S(2)}, u32[]{:S(2)}) collective-permute-start(f32[2,32,256]{2,1,0:T(8,128)S(1)} %pad_maximum_fusion.18), channel_id=1, source_target_pairs={{0,16},{8,24},{16,0},{24,8},{1,17},{9,25},{17,1},{25,9},{2,18},{10... | collective-permute-start | bytes 196616 | tf_op jit(solution)/shard_map/ppermute | solution.py:78
  60.7 6.1 %collective-permute-start.31 = (f32[2,32,256]{2,1,0:T(8,128)S(1)}, f32[2,32,256]{2,1,0:T(8,128)S(1)}, u32[]{:S(2)}, u32[]{:S(2)}) collective-permute-start(f32[2,32,256]{2,1,0:T(8,128)S(1)} %pad_maximum_fusion.19), channel_id=1, source_target_pairs={{0,24},{8,0},{16,8},{24,16},{1,25},{9,1},{17,9},{25,17},{2,26},{10... | collective-permute-start | bytes 196616 | tf_op jit(solution)/shard_map/ppermute | solution.py:78
  61.1 32.5 %collective-permute-start.6 = (f32[2,128,256]{2,1,0:T(8,128)S(1)}, f32[2,128,256]{2,1,0:T(8,128)S(1)}, u32[]{:S(2)}, u32[]{:S(2)}) collective-permute-start(f32[2,128,256]{2,1,0:T(8,128)S(1)} %pad_maximum_fusion.4), channel_id=1, source_target_pairs={{0,2},{1,3},{2,0},{3,1},{4,6},{5,7},{6,4},{7,5},{8,10},{9,11},{10,... | collective-permute-start | bytes 786440 | tf_op jit(solution)/shard_map/ppermute | solution.py:78
  63.7 35.5 %collective-permute-start.16 = (f32[2,128,256]{2,1,0:T(8,128)S(1)}, f32[2,128,256]{2,1,0:T(8,128)S(1)}, u32[]{:S(2)}, u32[]{:S(2)}) collective-permute-start(f32[2,128,256]{2,1,0:T(8,128)S(1)} %pad_maximum_fusion.5), channel_id=1, source_target_pairs={{0,2},{1,3},{2,0},{3,1},{4,6},{5,7},{6,4},{7,5},{8,10},{9,11},{10,... | collective-permute-start | bytes 786440 | tf_op jit(solution)/shard_map/ppermute | solution.py:78
  64.7 40.1 %collective-permute-start.24 = (f32[2,128,256]{2,1,0:T(8,128)S(1)}, f32[2,128,256]{2,1,0:T(8,128)S(1)}, u32[]{:S(2)}, u32[]{:S(2)}) collective-permute-start(f32[2,128,256]{2,1,0:T(8,128)S(1)} %pad_maximum_fusion.6), channel_id=1, source_target_pairs={{0,2},{1,3},{2,0},{3,1},{4,6},{5,7},{6,4},{7,5},{8,10},{9,11},{10,... | collective-permute-start | bytes 786440 | tf_op jit(solution)/shard_map/ppermute | solution.py:78
  66.8 43.2 %collective-permute-start.32 = (f32[2,128,256]{2,1,0:T(8,128)S(1)}, f32[2,128,256]{2,1,0:T(8,128)S(1)}, u32[]{:S(2)}, u32[]{:S(2)}) collective-permute-start(f32[2,128,256]{2,1,0:T(8,128)S(1)} %pad_maximum_fusion.7), channel_id=1, source_target_pairs={{0,2},{1,3},{2,0},{3,1},{4,6},{5,7},{6,4},{7,5},{8,10},{9,11},{10,... | collective-permute-start | bytes 786440 | tf_op jit(solution)/shard_map/ppermute | solution.py:78
  70.3 40.4 %collective-permute-start.8 = (f32[2,256,512]{2,1,0:T(8,128)S(1)}, f32[2,256,512]{2,1,0:T(8,128)S(1)}, u32[]{:S(2)}, u32[]{:S(2)}) collective-permute-start(f32[2,256,512]{2,1,0:T(8,128)S(1)} %get-tuple-element.118), channel_id=1, source_target_pairs={{0,4},{4,0},{1,5},{5,1},{2,6},{6,2},{3,7},{7,3},{8,12},{12,8},{9,1... | collective-permute-start | bytes 3145736 | tf_op jit(solution)/shard_map/ppermute | solution.py:78
  115.9 21.3 %collective-permute-start.9 = (f32[128,2,256]{2,0,1:T(8,128)}, f32[128,2,256]{2,0,1:T(8,128)}, u32[]{:S(2)}, u32[]{:S(2)}) collective-permute-start(f32[128,2,256]{2,0,1:T(8,128)} %bitcast.1165), channel_id=1, source_target_pairs={{0,1},{1,0},{2,3},{3,2},{4,5},{5,4},{6,7},{7,6},{8,9},{9,8},{10,11... | collective-permute-start | bytes 786440 | tf_op jit(solution)/shard_map/ppermute | solution.py:78
  123.2 15.0 %collective-permute-start.17 = (f32[128,2,256]{2,0,1:T(8,128)}, f32[128,2,256]{2,0,1:T(8,128)}, u32[]{:S(2)}, u32[]{:S(2)}) collective-permute-start(f32[128,2,256]{2,0,1:T(8,128)} %bitcast.1164), channel_id=1, source_target_pairs={{0,1},{1,0},{2,3},{3,2},{4,5},{5,4},{6,7},{7,6},{8,9},{9,8},{10,11... | collective-permute-start | bytes 786440 | tf_op jit(solution)/shard_map/ppermute | solution.py:78
  131.1 8.4 %collective-permute-start.25 = (f32[128,2,256]{2,0,1:T(8,128)}, f32[128,2,256]{2,0,1:T(8,128)}, u32[]{:S(2)}, u32[]{:S(2)}) collective-permute-start(f32[128,2,256]{2,0,1:T(8,128)} %bitcast.1163), channel_id=1, source_target_pairs={{0,1},{1,0},{2,3},{3,2},{4,5},{5,4},{6,7},{7,6},{8,9},{9,8},{10,11... | collective-permute-start | bytes 786440 | tf_op jit(solution)/shard_map/ppermute | solution.py:78
  135.8 8.4 %collective-permute-start.33 = (f32[128,2,256]{2,0,1:T(8,128)S(1)}, f32[128,2,256]{2,0,1:T(8,128)S(1)}, u32[]{:S(2)}, u32[]{:S(2)}) collective-permute-start(f32[128,2,256]{2,0,1:T(8,128)S(1)} %bitcast.1177), channel_id=1, source_target_pairs={{0,1},{1,0},{2,3},{3,2},{4,5},{5,4},{6,7},{7,6},{8,9},{9,8},{10,11... | collective-permute-start | bytes 786440 | tf_op jit(solution)/shard_map/ppermute | solution.py:78
  (10 other events, 73.7 us)

commit v2 on v1

v2 whole, which is shorter than its diff:
```python
import functools
import math

import jax
import jax.numpy as jnp
import numpy as np
from jax import lax
from jax.experimental import pallas as pl
from jax.experimental.pallas import tpu as pltpu
from jax.sharding import PartitionSpec as P

WEIGHTS = (2, 4, 4, 4, 2)
AHEAD = 2
SUBLANES, LANES = 8, 128
VMEM_LIMIT = 40 * 2**20
ANYWHERE = pl.BlockSpec(memory_space=pl.ANY)
IN_VMEM = pl.BlockSpec(memory_space=pltpu.VMEM)
IN_HBM = pl.BlockSpec(memory_space=pltpu.HBM)
IN_SMEM = pl.BlockSpec(memory_space=pltpu.SMEM)


def chunk_sizes(units):
    if units % sum(WEIGHTS):
        return [SUBLANES] * units
    return [SUBLANES * weight * units // sum(WEIGHTS) for weight in WEIGHTS]


def angle_tables(points):
    cosine = [[1.0, 0.0, -1.0, 0.0][4 * r // points] if 4 * r % points == 0 else math.cos(2 * math.pi * r / points) for r in range(points)]
    sine = [[0.0, 1.0, 0.0, -1.0][4 * r // points] if 4 * r % points == 0 else math.sin(2 * math.pi * r / points) for r in range(points)]
    return np.array([cosine, sine], np.float32)


def times_i(value, power):
    real, imag = value
    return [(real, imag), (-imag, real), (-real, -imag), (imag, -real)][power % 4]


def add(left, right):
    return (left[0] + right[0], left[1] + right[1])


def subtract(left, right):
    return (left[0] - right[0], left[1] - right[1])


def twiddle(value, index, points, sign):
    if 4 * index % points == 0:
        return times_i(value, sign * (4 * index // points))
    angle = sign * 2.0 * math.pi * index / points
    cosine, sine = math.cos(angle), math.sin(angle)
    real, imag = value
    return (real * cosine - imag * sine, imag * cosine + real * sine)


def transform(values, sign):
    points = len(values)
    if points == 1:
        return values
    if points % 2:
        return [
            functools.reduce(add, [twiddle(value, at * out % points, points, sign) for at, value in enumerate(values)])
            for out in range(points)
        ]
    even, odd = transform(values[::2], sign), transform(values[1::2], sign)
    odd = [twiddle(value, at, points, sign) for at, value in enumerate(odd)]
    return [add(e, o) for e, o in zip(even, odd)] + [subtract(e, o) for e, o in zip(even, odd)]


def at_rows(ref, start, size):
    return ref.at[:, 0, pl.ds(pl.multiple_of(start, SUBLANES), size), :]


def pack_copies(points, own, sources, pieces, sem, base, step):
    copies = []
    for gap in range(1, points):
        start = base + lax.rem(own - gap + points, points) * step
        for at, source in enumerate(sources):
            copies.append(pltpu.make_async_copy(at_rows(source, start, step), pieces[gap - 1].at[at], sem.at[len(copies)]))
    return copies


def pack_kernel(points, base, step, *refs):
    sources, pieces, sem = refs[:3], refs[3:-1], refs[-1]
    copies = pack_copies(points, lax.axis_index("ka"), sources, pieces, sem, base, step)
    for copy in copies:
        copy.start()
    for copy in copies:
        copy.wait()


def energy_kernel(points, base, step, later, scale, *refs):
    tables, sources, received = refs[0], refs[1:4], refs[4 : 3 + points]
    rest = refs[3 + points :]
    sigmas, pieces = rest[:points], rest[points:-3]
    mine, sem, own_sem = rest[-3:]
    own = lax.axis_index("ka")
    own_copies = [
        pltpu.make_async_copy(at_rows(source, base + own * step, step), mine.at[at], own_sem.at[at])
        for at, source in enumerate(sources)
    ]
    copies = pack_copies(points, own, sources, pieces, sem, *later) if later else []
    for copy in own_copies + copies:
        copy.start()
    for copy in own_copies:
        copy.wait()
    cosines = [tables[0, lax.rem(own * r, points)] for r in range(points)]
    sines = [tables[1, lax.rem(own * r, points)] for r in range(points)]
    blocks = [mine, *received]
    across = mine.shape[-1] // LANES
    root = points**-0.5

    def tile(index, carry):
        spot = (
            pl.ds(pl.multiple_of(lax.div(index, across) * SUBLANES, SUBLANES), SUBLANES),
            pl.ds(pl.multiple_of(lax.rem(index, across) * LANES, LANES), LANES),
        )
        lesser, greater, screen = (
            transform([(block[at, 0, *spot], block[at, 1, *spot]) for block in blocks], 1) for at in range(3)
        )
        values = []
        for r in range(points):
            less, great, inter = lesser[r], greater[r], screen[r]
            polar_real = less[0] * great[1] - less[1] * great[0]
            polar_imag = less[0] * great[0] + less[1] * great[1]
            inter_real = inter[0] * cosines[r] - inter[1] * sines[r] + polar_real * root
            inter_imag = inter[1] * cosines[r] + inter[0] * sines[r] + polar_imag * root
            values.append(
                (
                    (less[0] * inter_imag + less[1] * inter_real) * -scale,
                    (less[0] * inter_real - less[1] * inter_imag) * scale,
                )
            )
        for out, (real, imag) in zip(sigmas, transform(values, -1)):
            out[0, *spot] = real
            out[1, *spot] = imag
        return carry

    lax.fori_loop(0, step // SUBLANES * across, tile, 0)
    for copy in copies:
        copy.wait()


def assemble_kernel(points, step, *refs):
    parts, out = refs[:points], refs[points]
    own = lax.axis_index("ka")
    for gap in range(points):
        start = pl.multiple_of(lax.rem(own - gap + points, points) * step, SUBLANES)
        out[:, pl.ds(start, step), :] = parts[gap][...]


def split(value):
    high = value.astype(jnp.bfloat16)
    return high, (value - high.astype(jnp.float32)).astype(jnp.bfloat16)


def right_kernel(row_parts, group, *refs):
    pieces, high, low = refs[: row_parts * group], refs[-2], refs[-1]
    row_at, half = lax.axis_index("tr"), lax.axis_index("tc") // group
    depth, cols = pieces[0].shape[1:]
    for part in range(row_parts):
        place = lax.rem(half - row_at + part + row_parts, row_parts) * depth
        upper = pl.ds(pl.multiple_of(place, depth), depth)
        lower = pl.ds(pl.multiple_of(place + row_parts * depth, depth), depth)
        for gap in range(group):
            piece = pieces[part * group + gap]
            first = pl.ds(gap * cols, cols)
            second = pl.ds((group + gap) * cols, cols)
            real, imag = split(piece[0]), split(piece[1])
            for out, real_part, imag_part in zip((high, low), real, imag):
                out[upper, first] = real_part
                out[lower, second] = real_part
                out[upper, second] = imag_part
                out[lower, first] = -imag_part


def product_kernel(row_parts, group, *refs):
    sides, high, low, outs = refs[:row_parts], refs[row_parts], refs[row_parts + 1], refs[row_parts + 2 :]
    left = jnp.concatenate([side[at] for at in (0, 1) for side in sides], axis=1)
    left_high, left_low = split(left)
    cols = outs[0].shape[-1]
    for at in range(2):
        for gap in range(group):
            spot = pl.ds((at * group + gap) * cols, cols)
            right_high, right_low = high[:, spot], low[:, spot]
            dot = functools.partial(jnp.dot, preferred_element_type=jnp.float32)
            outs[gap][at] = dot(left_high, right_high) + (dot(left_high, right_low) + dot(left_low, right_high))


def final_kernel(group, sizes, *refs):
    count = len(sizes) * group
    parts, less, collision, after = refs[:count], refs[count], refs[-2], refs[-1]
    start = 0
    for at, size in enumerate(sizes):
        rows = pl.ds(start, size)
        total = parts[at * group][...]
        for part in parts[at * group + 1 : (at + 1) * group]:
            total = total + part[...]
        collision[:, 0, rows, :] = total
        after[:, 0, rows, :] = less[:, 0, rows, :] + total
        start += size


def call(kernel, out_shapes, in_specs, out_specs, args, scratch=(), after=()):
    count, skipped = len(args), len(after)

    def ordered(*refs):
        kernel(*refs[:count], *refs[count + skipped :])

    return pl.pallas_call(
        ordered,
        out_shape=out_shapes,
        in_specs=in_specs + [ANYWHERE] * skipped,
        out_specs=out_specs,
        scratch_shapes=scratch,
        cost_estimate=pl.CostEstimate(flops=1, bytes_accessed=1, transcendentals=0),
        compiler_params=pltpu.CompilerParams(vmem_limit_bytes=VMEM_LIMIT),
    )(*args, *after)


def body(green_less, green_great, screened):
    momenta, row_parts, col_parts = lax.axis_size("ka"), lax.axis_size("tr"), lax.axis_size("tc")
    col_at = lax.axis_index("tc")
    rows, cols = green_less.shape[2], green_less.shape[3]
    group = col_parts // row_parts
    member = col_at % group
    sizes = chunk_sizes(rows // momenta // SUBLANES)
    bases = [momenta * sum(sizes[:at]) for at in range(len(sizes))]
    length = rows * row_parts
    f32 = functools.partial(jax.ShapeDtypeStruct, dtype=jnp.float32)
    bf16 = functools.partial(jax.ShapeDtypeStruct, dtype=jnp.bfloat16)
    inputs = (green_less, green_great, screened)
    copies = 3 * (momenta - 1)
    scale = momenta**-1.5 * length**-0.5
    tables = jnp.asarray(angle_tables(momenta))

    def shift(value, axis, gap):
        if axis == "group":
            moves = [
                (part * group + m, part * group + (m + gap) % group) for part in range(row_parts) for m in range(group)
            ]
            return lax.ppermute(value, "tc", moves)
        if axis == "half":
            return lax.ppermute(value, "tc", [(j, (j + group * gap) % col_parts) for j in range(col_parts)])
        count = lax.axis_size(axis)
        return lax.ppermute(value, axis, [(s, (s + gap) % count) for s in range(count)])

    def send_pieces(pieces):
        return [shift(piece, "ka", -gap) for gap, piece in enumerate(pieces, 1)]

    def pack(at, after):
        step = sizes[at]
        return call(
            functools.partial(pack_kernel, momenta, bases[at], step),
            [f32((3, 2, step, cols))] * (momenta - 1),
            [IN_HBM] * 3,
            [ANYWHERE] * (momenta - 1),
            inputs,
            [pltpu.SemaphoreType.DMA((copies,))],
            after,
        )

    def energy(at, after):
        step, next_at = sizes[at], at + AHEAD
        later = (bases[next_at], sizes[next_at]) if next_at < len(sizes) else None
        outs = call(
            functools.partial(energy_kernel, momenta, bases[at], step, later, scale),
            [f32((2, step, cols))] * momenta + ([f32((3, 2, later[1], cols))] * (momenta - 1) if later else []),
            [IN_SMEM] + [IN_HBM] * 3 + [IN_VMEM] * (momenta - 1),
            [IN_VMEM] * momenta + ([ANYWHERE] * (momenta - 1) if later else []),
            (tables, *inputs, *received[at]),
            [
                pltpu.VMEM((3, 2, step, cols), jnp.float32),
                pltpu.SemaphoreType.DMA((copies,)),
                pltpu.SemaphoreType.DMA((3,)),
            ],
            after,
        )
        sigmas, pieces = outs[:momenta], outs[momenta:]
        parts = [sigmas[0]] + [shift(sigmas[gap], "ka", gap) for gap in range(1, momenta)]
        if later:
            received.append(send_pieces(pieces))
        return parts

    def assemble(at, parts, after):
        step = sizes[at]
        mine = call(
            functools.partial(assemble_kernel, momenta, step),
            f32((2, momenta * step, cols)),
            [IN_VMEM] * momenta,
            IN_VMEM,
            parts,
            (),
            after,
        )
        return [mine] + [shift(mine, "half", gap) for gap in range(1, row_parts)]

    def product(at, lefts, after):
        outs = call(
            functools.partial(product_kernel, row_parts, group),
            [f32((2, momenta * sizes[at], cols))] * group,
            [IN_VMEM] * (row_parts + 2),
            [IN_VMEM] * group,
            (*lefts, *right),
            (),
            after,
        )
        return [outs[0]] + [shift(outs[gap], "group", -gap) for gap in range(1, group)]

    received, last = [], ()
    for at in range(min(AHEAD, len(sizes))):
        pieces = pack(at, last)
        received.append(send_pieces(pieces))
        last = pieces[:1]

    blocks = green_less[:, 0].reshape(2, group, cols, cols)
    sides = [lax.dynamic_index_in_dim(blocks, member, 1, False)]
    for gap in range(1, group):
        sides.append(shift(lax.dynamic_index_in_dim(blocks, (member + gap) % group, 1, False), "group", gap))
    panels = list(sides)
    for gap in range(1, row_parts):
        panels += [shift(side, "tr", gap) for side in sides]
    extent = 2 * row_parts * cols

    lefts, results, right = [], [], None
    for at in range(len(sizes) + 1):
        if at < len(sizes):
            parts = energy(at, last)
            lefts.append(assemble(at, parts, ()))
            last = lefts[at][:1]
        if at == 1:
            right = call(
                functools.partial(right_kernel, row_parts, group),
                [bf16((extent, 2 * group * cols))] * 2,
                [IN_VMEM] * len(panels),
                [IN_VMEM] * 2,
                panels,
                (),
                last,
            )
        if at >= 1:
            results.append(product(at - 1, lefts[at - 1], last))
            last = results[-1][:1]

    return call(
        functools.partial(final_kernel, group, [momenta * step for step in sizes]),
        [f32(green_less.shape)] * 2,
        [IN_VMEM] * (len(sizes) * group + 1),
        [IN_VMEM] * 2,
        (*[part for result in results for part in result], green_less),
    )


def solution(mesh):
    spec = P(None, "ka", "tr", "tc")
    return jax.shard_map(body, mesh=mesh, in_specs=(spec,) * 3, out_specs=(spec,) * 2, check_vma=False)
```

time: 148 us -> 136 us (0.919); the launches traced: 147 us -> 136 us
  waiting for transfers between devices: 41.6 us -> 82.3 us
  other arithmetic: 34.9 us -> 0 us
  local copies, waits for them, and re-layouts: 21.6 us -> 2.68 us
  Pallas kernels: 0 us -> 14.4 us
  matrix products: 12.5 us -> 0 us
    ppermute x34 -> x43, waiting for transfers between devices: 41.6 us -> 82.3 us  [the longest x5 32.3 us: shift(): lax.ppermute(value, 'tc', [(j, (j + group * gap) % col_parts) for j in ra...]
    add x24 -> x0, other arithmetic: 28.8 us -> none  [the longest x20 25.8 us: add(): return (left[0] + right[0], left[1] + right[1])]
    pallas_call x0 -> x19, Pallas kernels: none -> 14.4 us  [call(): pl.pallas_call(ordered, out_shape=out_shapes, in_specs=in_specs + [ANYWHE...]
    dot_general x4 -> x0, matrix products: 12.5 us -> none  [body(): jnp.dot(left, right, precision=lax.Precision.HIGH, preferred_element_type...]
    squeeze x13 -> x1, local copies, waits for them, and re-layouts: 9.25 us -> 1.43 us  [body(): lax.dynamic_index_in_dim(blocks, (member + gap) % group, 1, False)]
    slice x7 -> x0, local copies, waits for them, and re-layouts: 4.16 us -> none  [the longest x4 1.63 us: body(): total = product[:, :, 0]]
    reshape x4 -> x0, local copies, waits for them, and re-layouts: 3.84 us -> none  [body(): product = product.reshape(momenta * step, 2, group, cols)]
    another operation x14 -> x0, other arithmetic: 2.4 us -> none  [the longest x1 2.23 us: body(): jnp.stack([less, green_great[:, 0], screened[:, 0]])]
  transfers between devices with their start and end apart: 34 -> 43, of which waited for: 8 -> 19; matrix products, arithmetic and copies ran while one was open for 38% -> 0% of each run, Pallas kernels for 0% -> 9%
where the time goes in v2:
time: 136 us
  waiting for transfers between devices  82.3 us (61%)
  starting transfers between devices  35.7 us (26%)
  Pallas kernels  14.4 us (11%)
  local copies, waits for them, and re-layouts  2.68 us (2%)
    ppermute x5, waiting for transfers between devices, shift(): lax.ppermute(value, 'tc', [(j, (j + group * gap) % col_parts) for j in ra...  32.3 us
    ppermute x32, waiting for transfers between devices, shift(): lax.ppermute(value, axis, [(s, (s + gap) % count) for s in range(count)])  28.4 us
    ppermute x32, starting transfers between devices, shift(): lax.ppermute(value, axis, [(s, (s + gap) % count) for s in range(count)])  25.7 us
    ppermute x6, waiting for transfers between devices, shift(): return lax.ppermute(value, 'tc', moves)  21.5 us
    pallas_call x19, Pallas kernels, call(): pl.pallas_call(ordered, out_shape=out_shapes, in_specs=in_specs + [ANYWHE...  14.4 us
    ppermute x6, starting transfers between devices, shift(): return lax.ppermute(value, 'tc', moves)  6.76 us
    ppermute x5, starting transfers between devices, shift(): lax.ppermute(value, 'tc', [(j, (j + group * gap) % col_parts) for j in ra...  3.23 us
  transfers between devices with their start and end apart: 43, of which 19 were waited for; matrix products, arithmetic and copies ran while one was open for 0% of the time, Pallas kernels for 9%

profile of v2, /device:TPU:0, one launch (start us, length us, event | category | flops | bytes accessed | tf_op | source)
XLA Modules:
  0.0 136.1 jit_solution(7943205241096556089)
XLA Ops:
  0.7 1.4 %dynamic-slice_bitcast_fusion = (f32[2,256,256]{2,1,0:T(8,128)S(1)}, f32[2,256,256]{2,1,0:T(8,128)S(1)}) fusion(f32[2,2,256,256]{3,2,1,0:T(8,128)} %bitcast.9, s32[]{:T(128)S(6)} %select_n.21, s32[]{:T(128)S(6)} %select_n.19), kind=kLoop, calls=%fused_computation | loop fusion | bytes 2097160 | tf_op jit(solution)/shard_map/jit(dynamic_index_in_dim)/squeeze | solution.py:319
  2.1 3.1 %collective-permute-start.7 = (f32[2,256,256]{2,1,0:T(8,128)S(1)}, f32[2,256,256]{2,1,0:T(8,128)S(1)}, u32[]{:S(2)}, u32[]{:S(2)}) collective-permute-start(f32[2,256,256]{2,1,0:T(8,128)S(1)} %get-tuple-element.96), channel_id=1, source_target_pairs={{0,1},{1,0},{2,3},{3,2},{4,5},{5,4},{6,7},{7,6},{8,9},{9,8},{10,11... | collective-permute-start | bytes 1572872 | tf_op jit(solution)/shard_map/ppermute | solution.py:242
  5.2 1.5 %collective-permute-start.8 = (f32[2,256,256]{2,1,0:T(8,128)S(1)}, f32[2,256,256]{2,1,0:T(8,128)S(1)}, u32[]{:S(2)}, u32[]{:S(2)}) collective-permute-start(f32[2,256,256]{2,1,0:T(8,128)S(1)} %get-tuple-element.97.refs_0_), channel_id=1, source_target_pairs={{0,4},{4,0},{1,5},{5,1},{2,6},{6,2},{3,7},{7,3},{8,12},{12,8},{9,1... | collective-permute-start | bytes 1572872 | tf_op jit(solution)/shard_map/ppermute | solution.py:246
  10.0 7.1 %collective-permute-done.7.refs_1_ = f32[2,256,256]{2,1,0:T(8,128)S(1)} collective-permute-done((f32[2,256,256]{2,1,0:T(8,128)S(1)}, f32[2,256,256]{2,1,0:T(8,128)S(1)}, u32[]{:S(2)}, u32[]{:S(2)}) %collective-permute-start.7) | collective-permute-done | bytes 524320 | tf_op jit(solution)/shard_map/ppermute | solution.py:242
  17.1 1.7 %collective-permute-start.9 = (f32[2,256,256]{2,1,0:T(8,128)S(1)}, f32[2,256,256]{2,1,0:T(8,128)S(1)}, u32[]{:S(2)}, u32[]{:S(2)}) collective-permute-start(f32[2,256,256]{2,1,0:T(8,128)S(1)} %collective-permute-done.7.refs_1_), channel_id=1, source_target_pairs={{0,4},{4,0},{1,5},{5,1},{2,6},{6,2},{3,7},{7,3},{8,12},{12,8},{9,1... | collective-permute-start | bytes 1572872 | tf_op jit(solution)/shard_map/ppermute | solution.py:246
  19.3 1.3 shard_map.61
  20.7 1.6 %collective-permute-start.4 = (f32[2,16,256]{2,1,0:T(8,128)S(1)}, f32[2,16,256]{2,1,0:T(8,128)S(1)}, u32[]{:S(2)}, u32[]{:S(2)}) collective-permute-start(f32[2,16,256]{2,1,0:T(8,128)S(1)} %get-tuple-element.55), channel_id=1, source_target_pairs={{0,16},{8,24},{16,0},{24,8},{1,17},{9,25},{17,1},{25,9},{2,18},{10... | collective-permute-start | bytes 98312 | tf_op jit(solution)/shard_map/ppermute | solution.py:246
  22.3 1.4 %collective-permute-start.5 = (f32[2,16,256]{2,1,0:T(8,128)S(1)}, f32[2,16,256]{2,1,0:T(8,128)S(1)}, u32[]{:S(2)}, u32[]{:S(2)}) collective-permute-start(f32[2,16,256]{2,1,0:T(8,128)S(1)} %get-tuple-element.56), channel_id=1, source_target_pairs={{0,24},{8,0},{16,8},{24,16},{1,25},{9,1},{17,9},{25,17},{2,26},{10... | collective-permute-start | bytes 98312 | tf_op jit(solution)/shard_map/ppermute | solution.py:246
  24.7 1.5 %collective-permute-start.11 = (f32[3,2,32,256]{3,2,1,0:T(8,128)S(1)}, f32[3,2,32,256]{3,2,1,0:T(8,128)S(1)}, u32[]{:S(2)}, u32[]{:S(2)}) collective-permute-start(f32[3,2,32,256]{3,2,1,0:T(8,128)S(1)} %get-tuple-element.57), channel_id=1, source_target_pairs={{0,16},{8,24},{16,0},{24,8},{1,17},{9,25},{17,1},{25,9},{2,18},{10... | collective-permute-start | bytes 589832 | tf_op jit(solution)/shard_map/ppermute | solution.py:246
  26.3 2.0 %collective-permute-done.10.refs_4_ = f32[3,2,32,256]{3,2,1,0:T(8,128)S(1)} collective-permute-done((f32[3,2,32,256]{3,2,1,0:T(8,128)S(1)}, f32[3,2,32,256]{3,2,1,0:T(8,128)S(1)}, u32[]{:S(2)}, u32[]{:S(2)}) %collective-permute-start.10) | collective-permute-done | bytes 196640 | tf_op jit(solution)/shard_map/ppermute | solution.py:246
  28.2 6.4 %collective-permute-done.11.refs_5_ = f32[3,2,32,256]{3,2,1,0:T(8,128)S(1)} collective-permute-done((f32[3,2,32,256]{3,2,1,0:T(8,128)S(1)}, f32[3,2,32,256]{3,2,1,0:T(8,128)S(1)}, u32[]{:S(2)}, u32[]{:S(2)}) %collective-permute-start.11) | collective-permute-done | bytes 196640 | tf_op jit(solution)/shard_map/ppermute | solution.py:246
  35.5 1.5 %shard_map.63 = (f32[2,32,256]{2,1,0:T(8,128)S(1)}, f32[2,32,256]{2,1,0:T(8,128)S(1)}, f32[2,32,256]{2,1,0:T(8,128)S(1)}, f32[2,32,256]{2,1,0:T(8,128)S(1)}, f32...) custom-call(f32[2,4]{1,0:T(2,128)S(1)} %copy-done.4, ...), custom_call_target="tpu_custom_call" | custom-call | flops 1 | bytes 1 | tf_op jit(solution)/shard_map/pallas_call | solution.py:210
  37.7 1.4 %collective-permute-start.15 = (f32[2,32,256]{2,1,0:T(8,128)S(1)}, f32[2,32,256]{2,1,0:T(8,128)S(1)}, u32[]{:S(2)}, u32[]{:S(2)}) collective-permute-start(f32[2,32,256]{2,1,0:T(8,128)S(1)} %get-tuple-element.62), channel_id=1, source_target_pairs={{0,24},{8,0},{16,8},{24,16},{1,25},{9,1},{17,9},{25,17},{2,26},{10... | collective-permute-start | bytes 196616 | tf_op jit(solution)/shard_map/ppermute | solution.py:246
  39.1 1.8 %collective-permute-done.13.refs_1_ = f32[2,32,256]{2,1,0:T(8,128)S(1)} collective-permute-done((f32[2,32,256]{2,1,0:T(8,128)S(1)}, f32[2,32,256]{2,1,0:T(8,128)S(1)}, u32[]{:S(2)}, u32[]{:S(2)}) %collective-permute-start.13) | collective-permute-done | bytes 65568 | tf_op jit(solution)/shard_map/ppermute | solution.py:246
  42.7 2.6 %collective-permute-start.6 = (f32[2,64,256]{2,1,0:T(8,128)S(1)}, f32[2,64,256]{2,1,0:T(8,128)S(1)}, u32[]{:S(2)}, u32[]{:S(2)}) collective-permute-start(f32[2,64,256]{2,1,0:T(8,128)S(1)} %shard_map.62.refs_7_.refs_0_), channel_id=1, source_target_pairs={{0,2},{1,3},{2,0},{3,1},{4,6},{5,7},{6,4},{7,5},{8,10},{9,11},{10,... | collective-permute-start | bytes 393224 | tf_op jit(solution)/shard_map/ppermute | solution.py:244
  46.3 11.6 %collective-permute-done.6.refs_1_ = f32[2,64,256]{2,1,0:T(8,128)S(1)} collective-permute-done((f32[2,64,256]{2,1,0:T(8,128)S(1)}, f32[2,64,256]{2,1,0:T(8,128)S(1)}, u32[]{:S(2)}, u32[]{:S(2)}) %collective-permute-start.6) | collective-permute-done | bytes 131104 | tf_op jit(solution)/shard_map/ppermute | solution.py:244
  59.1 1.3 shard_map.67
  62.3 1.9 %collective-permute-start.27 = (f32[3,2,32,256]{3,2,1,0:T(8,128)S(1)}, f32[3,2,32,256]{3,2,1,0:T(8,128)S(1)}, u32[]{:S(2)}, u32[]{:S(2)}) collective-permute-start(f32[3,2,32,256]{3,2,1,0:T(8,128)S(1)} %get-tuple-element.77), channel_id=1, source_target_pairs={{0,16},{8,24},{16,0},{24,8},{1,17},{9,25},{17,1},{25,9},{2,18},{10... | collective-permute-start | bytes 589832 | tf_op jit(solution)/shard_map/ppermute | solution.py:246
  64.2 2.3 %collective-permute-start.22 = (f32[2,32,256]{2,1,0:T(8,128)S(1)}, f32[2,32,256]{2,1,0:T(8,128)S(1)}, u32[]{:S(2)}, u32[]{:S(2)}) collective-permute-start(f32[2,32,256]{2,1,0:T(8,128)S(1)} %get-tuple-element.72), channel_id=1, source_target_pairs={{0,16},{8,24},{16,0},{24,8},{1,17},{9,25},{17,1},{25,9},{2,18},{10... | collective-permute-start | bytes 196616 | tf_op jit(solution)/shard_map/ppermute | solution.py:246
  66.5 8.5 %collective-permute-done.22.refs_2_ = f32[2,32,256]{2,1,0:T(8,128)S(1)} collective-permute-done((f32[2,32,256]{2,1,0:T(8,128)S(1)}, f32[2,32,256]{2,1,0:T(8,128)S(1)}, u32[]{:S(2)}, u32[]{:S(2)}) %collective-permute-start.22) | collective-permute-done | bytes 65568 | tf_op jit(solution)/shard_map/ppermute | solution.py:246
  75.4 1.9 %collective-permute-done.23.refs_3_ = f32[2,32,256]{2,1,0:T(8,128)S(1)} collective-permute-done((f32[2,32,256]{2,1,0:T(8,128)S(1)}, f32[2,32,256]{2,1,0:T(8,128)S(1)}, u32[]{:S(2)}, u32[]{:S(2)}) %collective-permute-start.23) | collective-permute-done | bytes 65568 | tf_op jit(solution)/shard_map/ppermute | solution.py:246
  82.0 1.3 collective-permute-done.29.refs_1_
  83.3 1.6 %collective-permute-done.30.refs_2_ = f32[2,32,256]{2,1,0:T(8,128)S(1)} collective-permute-done((f32[2,32,256]{2,1,0:T(8,128)S(1)}, f32[2,32,256]{2,1,0:T(8,128)S(1)}, u32[]{:S(2)}, u32[]{:S(2)}) %collective-permute-start.30) | collective-permute-done | bytes 65568 | tf_op jit(solution)/shard_map/ppermute | solution.py:246
  85.1 1.2 collective-permute-start.34
  87.2 15.7 %collective-permute-done.25.refs_1_ = f32[2,128,256]{2,1,0:T(8,128)S(1)} collective-permute-done((f32[2,128,256]{2,1,0:T(8,128)S(1)}, f32[2,128,256]{2,1,0:T(8,128)S(1)}, u32[]{:S(2)}, u32[]{:S(2)}) %collective-permute-start.25) | collective-permute-done | bytes 262176 | tf_op jit(solution)/shard_map/ppermute | solution.py:244
  105.9 1.4 %collective-permute-start.39 = (f32[2,16,256]{2,1,0:T(8,128)S(1)}, f32[2,16,256]{2,1,0:T(8,128)S(1)}, u32[]{:S(2)}, u32[]{:S(2)}) collective-permute-start(f32[2,16,256]{2,1,0:T(8,128)S(1)} %get-tuple-element.91), channel_id=1, source_target_pairs={{0,24},{8,0},{16,8},{24,16},{1,25},{9,1},{17,9},{25,17},{2,26},{10... | collective-permute-start | bytes 98312 | tf_op jit(solution)/shard_map/ppermute | solution.py:246
  109.3 1.5 %collective-permute-start.32 = (f32[2,128,256]{2,1,0:T(8,128)S(1)}, f32[2,128,256]{2,1,0:T(8,128)S(1)}, u32[]{:S(2)}, u32[]{:S(2)}) collective-permute-start(f32[2,128,256]{2,1,0:T(8,128)S(1)} %get-tuple-element.84), channel_id=1, source_target_pairs={{0,1},{1,0},{2,3},{3,2},{4,5},{5,4},{6,7},{7,6},{8,9},{9,8},{10,11... | collective-permute-start | bytes 786440 | tf_op jit(solution)/shard_map/ppermute | solution.py:242
  112.5 1.4 %collective-permute-start.16 = (f32[2,64,256]{2,1,0:T(8,128)S(1)}, f32[2,64,256]{2,1,0:T(8,128)S(1)}, u32[]{:S(2)}, u32[]{:S(2)}) collective-permute-start(f32[2,64,256]{2,1,0:T(8,128)S(1)} %get-tuple-element.66), channel_id=1, source_target_pairs={{0,1},{1,0},{2,3},{3,2},{4,5},{5,4},{6,7},{7,6},{8,9},{9,8},{10,11... | collective-permute-start | bytes 393224 | tf_op jit(solution)/shard_map/ppermute | solution.py:242
  113.9 5.0 %collective-permute-done.41.refs_1_ = f32[2,64,256]{2,1,0:T(8,128)S(1)} collective-permute-done((f32[2,64,256]{2,1,0:T(8,128)S(1)}, f32[2,64,256]{2,1,0:T(8,128)S(1)}, u32[]{:S(2)}, u32[]{:S(2)}) %collective-permute-start.41) | collective-permute-done | bytes 131104 | tf_op jit(solution)/shard_map/ppermute | solution.py:244
  120.2 13.0 %collective-permute-done.16.refs_1_ = f32[2,64,256]{2,1,0:T(8,128)S(1)} collective-permute-done((f32[2,64,256]{2,1,0:T(8,128)S(1)}, f32[2,64,256]{2,1,0:T(8,128)S(1)}, u32[]{:S(2)}, u32[]{:S(2)}) %collective-permute-start.16) | collective-permute-done | bytes 131104 | tf_op jit(solution)/shard_map/ppermute | solution.py:242
  133.2 1.4 %collective-permute-done.42.refs_9_ = f32[2,64,256]{2,1,0:T(8,128)S(1)} collective-permute-done((f32[2,64,256]{2,1,0:T(8,128)S(1)}, f32[2,64,256]{2,1,0:T(8,128)S(1)}, u32[]{:S(2)}, u32[]{:S(2)}) %collective-permute-start.42) | collective-permute-done | bytes 131104 | tf_op jit(solution)/shard_map/ppermute | solution.py:242
  134.6 1.5 %shard_map.77 = (f32[2,1,512,256]{3,2,1,0:T(8,128)}, f32[2,1,512,256]{3,2,1,0:T(8,128)}) custom-call(f32[2,64,256]{2,1,0:T(8,128)S(1)} %get-tuple-element.65.refs_7_.refs_0_, f32[2,64,256]{2,1,0:T(8,128)S(1)} %collective-permute-done.16.refs_1_, f32[2,128,256]{2,1,0:T(8,128)S(1)} %get-tuple-element.74.refs_7_.refs_2_, ...), custom_call_target="tpu_custom_call" | custom-call | flops 1 | bytes 1 | tf_op jit(solution)/shard_map/pallas_call | solution.py:210
  (84 shorter events, 26.3 us)
Async XLA Ops:
  2.1 15.0 %collective-permute-start.7 = (f32[2,256,256]{2,1,0:T(8,128)S(1)}, f32[2,256,256]{2,1,0:T(8,128)S(1)}, u32[]{:S(2)}, u32[]{:S(2)}) collective-permute-start(f32[2,256,256]{2,1,0:T(8,128)S(1)} %get-tuple-element.96), channel_id=1, source_target_pairs={{0,1},{1,0},{2,3},{3,2},{4,5},{5,4},{6,7},{7,6},{8,9},{9,8},{10,11... | collective-permute-start | bytes 1572872 | tf_op jit(solution)/shard_map/ppermute | solution.py:242
  5.2 37.5 %collective-permute-start.8 = (f32[2,256,256]{2,1,0:T(8,128)S(1)}, f32[2,256,256]{2,1,0:T(8,128)S(1)}, u32[]{:S(2)}, u32[]{:S(2)}) collective-permute-start(f32[2,256,256]{2,1,0:T(8,128)S(1)} %get-tuple-element.97.refs_0_), channel_id=1, source_target_pairs={{0,4},{4,0},{1,5},{5,1},{2,6},{6,2},{3,7},{7,3},{8,12},{12,8},{9,1... | collective-permute-start | bytes 1572872 | tf_op jit(solution)/shard_map/ppermute | solution.py:246
  8.2 11.0 %collective-permute-start = (f32[3,2,16,256]{3,2,1,0:T(8,128)S(1)}, f32[3,2,16,256]{3,2,1,0:T(8,128)S(1)}, u32[]{:S(2)}, u32[]{:S(2)}) collective-permute-start(f32[3,2,16,256]{3,2,1,0:T(8,128)S(1)} %get-tuple-element.49.refs_3_), channel_id=1, source_target_pairs={{0,24},{8,0},{16,8},{24,16},{1,25},{9,1},{17,9},{25,17},{2,26},{10... | collective-permute-start | bytes 294920 | tf_op jit(solution)/shard_map/ppermute | solution.py:246
  8.7 10.6 %collective-permute-start.1 = (f32[3,2,16,256]{3,2,1,0:T(8,128)S(1)}, f32[3,2,16,256]{3,2,1,0:T(8,128)S(1)}, u32[]{:S(2)}, u32[]{:S(2)}) collective-permute-start(f32[3,2,16,256]{3,2,1,0:T(8,128)S(1)} %get-tuple-element.50), channel_id=1, source_target_pairs={{0,16},{8,24},{16,0},{24,8},{1,17},{9,25},{17,1},{25,9},{2,18},{10... | collective-permute-start | bytes 294920 | tf_op jit(solution)/shard_map/ppermute | solution.py:246
  9.9 9.4 %collective-permute-start.2 = (f32[3,2,16,256]{3,2,1,0:T(8,128)S(1)}, f32[3,2,16,256]{3,2,1,0:T(8,128)S(1)}, u32[]{:S(2)}, u32[]{:S(2)}) collective-permute-start(f32[3,2,16,256]{3,2,1,0:T(8,128)S(1)} %get-tuple-element.51), channel_id=1, source_target_pairs={{0,8},{8,16},{16,24},{24,0},{1,9},{9,17},{17,25},{25,1},{2,10},{10... | collective-permute-start | bytes 294920 | tf_op jit(solution)/shard_map/ppermute | solution.py:246
  17.1 28.2 %collective-permute-start.9 = (f32[2,256,256]{2,1,0:T(8,128)S(1)}, f32[2,256,256]{2,1,0:T(8,128)S(1)}, u32[]{:S(2)}, u32[]{:S(2)}) collective-permute-start(f32[2,256,256]{2,1,0:T(8,128)S(1)} %collective-permute-done.7.refs_1_), channel_id=1, source_target_pairs={{0,4},{4,0},{1,5},{5,1},{2,6},{6,2},{3,7},{7,3},{8,12},{12,8},{9,1... | collective-permute-start | bytes 1572872 | tf_op jit(solution)/shard_map/ppermute | solution.py:246
  24.7 9.9 %collective-permute-start.11 = (f32[3,2,32,256]{3,2,1,0:T(8,128)S(1)}, f32[3,2,32,256]{3,2,1,0:T(8,128)S(1)}, u32[]{:S(2)}, u32[]{:S(2)}) collective-permute-start(f32[3,2,32,256]{3,2,1,0:T(8,128)S(1)} %get-tuple-element.57), channel_id=1, source_target_pairs={{0,16},{8,24},{16,0},{24,8},{1,17},{9,25},{17,1},{25,9},{2,18},{10... | collective-permute-start | bytes 589832 | tf_op jit(solution)/shard_map/ppermute | solution.py:246
  26.2 9.3 %collective-permute-start.12 = (f32[3,2,32,256]{3,2,1,0:T(8,128)S(1)}, f32[3,2,32,256]{3,2,1,0:T(8,128)S(1)}, u32[]{:S(2)}, u32[]{:S(2)}) collective-permute-start(f32[3,2,32,256]{3,2,1,0:T(8,128)S(1)} %get-tuple-element.58), channel_id=1, source_target_pairs={{0,8},{8,16},{16,24},{24,0},{1,9},{9,17},{17,25},{25,1},{2,10},{10... | collective-permute-start | bytes 589832 | tf_op jit(solution)/shard_map/ppermute | solution.py:246
  37.1 5.0 %collective-permute-start.14 = (f32[2,32,256]{2,1,0:T(8,128)S(1)}, f32[2,32,256]{2,1,0:T(8,128)S(1)}, u32[]{:S(2)}, u32[]{:S(2)}) collective-permute-start(f32[2,32,256]{2,1,0:T(8,128)S(1)} %get-tuple-element.61), channel_id=1, source_target_pairs={{0,16},{8,24},{16,0},{24,8},{1,17},{9,25},{17,1},{25,9},{2,18},{10... | collective-permute-start | bytes 196616 | tf_op jit(solution)/shard_map/ppermute | solution.py:246
  37.7 4.6 %collective-permute-start.15 = (f32[2,32,256]{2,1,0:T(8,128)S(1)}, f32[2,32,256]{2,1,0:T(8,128)S(1)}, u32[]{:S(2)}, u32[]{:S(2)}) collective-permute-start(f32[2,32,256]{2,1,0:T(8,128)S(1)} %get-tuple-element.62), channel_id=1, source_target_pairs={{0,24},{8,0},{16,8},{24,16},{1,25},{9,1},{17,9},{25,17},{2,26},{10... | collective-permute-start | bytes 196616 | tf_op jit(solution)/shard_map/ppermute | solution.py:246
  40.8 18.3 %collective-permute-start.18 = (f32[3,2,32,256]{3,2,1,0:T(8,128)S(1)}, f32[3,2,32,256]{3,2,1,0:T(8,128)S(1)}, u32[]{:S(2)}, u32[]{:S(2)}) collective-permute-start(f32[3,2,32,256]{3,2,1,0:T(8,128)S(1)} %get-tuple-element.67), channel_id=1, source_target_pairs={{0,24},{8,0},{16,8},{24,16},{1,25},{9,1},{17,9},{25,17},{2,26},{10... | collective-permute-start | bytes 589832 | tf_op jit(solution)/shard_map/ppermute | solution.py:246
  42.1 17.1 %collective-permute-start.19 = (f32[3,2,32,256]{3,2,1,0:T(8,128)S(1)}, f32[3,2,32,256]{3,2,1,0:T(8,128)S(1)}, u32[]{:S(2)}, u32[]{:S(2)}) collective-permute-start(f32[3,2,32,256]{3,2,1,0:T(8,128)S(1)} %get-tuple-element.68), channel_id=1, source_target_pairs={{0,16},{8,24},{16,0},{24,8},{1,17},{9,25},{17,1},{25,9},{2,18},{10... | collective-permute-start | bytes 589832 | tf_op jit(solution)/shard_map/ppermute | solution.py:246
  42.3 16.9 %collective-permute-start.20 = (f32[3,2,32,256]{3,2,1,0:T(8,128)S(1)}, f32[3,2,32,256]{3,2,1,0:T(8,128)S(1)}, u32[]{:S(2)}, u32[]{:S(2)}) collective-permute-start(f32[3,2,32,256]{3,2,1,0:T(8,128)S(1)} %get-tuple-element.69), channel_id=1, source_target_pairs={{0,8},{8,16},{16,24},{24,0},{1,9},{9,17},{17,25},{25,1},{2,10},{10... | collective-permute-start | bytes 589832 | tf_op jit(solution)/shard_map/ppermute | solution.py:246
  42.7 15.2 %collective-permute-start.6 = (f32[2,64,256]{2,1,0:T(8,128)S(1)}, f32[2,64,256]{2,1,0:T(8,128)S(1)}, u32[]{:S(2)}, u32[]{:S(2)}) collective-permute-start(f32[2,64,256]{2,1,0:T(8,128)S(1)} %shard_map.62.refs_7_.refs_0_), channel_id=1, source_target_pairs={{0,2},{1,3},{2,0},{3,1},{4,6},{5,7},{6,4},{7,5},{8,10},{9,11},{10,... | collective-permute-start | bytes 393224 | tf_op jit(solution)/shard_map/ppermute | solution.py:244
  45.3 32.0 %collective-permute-start.17 = (f32[2,128,256]{2,1,0:T(8,128)S(1)}, f32[2,128,256]{2,1,0:T(8,128)S(1)}, u32[]{:S(2)}, u32[]{:S(2)}) collective-permute-start(f32[2,128,256]{2,1,0:T(8,128)S(1)} %shard_map.64.refs_4_.refs_0_), channel_id=1, source_target_pairs={{0,2},{1,3},{2,0},{3,1},{4,6},{5,7},{6,4},{7,5},{8,10},{9,11},{10,... | collective-permute-start | bytes 786440 | tf_op jit(solution)/shard_map/ppermute | solution.py:244
  61.6 16.7 %collective-permute-start.26 = (f32[3,2,32,256]{3,2,1,0:T(8,128)S(1)}, f32[3,2,32,256]{3,2,1,0:T(8,128)S(1)}, u32[]{:S(2)}, u32[]{:S(2)}) collective-permute-start(f32[3,2,32,256]{3,2,1,0:T(8,128)S(1)} %get-tuple-element.76), channel_id=1, source_target_pairs={{0,24},{8,0},{16,8},{24,16},{1,25},{9,1},{17,9},{25,17},{2,26},{10... | collective-permute-start | bytes 589832 | tf_op jit(solution)/shard_map/ppermute | solution.py:246
  62.3 16.1 %collective-permute-start.27 = (f32[3,2,32,256]{3,2,1,0:T(8,128)S(1)}, f32[3,2,32,256]{3,2,1,0:T(8,128)S(1)}, u32[]{:S(2)}, u32[]{:S(2)}) collective-permute-start(f32[3,2,32,256]{3,2,1,0:T(8,128)S(1)} %get-tuple-element.77), channel_id=1, source_target_pairs={{0,16},{8,24},{16,0},{24,8},{1,17},{9,25},{17,1},{25,9},{2,18},{10... | collective-permute-start | bytes 589832 | tf_op jit(solution)/shard_map/ppermute | solution.py:246
  64.2 14.2 %collective-permute-start.28 = (f32[3,2,32,256]{3,2,1,0:T(8,128)S(1)}, f32[3,2,32,256]{3,2,1,0:T(8,128)S(1)}, u32[]{:S(2)}, u32[]{:S(2)}) collective-permute-start(f32[3,2,32,256]{3,2,1,0:T(8,128)S(1)} %get-tuple-element.78), channel_id=1, source_target_pairs={{0,8},{8,16},{16,24},{24,0},{1,9},{9,17},{17,25},{25,1},{2,10},{10... | collective-permute-start | bytes 589832 | tf_op jit(solution)/shard_map/ppermute | solution.py:246
  64.2 10.8 %collective-permute-start.22 = (f32[2,32,256]{2,1,0:T(8,128)S(1)}, f32[2,32,256]{2,1,0:T(8,128)S(1)}, u32[]{:S(2)}, u32[]{:S(2)}) collective-permute-start(f32[2,32,256]{2,1,0:T(8,128)S(1)} %get-tuple-element.72), channel_id=1, source_target_pairs={{0,16},{8,24},{16,0},{24,8},{1,17},{9,25},{17,1},{25,9},{2,18},{10... | collective-permute-start | bytes 196616 | tf_op jit(solution)/shard_map/ppermute | solution.py:246
  80.6 4.3 %collective-permute-start.30 = (f32[2,32,256]{2,1,0:T(8,128)S(1)}, f32[2,32,256]{2,1,0:T(8,128)S(1)}, u32[]{:S(2)}, u32[]{:S(2)}) collective-permute-start(f32[2,32,256]{2,1,0:T(8,128)S(1)} %get-tuple-element.81), channel_id=1, source_target_pairs={{0,16},{8,24},{16,0},{24,8},{1,17},{9,25},{17,1},{25,9},{2,18},{10... | collective-permute-start | bytes 196616 | tf_op jit(solution)/shard_map/ppermute | solution.py:246
  82.0 20.9 %collective-permute-start.25 = (f32[2,128,256]{2,1,0:T(8,128)S(1)}, f32[2,128,256]{2,1,0:T(8,128)S(1)}, u32[]{:S(2)}, u32[]{:S(2)}) collective-permute-start(f32[2,128,256]{2,1,0:T(8,128)S(1)} %shard_map.68.refs_4_.refs_0_), channel_id=1, source_target_pairs={{0,2},{1,3},{2,0},{3,1},{4,6},{5,7},{6,4},{7,5},{8,10},{9,11},{10,... | collective-permute-start | bytes 786440 | tf_op jit(solution)/shard_map/ppermute | solution.py:244
  84.9 25.9 %collective-permute-start.33 = (f32[2,128,256]{2,1,0:T(8,128)S(1)}, f32[2,128,256]{2,1,0:T(8,128)S(1)}, u32[]{:S(2)}, u32[]{:S(2)}) collective-permute-start(f32[2,128,256]{2,1,0:T(8,128)S(1)} %shard_map.71.refs_4_.refs_0_), channel_id=1, source_target_pairs={{0,2},{1,3},{2,0},{3,1},{4,6},{5,7},{6,4},{7,5},{8,10},{9,11},{10,... | collective-permute-start | bytes 786440 | tf_op jit(solution)/shard_map/ppermute | solution.py:244
  85.1 18.8 %collective-permute-start.34 = (f32[3,2,16,256]{3,2,1,0:T(8,128)S(1)}, f32[3,2,16,256]{3,2,1,0:T(8,128)S(1)}, u32[]{:S(2)}, u32[]{:S(2)}) collective-permute-start(f32[3,2,16,256]{3,2,1,0:T(8,128)S(1)} %get-tuple-element.85), channel_id=1, source_target_pairs={{0,24},{8,0},{16,8},{24,16},{1,25},{9,1},{17,9},{25,17},{2,26},{10... | collective-permute-start | bytes 294920 | tf_op jit(solution)/shard_map/ppermute | solution.py:246
  86.3 17.6 %collective-permute-start.35 = (f32[3,2,16,256]{3,2,1,0:T(8,128)S(1)}, f32[3,2,16,256]{3,2,1,0:T(8,128)S(1)}, u32[]{:S(2)}, u32[]{:S(2)}) collective-permute-start(f32[3,2,16,256]{3,2,1,0:T(8,128)S(1)} %get-tuple-element.86), channel_id=1, source_target_pairs={{0,16},{8,24},{16,0},{24,8},{1,17},{9,25},{17,1},{25,9},{2,18},{10... | collective-permute-start | bytes 294920 | tf_op jit(solution)/shard_map/ppermute | solution.py:246
  87.2 16.7 %collective-permute-start.36 = (f32[3,2,16,256]{3,2,1,0:T(8,128)S(1)}, f32[3,2,16,256]{3,2,1,0:T(8,128)S(1)}, u32[]{:S(2)}, u32[]{:S(2)}) collective-permute-start(f32[3,2,16,256]{3,2,1,0:T(8,128)S(1)} %get-tuple-element.87), channel_id=1, source_target_pairs={{0,8},{8,16},{16,24},{24,0},{1,9},{9,17},{17,25},{25,1},{2,10},{10... | collective-permute-start | bytes 294920 | tf_op jit(solution)/shard_map/ppermute | solution.py:246
  104.9 4.3 %collective-permute-start.38 = (f32[2,16,256]{2,1,0:T(8,128)S(1)}, f32[2,16,256]{2,1,0:T(8,128)S(1)}, u32[]{:S(2)}, u32[]{:S(2)}) collective-permute-start(f32[2,16,256]{2,1,0:T(8,128)S(1)} %get-tuple-element.90), channel_id=1, source_target_pairs={{0,16},{8,24},{16,0},{24,8},{1,17},{9,25},{17,1},{25,9},{2,18},{10... | collective-permute-start | bytes 98312 | tf_op jit(solution)/shard_map/ppermute | solution.py:246
  107.3 25.9 %collective-permute-start.24 = (f32[2,128,256]{2,1,0:T(8,128)S(1)}, f32[2,128,256]{2,1,0:T(8,128)S(1)}, u32[]{:S(2)}, u32[]{:S(2)}) collective-permute-start(f32[2,128,256]{2,1,0:T(8,128)S(1)} %get-tuple-element.75), channel_id=1, source_target_pairs={{0,1},{1,0},{2,3},{3,2},{4,5},{5,4},{6,7},{7,6},{8,9},{9,8},{10,11... | collective-permute-start | bytes 786440 | tf_op jit(solution)/shard_map/ppermute | solution.py:242
  109.2 9.7 %collective-permute-start.41 = (f32[2,64,256]{2,1,0:T(8,128)S(1)}, f32[2,64,256]{2,1,0:T(8,128)S(1)}, u32[]{:S(2)}, u32[]{:S(2)}) collective-permute-start(f32[2,64,256]{2,1,0:T(8,128)S(1)} %shard_map.74.refs_4_.refs_0_), channel_id=1, source_target_pairs={{0,2},{1,3},{2,0},{3,1},{4,6},{5,7},{6,4},{7,5},{8,10},{9,11},{10,... | collective-permute-start | bytes 393224 | tf_op jit(solution)/shard_map/ppermute | solution.py:244
  109.3 23.9 %collective-permute-start.32 = (f32[2,128,256]{2,1,0:T(8,128)S(1)}, f32[2,128,256]{2,1,0:T(8,128)S(1)}, u32[]{:S(2)}, u32[]{:S(2)}) collective-permute-start(f32[2,128,256]{2,1,0:T(8,128)S(1)} %get-tuple-element.84), channel_id=1, source_target_pairs={{0,1},{1,0},{2,3},{3,2},{4,5},{5,4},{6,7},{7,6},{8,9},{9,8},{10,11... | collective-permute-start | bytes 786440 | tf_op jit(solution)/shard_map/ppermute | solution.py:242
  111.8 22.8 %collective-permute-start.40 = (f32[2,128,256]{2,1,0:T(8,128)S(1)}, f32[2,128,256]{2,1,0:T(8,128)S(1)}, u32[]{:S(2)}, u32[]{:S(2)}) collective-permute-start(f32[2,128,256]{2,1,0:T(8,128)S(1)} %get-tuple-element.93), channel_id=1, source_target_pairs={{0,1},{1,0},{2,3},{3,2},{4,5},{5,4},{6,7},{7,6},{8,9},{9,8},{10,11... | collective-permute-start | bytes 786440 | tf_op jit(solution)/shard_map/ppermute | solution.py:242
  112.5 20.8 %collective-permute-start.16 = (f32[2,64,256]{2,1,0:T(8,128)S(1)}, f32[2,64,256]{2,1,0:T(8,128)S(1)}, u32[]{:S(2)}, u32[]{:S(2)}) collective-permute-start(f32[2,64,256]{2,1,0:T(8,128)S(1)} %get-tuple-element.66), channel_id=1, source_target_pairs={{0,1},{1,0},{2,3},{3,2},{4,5},{5,4},{6,7},{7,6},{8,9},{9,8},{10,11... | collective-permute-start | bytes 393224 | tf_op jit(solution)/shard_map/ppermute | solution.py:242
  120.1 14.5 %collective-permute-start.42 = (f32[2,64,256]{2,1,0:T(8,128)S(1)}, f32[2,64,256]{2,1,0:T(8,128)S(1)}, u32[]{:S(2)}, u32[]{:S(2)}) collective-permute-start(f32[2,64,256]{2,1,0:T(8,128)S(1)} %get-tuple-element.95), channel_id=1, source_target_pairs={{0,1},{1,0},{2,3},{3,2},{4,5},{5,4},{6,7},{7,6},{8,9},{9,8},{10,11... | collective-permute-start | bytes 393224 | tf_op jit(solution)/shard_map/ppermute | solution.py:242
  (16 other events, 79.7 us)

commit v3 on v2

--- a/solution.py
+++ b/solution.py
@@ -9,7 +9,7 @@
 from jax.experimental.pallas import tpu as pltpu
 from jax.sharding import PartitionSpec as P
 
-WEIGHTS = (2, 4, 4, 4, 2)
+WEIGHTS = (3, 5, 5, 3)
 AHEAD = 2
 SUBLANES, LANES = 8, 128
 VMEM_LIMIT = 40 * 2**20
@@ -71,43 +71,32 @@
     return ref.at[:, 0, pl.ds(pl.multiple_of(start, SUBLANES), size), :]
 
 
-def pack_copies(points, own, sources, pieces, sem, base, step):
-    copies = []
-    for gap in range(1, points):
-        start = base + lax.rem(own - gap + points, points) * step
-        for at, source in enumerate(sources):
-            copies.append(pltpu.make_async_copy(at_rows(source, start, step), pieces[gap - 1].at[at], sem.at[len(copies)]))
-    return copies
+def pack_copies(points, sources, pieces, sem, base, step):
+    return [
+        pltpu.make_async_copy(at_rows(source, base + part * step, step), pieces.at[part, at], sem.at[3 * part + at])
+        for part in range(points)
+        for at, source in enumerate(sources)
+    ]
 
 
 def pack_kernel(points, base, step, *refs):
-    sources, pieces, sem = refs[:3], refs[3:-1], refs[-1]
-    copies = pack_copies(points, lax.axis_index("ka"), sources, pieces, sem, base, step)
+    copies = pack_copies(points, refs[:3], *refs[3:], base, step)
     for copy in copies:
         copy.start()
     for copy in copies:
         copy.wait()
 
 
-def energy_kernel(points, base, step, later, scale, *refs):
-    tables, sources, received = refs[0], refs[1:4], refs[4 : 3 + points]
-    rest = refs[3 + points :]
-    sigmas, pieces = rest[:points], rest[points:-3]
-    mine, sem, own_sem = rest[-3:]
+def energy_kernel(points, step, later, scale, *refs):
+    tables, sources, received, sigmas, pieces = refs[0], refs[1:4], refs[4], refs[5 : 5 + points], refs[5 + points : -1]
     own = lax.axis_index("ka")
-    own_copies = [
-        pltpu.make_async_copy(at_rows(source, base + own * step, step), mine.at[at], own_sem.at[at])
-        for at, source in enumerate(sources)
-    ]
-    copies = pack_copies(points, own, sources, pieces, sem, *later) if later else []
-    for copy in own_copies + copies:
+    copies = pack_copies(points, sources, pieces[0], refs[-1], *later) if later else []
+    for copy in copies:
         copy.start()
-    for copy in own_copies:
-        copy.wait()
     cosines = [tables[0, lax.rem(own * r, points)] for r in range(points)]
     sines = [tables[1, lax.rem(own * r, points)] for r in range(points)]
-    blocks = [mine, *received]
-    across = mine.shape[-1] // LANES
+    blocks = [received.at[lax.rem(own + gap, points)] for gap in range(points)]
+    across = received.shape[-1] // LANES
     root = points**-0.5
 
     def tile(index, carry):
@@ -155,18 +144,18 @@
 
 
 def right_kernel(row_parts, group, *refs):
-    pieces, high, low = refs[: row_parts * group], refs[-2], refs[-1]
-    row_at, half = lax.axis_index("tr"), lax.axis_index("tc") // group
-    depth, cols = pieces[0].shape[1:]
+    pieces, high, low = refs[:group], refs[-2], refs[-1]
+    half = lax.axis_index("tc") // group
+    depth, cols = pieces[0].shape[2:]
     for part in range(row_parts):
-        place = lax.rem(half - row_at + part + row_parts, row_parts) * depth
+        place = lax.rem(half - part + row_parts, row_parts) * depth
         upper = pl.ds(pl.multiple_of(place, depth), depth)
         lower = pl.ds(pl.multiple_of(place + row_parts * depth, depth), depth)
         for gap in range(group):
-            piece = pieces[part * group + gap]
+            piece = pieces[gap]
             first = pl.ds(gap * cols, cols)
             second = pl.ds((group + gap) * cols, cols)
-            real, imag = split(piece[0]), split(piece[1])
+            real, imag = split(piece[part, 0]), split(piece[part, 1])
             for out, real_part, imag_part in zip((high, low), real, imag):
                 out[upper, first] = real_part
                 out[lower, second] = real_part
@@ -230,7 +219,7 @@
     f32 = functools.partial(jax.ShapeDtypeStruct, dtype=jnp.float32)
     bf16 = functools.partial(jax.ShapeDtypeStruct, dtype=jnp.bfloat16)
     inputs = (green_less, green_great, screened)
-    copies = 3 * (momenta - 1)
+    copies = 3 * momenta
     scale = momenta**-1.5 * length**-0.5
     tables = jnp.asarray(angle_tables(momenta))
 
@@ -246,15 +235,15 @@
         return lax.ppermute(value, axis, [(s, (s + gap) % count) for s in range(count)])
 
     def send_pieces(pieces):
-        return [shift(piece, "ka", -gap) for gap, piece in enumerate(pieces, 1)]
+        return lax.all_to_all(pieces, "ka", split_axis=0, concat_axis=0, tiled=True)
 
     def pack(at, after):
         step = sizes[at]
         return call(
             functools.partial(pack_kernel, momenta, bases[at], step),
-            [f32((3, 2, step, cols))] * (momenta - 1),
+            f32((momenta, 3, 2, step, cols)),
             [IN_HBM] * 3,
-            [ANYWHERE] * (momenta - 1),
+            ANYWHERE,
             inputs,
             [pltpu.SemaphoreType.DMA((copies,))],
             after,
@@ -264,22 +253,18 @@
         step, next_at = sizes[at], at + AHEAD
         later = (bases[next_at], sizes[next_at]) if next_at < len(sizes) else None
         outs = call(
-            functools.partial(energy_kernel, momenta, bases[at], step, later, scale),
-            [f32((2, step, cols))] * momenta + ([f32((3, 2, later[1], cols))] * (momenta - 1) if later else []),
-            [IN_SMEM] + [IN_HBM] * 3 + [IN_VMEM] * (momenta - 1),
-            [IN_VMEM] * momenta + ([ANYWHERE] * (momenta - 1) if later else []),
-            (tables, *inputs, *received[at]),
-            [
-                pltpu.VMEM((3, 2, step, cols), jnp.float32),
-                pltpu.SemaphoreType.DMA((copies,)),
-                pltpu.SemaphoreType.DMA((3,)),
-            ],
+            functools.partial(energy_kernel, momenta, step, later, scale),
+            [f32((2, step, cols))] * momenta + ([f32((momenta, 3, 2, later[1], cols))] if later else []),
+            [IN_SMEM] + [IN_HBM] * 3 + [IN_VMEM],
+            [IN_VMEM] * momenta + ([ANYWHERE] if later else []),
+            (tables, *inputs, received[at]),
+            [pltpu.SemaphoreType.DMA((copies,))],
             after,
         )
         sigmas, pieces = outs[:momenta], outs[momenta:]
         parts = [sigmas[0]] + [shift(sigmas[gap], "ka", gap) for gap in range(1, momenta)]
         if later:
-            received.append(send_pieces(pieces))
+            received.append(send_pieces(pieces[0]))
         return parts
 
     def assemble(at, parts, after):
@@ -311,15 +296,13 @@
     for at in range(min(AHEAD, len(sizes))):
         pieces = pack(at, last)
         received.append(send_pieces(pieces))
-        last = pieces[:1]
+        last = (pieces,)
 
     blocks = green_less[:, 0].reshape(2, group, cols, cols)
     sides = [lax.dynamic_index_in_dim(blocks, member, 1, False)]
     for gap in range(1, group):
         sides.append(shift(lax.dynamic_index_in_dim(blocks, (member + gap) % group, 1, False), "group", gap))
-    panels = list(sides)
-    for gap in range(1, row_parts):
-        panels += [shift(side, "tr", gap) for side in sides]
+    panels = [lax.all_gather(side, "tr") for side in sides]
     extent = 2 * row_parts * cols
 
     lefts, results, right = [], [], None

time: 136 us -> 162 us (1.19)
  waiting for transfers between devices: 82.3 us -> 66.8 us
  between operations: 1.02 us -> 14.4 us
  local copies, waits for them, and re-layouts: 2.68 us -> 15 us
  starting transfers between devices: 35.7 us -> 44.1 us
  Pallas kernels: 14.4 us -> 20.5 us
    ppermute x5 -> x4, waiting for transfers between devices: 32.3 us -> 4.7 us  [shift(): lax.ppermute(value, 'tc', [(j, (j + group * gap) % col_parts) for j in ra...]
    all_to_all x0 -> x4, starting transfers between devices: none -> 16.8 us  [send_pieces(): return lax.all_to_all(pieces, 'ka', split_axis=0, concat_axis=0, tiled=True)]
    ppermute x32 -> x12, starting transfers between devices: 25.7 us -> 11.5 us  [shift(): lax.ppermute(value, axis, [(s, (s + gap) % count) for s in range(count)])]
    unnamed x10 -> x52, local copies, waits for them, and re-layouts: 1.25 us -> 12.6 us
    ppermute x6 -> x5, waiting for transfers between devices: 21.5 us -> 28.9 us  [shift(): return lax.ppermute(value, 'tc', moves)]
    all_to_all x0 -> x4, waiting for transfers between devices: none -> 7.38 us  [send_pieces(): return lax.all_to_all(pieces, 'ka', split_axis=0, concat_axis=0, tiled=True)]
    pallas_call x19 -> x16, Pallas kernels: 14.4 us -> 20.5 us  [call(): pl.pallas_call(ordered, out_shape=out_shapes, in_specs=in_specs + [ANYWHE...]
    ppermute x6 -> x5, starting transfers between devices: 6.76 us -> 9.87 us  [shift(): return lax.ppermute(value, 'tc', moves)]
  transfers between devices with their start and end apart: 43 -> 27, of which waited for: 19 -> 15; matrix products, arithmetic and copies ran while one was open for 0% -> 0% of each run, Pallas kernels for 9% -> 12%
where the time goes in v3:
time: 162 us; the launch traced here: 161 us
  waiting for transfers between devices  66.8 us (41%)
  starting transfers between devices  44.1 us (27%)
  Pallas kernels  20.5 us (13%)
  local copies, waits for them, and re-layouts  15 us (9%)
  between operations  14.4 us (9%)
    ppermute x5, waiting for transfers between devices, shift(): return lax.ppermute(value, 'tc', moves)  28.9 us
    ppermute x12, waiting for transfers between devices, shift(): lax.ppermute(value, axis, [(s, (s + gap) % count) for s in range(count)])  25.8 us
    pallas_call x16, Pallas kernels, call(): pl.pallas_call(ordered, out_shape=out_shapes, in_specs=in_specs + [ANYWHE...  20.5 us
    all_to_all x4, starting transfers between devices, send_pieces(): return lax.all_to_all(pieces, 'ka', split_axis=0, concat_axis=0, tiled=True)  16.8 us
    unnamed x52, local copies, waits for them, and re-layouts  12.6 us
    ppermute x12, starting transfers between devices, shift(): lax.ppermute(value, axis, [(s, (s + gap) % count) for s in range(count)])  11.5 us
    ppermute x5, starting transfers between devices, shift(): return lax.ppermute(value, 'tc', moves)  9.87 us
    all_to_all x4, waiting for transfers between devices, send_pieces(): return lax.all_to_all(pieces, 'ka', split_axis=0, concat_axis=0, tiled=True)  7.38 us
  transfers between devices with their start and end apart: 27, of which 15 were waited for; matrix products, arithmetic and copies ran while one was open for 0% of the time, Pallas kernels for 12%

profile of v3, /device:TPU:0, one launch (start us, length us, event | category | flops | bytes accessed | tf_op | source)
XLA Modules:
  0.0 160.8 jit_solution(460082039531944989)
XLA Ops:
  7.3 2.4 %dynamic-slice_bitcast_fusion = (f32[2,256,256]{2,1,0:T(8,128)}, f32[2,1,256,256]{3,2,1,0:T(8,128)}) fusion(f32[2,2,256,256]{3,2,1,0:T(8,128)} %bitcast.5, s32[]{:T(128)S(6)} %select_n.21, s32[]{:T(128)S(6)} %select_n.19), kind=kLoop, calls=%fused_computation | loop fusion | bytes 2097160 | tf_op jit(solution)/shard_map/jit(dynamic_index_in_dim)/squeeze | solution.py:304
  12.3 4.2 %all-to-all-start = ((f32[4,3,2,24,256]{4,3,2,1,0:T(8,128)}), f32[4,3,2,24,256]{4,3,2,1,0:T(8,128)}, u32[]{:S(2)}, u32[]{:S(2)}) async-start(f32[4,3,2,24,256]{4,3,2,1,0:T(8,128)} %copy-done.10), calls=%async_computation | async-start | bytes 1179648 | tf_op jit(solution)/shard_map/all_to_all | solution.py:238
  19.3 7.4 %all-to-all-done.refs_4_ = f32[4,3,2,24,256]{4,3,2,1,0:T(8,128)} async-done(((f32[4,3,2,24,256]{4,3,2,1,0:T(8,128)}), f32[4,3,2,24,256]{4,3,2,1,0:T(8,128)}, u32[]{:S(2)}, u32[]{:S(2)}) %all-to-all-start) | async-done | bytes 589856 | tf_op jit(solution)/shard_map/all_to_all | solution.py:238
  26.6 4.2 %all-to-all-start.1 = ((f32[4,3,2,40,256]{4,3,2,1,0:T(8,128)}), f32[4,3,2,40,256]{4,3,2,1,0:T(8,128)}, u32[]{:S(2)}, u32[]{:S(2)}) async-start(f32[4,3,2,40,256]{4,3,2,1,0:T(8,128)} %copy-done.8), calls=%async_computation.1 | async-start | bytes 1966080 | tf_op jit(solution)/shard_map/all_to_all | solution.py:238
  30.9 2.5 %collective-permute-start.4 = (f32[2,256,256]{2,1,0:T(8,128)}, f32[2,256,256]{2,1,0:T(8,128)}, u32[]{:S(2)}, u32[]{:S(2)}) collective-permute-start(f32[2,256,256]{2,1,0:T(8,128)} %get-tuple-element.58), channel_id=1, source_target_pairs={{0,1},{1,0},{2,3},{3,2},{4,5},{5,4},{6,7},{7,6},{8,9},{9,8},{10,11... | collective-permute-start | bytes 1572872 | tf_op jit(solution)/shard_map/ppermute | solution.py:231
  33.4 12.7 %collective-permute-done.4 = f32[2,256,256]{2,1,0:T(8,128)} collective-permute-done((f32[2,256,256]{2,1,0:T(8,128)}, f32[2,256,256]{2,1,0:T(8,128)}, u32[]{:S(2)}, u32[]{:S(2)}) %collective-permute-start.4) | collective-permute-done | bytes 524320 | tf_op jit(solution)/shard_map/ppermute | solution.py:231
  47.4 2.1 %shard_map.61 = (f32[2,24,256]{2,1,0:T(8,128)S(1)}, f32[2,24,256]{2,1,0:T(8,128)S(1)}, f32[2,24,256]{2,1,0:T(8,128)S(1)}, f32[2,24,256]{2,1,0:T(8,128)S(1)}, f32[4,3,2,40,256]{4,3,2,1,0:T(8,128)S(1)}) custom-call(f32[2,4]{1,0:T(2,128)S(1)} %copy-done.21, f32[2,1,512,256]{3,2,1,0:T(8,128)S(1)} %copy-done, f32[2,1,512,256]{3,2,1,0:T(8,128)S(1)} %copy-done.1, ...), custom_call_target="tpu_custom_call" | custom-call | flops 1 | bytes 1 | tf_op jit(solution)/shard_map/pallas_call | solution.py:199
  50.4 4.2 %all-to-all-start.2 = ((f32[4,3,2,40,256]{4,3,2,1,0:T(8,128)}), f32[4,3,2,40,256]{4,3,2,1,0:T(8,128)}, u32[]{:S(2)}, u32[]{:S(2)}) async-start(f32[4,3,2,40,256]{4,3,2,1,0:T(8,128)} %copy-done.17), calls=%async_computation.2 | async-start | bytes 1966080 | tf_op jit(solution)/shard_map/all_to_all | solution.py:238
  55.1 1.7 %collective-permute-start.1 = (f32[2,24,256]{2,1,0:T(8,128)S(1)}, f32[2,24,256]{2,1,0:T(8,128)S(1)}, u32[]{:S(2)}, u32[]{:S(2)}) collective-permute-start(f32[2,24,256]{2,1,0:T(8,128)S(1)} %get-tuple-element.32), channel_id=1, source_target_pairs={{0,16},{8,24},{16,0},{24,8},{1,17},{9,25},{17,1},{25,9},{2,18},{10... | collective-permute-start | bytes 147464 | tf_op jit(solution)/shard_map/ppermute | solution.py:235
  58.1 10.8 %collective-permute-done.refs_1_ = f32[2,24,256]{2,1,0:T(8,128)S(1)} collective-permute-done((f32[2,24,256]{2,1,0:T(8,128)S(1)}, f32[2,24,256]{2,1,0:T(8,128)S(1)}, u32[]{:S(2)}, u32[]{:S(2)}) %collective-permute-start) | collective-permute-done | bytes 49184 | tf_op jit(solution)/shard_map/ppermute | solution.py:235
  70.6 2.8 %collective-permute-start.3 = (f32[2,96,256]{2,1,0:T(8,128)}, f32[2,96,256]{2,1,0:T(8,128)}, u32[]{:S(2)}, u32[]{:S(2)}) collective-permute-start(f32[2,96,256]{2,1,0:T(8,128)} %shard_map.62.refs_5_.refs_0_), channel_id=1, source_target_pairs={{0,2},{1,3},{2,0},{3,1},{4,6},{5,7},{6,4},{7,5},{8,10},{9,11},{10,... | collective-permute-start | bytes 589832 | tf_op jit(solution)/shard_map/ppermute | solution.py:233
  73.3 2.1 %shard_map.63 = (f32[2,40,256]{2,1,0:T(8,128)S(1)}, f32[2,40,256]{2,1,0:T(8,128)S(1)}, f32[2,40,256]{2,1,0:T(8,128)S(1)}, f32[2,40,256]{2,1,0:T(8,128)S(1)}, f32[4,3,2,24,256]{4,3,2,1,0:T(8,128)S(1)}) custom-call(f32[2,4]{1,0:T(2,128)S(1)} %copy-done.21, f32[2,1,512,256]{3,2,1,0:T(8,128)S(1)} %copy-done, f32[2,1,512,256]{3,2,1,0:T(8,128)S(1)} %copy-done.1, ...), custom_call_target="tpu_custom_call" | custom-call | flops 1 | bytes 1 | tf_op jit(solution)/shard_map/pallas_call | solution.py:199
  76.2 4.2 %all-to-all-start.3 = ((f32[4,3,2,24,256]{4,3,2,1,0:T(8,128)}), f32[4,3,2,24,256]{4,3,2,1,0:T(8,128)}, u32[]{:S(2)}, u32[]{:S(2)}) async-start(f32[4,3,2,24,256]{4,3,2,1,0:T(8,128)} %copy-done.20), calls=%async_computation.3 | async-start | bytes 1179648 | tf_op jit(solution)/shard_map/all_to_all | solution.py:238
  80.9 1.7 %collective-permute-start.6 = (f32[2,40,256]{2,1,0:T(8,128)S(1)}, f32[2,40,256]{2,1,0:T(8,128)S(1)}, u32[]{:S(2)}, u32[]{:S(2)}) collective-permute-start(f32[2,40,256]{2,1,0:T(8,128)S(1)} %get-tuple-element.36), channel_id=1, source_target_pairs={{0,16},{8,24},{16,0},{24,8},{1,17},{9,25},{17,1},{25,9},{2,18},{10... | collective-permute-start | bytes 245768 | tf_op jit(solution)/shard_map/ppermute | solution.py:235
  83.9 7.3 %collective-permute-done.5.refs_1_ = f32[2,40,256]{2,1,0:T(8,128)S(1)} collective-permute-done((f32[2,40,256]{2,1,0:T(8,128)S(1)}, f32[2,40,256]{2,1,0:T(8,128)S(1)}, u32[]{:S(2)}, u32[]{:S(2)}) %collective-permute-start.5) | collective-permute-done | bytes 81952 | tf_op jit(solution)/shard_map/ppermute | solution.py:235
  95.5 2.7 %shard_map.66 = (f32[2,96,256]{2,1,0:T(8,128)S(1)}, f32[2,96,256]{2,1,0:T(8,128)S(1)}) custom-call(f32[2,96,256]{2,1,0:T(8,128)} %shard_map.62.refs_5_.refs_0_, f32[2,96,256]{2,1,0:T(8,128)} %collective-permute-done.3.refs_1_, bf16[1024,1024]{1,0:T(8,128)(2,1)S(1)} %get-tuple-element.38.refs_2_, bf16[1024,1024]{1,0:T(8,128)(2,1)S(1)} %get-tuple-element.39.refs_3_, ...), custom_call_target="tpu_custom_call" | custom-call | flops 1 | bytes 1 | tf_op jit(solution)/shard_map/pallas_call | solution.py:199
  98.8 1.8 %shard_map.67 = (f32[2,40,256]{2,1,0:T(8,128)S(1)}, f32[2,40,256]{2,1,0:T(8,128)S(1)}, f32[2,40,256]{2,1,0:T(8,128)S(1)}, f32[2,40,256]{2,1,0:T(8,128)S(1)}) custom-call(f32[2,4]{1,0:T(2,128)S(1)} %copy-done.22, f32[2,1,512,256]{3,2,1,0:T(8,128)S(1)} %copy-done, f32[2,1,512,256]{3,2,1,0:T(8,128)S(1)} %copy-done.1, f32[2,1,512,256]{3,2,1,0:T(8,128)S(1)} %copy-done.3, ...), custom_call_target="tpu_custom_call" | custom-call | flops 1 | bytes 1 | tf_op jit(solution)/shard_map/pallas_call | solution.py:199
  103.1 1.4 collective-permute-done.10.refs_1_
  104.5 1.8 %collective-permute-done.11.refs_2_ = f32[2,40,256]{2,1,0:T(8,128)S(1)} collective-permute-done((f32[2,40,256]{2,1,0:T(8,128)S(1)}, f32[2,40,256]{2,1,0:T(8,128)S(1)}, u32[]{:S(2)}, u32[]{:S(2)}) %collective-permute-start.11) | collective-permute-done | bytes 81952 | tf_op jit(solution)/shard_map/ppermute | solution.py:235
  107.0 2.8 %collective-permute-start.14 = (f32[2,160,256]{2,1,0:T(8,128)}, f32[2,160,256]{2,1,0:T(8,128)}, u32[]{:S(2)}, u32[]{:S(2)}) collective-permute-start(f32[2,160,256]{2,1,0:T(8,128)} %shard_map.68.refs_4_.refs_0_), channel_id=1, source_target_pairs={{0,2},{1,3},{2,0},{3,1},{4,6},{5,7},{6,4},{7,5},{8,10},{9,11},{10,... | collective-permute-start | bytes 983048 | tf_op jit(solution)/shard_map/ppermute | solution.py:233
  110.7 2.2 %shard_map.69 = (f32[2,160,256]{2,1,0:T(8,128)S(1)}, f32[2,160,256]{2,1,0:T(8,128)S(1)}) custom-call(f32[2,160,256]{2,1,0:T(8,128)S(1)} %shard_map.64.refs_2_.refs_4_.refs_0_, f32[2,160,256]{2,1,0:T(8,128)} %collective-permute-done.9.refs_1_, bf16[1024,1024]{1,0:T(8,128)(2,1)S(1)} %get-tuple-element.38.refs_2_, ...), custom_call_target="tpu_custom_call" | custom-call | flops 1 | bytes 1 | tf_op jit(solution)/shard_map/pallas_call | solution.py:199
  115.4 1.6 shard_map.70
  117.7 1.4 collective-permute-start.17
  119.1 1.4 collective-permute-done.15.refs_1_
  121.7 1.7 %collective-permute-start.13 = (f32[2,160,256]{2,1,0:T(8,128)}, f32[2,160,256]{2,1,0:T(8,128)S(1)}, u32[]{:S(2)}, u32[]{:S(2)}) collective-permute-start(f32[2,160,256]{2,1,0:T(8,128)} %copy-done.23), channel_id=1, source_target_pairs={{0,1},{1,0},{2,3},{3,2},{4,5},{5,4},{6,7},{7,6},{8,9},{9,8},{10,11... | collective-permute-start | bytes 983048 | tf_op jit(solution)/shard_map/ppermute | solution.py:231
  123.4 2.3 %collective-permute-done.14.refs_1_ = f32[2,160,256]{2,1,0:T(8,128)} collective-permute-done((f32[2,160,256]{2,1,0:T(8,128)}, f32[2,160,256]{2,1,0:T(8,128)}, u32[]{:S(2)}, u32[]{:S(2)}) %collective-permute-start.14) | collective-permute-done | bytes 327712 | tf_op jit(solution)/shard_map/ppermute | solution.py:233
  125.7 2.3 %shard_map.72 = (f32[2,160,256]{2,1,0:T(8,128)S(1)}, f32[2,160,256]{2,1,0:T(8,128)S(1)}) custom-call(f32[2,160,256]{2,1,0:T(8,128)} %shard_map.68.refs_4_.refs_0_, f32[2,160,256]{2,1,0:T(8,128)} %collective-permute-done.14.refs_1_, bf16[1024,1024]{1,0:T(8,128)(2,1)S(1)} %copy-done.5, bf16[1024,1024]{1,0:T(8,128)(2,1)S(1)} %copy-done.7, ...), custom_call_target="tpu_custom_call" | custom-call | flops 1 | bytes 1 | tf_op jit(solution)/shard_map/pallas_call | solution.py:199
  128.0 5.0 %collective-permute-start.18 = (f32[2,160,256]{2,1,0:T(8,128)S(1)}, f32[2,160,256]{2,1,0:T(8,128)S(1)}, u32[]{:S(2)}, u32[]{:S(2)}) collective-permute-start(f32[2,160,256]{2,1,0:T(8,128)S(1)} %get-tuple-element.55), channel_id=1, source_target_pairs={{0,1},{1,0},{2,3},{3,2},{4,5},{5,4},{6,7},{7,6},{8,9},{9,8},{10,11... | collective-permute-start | bytes 983048 | tf_op jit(solution)/shard_map/ppermute | solution.py:231
  133.1 1.4 collective-permute-done.19.refs_1_
  136.2 12.0 %collective-permute-done.8.refs_1_ = f32[2,96,256]{2,1,0:T(8,128)S(1)} collective-permute-done((f32[2,96,256]{2,1,0:T(8,128)S(1)}, f32[2,96,256]{2,1,0:T(8,128)S(1)}, u32[]{:S(2)}, u32[]{:S(2)}) %collective-permute-start.8) | collective-permute-done | bytes 196640 | tf_op jit(solution)/shard_map/ppermute | solution.py:231
  148.2 4.2 %collective-permute-done.20.refs_7_ = f32[2,96,256]{2,1,0:T(8,128)S(1)} collective-permute-done((f32[2,96,256]{2,1,0:T(8,128)S(1)}, f32[2,96,256]{2,1,0:T(8,128)S(1)}, u32[]{:S(2)}, u32[]{:S(2)}) %collective-permute-start.20) | collective-permute-done | bytes 196640 | tf_op jit(solution)/shard_map/ppermute | solution.py:231
  152.4 1.5 shard_map.74
  (93 shorter events, 28.8 us)
Async XLA Ops:
  7.2 85.2 %all-gather.5.cloned.1.call-start = ((), (), s32[]{:S(2)}) async-start(), calls=%async_computation.4 | async-start | bytes 1572864 | tf_op jit(solution)/shard_map/all_gather | solution.py:305
  12.3 14.4 %all-to-all-start = ((f32[4,3,2,24,256]{4,3,2,1,0:T(8,128)}), f32[4,3,2,24,256]{4,3,2,1,0:T(8,128)}, u32[]{:S(2)}, u32[]{:S(2)}) async-start(f32[4,3,2,24,256]{4,3,2,1,0:T(8,128)} %copy-done.10), calls=%async_computation | async-start | bytes 1179648 | tf_op jit(solution)/shard_map/all_to_all | solution.py:238
  19.3 26.9 %copy-start.21 = (f32[2,4]{1,0:T(2,128)S(1)}, f32[2,4]{1,0:T(2,128)}, u32[]{:S(2)}) copy-start(f32[2,4]{1,0:T(2,128)} %constant.30.clone.refs_0_) | copy-start | bytes 100
  26.6 23.8 %all-to-all-start.1 = ((f32[4,3,2,40,256]{4,3,2,1,0:T(8,128)}), f32[4,3,2,40,256]{4,3,2,1,0:T(8,128)}, u32[]{:S(2)}, u32[]{:S(2)}) async-start(f32[4,3,2,40,256]{4,3,2,1,0:T(8,128)} %copy-done.8), calls=%async_computation.1 | async-start | bytes 1966080 | tf_op jit(solution)/shard_map/all_to_all | solution.py:238
  30.9 61.6 %all-gather.7.cloned.1.call-start = ((), (), s32[]{:S(2)}) async-start(), calls=%async_computation.5 | async-start | bytes 1572864 | tf_op jit(solution)/shard_map/all_gather | solution.py:305
  30.9 15.2 %collective-permute-start.4 = (f32[2,256,256]{2,1,0:T(8,128)}, f32[2,256,256]{2,1,0:T(8,128)}, u32[]{:S(2)}, u32[]{:S(2)}) collective-permute-start(f32[2,256,256]{2,1,0:T(8,128)} %get-tuple-element.58), channel_id=1, source_target_pairs={{0,1},{1,0},{2,3},{3,2},{4,5},{5,4},{6,7},{7,6},{8,9},{9,8},{10,11... | collective-permute-start | bytes 1572872 | tf_op jit(solution)/shard_map/ppermute | solution.py:231
  50.4 25.8 %all-to-all-start.2 = ((f32[4,3,2,40,256]{4,3,2,1,0:T(8,128)}), f32[4,3,2,40,256]{4,3,2,1,0:T(8,128)}, u32[]{:S(2)}, u32[]{:S(2)}) async-start(f32[4,3,2,40,256]{4,3,2,1,0:T(8,128)} %copy-done.17), calls=%async_computation.2 | async-start | bytes 1966080 | tf_op jit(solution)/shard_map/all_to_all | solution.py:238
  54.6 14.3 %collective-permute-start = (f32[2,24,256]{2,1,0:T(8,128)S(1)}, f32[2,24,256]{2,1,0:T(8,128)S(1)}, u32[]{:S(2)}, u32[]{:S(2)}) collective-permute-start(f32[2,24,256]{2,1,0:T(8,128)S(1)} %get-tuple-element.31), channel_id=1, source_target_pairs={{0,8},{8,16},{16,24},{24,0},{1,9},{9,17},{17,25},{25,1},{2,10},{10... | collective-permute-start | bytes 147464 | tf_op jit(solution)/shard_map/ppermute | solution.py:235
  55.1 14.8 %collective-permute-start.1 = (f32[2,24,256]{2,1,0:T(8,128)S(1)}, f32[2,24,256]{2,1,0:T(8,128)S(1)}, u32[]{:S(2)}, u32[]{:S(2)}) collective-permute-start(f32[2,24,256]{2,1,0:T(8,128)S(1)} %get-tuple-element.32), channel_id=1, source_target_pairs={{0,16},{8,24},{16,0},{24,8},{1,17},{9,25},{17,1},{25,9},{2,18},{10... | collective-permute-start | bytes 147464 | tf_op jit(solution)/shard_map/ppermute | solution.py:235
  56.8 13.1 %collective-permute-start.2 = (f32[2,24,256]{2,1,0:T(8,128)S(1)}, f32[2,24,256]{2,1,0:T(8,128)S(1)}, u32[]{:S(2)}, u32[]{:S(2)}) collective-permute-start(f32[2,24,256]{2,1,0:T(8,128)S(1)} %get-tuple-element.33), channel_id=1, source_target_pairs={{0,24},{8,0},{16,8},{24,16},{1,25},{9,1},{17,9},{25,17},{2,26},{10... | collective-permute-start | bytes 147464 | tf_op jit(solution)/shard_map/ppermute | solution.py:235
  70.6 24.9 %collective-permute-start.3 = (f32[2,96,256]{2,1,0:T(8,128)}, f32[2,96,256]{2,1,0:T(8,128)}, u32[]{:S(2)}, u32[]{:S(2)}) collective-permute-start(f32[2,96,256]{2,1,0:T(8,128)} %shard_map.62.refs_5_.refs_0_), channel_id=1, source_target_pairs={{0,2},{1,3},{2,0},{3,1},{4,6},{5,7},{6,4},{7,5},{8,10},{9,11},{10,... | collective-permute-start | bytes 589832 | tf_op jit(solution)/shard_map/ppermute | solution.py:233
  76.2 38.1 %all-to-all-start.3 = ((f32[4,3,2,24,256]{4,3,2,1,0:T(8,128)}), f32[4,3,2,24,256]{4,3,2,1,0:T(8,128)}, u32[]{:S(2)}, u32[]{:S(2)}) async-start(f32[4,3,2,24,256]{4,3,2,1,0:T(8,128)} %copy-done.20), calls=%async_computation.3 | async-start | bytes 1179648 | tf_op jit(solution)/shard_map/all_to_all | solution.py:238
  80.4 10.8 %collective-permute-start.5 = (f32[2,40,256]{2,1,0:T(8,128)S(1)}, f32[2,40,256]{2,1,0:T(8,128)S(1)}, u32[]{:S(2)}, u32[]{:S(2)}) collective-permute-start(f32[2,40,256]{2,1,0:T(8,128)S(1)} %get-tuple-element.35), channel_id=1, source_target_pairs={{0,8},{8,16},{16,24},{24,0},{1,9},{9,17},{17,25},{25,1},{2,10},{10... | collective-permute-start | bytes 245768 | tf_op jit(solution)/shard_map/ppermute | solution.py:235
  80.9 11.3 %collective-permute-start.6 = (f32[2,40,256]{2,1,0:T(8,128)S(1)}, f32[2,40,256]{2,1,0:T(8,128)S(1)}, u32[]{:S(2)}, u32[]{:S(2)}) collective-permute-start(f32[2,40,256]{2,1,0:T(8,128)S(1)} %get-tuple-element.36), channel_id=1, source_target_pairs={{0,16},{8,24},{16,0},{24,8},{1,17},{9,25},{17,1},{25,9},{2,18},{10... | collective-permute-start | bytes 245768 | tf_op jit(solution)/shard_map/ppermute | solution.py:235
  82.5 9.6 %collective-permute-start.7 = (f32[2,40,256]{2,1,0:T(8,128)S(1)}, f32[2,40,256]{2,1,0:T(8,128)S(1)}, u32[]{:S(2)}, u32[]{:S(2)}) collective-permute-start(f32[2,40,256]{2,1,0:T(8,128)S(1)} %get-tuple-element.37), channel_id=1, source_target_pairs={{0,24},{8,0},{16,8},{24,16},{1,25},{9,1},{17,9},{25,17},{2,26},{10... | collective-permute-start | bytes 245768 | tf_op jit(solution)/shard_map/ppermute | solution.py:235
  92.2 18.5 %collective-permute-start.9 = (f32[2,160,256]{2,1,0:T(8,128)S(1)}, f32[2,160,256]{2,1,0:T(8,128)}, u32[]{:S(2)}, u32[]{:S(2)}) collective-permute-start(f32[2,160,256]{2,1,0:T(8,128)S(1)} %shard_map.64.refs_2_.refs_4_.refs_0_), channel_id=1, source_target_pairs={{0,2},{1,3},{2,0},{3,1},{4,6},{5,7},{6,4},{7,5},{8,10},{9,11},{10,... | collective-permute-start | bytes 983048 | tf_op jit(solution)/shard_map/ppermute | solution.py:233
  95.5 15.3 %copy-start.4 = (bf16[1024,1024]{1,0:T(8,128)(2,1)}, bf16[1024,1024]{1,0:T(8,128)(2,1)S(1)}, u32[]{:S(2)}) copy-start(bf16[1024,1024]{1,0:T(8,128)(2,1)S(1)} %get-tuple-element.38.refs_2_) | copy-start | bytes 6291460
  95.5 15.3 %copy-start.6 = (bf16[1024,1024]{1,0:T(8,128)(2,1)}, bf16[1024,1024]{1,0:T(8,128)(2,1)S(1)}, u32[]{:S(2)}) copy-start(bf16[1024,1024]{1,0:T(8,128)(2,1)S(1)} %get-tuple-element.39.refs_3_) | copy-start | bytes 6291460
  100.6 3.9 %collective-permute-start.10 = (f32[2,40,256]{2,1,0:T(8,128)S(1)}, f32[2,40,256]{2,1,0:T(8,128)S(1)}, u32[]{:S(2)}, u32[]{:S(2)}) collective-permute-start(f32[2,40,256]{2,1,0:T(8,128)S(1)} %get-tuple-element.44), channel_id=1, source_target_pairs={{0,8},{8,16},{16,24},{24,0},{1,9},{9,17},{17,25},{25,1},{2,10},{10... | collective-permute-start | bytes 245768 | tf_op jit(solution)/shard_map/ppermute | solution.py:235
  101.7 4.6 %collective-permute-start.11 = (f32[2,40,256]{2,1,0:T(8,128)S(1)}, f32[2,40,256]{2,1,0:T(8,128)S(1)}, u32[]{:S(2)}, u32[]{:S(2)}) collective-permute-start(f32[2,40,256]{2,1,0:T(8,128)S(1)} %get-tuple-element.45), channel_id=1, source_target_pairs={{0,16},{8,24},{16,0},{24,8},{1,17},{9,25},{17,1},{25,9},{2,18},{10... | collective-permute-start | bytes 245768 | tf_op jit(solution)/shard_map/ppermute | solution.py:235
  102.0 4.3 %collective-permute-start.12 = (f32[2,40,256]{2,1,0:T(8,128)S(1)}, f32[2,40,256]{2,1,0:T(8,128)S(1)}, u32[]{:S(2)}, u32[]{:S(2)}) collective-permute-start(f32[2,40,256]{2,1,0:T(8,128)S(1)} %get-tuple-element.46), channel_id=1, source_target_pairs={{0,24},{8,0},{16,8},{24,16},{1,25},{9,1},{17,9},{25,17},{2,26},{10... | collective-permute-start | bytes 245768 | tf_op jit(solution)/shard_map/ppermute | solution.py:235
  107.0 18.7 %collective-permute-start.14 = (f32[2,160,256]{2,1,0:T(8,128)}, f32[2,160,256]{2,1,0:T(8,128)}, u32[]{:S(2)}, u32[]{:S(2)}) collective-permute-start(f32[2,160,256]{2,1,0:T(8,128)} %shard_map.68.refs_4_.refs_0_), channel_id=1, source_target_pairs={{0,2},{1,3},{2,0},{3,1},{4,6},{5,7},{6,4},{7,5},{8,10},{9,11},{10,... | collective-permute-start | bytes 983048 | tf_op jit(solution)/shard_map/ppermute | solution.py:233
  116.9 3.6 %collective-permute-start.15 = (f32[2,24,256]{2,1,0:T(8,128)S(1)}, f32[2,24,256]{2,1,0:T(8,128)S(1)}, u32[]{:S(2)}, u32[]{:S(2)}) collective-permute-start(f32[2,24,256]{2,1,0:T(8,128)S(1)} %get-tuple-element.51), channel_id=1, source_target_pairs={{0,8},{8,16},{16,24},{24,0},{1,9},{9,17},{17,25},{25,1},{2,10},{10... | collective-permute-start | bytes 147464 | tf_op jit(solution)/shard_map/ppermute | solution.py:235
  117.1 4.4 %collective-permute-start.16 = (f32[2,24,256]{2,1,0:T(8,128)S(1)}, f32[2,24,256]{2,1,0:T(8,128)S(1)}, u32[]{:S(2)}, u32[]{:S(2)}) collective-permute-start(f32[2,24,256]{2,1,0:T(8,128)S(1)} %get-tuple-element.52), channel_id=1, source_target_pairs={{0,16},{8,24},{16,0},{24,8},{1,17},{9,25},{17,1},{25,9},{2,18},{10... | collective-permute-start | bytes 147464 | tf_op jit(solution)/shard_map/ppermute | solution.py:235
  117.7 3.9 %collective-permute-start.17 = (f32[2,24,256]{2,1,0:T(8,128)S(1)}, f32[2,24,256]{2,1,0:T(8,128)S(1)}, u32[]{:S(2)}, u32[]{:S(2)}) collective-permute-start(f32[2,24,256]{2,1,0:T(8,128)S(1)} %get-tuple-element.53), channel_id=1, source_target_pairs={{0,24},{8,0},{16,8},{24,16},{1,25},{9,1},{17,9},{25,17},{2,26},{10... | collective-permute-start | bytes 147464 | tf_op jit(solution)/shard_map/ppermute | solution.py:235
  121.6 13.0 %collective-permute-start.19 = (f32[2,96,256]{2,1,0:T(8,128)S(1)}, f32[2,96,256]{2,1,0:T(8,128)S(1)}, u32[]{:S(2)}, u32[]{:S(2)}) collective-permute-start(f32[2,96,256]{2,1,0:T(8,128)S(1)} %shard_map.71.refs_4_.refs_0_), channel_id=1, source_target_pairs={{0,2},{1,3},{2,0},{3,1},{4,6},{5,7},{6,4},{7,5},{8,10},{9,11},{10,... | collective-permute-start | bytes 589832 | tf_op jit(solution)/shard_map/ppermute | solution.py:233
  121.7 26.5 %collective-permute-start.13 = (f32[2,160,256]{2,1,0:T(8,128)}, f32[2,160,256]{2,1,0:T(8,128)S(1)}, u32[]{:S(2)}, u32[]{:S(2)}) collective-permute-start(f32[2,160,256]{2,1,0:T(8,128)} %copy-done.23), channel_id=1, source_target_pairs={{0,1},{1,0},{2,3},{3,2},{4,5},{5,4},{6,7},{7,6},{8,9},{9,8},{10,11... | collective-permute-start | bytes 983048 | tf_op jit(solution)/shard_map/ppermute | solution.py:231
  128.0 24.4 %collective-permute-start.18 = (f32[2,160,256]{2,1,0:T(8,128)S(1)}, f32[2,160,256]{2,1,0:T(8,128)S(1)}, u32[]{:S(2)}, u32[]{:S(2)}) collective-permute-start(f32[2,160,256]{2,1,0:T(8,128)S(1)} %get-tuple-element.55), channel_id=1, source_target_pairs={{0,1},{1,0},{2,3},{3,2},{4,5},{5,4},{6,7},{7,6},{8,9},{9,8},{10,11... | collective-permute-start | bytes 983048 | tf_op jit(solution)/shard_map/ppermute | solution.py:231
  133.0 15.2 %collective-permute-start.8 = (f32[2,96,256]{2,1,0:T(8,128)S(1)}, f32[2,96,256]{2,1,0:T(8,128)S(1)}, u32[]{:S(2)}, u32[]{:S(2)}) collective-permute-start(f32[2,96,256]{2,1,0:T(8,128)S(1)} %copy-done.25), channel_id=1, source_target_pairs={{0,1},{1,0},{2,3},{3,2},{4,5},{5,4},{6,7},{7,6},{8,9},{9,8},{10,11... | collective-permute-start | bytes 589832 | tf_op jit(solution)/shard_map/ppermute | solution.py:231
  134.5 17.9 %copy-start.14 = (f32[2,160,256]{2,1,0:T(8,128)S(1)}, f32[2,160,256]{2,1,0:T(8,128)}, u32[]{:S(2)}) copy-start(f32[2,160,256]{2,1,0:T(8,128)} %copy-done.12) | copy-start | bytes 983044
  134.5 17.9 %copy-start.19 = (f32[2,96,256]{2,1,0:T(8,128)S(1)}, f32[2,96,256]{2,1,0:T(8,128)}, u32[]{:S(2)}) copy-start(f32[2,96,256]{2,1,0:T(8,128)} %copy-done.18) | copy-start | bytes 589828
  135.7 16.7 %collective-permute-start.20 = (f32[2,96,256]{2,1,0:T(8,128)S(1)}, f32[2,96,256]{2,1,0:T(8,128)S(1)}, u32[]{:S(2)}, u32[]{:S(2)}) collective-permute-start(f32[2,96,256]{2,1,0:T(8,128)S(1)} %get-tuple-element.57), channel_id=1, source_target_pairs={{0,1},{1,0},{2,3},{3,2},{4,5},{5,4},{6,7},{7,6},{8,9},{9,8},{10,11... | collective-permute-start | bytes 589832 | tf_op jit(solution)/shard_map/ppermute | solution.py:231
  (21 other events, 60.5 us)
Sparse Core Ops, SparseCore 0:
  9.8 23.9 all-gather.4
  46.3 22.8 all-gather.6

commit v4 on v3

v4 whole, which is shorter than its diff:
```python
import functools
import math

import jax
import jax.numpy as jnp
import numpy as np
from jax import lax
from jax.experimental import pallas as pl
from jax.experimental.pallas import tpu as pltpu
from jax.sharding import PartitionSpec as P

CORES = 2
WEIGHTS = (5, 10, 11, 6)
SUBLANES, LANES = 8, 128
VMEM_LIMIT = 40 * 2**20
ANYWHERE = pl.BlockSpec(memory_space=pl.ANY)
IN_VMEM = pl.BlockSpec(memory_space=pltpu.VMEM)
IN_HBM = pl.BlockSpec(memory_space=pltpu.HBM)
IN_SMEM = pl.BlockSpec(memory_space=pltpu.SMEM)


def chunk_sizes(units):
    if units % sum(WEIGHTS):
        return [SUBLANES * part for part in (units // 2, units - units // 2) if part]
    return [SUBLANES * weight * units // sum(WEIGHTS) for weight in WEIGHTS]


def angle_tables(points):
    cosine = [[1.0, 0.0, -1.0, 0.0][4 * r // points] if 4 * r % points == 0 else math.cos(2 * math.pi * r / points) for r in range(points)]
    sine = [[0.0, 1.0, 0.0, -1.0][4 * r // points] if 4 * r % points == 0 else math.sin(2 * math.pi * r / points) for r in range(points)]
    return np.array([cosine, sine], np.float32)


def times_i(value, power):
    real, imag = value
    return [(real, imag), (-imag, real), (-real, -imag), (imag, -real)][power % 4]


def add(left, right):
    return (left[0] + right[0], left[1] + right[1])


def subtract(left, right):
    return (left[0] - right[0], left[1] - right[1])


def twiddle(value, index, points, sign):
    if 4 * index % points == 0:
        return times_i(value, sign * (4 * index // points))
    angle = sign * 2.0 * math.pi * index / points
    cosine, sine = math.cos(angle), math.sin(angle)
    real, imag = value
    return (real * cosine - imag * sine, imag * cosine + real * sine)


def transform(values, sign):
    points = len(values)
    if points == 1:
        return values
    if points % 2:
        return [
            functools.reduce(add, [twiddle(value, at * out % points, points, sign) for at, value in enumerate(values)])
            for out in range(points)
        ]
    even, odd = transform(values[::2], sign), transform(values[1::2], sign)
    odd = [twiddle(value, at, points, sign) for at, value in enumerate(odd)]
    return [add(e, o) for e, o in zip(even, odd)] + [subtract(e, o) for e, o in zip(even, odd)]


def at_rows(ref, start, size):
    return ref.at[:, 0, pl.ds(pl.multiple_of(start, SUBLANES), size), :]


def pack_kernel(chips, base, step, *refs):
    sources, pieces, sem = refs[:3], refs[3:-1], refs[-1]
    chip = lax.axis_index("ka") // CORES
    copies = []
    for gap, piece in enumerate(pieces):
        start = base + lax.rem(chip - gap + chips, chips) * step
        for at, source in enumerate(sources):
            copies.append(pltpu.make_async_copy(at_rows(source, start, step), piece.at[at], sem.at[len(copies)]))
    for copy in copies:
        copy.start()
    for copy in copies:
        copy.wait()


def rotate(value, cosine, sine):
    return (value[0] * cosine - value[1] * sine, value[1] * cosine + value[0] * sine)


def energy_kernel(chips, scale, tables, *refs):
    here, other, sigmas = refs[:chips], refs[chips : 2 * chips], refs[2 * chips :]
    points = chips * CORES
    own = lax.axis_index("ka")
    side = (1 - 2 * lax.rem(own, CORES)).astype(jnp.float32)
    cosines = [tables[0, lax.rem(own * r, points)] for r in range(points)]
    sines = [tables[1, lax.rem(own * r, points)] for r in range(points)]
    step, across = here[0].shape[2], here[0].shape[3] // LANES
    root = points**-0.5

    def join(first, second):
        out = []
        for r in range(points):
            left, right = first[r % chips], second[r % chips]
            if 2 * r % points == 0:
                out.append(add(left, right) if r == 0 else subtract(left, right))
            elif 4 * r % points == 0:
                turned = (-right[1] * side, right[0] * side)
                out.append(add(left, turned) if 4 * r == points else subtract(left, turned))
            else:
                angle = 2.0 * math.pi * r / points
                out.append(add(left, rotate(right, math.cos(angle), math.sin(angle) * side)))
        return out

    def tile(index, carry):
        spot = (
            pl.ds(pl.multiple_of(lax.div(index, across) * SUBLANES, SUBLANES), SUBLANES),
            pl.ds(pl.multiple_of(lax.rem(index, across) * LANES, LANES), LANES),
        )
        lesser, greater, screen = (
            join(*(transform([(ref[at, 0, *spot], ref[at, 1, *spot]) for ref in group], 1) for group in (here, other)))
            for at in range(3)
        )
        values = []
        for r in range(points):
            less, great = lesser[r], greater[r]
            inter = screen[r] if r == 0 else rotate(screen[r], cosines[r], sines[r])
            polar_real = less[0] * great[1] - less[1] * great[0]
            polar_imag = less[0] * great[0] + less[1] * great[1]
            inter_real = inter[0] + polar_real * root
            inter_imag = inter[1] + polar_imag * root
            values.append(
                (
                    (less[0] * inter_imag + less[1] * inter_real) * -scale,
                    (less[0] * inter_real - less[1] * inter_imag) * scale,
                )
            )
        folded = [add(values[r], values[r + chips]) for r in range(chips)]
        for out, (real, imag) in zip(sigmas, transform(folded, -1)):
            out[0, *spot] = real
            out[1, *spot] = imag
        return carry

    lax.fori_loop(0, step // SUBLANES * across, tile, 0)


def split(value):
    high = value.astype(jnp.bfloat16)
    return high, (value - high.astype(jnp.float32)).astype(jnp.bfloat16)


def right_kernel(row_parts, group, *refs):
    pieces, high, low = refs[: row_parts * group], refs[-2], refs[-1]
    row_at, half = lax.axis_index("tr"), lax.axis_index("tc") // group
    depth, cols = pieces[0].shape[1:]
    for part in range(row_parts):
        place = lax.rem(half - row_at + part + row_parts, row_parts) * depth
        upper = pl.ds(pl.multiple_of(place, depth), depth)
        lower = pl.ds(pl.multiple_of(place + row_parts * depth, depth), depth)
        for gap in range(group):
            piece = pieces[part * group + gap]
            first = pl.ds(gap * cols, cols)
            second = pl.ds((group + gap) * cols, cols)
            real, imag = split(piece[0]), split(piece[1])
            for out, real_part, imag_part in zip((high, low), real, imag):
                out[upper, first] = real_part
                out[lower, second] = real_part
                out[upper, second] = imag_part
                out[lower, first] = -imag_part


def product_kernel(row_parts, group, chips, *refs):
    count = row_parts * chips
    sides, high, low, outs = refs[:count], refs[count], refs[count + 1], refs[count + 2 :]
    left = jnp.concatenate(
        [
            jnp.concatenate([sides[gap * row_parts + part][at] for at in (0, 1) for part in range(row_parts)], axis=1)
            for gap in range(chips)
        ],
        axis=0,
    )
    left_high, left_low = split(left)
    cols = outs[0].shape[-1]
    for at in range(2):
        for gap in range(group):
            spot = pl.ds((at * group + gap) * cols, cols)
            right_high, right_low = high[:, spot], low[:, spot]
            dot = functools.partial(jnp.dot, preferred_element_type=jnp.float32)
            outs[gap][at] = dot(left_high, right_high) + (dot(left_high, right_low) + dot(left_low, right_high))


def final_kernel(group, chips, sizes, *refs):
    count = len(sizes) * group
    parts, less, collision, after = refs[:count], refs[count], refs[-2], refs[-1]
    chip = lax.axis_index("ka") // CORES
    base = 0
    for at, step in enumerate(sizes):
        for gap in range(chips):
            start = base + lax.rem(chip - gap + chips, chips) * step
            rows = pl.ds(pl.multiple_of(start, SUBLANES), step)
            spot = pl.ds(gap * step, step)
            total = parts[at * group][:, spot, :]
            for part in parts[at * group + 1 : (at + 1) * group]:
                total = total + part[:, spot, :]
            collision[:, 0, rows, :] = total
            after[:, 0, rows, :] = less[:, 0, rows, :] + total
        base += chips * step


def call(kernel, out_shapes, in_specs, out_specs, args, scratch=(), after=()):
    count, skipped = len(args), len(after)

    def ordered(*refs):
        kernel(*refs[:count], *refs[count + skipped :])

    return pl.pallas_call(
        ordered,
        out_shape=out_shapes,
        in_specs=in_specs + [ANYWHERE] * skipped,
        out_specs=out_specs,
        scratch_shapes=scratch,
        cost_estimate=pl.CostEstimate(flops=1, bytes_accessed=1, transcendentals=0),
        compiler_params=pltpu.CompilerParams(vmem_limit_bytes=VMEM_LIMIT),
    )(*args, *after)


def body(green_less, green_great, screened):
    momenta, row_parts, col_parts = lax.axis_size("ka"), lax.axis_size("tr"), lax.axis_size("tc")
    member = lax.axis_index("tc") % (col_parts // row_parts)
    rows, cols = green_less.shape[2], green_less.shape[3]
    group, chips = col_parts // row_parts, momenta // CORES
    sizes = chunk_sizes(rows // chips // SUBLANES)
    bases = [chips * sum(sizes[:at]) for at in range(len(sizes))]
    f32 = functools.partial(jax.ShapeDtypeStruct, dtype=jnp.float32)
    bf16 = functools.partial(jax.ShapeDtypeStruct, dtype=jnp.bfloat16)
    inputs = (green_less, green_great, screened)
    scale = momenta**-1.5 * (rows * row_parts) ** -0.5
    tables = jnp.asarray(angle_tables(momenta))

    def to_chip(value, gap):
        moves = [
            (chip * CORES + core, (chip + gap) % chips * CORES + core) for chip in range(chips) for core in range(CORES)
        ]
        return lax.ppermute(value, "ka", moves)

    def to_core(value):
        return lax.ppermute(value, "ka", [(s, s + 1 - 2 * (s % CORES)) for s in range(momenta)])

    def to_panel(value, rows_on, cols_on):
        moves = []
        for i in range(row_parts):
            for j in range(col_parts):
                column = j // group * group + (j + cols_on) % group
                moves.append((i * col_parts + j, (i + rows_on) % row_parts * col_parts + column))
        return lax.ppermute(value, ("tr", "tc"), moves)

    def to_half(value, gap):
        return lax.ppermute(value, "tc", [(j, (j + group * gap) % col_parts) for j in range(col_parts)])

    def pack(at, after):
        step = sizes[at]
        return call(
            functools.partial(pack_kernel, chips, bases[at], step),
            [f32((3, 2, step, cols))] * chips,
            [IN_HBM] * 3,
            [ANYWHERE] * chips,
            inputs,
            [pltpu.SemaphoreType.DMA((3 * chips,))],
            after,
        )

    def forward(pieces):
        return [to_chip(pieces[gap], -gap) for gap in range(1, chips)], to_core(pieces[0])

    def energy(at, here, other, after):
        return call(
            functools.partial(energy_kernel, chips, scale),
            [f32((2, sizes[at], cols))] * chips,
            [IN_SMEM] + [IN_VMEM] * momenta,
            [IN_VMEM] * chips,
            (tables, *here, *other),
            (),
            after,
        )

    def product(at, lefts, after):
        outs = call(
            functools.partial(product_kernel, row_parts, group, chips),
            [f32((2, chips * sizes[at], cols))] * group,
            [IN_VMEM] * (len(lefts) + 2),
            [IN_VMEM] * group,
            (*lefts, *right),
            (),
            after,
        )
        return [outs[0]] + [to_panel(outs[gap], 0, -gap) for gap in range(1, group)]

    pieces = [pack(0, ())]
    sent = [forward(pieces[0])]

    blocks = green_less[:, 0].reshape(2, group, cols, cols)
    panels = []
    for rows_on in range(row_parts):
        for cols_on in range(group):
            block = lax.dynamic_index_in_dim(blocks, (member + cols_on) % group, 1, False)
            panels.append(to_panel(block, rows_on, cols_on) if rows_on + cols_on else block)
    extent = 2 * row_parts * cols

    lefts, results, right, last = [], [], None, ()
    for at in range(len(sizes) + 1):
        if at < len(sizes):
            across, beside = sent[at]
            if at + 1 < len(sizes):
                pieces.append(pack(at + 1, (across[0], *last)))
                sent.append(forward(pieces[at + 1]))
            here = [pieces[at][0], *across]
            other = [beside, *(to_core(piece) for piece in across)]
            sigmas = energy(at, here, other, last)
            owned = [sigmas[0]] + [to_chip(sigmas[gap], gap) for gap in range(1, chips)]
            lefts.append([part for own in owned for part in [own] + [to_half(own, gap) for gap in range(1, row_parts)]])
            last = sigmas[:1]
        if at == 1:
            right = call(
                functools.partial(right_kernel, row_parts, group),
                [bf16((extent, 2 * group * cols))] * 2,
                [IN_VMEM] * len(panels),
                [IN_VMEM] * 2,
                panels,
                (),
                last,
            )
        if at >= 1:
            results.append(product(at - 1, lefts[at - 1], last))
            last = results[-1][:1]

    return call(
        functools.partial(final_kernel, group, chips, sizes),
        [f32(green_less.shape)] * 2,
        [IN_VMEM] * (len(sizes) * group + 1),
        [IN_VMEM] * 2,
        (*[part for result in results for part in result], green_less),
    )


def solution(mesh):
    spec = P(None, "ka", "tr", "tc")
    return jax.shard_map(body, mesh=mesh, in_specs=(spec,) * 3, out_specs=(spec,) * 2, check_vma=False)
```

time: 162 us -> 128 us (0.79)
  between operations: 14.4 us -> 0.84 us
  starting transfers between devices: 44.1 us -> 33.6 us
  local copies, waits for them, and re-layouts: 15 us -> 4.54 us
  waiting for transfers between devices: 66.8 us -> 72.9 us
  Pallas kernels: 20.5 us -> 15.5 us
    all_to_all x4 -> x0, starting transfers between devices: 16.8 us -> none  [send_pieces(): return lax.all_to_all(pieces, 'ka', split_axis=0, concat_axis=0, tiled=True)]
    ppermute x21 -> x31, waiting for transfers between devices: 59.4 us -> 72.9 us  [the longest x8 35 us: to_half(): lax.ppermute(value, 'tc', [(j, (j + group * gap) % col_parts) for j in ra...]
    unnamed x52 -> x18, local copies, waits for them, and re-layouts: 12.6 us -> 4.47 us
    all_to_all x4 -> x0, waiting for transfers between devices: 7.38 us -> none  [send_pieces(): return lax.all_to_all(pieces, 'ka', split_axis=0, concat_axis=0, tiled=True)]
    ppermute x21 -> x31, starting transfers between devices: 27.2 us -> 33.6 us  [the longest x7 12.1 us: to_panel(): return lax.ppermute(value, ('tr', 'tc'), moves)]
    pallas_call x16 -> x14, Pallas kernels: 20.5 us -> 15.5 us  [call(): pl.pallas_call(ordered, out_shape=out_shapes, in_specs=in_specs + [ANYWHE...]
    squeeze x1, local copies, waits for them, and re-layouts: 2.4 us -> 0.07 us  [body(): lax.dynamic_index_in_dim(blocks, (member + cols_on) % group, 1, False)]
  transfers between devices with their start and end apart: 27 -> 31, of which waited for: 15 -> 15; matrix products, arithmetic and copies ran while one was open for 0% -> 0% of each run, Pallas kernels for 12% -> 10%
where the time goes in v4:
time: 128 us; the launch traced here: 127 us
  waiting for transfers between devices  72.9 us (57%)
  starting transfers between devices  33.6 us (26%)
  Pallas kernels  15.5 us (12%)
  local copies, waits for them, and re-layouts  4.54 us (4%)
    ppermute x8, waiting for transfers between devices, to_half(): lax.ppermute(value, 'tc', [(j, (j + group * gap) % col_parts) for j in ra...  35 us
    ppermute x8, waiting for transfers between devices, to_chip(): return lax.ppermute(value, 'ka', moves)  29.2 us
    pallas_call x14, Pallas kernels, call(): pl.pallas_call(ordered, out_shape=out_shapes, in_specs=in_specs + [ANYWHE...  15.5 us
    ppermute x7, starting transfers between devices, to_panel(): return lax.ppermute(value, ('tr', 'tc'), moves)  12.1 us
    ppermute x8, starting transfers between devices, to_chip(): return lax.ppermute(value, 'ka', moves)  11.2 us
    ppermute x8, starting transfers between devices, to_half(): lax.ppermute(value, 'tc', [(j, (j + group * gap) % col_parts) for j in ra...  8.78 us
    ppermute x7, waiting for transfers between devices, to_panel(): return lax.ppermute(value, ('tr', 'tc'), moves)  8.74 us
    unnamed x18, local copies, waits for them, and re-layouts  4.47 us
  transfers between devices with their start and end apart: 31, of which 15 were waited for; matrix products, arithmetic and copies ran while one was open for 0% of the time, Pallas kernels for 10%

profile of v4, /device:TPU:0, one launch (start us, length us, event | category | flops | bytes accessed | tf_op | source)
XLA Modules:
  0.0 127.4 jit_solution(12215189134713841038)
XLA Ops:
  0.6 1.2 copy-done
  1.9 1.2 copy-done.2
  3.1 1.2 copy-done.4
  5.1 3.0 %collective-permute-start = (f32[3,2,40,256]{3,2,1,0:T(8,128)S(1)}, f32[3,2,40,256]{3,2,1,0:T(8,128)S(1)}, u32[]{:S(2)}, u32[]{:S(2)}) collective-permute-start(f32[3,2,40,256]{3,2,1,0:T(8,128)S(1)} %get-tuple-element.29), channel_id=1, source_target_pairs={{0,16},{8,24},{16,0},{24,8},{1,17},{9,25},{17,1},{25,9},{2,18},{10... | collective-permute-start | bytes 737288 | tf_op jit(solution)/shard_map/ppermute | solution.py:245
  8.1 6.0 %collective-permute-done.refs_2_.refs_3_ = f32[3,2,40,256]{3,2,1,0:T(8,128)S(1)} collective-permute-done((f32[3,2,40,256]{3,2,1,0:T(8,128)S(1)}, f32[3,2,40,256]{3,2,1,0:T(8,128)S(1)}, u32[]{:S(2)}, u32[]{:S(2)}) %collective-permute-start) | collective-permute-done | bytes 245792 | tf_op jit(solution)/shard_map/ppermute | solution.py:245
  16.0 1.7 %collective-permute-start.9 = (f32[3,2,80,256]{3,2,1,0:T(8,128)}, f32[3,2,80,256]{3,2,1,0:T(8,128)}, u32[]{:S(2)}, u32[]{:S(2)}) collective-permute-start(f32[3,2,80,256]{3,2,1,0:T(8,128)} %get-tuple-element.33), channel_id=1, source_target_pairs={{0,16},{8,24},{16,0},{24,8},{1,17},{9,25},{17,1},{25,9},{2,18},{10... | collective-permute-start | bytes 1474568 | tf_op jit(solution)/shard_map/ppermute | solution.py:245
  18.3 1.6 %collective-permute-start.6 = (f32[2,256,256]{2,1,0:T(8,128)S(1)}, f32[2,256,256]{2,1,0:T(8,128)S(1)}, u32[]{:S(2)}, u32[]{:S(2)}) collective-permute-start(f32[2,256,256]{2,1,0:T(8,128)S(1)} %get-tuple-element.54), channel_id=1, source_target_pairs={{0,1},{1,0},{2,3},{3,2},{4,5},{5,4},{6,7},{7,6},{8,9},{9,8},{10,11... | collective-permute-start | bytes 1572872 | tf_op jit(solution)/shard_map/ppermute | solution.py:256
  20.0 1.5 %collective-permute-start.7 = (f32[2,256,256]{2,1,0:T(8,128)S(1)}, f32[2,256,256]{2,1,0:T(8,128)S(1)}, u32[]{:S(2)}, u32[]{:S(2)}) collective-permute-start(f32[2,256,256]{2,1,0:T(8,128)S(1)} %get-tuple-element.55.refs_0_), channel_id=1, source_target_pairs={{0,4},{1,5},{2,6},{3,7},{4,0},{5,1},{6,2},{7,3},{8,12},{9,13},{10,... | collective-permute-start | bytes 1572872 | tf_op jit(solution)/shard_map/ppermute | solution.py:256
  21.5 1.4 %shard_map.60 = (f32[2,40,256]{2,1,0:T(8,128)S(1)}, f32[2,40,256]{2,1,0:T(8,128)S(1)}) custom-call(f32[2,4]{1,0:T(2,128)S(1)} %copy-done.8, f32[3,2,40,256]{3,2,1,0:T(8,128)} %get-tuple-element.28.refs_1_, f32[3,2,40,256]{3,2,1,0:T(8,128)S(1)} %collective-permute-done.refs_2_.refs_3_, f32[3,2,40,256]{3,2,1,0:T(8,128)} %collective-permute-done.1.refs_3_, ...), custom_call_target="tpu_custom_call" | custom-call | flops 1 | bytes 1 | tf_op jit(solution)/shard_map/pallas_call | solution.py:217
  22.9 5.8 %collective-permute-done.9.refs_2_.refs_3_ = f32[3,2,80,256]{3,2,1,0:T(8,128)} collective-permute-done((f32[3,2,80,256]{3,2,1,0:T(8,128)}, f32[3,2,80,256]{3,2,1,0:T(8,128)}, u32[]{:S(2)}, u32[]{:S(2)}) %collective-permute-start.9) | collective-permute-done | bytes 491552 | tf_op jit(solution)/shard_map/ppermute | solution.py:245
  29.5 1.5 %collective-permute-start.16 = (f32[3,2,88,256]{3,2,1,0:T(8,128)S(1)}, f32[3,2,88,256]{3,2,1,0:T(8,128)S(1)}, u32[]{:S(2)}, u32[]{:S(2)}) collective-permute-start(f32[3,2,88,256]{3,2,1,0:T(8,128)S(1)} %get-tuple-element.41), channel_id=1, source_target_pairs={{0,16},{8,24},{16,0},{24,8},{1,17},{9,25},{17,1},{25,9},{2,18},{10... | collective-permute-start | bytes 1622024 | tf_op jit(solution)/shard_map/ppermute | solution.py:245
  32.2 2.5 %collective-permute-start.8 = (f32[2,256,256]{2,1,0:T(8,128)S(1)}, f32[2,256,256]{2,1,0:T(8,128)S(1)}, u32[]{:S(2)}, u32[]{:S(2)}) collective-permute-start(f32[2,256,256]{2,1,0:T(8,128)S(1)} %get-tuple-element.54), channel_id=1, source_target_pairs={{0,5},{1,4},{2,7},{3,6},{4,1},{5,0},{6,3},{7,2},{8,13},{9,12},{10,... | collective-permute-start | bytes 1572872 | tf_op jit(solution)/shard_map/ppermute | solution.py:256
  35.3 8.5 %collective-permute-done.4.refs_2_ = f32[2,40,256]{2,1,0:T(8,128)S(1)} collective-permute-done((f32[2,40,256]{2,1,0:T(8,128)S(1)}, f32[2,40,256]{2,1,0:T(8,128)S(1)}, u32[]{:S(2)}, u32[]{:S(2)}) %collective-permute-start.4) | collective-permute-done | bytes 81952 | tf_op jit(solution)/shard_map/ppermute | solution.py:245
  44.3 2.2 %collective-permute-start.3 = (f32[2,40,256]{2,1,0:T(8,128)S(1)}, f32[2,40,256]{2,1,0:T(8,128)S(1)}, u32[]{:S(2)}, u32[]{:S(2)}) collective-permute-start(f32[2,40,256]{2,1,0:T(8,128)S(1)} %get-tuple-element.30.refs_5_.refs_0_.refs_4_), channel_id=1, source_target_pairs={{0,2},{1,3},{2,0},{3,1},{4,6},{5,7},{6,4},{7,5},{8,10},{9,11},{10,... | collective-permute-start | bytes 245768 | tf_op jit(solution)/shard_map/ppermute | solution.py:259
  47.3 1.8 %shard_map.62 = (f32[2,80,256]{2,1,0:T(8,128)S(1)}, f32[2,80,256]{2,1,0:T(8,128)S(1)}) custom-call(f32[2,4]{1,0:T(2,128)S(1)} %copy-done.8, f32[3,2,80,256]{3,2,1,0:T(8,128)S(1)} %copy-done.7, f32[3,2,80,256]{3,2,1,0:T(8,128)} %collective-permute-done.9.refs_2_.refs_3_, f32[3,2,80,256]{3,2,1,0:T(8,128)S(1)} %collective-permute-done.10.refs_3_, ...), custom_call_target="tpu_custom_call" | custom-call | flops 1 | bytes 1 | tf_op jit(solution)/shard_map/pallas_call | solution.py:217
  49.7 4.2 %collective-permute-done.3.refs_1_ = f32[2,40,256]{2,1,0:T(8,128)S(1)} collective-permute-done((f32[2,40,256]{2,1,0:T(8,128)S(1)}, f32[2,40,256]{2,1,0:T(8,128)S(1)}, u32[]{:S(2)}, u32[]{:S(2)}) %collective-permute-start.3) | collective-permute-done | bytes 81952 | tf_op jit(solution)/shard_map/ppermute | solution.py:259
  54.9 1.2 shard_map.64
  56.6 1.2 collective-permute-start.23
  58.7 1.3 %shard_map.66 = (f32[2,88,256]{2,1,0:T(8,128)S(1)}, f32[2,88,256]{2,1,0:T(8,128)S(1)}) custom-call(f32[2,4]{1,0:T(2,128)S(1)} %copy-done.8, f32[3,2,88,256]{3,2,1,0:T(8,128)S(1)} %get-tuple-element.40.refs_1_, f32[3,2,88,256]{3,2,1,0:T(8,128)S(1)} %collective-permute-done.16.refs_2_.refs_3_, f32[3,2,88,256]{3,2,1,0:T(8,128)S(1)} %collective-permute-done.17.refs_3_, ...), custom_call_target="tpu_custom_call" | custom-call | flops 1 | bytes 1 | tf_op jit(solution)/shard_map/pallas_call | solution.py:217
  61.2 5.4 %collective-permute-done.23.refs_2_ = f32[3,2,48,256]{3,2,1,0:T(8,128)S(1)} collective-permute-done((f32[3,2,48,256]{3,2,1,0:T(8,128)S(1)}, f32[3,2,48,256]{3,2,1,0:T(8,128)S(1)}, u32[]{:S(2)}, u32[]{:S(2)}) %collective-permute-start.23) | collective-permute-done | bytes 294944 | tf_op jit(solution)/shard_map/ppermute | solution.py:245
  66.6 3.5 %collective-permute-done.14.refs_2_ = f32[2,80,256]{2,1,0:T(8,128)S(1)} collective-permute-done((f32[2,80,256]{2,1,0:T(8,128)S(1)}, f32[2,80,256]{2,1,0:T(8,128)S(1)}, u32[]{:S(2)}, u32[]{:S(2)}) %collective-permute-start.14) | collective-permute-done | bytes 163872 | tf_op jit(solution)/shard_map/ppermute | solution.py:245
  70.3 2.7 %collective-permute-start.20 = (f32[2,88,256]{2,1,0:T(8,128)S(1)}, f32[2,88,256]{2,1,0:T(8,128)S(1)}, u32[]{:S(2)}, u32[]{:S(2)}) collective-permute-start(f32[2,88,256]{2,1,0:T(8,128)S(1)} %get-tuple-element.42.refs_6_.refs_0_), channel_id=1, source_target_pairs={{0,2},{1,3},{2,0},{3,1},{4,6},{5,7},{6,4},{7,5},{8,10},{9,11},{10,... | collective-permute-start | bytes 540680 | tf_op jit(solution)/shard_map/ppermute | solution.py:259
  73.2 14.4 %collective-permute-done.15.refs_3_ = f32[2,80,256]{2,1,0:T(8,128)S(1)} collective-permute-done((f32[2,80,256]{2,1,0:T(8,128)S(1)}, f32[2,80,256]{2,1,0:T(8,128)S(1)}, u32[]{:S(2)}, u32[]{:S(2)}) %collective-permute-start.15) | collective-permute-done | bytes 163872 | tf_op jit(solution)/shard_map/ppermute | solution.py:259
  87.7 1.2 shard_map.67
  91.2 1.9 %collective-permute-done.22.refs_3_ = f32[2,88,256]{2,1,0:T(8,128)S(1)} collective-permute-done((f32[2,88,256]{2,1,0:T(8,128)S(1)}, f32[2,88,256]{2,1,0:T(8,128)S(1)}, u32[]{:S(2)}, u32[]{:S(2)}) %collective-permute-start.22) | collective-permute-done | bytes 180256 | tf_op jit(solution)/shard_map/ppermute | solution.py:259
  93.1 1.3 %shard_map.70 = (f32[2,176,256]{2,1,0:T(8,128)S(1)}, f32[2,176,256]{2,1,0:T(8,128)S(1)}) custom-call(f32[2,88,256]{2,1,0:T(8,128)S(1)} %get-tuple-element.42.refs_6_.refs_0_, f32[2,88,256]{2,1,0:T(8,128)S(1)} %collective-permute-done.20.refs_1_, f32[2,88,256]{2,1,0:T(8,128)S(1)} %collective-permute-done.21.refs_2_, ...), custom_call_target="tpu_custom_call" | custom-call | flops 1 | bytes 1 | tf_op jit(solution)/shard_map/pallas_call | solution.py:217
  94.5 2.0 %collective-permute-start.19 = (f32[2,160,256]{2,1,0:T(8,128)S(1)}, f32[2,160,256]{2,1,0:T(8,128)S(1)}, u32[]{:S(2)}, u32[]{:S(2)}) collective-permute-start(f32[2,160,256]{2,1,0:T(8,128)S(1)} %get-tuple-element.44), channel_id=1, source_target_pairs={{0,1},{1,0},{2,3},{3,2},{4,5},{5,4},{6,7},{7,6},{8,9},{9,8},{10,11... | collective-permute-start | bytes 983048 | tf_op jit(solution)/shard_map/ppermute | solution.py:256
  96.9 2.5 %collective-permute-start.29 = (f32[2,48,256]{2,1,0:T(8,128)S(1)}, f32[2,48,256]{2,1,0:T(8,128)S(1)}, u32[]{:S(2)}, u32[]{:S(2)}) collective-permute-start(f32[2,48,256]{2,1,0:T(8,128)S(1)} %collective-permute-done.28.refs_2_), channel_id=1, source_target_pairs={{0,2},{1,3},{2,0},{3,1},{4,6},{5,7},{6,4},{7,5},{8,10},{9,11},{10,... | collective-permute-start | bytes 294920 | tf_op jit(solution)/shard_map/ppermute | solution.py:259
  99.4 12.0 %collective-permute-done.27.refs_1_ = f32[2,48,256]{2,1,0:T(8,128)S(1)} collective-permute-done((f32[2,48,256]{2,1,0:T(8,128)S(1)}, f32[2,48,256]{2,1,0:T(8,128)S(1)}, u32[]{:S(2)}, u32[]{:S(2)}) %collective-permute-start.27) | collective-permute-done | bytes 98336 | tf_op jit(solution)/shard_map/ppermute | solution.py:259
  113.7 4.2 %collective-permute-start.30 = (f32[2,96,256]{2,1,0:T(8,128)S(1)}, f32[2,96,256]{2,1,0:T(8,128)S(1)}, u32[]{:S(2)}, u32[]{:S(2)}) collective-permute-start(f32[2,96,256]{2,1,0:T(8,128)S(1)} %get-tuple-element.53), channel_id=1, source_target_pairs={{0,1},{1,0},{2,3},{3,2},{4,5},{5,4},{6,7},{7,6},{8,9},{9,8},{10,11... | collective-permute-start | bytes 589832 | tf_op jit(solution)/shard_map/ppermute | solution.py:256
  117.9 8.0 %collective-permute-done.12.refs_1_ = f32[2,80,256]{2,1,0:T(8,128)S(1)} collective-permute-done((f32[2,80,256]{2,1,0:T(8,128)S(1)}, f32[2,80,256]{2,1,0:T(8,128)S(1)}, u32[]{:S(2)}, u32[]{:S(2)}) %collective-permute-start.12) | collective-permute-done | bytes 163872 | tf_op jit(solution)/shard_map/ppermute | solution.py:256
  125.9 1.5 %shard_map.72 = (f32[2,1,512,256]{3,2,1,0:T(8,128)}, f32[2,1,512,256]{3,2,1,0:T(8,128)}) custom-call(f32[2,80,256]{2,1,0:T(8,128)S(1)} %get-tuple-element.37.refs_5_.refs_4_.refs_0_, f32[2,80,256]{2,1,0:T(8,128)S(1)} %collective-permute-done.12.refs_1_, f32[2,160,256]{2,1,0:T(8,128)S(1)} %get-tuple-element.43.refs_5_.refs_2_, ...), custom_call_target="tpu_custom_call" | custom-call | flops 1 | bytes 1 | tf_op jit(solution)/shard_map/pallas_call | solution.py:217
  (63 shorter events, 16.7 us)
Async XLA Ops:
  5.1 16.4 %copy-start.8 = (f32[2,4]{1,0:T(2,128)S(1)}, f32[2,4]{1,0:T(2,128)}, u32[]{:S(2)}) copy-start(f32[2,4]{1,0:T(2,128)} %constant.42.clone.refs_0_) | copy-start | bytes 100
  5.1 9.0 %collective-permute-start = (f32[3,2,40,256]{3,2,1,0:T(8,128)S(1)}, f32[3,2,40,256]{3,2,1,0:T(8,128)S(1)}, u32[]{:S(2)}, u32[]{:S(2)}) collective-permute-start(f32[3,2,40,256]{3,2,1,0:T(8,128)S(1)} %get-tuple-element.29), channel_id=1, source_target_pairs={{0,16},{8,24},{16,0},{24,8},{1,17},{9,25},{17,1},{25,9},{2,18},{10... | collective-permute-start | bytes 737288 | tf_op jit(solution)/shard_map/ppermute | solution.py:245
  16.0 12.7 %collective-permute-start.9 = (f32[3,2,80,256]{3,2,1,0:T(8,128)}, f32[3,2,80,256]{3,2,1,0:T(8,128)}, u32[]{:S(2)}, u32[]{:S(2)}) collective-permute-start(f32[3,2,80,256]{3,2,1,0:T(8,128)} %get-tuple-element.33), channel_id=1, source_target_pairs={{0,16},{8,24},{16,0},{24,8},{1,17},{9,25},{17,1},{25,9},{2,18},{10... | collective-permute-start | bytes 1474568 | tf_op jit(solution)/shard_map/ppermute | solution.py:245
  17.7 3.8 %collective-permute-start.1 = (f32[3,2,40,256]{3,2,1,0:T(8,128)}, f32[3,2,40,256]{3,2,1,0:T(8,128)}, u32[]{:S(2)}, u32[]{:S(2)}) collective-permute-start(f32[3,2,40,256]{3,2,1,0:T(8,128)} %get-tuple-element.28.refs_1_), channel_id=1, source_target_pairs={{0,8},{8,0},{16,24},{24,16},{1,9},{9,1},{17,25},{25,17},{2,10},{10... | collective-permute-start | bytes 737288 | tf_op jit(solution)/shard_map/ppermute | solution.py:248
  17.7 3.8 %collective-permute-start.2 = (f32[3,2,40,256]{3,2,1,0:T(8,128)S(1)}, f32[3,2,40,256]{3,2,1,0:T(8,128)S(1)}, u32[]{:S(2)}, u32[]{:S(2)}) collective-permute-start(f32[3,2,40,256]{3,2,1,0:T(8,128)S(1)} %collective-permute-done.refs_2_.refs_3_), channel_id=1, source_target_pairs={{0,8},{8,0},{16,24},{24,16},{1,9},{9,1},{17,25},{25,17},{2,10},{10... | collective-permute-start | bytes 737288 | tf_op jit(solution)/shard_map/ppermute | solution.py:248
  18.3 13.9 %collective-permute-start.6 = (f32[2,256,256]{2,1,0:T(8,128)S(1)}, f32[2,256,256]{2,1,0:T(8,128)S(1)}, u32[]{:S(2)}, u32[]{:S(2)}) collective-permute-start(f32[2,256,256]{2,1,0:T(8,128)S(1)} %get-tuple-element.54), channel_id=1, source_target_pairs={{0,1},{1,0},{2,3},{3,2},{4,5},{5,4},{6,7},{7,6},{8,9},{9,8},{10,11... | collective-permute-start | bytes 1572872 | tf_op jit(solution)/shard_map/ppermute | solution.py:256
  20.0 14.8 %collective-permute-start.7 = (f32[2,256,256]{2,1,0:T(8,128)S(1)}, f32[2,256,256]{2,1,0:T(8,128)S(1)}, u32[]{:S(2)}, u32[]{:S(2)}) collective-permute-start(f32[2,256,256]{2,1,0:T(8,128)S(1)} %get-tuple-element.55.refs_0_), channel_id=1, source_target_pairs={{0,4},{1,5},{2,6},{3,7},{4,0},{5,1},{6,2},{7,3},{8,12},{9,13},{10,... | collective-permute-start | bytes 1572872 | tf_op jit(solution)/shard_map/ppermute | solution.py:256
  29.5 14.4 %collective-permute-start.16 = (f32[3,2,88,256]{3,2,1,0:T(8,128)S(1)}, f32[3,2,88,256]{3,2,1,0:T(8,128)S(1)}, u32[]{:S(2)}, u32[]{:S(2)}) collective-permute-start(f32[3,2,88,256]{3,2,1,0:T(8,128)S(1)} %get-tuple-element.41), channel_id=1, source_target_pairs={{0,16},{8,24},{16,0},{24,8},{1,17},{9,25},{17,1},{25,9},{2,18},{10... | collective-permute-start | bytes 1622024 | tf_op jit(solution)/shard_map/ppermute | solution.py:245
  31.0 13.4 %collective-permute-start.10 = (f32[3,2,80,256]{3,2,1,0:T(8,128)S(1)}, f32[3,2,80,256]{3,2,1,0:T(8,128)S(1)}, u32[]{:S(2)}, u32[]{:S(2)}) collective-permute-start(f32[3,2,80,256]{3,2,1,0:T(8,128)S(1)} %copy-done.7), channel_id=1, source_target_pairs={{0,8},{8,0},{16,24},{24,16},{1,9},{9,1},{17,25},{25,17},{2,10},{10... | collective-permute-start | bytes 1474568 | tf_op jit(solution)/shard_map/ppermute | solution.py:248
  31.0 15.6 %collective-permute-start.11 = (f32[3,2,80,256]{3,2,1,0:T(8,128)}, f32[3,2,80,256]{3,2,1,0:T(8,128)S(1)}, u32[]{:S(2)}, u32[]{:S(2)}) collective-permute-start(f32[3,2,80,256]{3,2,1,0:T(8,128)} %collective-permute-done.9.refs_2_.refs_3_), channel_id=1, source_target_pairs={{0,8},{8,0},{16,24},{24,16},{1,9},{9,1},{17,25},{25,17},{2,10},{10... | collective-permute-start | bytes 1474568 | tf_op jit(solution)/shard_map/ppermute | solution.py:248
  32.2 16.9 %collective-permute-start.8 = (f32[2,256,256]{2,1,0:T(8,128)S(1)}, f32[2,256,256]{2,1,0:T(8,128)S(1)}, u32[]{:S(2)}, u32[]{:S(2)}) collective-permute-start(f32[2,256,256]{2,1,0:T(8,128)S(1)} %get-tuple-element.54), channel_id=1, source_target_pairs={{0,5},{1,4},{2,7},{3,6},{4,1},{5,0},{6,3},{7,2},{8,13},{9,12},{10,... | collective-permute-start | bytes 1572872 | tf_op jit(solution)/shard_map/ppermute | solution.py:256
  34.7 9.1 %collective-permute-start.4 = (f32[2,40,256]{2,1,0:T(8,128)S(1)}, f32[2,40,256]{2,1,0:T(8,128)S(1)}, u32[]{:S(2)}, u32[]{:S(2)}) collective-permute-start(f32[2,40,256]{2,1,0:T(8,128)S(1)} %get-tuple-element.31), channel_id=1, source_target_pairs={{0,16},{8,24},{16,0},{24,8},{1,17},{9,25},{17,1},{25,9},{2,18},{10... | collective-permute-start | bytes 245768 | tf_op jit(solution)/shard_map/ppermute | solution.py:245
  43.8 14.9 %collective-permute-start.17 = (f32[3,2,88,256]{3,2,1,0:T(8,128)S(1)}, f32[3,2,88,256]{3,2,1,0:T(8,128)S(1)}, u32[]{:S(2)}, u32[]{:S(2)}) collective-permute-start(f32[3,2,88,256]{3,2,1,0:T(8,128)S(1)} %get-tuple-element.40.refs_1_), channel_id=1, source_target_pairs={{0,8},{8,0},{16,24},{24,16},{1,9},{9,1},{17,25},{25,17},{2,10},{10... | collective-permute-start | bytes 1622024 | tf_op jit(solution)/shard_map/ppermute | solution.py:248
  43.8 14.9 %collective-permute-start.18 = (f32[3,2,88,256]{3,2,1,0:T(8,128)S(1)}, f32[3,2,88,256]{3,2,1,0:T(8,128)S(1)}, u32[]{:S(2)}, u32[]{:S(2)}) collective-permute-start(f32[3,2,88,256]{3,2,1,0:T(8,128)S(1)} %collective-permute-done.16.refs_2_.refs_3_), channel_id=1, source_target_pairs={{0,8},{8,0},{16,24},{24,16},{1,9},{9,1},{17,25},{25,17},{2,10},{10... | collective-permute-start | bytes 1622024 | tf_op jit(solution)/shard_map/ppermute | solution.py:248
  44.3 9.5 %collective-permute-start.3 = (f32[2,40,256]{2,1,0:T(8,128)S(1)}, f32[2,40,256]{2,1,0:T(8,128)S(1)}, u32[]{:S(2)}, u32[]{:S(2)}) collective-permute-start(f32[2,40,256]{2,1,0:T(8,128)S(1)} %get-tuple-element.30.refs_5_.refs_0_.refs_4_), channel_id=1, source_target_pairs={{0,2},{1,3},{2,0},{3,1},{4,6},{5,7},{6,4},{7,5},{8,10},{9,11},{10,... | collective-permute-start | bytes 245768 | tf_op jit(solution)/shard_map/ppermute | solution.py:259
  46.6 8.4 %collective-permute-start.5 = (f32[2,40,256]{2,1,0:T(8,128)S(1)}, f32[2,40,256]{2,1,0:T(8,128)S(1)}, u32[]{:S(2)}, u32[]{:S(2)}) collective-permute-start(f32[2,40,256]{2,1,0:T(8,128)S(1)} %collective-permute-done.4.refs_2_), channel_id=1, source_target_pairs={{0,2},{1,3},{2,0},{3,1},{4,6},{5,7},{6,4},{7,5},{8,10},{9,11},{10,... | collective-permute-start | bytes 245768 | tf_op jit(solution)/shard_map/ppermute | solution.py:259
  56.6 10.0 %collective-permute-start.23 = (f32[3,2,48,256]{3,2,1,0:T(8,128)S(1)}, f32[3,2,48,256]{3,2,1,0:T(8,128)S(1)}, u32[]{:S(2)}, u32[]{:S(2)}) collective-permute-start(f32[3,2,48,256]{3,2,1,0:T(8,128)S(1)} %get-tuple-element.47), channel_id=1, source_target_pairs={{0,16},{8,24},{16,0},{24,8},{1,17},{9,25},{17,1},{25,9},{2,18},{10... | collective-permute-start | bytes 884744 | tf_op jit(solution)/shard_map/ppermute | solution.py:245
  57.8 12.3 %collective-permute-start.14 = (f32[2,80,256]{2,1,0:T(8,128)S(1)}, f32[2,80,256]{2,1,0:T(8,128)S(1)}, u32[]{:S(2)}, u32[]{:S(2)}) collective-permute-start(f32[2,80,256]{2,1,0:T(8,128)S(1)} %get-tuple-element.39), channel_id=1, source_target_pairs={{0,16},{8,24},{16,0},{24,8},{1,17},{9,25},{17,1},{25,9},{2,18},{10... | collective-permute-start | bytes 491528 | tf_op jit(solution)/shard_map/ppermute | solution.py:245
  60.0 13.1 %collective-permute-start.21 = (f32[2,88,256]{2,1,0:T(8,128)S(1)}, f32[2,88,256]{2,1,0:T(8,128)S(1)}, u32[]{:S(2)}, u32[]{:S(2)}) collective-permute-start(f32[2,88,256]{2,1,0:T(8,128)S(1)} %get-tuple-element.45), channel_id=1, source_target_pairs={{0,16},{8,24},{16,0},{24,8},{1,17},{9,25},{17,1},{25,9},{2,18},{10... | collective-permute-start | bytes 540680 | tf_op jit(solution)/shard_map/ppermute | solution.py:245
  61.2 9.1 %collective-permute-start.13 = (f32[2,80,256]{2,1,0:T(8,128)S(1)}, f32[2,80,256]{2,1,0:T(8,128)S(1)}, u32[]{:S(2)}, u32[]{:S(2)}) collective-permute-start(f32[2,80,256]{2,1,0:T(8,128)S(1)} %get-tuple-element.34.refs_4_.refs_6_.refs_0_), channel_id=1, source_target_pairs={{0,2},{1,3},{2,0},{3,1},{4,6},{5,7},{6,4},{7,5},{8,10},{9,11},{10,... | collective-permute-start | bytes 491528 | tf_op jit(solution)/shard_map/ppermute | solution.py:259
  61.2 27.7 %collective-permute-start.24 = (f32[3,2,48,256]{3,2,1,0:T(8,128)S(1)}, f32[3,2,48,256]{3,2,1,0:T(8,128)S(1)}, u32[]{:S(2)}, u32[]{:S(2)}) collective-permute-start(f32[3,2,48,256]{3,2,1,0:T(8,128)S(1)} %get-tuple-element.46.refs_1_), channel_id=1, source_target_pairs={{0,8},{8,0},{16,24},{24,16},{1,9},{9,1},{17,25},{25,17},{2,10},{10... | collective-permute-start | bytes 884744 | tf_op jit(solution)/shard_map/ppermute | solution.py:248
  66.6 22.2 %collective-permute-start.25 = (f32[3,2,48,256]{3,2,1,0:T(8,128)S(1)}, f32[3,2,48,256]{3,2,1,0:T(8,128)S(1)}, u32[]{:S(2)}, u32[]{:S(2)}) collective-permute-start(f32[3,2,48,256]{3,2,1,0:T(8,128)S(1)} %collective-permute-done.23.refs_2_), channel_id=1, source_target_pairs={{0,8},{8,0},{16,24},{24,16},{1,9},{9,1},{17,25},{25,17},{2,10},{10... | collective-permute-start | bytes 884744 | tf_op jit(solution)/shard_map/ppermute | solution.py:248
  70.1 17.5 %collective-permute-start.15 = (f32[2,80,256]{2,1,0:T(8,128)S(1)}, f32[2,80,256]{2,1,0:T(8,128)S(1)}, u32[]{:S(2)}, u32[]{:S(2)}) collective-permute-start(f32[2,80,256]{2,1,0:T(8,128)S(1)} %collective-permute-done.14.refs_2_), channel_id=1, source_target_pairs={{0,2},{1,3},{2,0},{3,1},{4,6},{5,7},{6,4},{7,5},{8,10},{9,11},{10,... | collective-permute-start | bytes 491528 | tf_op jit(solution)/shard_map/ppermute | solution.py:259
  70.3 20.8 %collective-permute-start.20 = (f32[2,88,256]{2,1,0:T(8,128)S(1)}, f32[2,88,256]{2,1,0:T(8,128)S(1)}, u32[]{:S(2)}, u32[]{:S(2)}) collective-permute-start(f32[2,88,256]{2,1,0:T(8,128)S(1)} %get-tuple-element.42.refs_6_.refs_0_), channel_id=1, source_target_pairs={{0,2},{1,3},{2,0},{3,1},{4,6},{5,7},{6,4},{7,5},{8,10},{9,11},{10,... | collective-permute-start | bytes 540680 | tf_op jit(solution)/shard_map/ppermute | solution.py:259
  73.1 20.0 %collective-permute-start.22 = (f32[2,88,256]{2,1,0:T(8,128)S(1)}, f32[2,88,256]{2,1,0:T(8,128)S(1)}, u32[]{:S(2)}, u32[]{:S(2)}) collective-permute-start(f32[2,88,256]{2,1,0:T(8,128)S(1)} %collective-permute-done.21.refs_2_), channel_id=1, source_target_pairs={{0,2},{1,3},{2,0},{3,1},{4,6},{5,7},{6,4},{7,5},{8,10},{9,11},{10,... | collective-permute-start | bytes 540680 | tf_op jit(solution)/shard_map/ppermute | solution.py:259
  89.9 7.0 %collective-permute-start.28 = (f32[2,48,256]{2,1,0:T(8,128)S(1)}, f32[2,48,256]{2,1,0:T(8,128)S(1)}, u32[]{:S(2)}, u32[]{:S(2)}) collective-permute-start(f32[2,48,256]{2,1,0:T(8,128)S(1)} %get-tuple-element.51), channel_id=1, source_target_pairs={{0,16},{8,24},{16,0},{24,8},{1,17},{9,25},{17,1},{25,9},{2,18},{10... | collective-permute-start | bytes 294920 | tf_op jit(solution)/shard_map/ppermute | solution.py:245
  94.4 31.5 %collective-permute-start.26 = (f32[2,176,256]{2,1,0:T(8,128)S(1)}, f32[2,176,256]{2,1,0:T(8,128)S(1)}, u32[]{:S(2)}, u32[]{:S(2)}) collective-permute-start(f32[2,176,256]{2,1,0:T(8,128)S(1)} %get-tuple-element.50), channel_id=1, source_target_pairs={{0,1},{1,0},{2,3},{3,2},{4,5},{5,4},{6,7},{7,6},{8,9},{9,8},{10,11... | collective-permute-start | bytes 1081352 | tf_op jit(solution)/shard_map/ppermute | solution.py:256
  94.5 31.4 %collective-permute-start.19 = (f32[2,160,256]{2,1,0:T(8,128)S(1)}, f32[2,160,256]{2,1,0:T(8,128)S(1)}, u32[]{:S(2)}, u32[]{:S(2)}) collective-permute-start(f32[2,160,256]{2,1,0:T(8,128)S(1)} %get-tuple-element.44), channel_id=1, source_target_pairs={{0,1},{1,0},{2,3},{3,2},{4,5},{5,4},{6,7},{7,6},{8,9},{9,8},{10,11... | collective-permute-start | bytes 983048 | tf_op jit(solution)/shard_map/ppermute | solution.py:256
  96.5 15.0 %collective-permute-start.27 = (f32[2,48,256]{2,1,0:T(8,128)S(1)}, f32[2,48,256]{2,1,0:T(8,128)S(1)}, u32[]{:S(2)}, u32[]{:S(2)}) collective-permute-start(f32[2,48,256]{2,1,0:T(8,128)S(1)} %get-tuple-element.48.refs_6_.refs_0_), channel_id=1, source_target_pairs={{0,2},{1,3},{2,0},{3,1},{4,6},{5,7},{6,4},{7,5},{8,10},{9,11},{10,... | collective-permute-start | bytes 294920 | tf_op jit(solution)/shard_map/ppermute | solution.py:259
  96.9 15.6 %collective-permute-start.29 = (f32[2,48,256]{2,1,0:T(8,128)S(1)}, f32[2,48,256]{2,1,0:T(8,128)S(1)}, u32[]{:S(2)}, u32[]{:S(2)}) collective-permute-start(f32[2,48,256]{2,1,0:T(8,128)S(1)} %collective-permute-done.28.refs_2_), channel_id=1, source_target_pairs={{0,2},{1,3},{2,0},{3,1},{4,6},{5,7},{6,4},{7,5},{8,10},{9,11},{10,... | collective-permute-start | bytes 294920 | tf_op jit(solution)/shard_map/ppermute | solution.py:259
  113.7 12.3 %collective-permute-start.30 = (f32[2,96,256]{2,1,0:T(8,128)S(1)}, f32[2,96,256]{2,1,0:T(8,128)S(1)}, u32[]{:S(2)}, u32[]{:S(2)}) collective-permute-start(f32[2,96,256]{2,1,0:T(8,128)S(1)} %get-tuple-element.53), channel_id=1, source_target_pairs={{0,1},{1,0},{2,3},{3,2},{4,5},{5,4},{6,7},{7,6},{8,9},{9,8},{10,11... | collective-permute-start | bytes 589832 | tf_op jit(solution)/shard_map/ppermute | solution.py:256
  117.9 8.1 %collective-permute-start.12 = (f32[2,80,256]{2,1,0:T(8,128)S(1)}, f32[2,80,256]{2,1,0:T(8,128)S(1)}, u32[]{:S(2)}, u32[]{:S(2)}) collective-permute-start(f32[2,80,256]{2,1,0:T(8,128)S(1)} %get-tuple-element.38), channel_id=1, source_target_pairs={{0,1},{1,0},{2,3},{3,2},{4,5},{5,4},{6,7},{7,6},{8,9},{9,8},{10,11... | collective-permute-start | bytes 491528 | tf_op jit(solution)/shard_map/ppermute | solution.py:256
  (8 other events, 51.1 us)

commit v5 on v4

--- a/solution.py
+++ b/solution.py
@@ -13,6 +13,7 @@
 WEIGHTS = (5, 10, 11, 6)
 SUBLANES, LANES = 8, 128
 VMEM_LIMIT = 40 * 2**20
+FIRST_LIMIT = 62 * 2**20
 ANYWHERE = pl.BlockSpec(memory_space=pl.ANY)
 IN_VMEM = pl.BlockSpec(memory_space=pltpu.VMEM)
 IN_HBM = pl.BlockSpec(memory_space=pltpu.HBM)
@@ -71,8 +72,8 @@
     return ref.at[:, 0, pl.ds(pl.multiple_of(start, SUBLANES), size), :]
 
 
-def pack_kernel(chips, base, step, *refs):
-    sources, pieces, sem = refs[:3], refs[3:-1], refs[-1]
+def pack_kernel(chips, base, step, passed, *refs):
+    sources, pieces, sem = refs[:3], refs[3 + 2 * passed : -1], refs[-1]
     chip = lax.axis_index("ka") // CORES
     copies = []
     for gap, piece in enumerate(pieces):
@@ -208,7 +209,7 @@
         base += chips * step
 
 
-def call(kernel, out_shapes, in_specs, out_specs, args, scratch=(), after=()):
+def call(kernel, out_shapes, in_specs, out_specs, args, scratch=(), after=(), limit=VMEM_LIMIT, aliases=None):
     count, skipped = len(args), len(after)
 
     def ordered(*refs):
@@ -220,8 +221,9 @@
         in_specs=in_specs + [ANYWHERE] * skipped,
         out_specs=out_specs,
         scratch_shapes=scratch,
+        input_output_aliases=aliases or {},
         cost_estimate=pl.CostEstimate(flops=1, bytes_accessed=1, transcendentals=0),
-        compiler_params=pltpu.CompilerParams(vmem_limit_bytes=VMEM_LIMIT),
+        compiler_params=pltpu.CompilerParams(vmem_limit_bytes=limit),
     )(*args, *after)
 
 
@@ -258,16 +260,32 @@
     def to_half(value, gap):
         return lax.ppermute(value, "tc", [(j, (j + group * gap) % col_parts) for j in range(col_parts)])
 
-    def pack(at, after):
-        step = sizes[at]
-        return call(
-            functools.partial(pack_kernel, chips, bases[at], step),
-            [f32((3, 2, step, cols))] * chips,
-            [IN_HBM] * 3,
-            [ANYWHERE] * chips,
-            inputs,
+    def pack(at, passed, after):
+        step, count = sizes[at], len(passed)
+        outs = call(
+            functools.partial(pack_kernel, chips, bases[at], step, count),
+            [f32(value.shape) for value in passed] + [f32((3, 2, step, cols))] * chips,
+            [IN_HBM] * 3 + [ANYWHERE] * count,
+            [ANYWHERE] * (count + chips),
+            (*inputs, *passed),
             [pltpu.SemaphoreType.DMA((3 * chips,))],
             after,
+            FIRST_LIMIT if at == 0 else VMEM_LIMIT,
+            {3 + spot: spot for spot in range(count)},
+        )
+        return outs[count:], outs[:count]
+
+    def gate(passed, after):
+        count = len(passed)
+        return call(
+            lambda *refs: None,
+            [f32(value.shape) for value in passed],
+            [ANYWHERE] * count,
+            [ANYWHERE] * count,
+            passed,
+            (),
+            after,
+            aliases={spot: spot for spot in range(count)},
         )
 
     def forward(pieces):
@@ -296,7 +314,7 @@
         )
         return [outs[0]] + [to_panel(outs[gap], 0, -gap) for gap in range(1, group)]
 
-    pieces = [pack(0, ())]
+    pieces = [pack(0, (), ())[0]]
     sent = [forward(pieces[0])]
 
     blocks = green_less[:, 0].reshape(2, group, cols, cols)
@@ -307,32 +325,42 @@
             panels.append(to_panel(block, rows_on, cols_on) if rows_on + cols_on else block)
     extent = 2 * row_parts * cols
 
-    lefts, results, right, last = [], [], None, ()
+    lefts, results, last, arrived, returned = [], [], (), (), ()
     for at in range(len(sizes) + 1):
         if at < len(sizes):
             across, beside = sent[at]
             if at + 1 < len(sizes):
-                pieces.append(pack(at + 1, (across[0], *last)))
-                sent.append(forward(pieces[at + 1]))
+                fresh, across = pack(at + 1, across, (*arrived, *last))
+                pieces.append(fresh)
+                sent.append(forward(fresh))
+            else:
+                across = gate(across, (*arrived, *last))
+            gates = panels[1:group]
+            if at == 1:
+                right = call(
+                    functools.partial(right_kernel, row_parts, group),
+                    [bf16((extent, 2 * group * cols))] * 2,
+                    [IN_VMEM] * len(panels),
+                    [IN_VMEM] * 2,
+                    panels,
+                    (),
+                    across,
+                )
+                gates = right
             here = [pieces[at][0], *across]
             other = [beside, *(to_core(piece) for piece in across)]
-            sigmas = energy(at, here, other, last)
+            sigmas = energy(at, here, other, gates)
             owned = [sigmas[0]] + [to_chip(sigmas[gap], gap) for gap in range(1, chips)]
             lefts.append([part for own in owned for part in [own] + [to_half(own, gap) for gap in range(1, row_parts)]])
+            returned = owned[1:2]
+            arrived = (*returned, *lefts[at][1:2])
+            if at == 0:
+                arrived += tuple(panels[group:])
             last = sigmas[:1]
-        if at == 1:
-            right = call(
-                functools.partial(right_kernel, row_parts, group),
-                [bf16((extent, 2 * group * cols))] * 2,
-                [IN_VMEM] * len(panels),
-                [IN_VMEM] * 2,
-                panels,
-                (),
-                last,
-            )
         if at >= 1:
-            results.append(product(at - 1, lefts[at - 1], last))
-            last = results[-1][:1]
+            gates = (*last, *(returned if at + 1 == len(sizes) else ()), *(results[-1][1:] if results else ()))
+            results.append(product(at - 1, lefts[at - 1], gates))
+            last, returned = results[-1][:1], ()
 
     return call(
         functools.partial(final_kernel, group, chips, sizes),

time: 128 us -> 129 us (level)
  Pallas kernels: 15.5 us -> 29.4 us
  waiting for transfers between devices: 72.9 us -> 66 us
  local copies, waits for them, and re-layouts: 4.54 us -> 0.1 us
  starting transfers between devices: 33.6 us -> 32 us
    ppermute x8, waiting for transfers between devices: 29.2 us -> 2.51 us  [to_chip(): return lax.ppermute(value, 'ka', moves)]
    ppermute x7, waiting for transfers between devices: 8.74 us -> 34.1 us  [to_panel(): return lax.ppermute(value, ('tr', 'tc'), moves)]
    pallas_call x14 -> x15, Pallas kernels: 15.5 us -> 29.4 us  [call(): pl.pallas_call(ordered, out_shape=out_shapes, in_specs=in_specs + [ANYWHE...]
    ppermute x8, waiting for transfers between devices: 35 us -> 26.2 us  [to_half(): lax.ppermute(value, 'tc', [(j, (j + group * gap) % col_parts) for j in ra...]
    ppermute x8, starting transfers between devices: 8.78 us -> 13.6 us  [to_half(): lax.ppermute(value, 'tc', [(j, (j + group * gap) % col_parts) for j in ra...]
    unnamed x18 -> x10, local copies, waits for them, and re-layouts: 4.47 us -> 0.03 us
    ppermute x8, waiting for transfers between devices: 0.02 us -> 3.23 us  [to_core(): lax.ppermute(value, 'ka', [(s, s + 1 - 2 * (s % CORES)) for s in range(mo...]
    ppermute x7, starting transfers between devices: 12.1 us -> 9.12 us  [to_panel(): return lax.ppermute(value, ('tr', 'tc'), moves)]
  transfers between devices with their start and end apart: 31 -> 31, of which waited for: 15 -> 15; matrix products, arithmetic and copies ran while one was open for 0% -> 0% of each run, Pallas kernels for 10% -> 7%
where the time goes in v5:
time: 129 us; the launch traced here: 128 us
  waiting for transfers between devices  66 us (51%)
  starting transfers between devices  32 us (25%)
  Pallas kernels  29.4 us (23%)
    ppermute x7, waiting for transfers between devices, to_panel(): return lax.ppermute(value, ('tr', 'tc'), moves)  34.1 us
    pallas_call x15, Pallas kernels, call(): pl.pallas_call(ordered, out_shape=out_shapes, in_specs=in_specs + [ANYWHE...  29.4 us
    ppermute x8, waiting for transfers between devices, to_half(): lax.ppermute(value, 'tc', [(j, (j + group * gap) % col_parts) for j in ra...  26.2 us
    ppermute x8, starting transfers between devices, to_half(): lax.ppermute(value, 'tc', [(j, (j + group * gap) % col_parts) for j in ra...  13.6 us
    ppermute x7, starting transfers between devices, to_panel(): return lax.ppermute(value, ('tr', 'tc'), moves)  9.12 us
    ppermute x8, starting transfers between devices, to_chip(): return lax.ppermute(value, 'ka', moves)  9.12 us
    ppermute x8, waiting for transfers between devices, to_core(): lax.ppermute(value, 'ka', [(s, s + 1 - 2 * (s % CORES)) for s in range(mo...  3.23 us
  transfers between devices with their start and end apart: 31, of which 15 were waited for; matrix products, arithmetic and copies ran while one was open for 0% of the time, Pallas kernels for 7%

profile of v5, /device:TPU:0, one launch (start us, length us, event | category | flops | bytes accessed | tf_op | source)
XLA Modules:
  0.0 128.5 jit_solution(16474391457977095127)
XLA Ops:
  0.6 16.1 %shard_map.59 = (f32[3,2,40,256]{3,2,1,0:T(8,128)}, f32[3,2,40,256]{3,2,1,0:T(8,128)}) custom-call(f32[2,1,512,256]{3,2,1,0:T(8,128)} %refs_8_.1, f32[2,1,512,256]{3,2,1,0:T(8,128)} %refs_1_.7, f32[2,1,512,256]{3,2,1,0:T(8,128)} %refs_2_.7), custom_call_target="tpu_custom_call" | custom-call | flops 1 | bytes 1 | tf_op jit(solution)/shard_map/pallas_call | solution.py:218
  16.7 3.0 %collective-permute-start = (f32[3,2,40,256]{3,2,1,0:T(8,128)}, f32[3,2,40,256]{3,2,1,0:T(8,128)S(1)}, u32[]{:S(2)}, u32[]{:S(2)}) collective-permute-start(f32[3,2,40,256]{3,2,1,0:T(8,128)} %get-tuple-element.32), channel_id=1, source_target_pairs={{0,16},{8,24},{16,0},{24,8},{1,17},{9,25},{17,1},{25,9},{2,18},{10... | collective-permute-start | bytes 737288 | tf_op jit(solution)/shard_map/ppermute | solution.py:247
  19.8 1.6 %collective-permute-start.3 = (f32[2,256,256]{2,1,0:T(8,128)S(1)}, f32[2,256,256]{2,1,0:T(8,128)S(1)}, u32[]{:S(2)}, u32[]{:S(2)}) collective-permute-start(f32[2,256,256]{2,1,0:T(8,128)S(1)} %get-tuple-element.61), channel_id=1, source_target_pairs={{0,1},{1,0},{2,3},{3,2},{4,5},{5,4},{6,7},{7,6},{8,9},{9,8},{10,11... | collective-permute-start | bytes 1572872 | tf_op jit(solution)/shard_map/ppermute | solution.py:258
  21.5 1.5 %collective-permute-start.7 = (f32[2,256,256]{2,1,0:T(8,128)S(1)}, f32[2,256,256]{2,1,0:T(8,128)S(1)}, u32[]{:S(2)}, u32[]{:S(2)}) collective-permute-start(f32[2,256,256]{2,1,0:T(8,128)S(1)} %get-tuple-element.60.refs_0_), channel_id=1, source_target_pairs={{0,4},{1,5},{2,6},{3,7},{4,0},{5,1},{6,2},{7,3},{8,12},{9,13},{10,... | collective-permute-start | bytes 1572872 | tf_op jit(solution)/shard_map/ppermute | solution.py:258
  23.4 2.5 %collective-permute-done.refs_3_ = f32[3,2,40,256]{3,2,1,0:T(8,128)S(1)} collective-permute-done((f32[3,2,40,256]{3,2,1,0:T(8,128)}, f32[3,2,40,256]{3,2,1,0:T(8,128)S(1)}, u32[]{:S(2)}, u32[]{:S(2)}) %collective-permute-start) | collective-permute-done | bytes 245792 | tf_op jit(solution)/shard_map/ppermute | solution.py:247
  26.6 1.8 %collective-permute-start.9 = (f32[3,2,80,256]{3,2,1,0:T(8,128)S(1)}, f32[3,2,80,256]{3,2,1,0:T(8,128)S(1)}, u32[]{:S(2)}, u32[]{:S(2)}) collective-permute-start(f32[3,2,80,256]{3,2,1,0:T(8,128)S(1)} %get-tuple-element.36), channel_id=1, source_target_pairs={{0,16},{8,24},{16,0},{24,8},{1,17},{9,25},{17,1},{25,9},{2,18},{10... | collective-permute-start | bytes 1474568 | tf_op jit(solution)/shard_map/ppermute | solution.py:247
  28.4 1.5 %collective-permute-done.2.refs_4_ = f32[3,2,40,256]{3,2,1,0:T(8,128)S(1)} collective-permute-done((f32[3,2,40,256]{3,2,1,0:T(8,128)S(1)}, f32[3,2,40,256]{3,2,1,0:T(8,128)S(1)}, u32[]{:S(2)}, u32[]{:S(2)}) %collective-permute-start.2) | collective-permute-done | bytes 245792 | tf_op jit(solution)/shard_map/ppermute | solution.py:250
  29.9 4.8 %collective-permute-done.3.refs_5_.refs_1_ = f32[2,256,256]{2,1,0:T(8,128)S(1)} collective-permute-done((f32[2,256,256]{2,1,0:T(8,128)S(1)}, f32[2,256,256]{2,1,0:T(8,128)S(1)}, u32[]{:S(2)}, u32[]{:S(2)}) %collective-permute-start.3) | collective-permute-done | bytes 524320 | tf_op jit(solution)/shard_map/ppermute | solution.py:258
  35.7 2.7 %collective-permute-start.4 = (f32[2,40,256]{2,1,0:T(8,128)S(1)}, f32[2,40,256]{2,1,0:T(8,128)S(1)}, u32[]{:S(2)}, u32[]{:S(2)}) collective-permute-start(f32[2,40,256]{2,1,0:T(8,128)S(1)} %get-tuple-element.34.refs_8_.refs_0_), channel_id=1, source_target_pairs={{0,2},{1,3},{2,0},{3,1},{4,6},{5,7},{6,4},{7,5},{8,10},{9,11},{10,... | collective-permute-start | bytes 245768 | tf_op jit(solution)/shard_map/ppermute | solution.py:261
  38.9 7.2 %collective-permute-done.7.refs_6_.refs_2_ = f32[2,256,256]{2,1,0:T(8,128)S(1)} collective-permute-done((f32[2,256,256]{2,1,0:T(8,128)S(1)}, f32[2,256,256]{2,1,0:T(8,128)S(1)}, u32[]{:S(2)}, u32[]{:S(2)}) %collective-permute-start.7) | collective-permute-done | bytes 524320 | tf_op jit(solution)/shard_map/ppermute | solution.py:258
  46.1 1.2 collective-permute-done.8.refs_7_.refs_3_
  50.1 1.3 %shard_map.64 = (f32[2,80,256]{2,1,0:T(8,128)S(1)}, f32[2,80,256]{2,1,0:T(8,128)S(1)}) custom-call(f32[2,4]{1,0:T(2,128)S(1)} %copy-done.4, f32[3,2,80,256]{3,2,1,0:T(8,128)S(1)} %get-tuple-element.40.refs_1_, f32[3,2,80,256]{3,2,1,0:T(8,128)S(1)} %get-tuple-element.37.refs_4_.refs_2_, f32[3,2,80,256]{3,2,1,0:T(8,128)S(1)} %collective-permute-done.10.refs_3_, ...), custom_call_target="tpu_custom_call" | custom-call | flops 1 | bytes 1 | tf_op jit(solution)/shard_map/pallas_call | solution.py:218
  51.4 2.5 %collective-permute-start.13 = (f32[2,80,256]{2,1,0:T(8,128)S(1)}, f32[2,80,256]{2,1,0:T(8,128)S(1)}, u32[]{:S(2)}, u32[]{:S(2)}) collective-permute-start(f32[2,80,256]{2,1,0:T(8,128)S(1)} %get-tuple-element.41.refs_6_.refs_0_), channel_id=1, source_target_pairs={{0,2},{1,3},{2,0},{3,1},{4,6},{5,7},{6,4},{7,5},{8,10},{9,11},{10,... | collective-permute-start | bytes 491528 | tf_op jit(solution)/shard_map/ppermute | solution.py:261
  55.2 10.5 %collective-permute-done.6.refs_3_ = f32[2,40,256]{2,1,0:T(8,128)S(1)} collective-permute-done((f32[2,40,256]{2,1,0:T(8,128)S(1)}, f32[2,40,256]{2,1,0:T(8,128)S(1)}, u32[]{:S(2)}, u32[]{:S(2)}) %collective-permute-start.6) | collective-permute-done | bytes 81952 | tf_op jit(solution)/shard_map/ppermute | solution.py:261
  65.7 1.2 shard_map.65
  69.4 1.3 %shard_map.67 = (f32[2,88,256]{2,1,0:T(8,128)S(1)}, f32[2,88,256]{2,1,0:T(8,128)S(1)}) custom-call(f32[2,4]{1,0:T(2,128)S(1)} %copy-done.4, f32[3,2,88,256]{3,2,1,0:T(8,128)S(1)} %get-tuple-element.45.refs_1_, f32[3,2,88,256]{3,2,1,0:T(8,128)S(1)} %get-tuple-element.47.refs_2_, f32[3,2,88,256]{3,2,1,0:T(8,128)S(1)} %collective-permute-done.17.refs_3_, ...), custom_call_target="tpu_custom_call" | custom-call | flops 1 | bytes 1 | tf_op jit(solution)/shard_map/pallas_call | solution.py:218
  70.7 1.9 %collective-permute-start.20 = (f32[2,88,256]{2,1,0:T(8,128)S(1)}, f32[2,88,256]{2,1,0:T(8,128)S(1)}, u32[]{:S(2)}, u32[]{:S(2)}) collective-permute-start(f32[2,88,256]{2,1,0:T(8,128)S(1)} %get-tuple-element.48.refs_6_.refs_0_), channel_id=1, source_target_pairs={{0,2},{1,3},{2,0},{3,1},{4,6},{5,7},{6,4},{7,5},{8,10},{9,11},{10,... | collective-permute-start | bytes 540680 | tf_op jit(solution)/shard_map/ppermute | solution.py:261
  73.1 2.3 %collective-permute-start.12 = (f32[2,80,256]{2,1,0:T(8,128)S(1)}, f32[2,80,256]{2,1,0:T(8,128)S(1)}, u32[]{:S(2)}, u32[]{:S(2)}) collective-permute-start(f32[2,80,256]{2,1,0:T(8,128)S(1)} %get-tuple-element.43), channel_id=1, source_target_pairs={{0,1},{1,0},{2,3},{3,2},{4,5},{5,4},{6,7},{7,6},{8,9},{9,8},{10,11... | collective-permute-start | bytes 491528 | tf_op jit(solution)/shard_map/ppermute | solution.py:258
  75.5 6.9 %collective-permute-done.12.refs_7_.refs_1_ = f32[2,80,256]{2,1,0:T(8,128)S(1)} collective-permute-done((f32[2,80,256]{2,1,0:T(8,128)S(1)}, f32[2,80,256]{2,1,0:T(8,128)S(1)}, u32[]{:S(2)}, u32[]{:S(2)}) %collective-permute-start.12) | collective-permute-done | bytes 163872 | tf_op jit(solution)/shard_map/ppermute | solution.py:258
  82.4 6.8 %collective-permute-done.15.refs_3_ = f32[2,80,256]{2,1,0:T(8,128)S(1)} collective-permute-done((f32[2,80,256]{2,1,0:T(8,128)S(1)}, f32[2,80,256]{2,1,0:T(8,128)S(1)}, u32[]{:S(2)}, u32[]{:S(2)}) %collective-permute-start.15) | collective-permute-done | bytes 163872 | tf_op jit(solution)/shard_map/ppermute | solution.py:261
  89.2 1.2 shard_map.68
  90.6 3.3 %collective-permute-start.22 = (f32[2,88,256]{2,1,0:T(8,128)S(1)}, f32[2,88,256]{2,1,0:T(8,128)S(1)}, u32[]{:S(2)}, u32[]{:S(2)}) collective-permute-start(f32[2,88,256]{2,1,0:T(8,128)S(1)} %collective-permute-done.21.refs_1_.refs_2_), channel_id=1, source_target_pairs={{0,2},{1,3},{2,0},{3,1},{4,6},{5,7},{6,4},{7,5},{8,10},{9,11},{10,... | collective-permute-start | bytes 540680 | tf_op jit(solution)/shard_map/ppermute | solution.py:261
  95.5 9.0 %collective-permute-done.19.refs_8_.refs_3_ = f32[2,160,256]{2,1,0:T(8,128)S(1)} collective-permute-done((f32[2,160,256]{2,1,0:T(8,128)S(1)}, f32[2,160,256]{2,1,0:T(8,128)S(1)}, u32[]{:S(2)}, u32[]{:S(2)}) %collective-permute-start.19) | collective-permute-done | bytes 327712 | tf_op jit(solution)/shard_map/ppermute | solution.py:258
  104.5 1.3 %shard_map.71 = (f32[2,176,256]{2,1,0:T(8,128)S(1)}, f32[2,176,256]{2,1,0:T(8,128)S(1)}) custom-call(f32[2,88,256]{2,1,0:T(8,128)S(1)} %get-tuple-element.48.refs_6_.refs_0_, f32[2,88,256]{2,1,0:T(8,128)S(1)} %collective-permute-done.20.refs_2_.refs_1_, f32[2,88,256]{2,1,0:T(8,128)S(1)} %collective-permute-done.21.refs_1_.refs_2_, ...), custom_call_target="tpu_custom_call" | custom-call | flops 1 | bytes 1 | tf_op jit(solution)/shard_map/pallas_call | solution.py:218
  105.8 1.6 %collective-permute-start.27 = (f32[2,176,256]{2,1,0:T(8,128)S(1)}, f32[2,176,256]{2,1,0:T(8,128)S(1)}, u32[]{:S(2)}, u32[]{:S(2)}) collective-permute-start(f32[2,176,256]{2,1,0:T(8,128)S(1)} %get-tuple-element.57), channel_id=1, source_target_pairs={{0,1},{1,0},{2,3},{3,2},{4,5},{5,4},{6,7},{7,6},{8,9},{9,8},{10,11... | collective-permute-start | bytes 1081352 | tf_op jit(solution)/shard_map/ppermute | solution.py:258
  107.4 1.8 %collective-permute-start.28 = (f32[2,48,256]{2,1,0:T(8,128)S(1)}, f32[2,48,256]{2,1,0:T(8,128)S(1)}, u32[]{:S(2)}, u32[]{:S(2)}) collective-permute-start(f32[2,48,256]{2,1,0:T(8,128)S(1)} %get-tuple-element.54.refs_6_.refs_0_), channel_id=1, source_target_pairs={{0,2},{1,3},{2,0},{3,1},{4,6},{5,7},{6,4},{7,5},{8,10},{9,11},{10,... | collective-permute-start | bytes 294920 | tf_op jit(solution)/shard_map/ppermute | solution.py:261
  109.1 1.2 collective-permute-start.29
  110.3 7.9 %collective-permute-done.28.refs_1_ = f32[2,48,256]{2,1,0:T(8,128)S(1)} collective-permute-done((f32[2,48,256]{2,1,0:T(8,128)S(1)}, f32[2,48,256]{2,1,0:T(8,128)S(1)}, u32[]{:S(2)}, u32[]{:S(2)}) %collective-permute-start.28) | collective-permute-done | bytes 98336 | tf_op jit(solution)/shard_map/ppermute | solution.py:261
  120.0 1.1 shard_map.72
  121.2 1.6 %collective-permute-start.30 = (f32[2,96,256]{2,1,0:T(8,128)S(1)}, f32[2,96,256]{2,1,0:T(8,128)S(1)}, u32[]{:S(2)}, u32[]{:S(2)}) collective-permute-start(f32[2,96,256]{2,1,0:T(8,128)S(1)} %get-tuple-element.59), channel_id=1, source_target_pairs={{0,1},{1,0},{2,3},{3,2},{4,5},{5,4},{6,7},{7,6},{8,9},{9,8},{10,11... | collective-permute-start | bytes 589832 | tf_op jit(solution)/shard_map/ppermute | solution.py:258
  122.8 4.2 %collective-permute-done.30.refs_7_ = f32[2,96,256]{2,1,0:T(8,128)S(1)} collective-permute-done((f32[2,96,256]{2,1,0:T(8,128)S(1)}, f32[2,96,256]{2,1,0:T(8,128)S(1)}, u32[]{:S(2)}, u32[]{:S(2)}) %collective-permute-start.30) | collective-permute-done | bytes 196640 | tf_op jit(solution)/shard_map/ppermute | solution.py:258
  127.0 1.5 %shard_map.73 = (f32[2,1,512,256]{3,2,1,0:T(8,128)}, f32[2,1,512,256]{3,2,1,0:T(8,128)}) custom-call(f32[2,80,256]{2,1,0:T(8,128)S(1)} %get-tuple-element.42.refs_6_.refs_0_, f32[2,80,256]{2,1,0:T(8,128)S(1)} %collective-permute-done.12.refs_7_.refs_1_, f32[2,160,256]{2,1,0:T(8,128)S(1)} %get-tuple-element.49.refs_3_.refs_2_, ...), custom_call_target="tpu_custom_call" | custom-call | flops 1 | bytes 1 | tf_op jit(solution)/shard_map/pallas_call | solution.py:218
  (56 shorter events, 13.3 us)
Async XLA Ops:
  0.6 19.1 %copy-start = (f32[2,1,512,256]{3,2,1,0:T(8,128)S(1)}, f32[2,1,512,256]{3,2,1,0:T(8,128)}, u32[]{:S(2)}) copy-start(f32[2,1,512,256]{3,2,1,0:T(8,128)} %refs_8_.1) | copy-start | bytes 3145732
  16.7 9.2 %collective-permute-start = (f32[3,2,40,256]{3,2,1,0:T(8,128)}, f32[3,2,40,256]{3,2,1,0:T(8,128)S(1)}, u32[]{:S(2)}, u32[]{:S(2)}) collective-permute-start(f32[3,2,40,256]{3,2,1,0:T(8,128)} %get-tuple-element.32), channel_id=1, source_target_pairs={{0,16},{8,24},{16,0},{24,8},{1,17},{9,25},{17,1},{25,9},{2,18},{10... | collective-permute-start | bytes 737288 | tf_op jit(solution)/shard_map/ppermute | solution.py:247
  19.8 14.9 %collective-permute-start.3 = (f32[2,256,256]{2,1,0:T(8,128)S(1)}, f32[2,256,256]{2,1,0:T(8,128)S(1)}, u32[]{:S(2)}, u32[]{:S(2)}) collective-permute-start(f32[2,256,256]{2,1,0:T(8,128)S(1)} %get-tuple-element.61), channel_id=1, source_target_pairs={{0,1},{1,0},{2,3},{3,2},{4,5},{5,4},{6,7},{7,6},{8,9},{9,8},{10,11... | collective-permute-start | bytes 1572872 | tf_op jit(solution)/shard_map/ppermute | solution.py:258
  21.5 6.9 %collective-permute-start.1 = (f32[3,2,40,256]{3,2,1,0:T(8,128)}, f32[3,2,40,256]{3,2,1,0:T(8,128)S(1)}, u32[]{:S(2)}, u32[]{:S(2)}) collective-permute-start(f32[3,2,40,256]{3,2,1,0:T(8,128)} %get-tuple-element.31.refs_1_), channel_id=1, source_target_pairs={{0,8},{8,0},{16,24},{24,16},{1,9},{9,1},{17,25},{25,17},{2,10},{10... | collective-permute-start | bytes 737288 | tf_op jit(solution)/shard_map/ppermute | solution.py:250
  21.5 24.6 %collective-permute-start.7 = (f32[2,256,256]{2,1,0:T(8,128)S(1)}, f32[2,256,256]{2,1,0:T(8,128)S(1)}, u32[]{:S(2)}, u32[]{:S(2)}) collective-permute-start(f32[2,256,256]{2,1,0:T(8,128)S(1)} %get-tuple-element.60.refs_0_), channel_id=1, source_target_pairs={{0,4},{1,5},{2,6},{3,7},{4,0},{5,1},{6,2},{7,3},{8,12},{9,13},{10,... | collective-permute-start | bytes 1572872 | tf_op jit(solution)/shard_map/ppermute | solution.py:258
  23.0 24.3 %collective-permute-start.8 = (f32[2,256,256]{2,1,0:T(8,128)S(1)}, f32[2,256,256]{2,1,0:T(8,128)S(1)}, u32[]{:S(2)}, u32[]{:S(2)}) collective-permute-start(f32[2,256,256]{2,1,0:T(8,128)S(1)} %get-tuple-element.61), channel_id=1, source_target_pairs={{0,5},{1,4},{2,7},{3,6},{4,1},{5,0},{6,3},{7,2},{8,13},{9,12},{10,... | collective-permute-start | bytes 1572872 | tf_op jit(solution)/shard_map/ppermute | solution.py:258
  26.6 20.7 %collective-permute-start.9 = (f32[3,2,80,256]{3,2,1,0:T(8,128)S(1)}, f32[3,2,80,256]{3,2,1,0:T(8,128)S(1)}, u32[]{:S(2)}, u32[]{:S(2)}) collective-permute-start(f32[3,2,80,256]{3,2,1,0:T(8,128)S(1)} %get-tuple-element.36), channel_id=1, source_target_pairs={{0,16},{8,24},{16,0},{24,8},{1,17},{9,25},{17,1},{25,9},{2,18},{10... | collective-permute-start | bytes 1474568 | tf_op jit(solution)/shard_map/ppermute | solution.py:247
  28.4 1.5 %collective-permute-start.2 = (f32[3,2,40,256]{3,2,1,0:T(8,128)S(1)}, f32[3,2,40,256]{3,2,1,0:T(8,128)S(1)}, u32[]{:S(2)}, u32[]{:S(2)}) collective-permute-start(f32[3,2,40,256]{3,2,1,0:T(8,128)S(1)} %get-tuple-element.33.refs_2_), channel_id=1, source_target_pairs={{0,8},{8,0},{16,24},{24,16},{1,9},{9,1},{17,25},{25,17},{2,10},{10... | collective-permute-start | bytes 737288 | tf_op jit(solution)/shard_map/ppermute | solution.py:250
  35.7 11.7 %collective-permute-start.4 = (f32[2,40,256]{2,1,0:T(8,128)S(1)}, f32[2,40,256]{2,1,0:T(8,128)S(1)}, u32[]{:S(2)}, u32[]{:S(2)}) collective-permute-start(f32[2,40,256]{2,1,0:T(8,128)S(1)} %get-tuple-element.34.refs_8_.refs_0_), channel_id=1, source_target_pairs={{0,2},{1,3},{2,0},{3,1},{4,6},{5,7},{6,4},{7,5},{8,10},{9,11},{10,... | collective-permute-start | bytes 245768 | tf_op jit(solution)/shard_map/ppermute | solution.py:261
  38.3 9.0 %collective-permute-start.5 = (f32[2,40,256]{2,1,0:T(8,128)S(1)}, f32[2,40,256]{2,1,0:T(8,128)S(1)}, u32[]{:S(2)}, u32[]{:S(2)}) collective-permute-start(f32[2,40,256]{2,1,0:T(8,128)S(1)} %get-tuple-element.35), channel_id=1, source_target_pairs={{0,16},{8,24},{16,0},{24,8},{1,17},{9,25},{17,1},{25,9},{2,18},{10... | collective-permute-start | bytes 245768 | tf_op jit(solution)/shard_map/ppermute | solution.py:247
  46.1 3.3 %collective-permute-start.10 = (f32[3,2,80,256]{3,2,1,0:T(8,128)S(1)}, f32[3,2,80,256]{3,2,1,0:T(8,128)S(1)}, u32[]{:S(2)}, u32[]{:S(2)}) collective-permute-start(f32[3,2,80,256]{3,2,1,0:T(8,128)S(1)} %get-tuple-element.40.refs_1_), channel_id=1, source_target_pairs={{0,8},{8,0},{16,24},{24,16},{1,9},{9,1},{17,25},{25,17},{2,10},{10... | collective-permute-start | bytes 1474568 | tf_op jit(solution)/shard_map/ppermute | solution.py:250
  48.1 1.9 %collective-permute-start.11 = (f32[3,2,80,256]{3,2,1,0:T(8,128)S(1)}, f32[3,2,80,256]{3,2,1,0:T(8,128)S(1)}, u32[]{:S(2)}, u32[]{:S(2)}) collective-permute-start(f32[3,2,80,256]{3,2,1,0:T(8,128)S(1)} %get-tuple-element.37.refs_4_.refs_2_), channel_id=1, source_target_pairs={{0,8},{8,0},{16,24},{24,16},{1,9},{9,1},{17,25},{25,17},{2,10},{10... | collective-permute-start | bytes 1474568 | tf_op jit(solution)/shard_map/ppermute | solution.py:250
  48.2 18.7 %collective-permute-start.16 = (f32[3,2,88,256]{3,2,1,0:T(8,128)S(1)}, f32[3,2,88,256]{3,2,1,0:T(8,128)S(1)}, u32[]{:S(2)}, u32[]{:S(2)}) collective-permute-start(f32[3,2,88,256]{3,2,1,0:T(8,128)S(1)} %get-tuple-element.46), channel_id=1, source_target_pairs={{0,16},{8,24},{16,0},{24,8},{1,17},{9,25},{17,1},{25,9},{2,18},{10... | collective-permute-start | bytes 1622024 | tf_op jit(solution)/shard_map/ppermute | solution.py:247
  51.4 15.5 %collective-permute-start.13 = (f32[2,80,256]{2,1,0:T(8,128)S(1)}, f32[2,80,256]{2,1,0:T(8,128)S(1)}, u32[]{:S(2)}, u32[]{:S(2)}) collective-permute-start(f32[2,80,256]{2,1,0:T(8,128)S(1)} %get-tuple-element.41.refs_6_.refs_0_), channel_id=1, source_target_pairs={{0,2},{1,3},{2,0},{3,1},{4,6},{5,7},{6,4},{7,5},{8,10},{9,11},{10,... | collective-permute-start | bytes 491528 | tf_op jit(solution)/shard_map/ppermute | solution.py:261
  53.9 13.0 %collective-permute-start.14 = (f32[2,80,256]{2,1,0:T(8,128)S(1)}, f32[2,80,256]{2,1,0:T(8,128)S(1)}, u32[]{:S(2)}, u32[]{:S(2)}) collective-permute-start(f32[2,80,256]{2,1,0:T(8,128)S(1)} %get-tuple-element.44), channel_id=1, source_target_pairs={{0,16},{8,24},{16,0},{24,8},{1,17},{9,25},{17,1},{25,9},{2,18},{10... | collective-permute-start | bytes 491528 | tf_op jit(solution)/shard_map/ppermute | solution.py:247
  55.0 10.6 %collective-permute-start.6 = (f32[2,40,256]{2,1,0:T(8,128)S(1)}, f32[2,40,256]{2,1,0:T(8,128)S(1)}, u32[]{:S(2)}, u32[]{:S(2)}) collective-permute-start(f32[2,40,256]{2,1,0:T(8,128)S(1)} %collective-permute-done.5.refs_4_.refs_2_), channel_id=1, source_target_pairs={{0,2},{1,3},{2,0},{3,1},{4,6},{5,7},{6,4},{7,5},{8,10},{9,11},{10,... | collective-permute-start | bytes 245768 | tf_op jit(solution)/shard_map/ppermute | solution.py:261
  55.2 13.1 %collective-permute-start.17 = (f32[3,2,88,256]{3,2,1,0:T(8,128)S(1)}, f32[3,2,88,256]{3,2,1,0:T(8,128)S(1)}, u32[]{:S(2)}, u32[]{:S(2)}) collective-permute-start(f32[3,2,88,256]{3,2,1,0:T(8,128)S(1)} %get-tuple-element.45.refs_1_), channel_id=1, source_target_pairs={{0,8},{8,0},{16,24},{24,16},{1,9},{9,1},{17,25},{25,17},{2,10},{10... | collective-permute-start | bytes 1622024 | tf_op jit(solution)/shard_map/ppermute | solution.py:250
  67.4 2.0 %collective-permute-start.18 = (f32[3,2,88,256]{3,2,1,0:T(8,128)S(1)}, f32[3,2,88,256]{3,2,1,0:T(8,128)S(1)}, u32[]{:S(2)}, u32[]{:S(2)}) collective-permute-start(f32[3,2,88,256]{3,2,1,0:T(8,128)S(1)} %get-tuple-element.47.refs_2_), channel_id=1, source_target_pairs={{0,8},{8,0},{16,24},{24,16},{1,9},{9,1},{17,25},{25,17},{2,10},{10... | collective-permute-start | bytes 1622024 | tf_op jit(solution)/shard_map/ppermute | solution.py:250
  67.5 22.9 %collective-permute-start.23 = (f32[3,2,48,256]{3,2,1,0:T(8,128)S(1)}, f32[3,2,48,256]{3,2,1,0:T(8,128)S(1)}, u32[]{:S(2)}, u32[]{:S(2)}) collective-permute-start(f32[3,2,48,256]{3,2,1,0:T(8,128)S(1)} %get-tuple-element.53), channel_id=1, source_target_pairs={{0,16},{8,24},{16,0},{24,8},{1,17},{9,25},{17,1},{25,9},{2,18},{10... | collective-permute-start | bytes 884744 | tf_op jit(solution)/shard_map/ppermute | solution.py:247
  70.7 19.7 %collective-permute-start.20 = (f32[2,88,256]{2,1,0:T(8,128)S(1)}, f32[2,88,256]{2,1,0:T(8,128)S(1)}, u32[]{:S(2)}, u32[]{:S(2)}) collective-permute-start(f32[2,88,256]{2,1,0:T(8,128)S(1)} %get-tuple-element.48.refs_6_.refs_0_), channel_id=1, source_target_pairs={{0,2},{1,3},{2,0},{3,1},{4,6},{5,7},{6,4},{7,5},{8,10},{9,11},{10,... | collective-permute-start | bytes 540680 | tf_op jit(solution)/shard_map/ppermute | solution.py:261
  72.6 17.8 %collective-permute-start.21 = (f32[2,88,256]{2,1,0:T(8,128)S(1)}, f32[2,88,256]{2,1,0:T(8,128)S(1)}, u32[]{:S(2)}, u32[]{:S(2)}) collective-permute-start(f32[2,88,256]{2,1,0:T(8,128)S(1)} %get-tuple-element.51), channel_id=1, source_target_pairs={{0,16},{8,24},{16,0},{24,8},{1,17},{9,25},{17,1},{25,9},{2,18},{10... | collective-permute-start | bytes 540680 | tf_op jit(solution)/shard_map/ppermute | solution.py:247
  73.1 9.2 %collective-permute-start.12 = (f32[2,80,256]{2,1,0:T(8,128)S(1)}, f32[2,80,256]{2,1,0:T(8,128)S(1)}, u32[]{:S(2)}, u32[]{:S(2)}) collective-permute-start(f32[2,80,256]{2,1,0:T(8,128)S(1)} %get-tuple-element.43), channel_id=1, source_target_pairs={{0,1},{1,0},{2,3},{3,2},{4,5},{5,4},{6,7},{7,6},{8,9},{9,8},{10,11... | collective-permute-start | bytes 491528 | tf_op jit(solution)/shard_map/ppermute | solution.py:258
  75.4 13.8 %collective-permute-start.15 = (f32[2,80,256]{2,1,0:T(8,128)S(1)}, f32[2,80,256]{2,1,0:T(8,128)S(1)}, u32[]{:S(2)}, u32[]{:S(2)}) collective-permute-start(f32[2,80,256]{2,1,0:T(8,128)S(1)} %collective-permute-done.14.refs_4_.refs_2_), channel_id=1, source_target_pairs={{0,2},{1,3},{2,0},{3,1},{4,6},{5,7},{6,4},{7,5},{8,10},{9,11},{10,... | collective-permute-start | bytes 491528 | tf_op jit(solution)/shard_map/ppermute | solution.py:261
  82.4 11.5 %collective-permute-start.24 = (f32[3,2,48,256]{3,2,1,0:T(8,128)S(1)}, f32[3,2,48,256]{3,2,1,0:T(8,128)S(1)}, u32[]{:S(2)}, u32[]{:S(2)}) collective-permute-start(f32[3,2,48,256]{3,2,1,0:T(8,128)S(1)} %get-tuple-element.52.refs_1_), channel_id=1, source_target_pairs={{0,8},{8,0},{16,24},{24,16},{1,9},{9,1},{17,25},{25,17},{2,10},{10... | collective-permute-start | bytes 884744 | tf_op jit(solution)/shard_map/ppermute | solution.py:250
  90.4 3.4 %collective-permute-start.25 = (f32[3,2,48,256]{3,2,1,0:T(8,128)S(1)}, f32[3,2,48,256]{3,2,1,0:T(8,128)S(1)}, u32[]{:S(2)}, u32[]{:S(2)}) collective-permute-start(f32[3,2,48,256]{3,2,1,0:T(8,128)S(1)} %shard_map.69.refs_2_), channel_id=1, source_target_pairs={{0,8},{8,0},{16,24},{24,16},{1,9},{9,1},{17,25},{25,17},{2,10},{10... | collective-permute-start | bytes 884744 | tf_op jit(solution)/shard_map/ppermute | solution.py:250
  90.5 14.0 %collective-permute-start.19 = (f32[2,160,256]{2,1,0:T(8,128)S(1)}, f32[2,160,256]{2,1,0:T(8,128)S(1)}, u32[]{:S(2)}, u32[]{:S(2)}) collective-permute-start(f32[2,160,256]{2,1,0:T(8,128)S(1)} %get-tuple-element.50), channel_id=1, source_target_pairs={{0,1},{1,0},{2,3},{3,2},{4,5},{5,4},{6,7},{7,6},{8,9},{9,8},{10,11... | collective-permute-start | bytes 983048 | tf_op jit(solution)/shard_map/ppermute | solution.py:258
  90.6 13.9 %collective-permute-start.22 = (f32[2,88,256]{2,1,0:T(8,128)S(1)}, f32[2,88,256]{2,1,0:T(8,128)S(1)}, u32[]{:S(2)}, u32[]{:S(2)}) collective-permute-start(f32[2,88,256]{2,1,0:T(8,128)S(1)} %collective-permute-done.21.refs_1_.refs_2_), channel_id=1, source_target_pairs={{0,2},{1,3},{2,0},{3,1},{4,6},{5,7},{6,4},{7,5},{8,10},{9,11},{10,... | collective-permute-start | bytes 540680 | tf_op jit(solution)/shard_map/ppermute | solution.py:261
  94.9 9.6 %collective-permute-start.26 = (f32[2,48,256]{2,1,0:T(8,128)S(1)}, f32[2,48,256]{2,1,0:T(8,128)S(1)}, u32[]{:S(2)}, u32[]{:S(2)}) collective-permute-start(f32[2,48,256]{2,1,0:T(8,128)S(1)} %get-tuple-element.55), channel_id=1, source_target_pairs={{0,16},{8,24},{16,0},{24,8},{1,17},{9,25},{17,1},{25,9},{2,18},{10... | collective-permute-start | bytes 294920 | tf_op jit(solution)/shard_map/ppermute | solution.py:247
  105.8 14.3 %collective-permute-start.27 = (f32[2,176,256]{2,1,0:T(8,128)S(1)}, f32[2,176,256]{2,1,0:T(8,128)S(1)}, u32[]{:S(2)}, u32[]{:S(2)}) collective-permute-start(f32[2,176,256]{2,1,0:T(8,128)S(1)} %get-tuple-element.57), channel_id=1, source_target_pairs={{0,1},{1,0},{2,3},{3,2},{4,5},{5,4},{6,7},{7,6},{8,9},{9,8},{10,11... | collective-permute-start | bytes 1081352 | tf_op jit(solution)/shard_map/ppermute | solution.py:258
  107.4 10.8 %collective-permute-start.28 = (f32[2,48,256]{2,1,0:T(8,128)S(1)}, f32[2,48,256]{2,1,0:T(8,128)S(1)}, u32[]{:S(2)}, u32[]{:S(2)}) collective-permute-start(f32[2,48,256]{2,1,0:T(8,128)S(1)} %get-tuple-element.54.refs_6_.refs_0_), channel_id=1, source_target_pairs={{0,2},{1,3},{2,0},{3,1},{4,6},{5,7},{6,4},{7,5},{8,10},{9,11},{10,... | collective-permute-start | bytes 294920 | tf_op jit(solution)/shard_map/ppermute | solution.py:261
  109.1 10.1 %collective-permute-start.29 = (f32[2,48,256]{2,1,0:T(8,128)S(1)}, f32[2,48,256]{2,1,0:T(8,128)S(1)}, u32[]{:S(2)}, u32[]{:S(2)}) collective-permute-start(f32[2,48,256]{2,1,0:T(8,128)S(1)} %collective-permute-done.26.refs_7_.refs_2_), channel_id=1, source_target_pairs={{0,2},{1,3},{2,0},{3,1},{4,6},{5,7},{6,4},{7,5},{8,10},{9,11},{10,... | collective-permute-start | bytes 294920 | tf_op jit(solution)/shard_map/ppermute | solution.py:261
  121.2 5.8 %collective-permute-start.30 = (f32[2,96,256]{2,1,0:T(8,128)S(1)}, f32[2,96,256]{2,1,0:T(8,128)S(1)}, u32[]{:S(2)}, u32[]{:S(2)}) collective-permute-start(f32[2,96,256]{2,1,0:T(8,128)S(1)} %get-tuple-element.59), channel_id=1, source_target_pairs={{0,1},{1,0},{2,3},{3,2},{4,5},{5,4},{6,7},{7,6},{8,9},{9,8},{10,11... | collective-permute-start | bytes 589832 | tf_op jit(solution)/shard_map/ppermute | solution.py:258
  (4 other events, 45.2 us)

commit v6 on v5

--- a/solution.py
+++ b/solution.py
@@ -13,7 +13,7 @@
 WEIGHTS = (5, 10, 11, 6)
 SUBLANES, LANES = 8, 128
 VMEM_LIMIT = 40 * 2**20
-FIRST_LIMIT = 62 * 2**20
+FIRST_LIMIT = 56 * 2**20
 ANYWHERE = pl.BlockSpec(memory_space=pl.ANY)
 IN_VMEM = pl.BlockSpec(memory_space=pltpu.VMEM)
 IN_HBM = pl.BlockSpec(memory_space=pltpu.HBM)
@@ -91,7 +91,7 @@
 
 
 def energy_kernel(chips, scale, tables, *refs):
-    here, other, sigmas = refs[:chips], refs[chips : 2 * chips], refs[2 * chips :]
+    here, other, returned, sigmas = refs[:chips], refs[chips : 2 * chips], refs[2 * chips : -chips], refs[-chips:]
     points = chips * CORES
     own = lax.axis_index("ka")
     side = (1 - 2 * lax.rem(own, CORES)).astype(jnp.float32)
@@ -144,6 +144,10 @@
         return carry
 
     lax.fori_loop(0, step // SUBLANES * across, tile, 0)
+    place = step
+    for value in returned:
+        sigmas[0][:, place : place + value.shape[1], :] = value[...]
+        place += value.shape[1]
 
 
 def split(value):
@@ -151,19 +155,18 @@
     return high, (value - high.astype(jnp.float32)).astype(jnp.bfloat16)
 
 
-def right_kernel(row_parts, group, *refs):
-    pieces, high, low = refs[: row_parts * group], refs[-2], refs[-1]
-    row_at, half = lax.axis_index("tr"), lax.axis_index("tc") // group
-    depth, cols = pieces[0].shape[1:]
+def right_kernel(group, *refs):
+    pieces, high, low = refs[:group], refs[-2], refs[-1]
+    half = lax.axis_index("tc") // group
+    row_parts, _, depth, cols = pieces[0].shape
     for part in range(row_parts):
-        place = lax.rem(half - row_at + part + row_parts, row_parts) * depth
+        place = lax.rem(half - part + row_parts, row_parts) * depth
         upper = pl.ds(pl.multiple_of(place, depth), depth)
         lower = pl.ds(pl.multiple_of(place + row_parts * depth, depth), depth)
-        for gap in range(group):
-            piece = pieces[part * group + gap]
+        for gap, piece in enumerate(pieces):
             first = pl.ds(gap * cols, cols)
             second = pl.ds((group + gap) * cols, cols)
-            real, imag = split(piece[0]), split(piece[1])
+            real, imag = split(piece[part, 0]), split(piece[part, 1])
             for out, real_part, imag_part in zip((high, low), real, imag):
                 out[upper, first] = real_part
                 out[lower, second] = real_part
@@ -171,13 +174,13 @@
                 out[lower, first] = -imag_part
 
 
-def product_kernel(row_parts, group, chips, *refs):
-    count = row_parts * chips
-    sides, high, low, outs = refs[:count], refs[count], refs[count + 1], refs[count + 2 :]
+def product_kernel(group, spans, *refs):
+    count = len({part for parts, _, _ in spans for part in parts})
+    high, low, outs = refs[count], refs[count + 1], refs[count + 2 :]
     left = jnp.concatenate(
         [
-            jnp.concatenate([sides[gap * row_parts + part][at] for at in (0, 1) for part in range(row_parts)], axis=1)
-            for gap in range(chips)
+            jnp.concatenate([refs[part][at, start : start + size, :] for at in (0, 1) for part in parts], axis=1)
+            for parts, start, size in spans
         ],
         axis=0,
     )
@@ -266,7 +269,7 @@
             functools.partial(pack_kernel, chips, bases[at], step, count),
             [f32(value.shape) for value in passed] + [f32((3, 2, step, cols))] * chips,
             [IN_HBM] * 3 + [ANYWHERE] * count,
-            [ANYWHERE] * (count + chips),
+            [ANYWHERE] * count + [ANYWHERE if at else IN_VMEM] * chips,
             (*inputs, *passed),
             [pltpu.SemaphoreType.DMA((3 * chips,))],
             after,
@@ -291,24 +294,40 @@
     def forward(pieces):
         return [to_chip(pieces[gap], -gap) for gap in range(1, chips)], to_core(pieces[0])
 
-    def energy(at, here, other, after):
+    def energy(at, here, other, returned, after):
+        step = sizes[at]
+        height = step + sum(value.shape[1] for value in returned)
         return call(
             functools.partial(energy_kernel, chips, scale),
-            [f32((2, sizes[at], cols))] * chips,
-            [IN_SMEM] + [IN_VMEM] * momenta,
+            [f32((2, height, cols))] + [f32((2, step, cols))] * (chips - 1),
+            [IN_SMEM] + [IN_VMEM] * (momenta + len(returned)),
             [IN_VMEM] * chips,
-            (tables, *here, *other),
+            (tables, *here, *other, *returned),
             (),
             after,
         )
 
-    def product(at, lefts, after):
+    def sides(value):
+        return [value] + [to_half(value, gap) for gap in range(1, row_parts)]
+
+    def product(at, after):
+        step = sizes[at]
+        arrays, spans = list(lefts[at]), [(range(row_parts), 0, step)]
+        if at + 1 < len(sizes):
+            arrays += lefts[at + 1]
+            spans += [
+                (range(row_parts, 2 * row_parts), sizes[at + 1] + gap * step, step) for gap in range(chips - 1)
+            ]
+        else:
+            for gap in range(chips - 1):
+                spans.append((range(len(arrays), len(arrays) + row_parts), 0, step))
+                arrays += sides(returned[gap])
         outs = call(
-            functools.partial(product_kernel, row_parts, group, chips),
-            [f32((2, chips * sizes[at], cols))] * group,
-            [IN_VMEM] * (len(lefts) + 2),
+            functools.partial(product_kernel, group, spans),
+            [f32((2, chips * step, cols))] * group,
+            [IN_VMEM] * (len(arrays) + 2),
             [IN_VMEM] * group,
-            (*lefts, *right),
+            (*arrays, *right),
             (),
             after,
         )
@@ -319,48 +338,48 @@
 
     blocks = green_less[:, 0].reshape(2, group, cols, cols)
     panels = []
-    for rows_on in range(row_parts):
-        for cols_on in range(group):
-            block = lax.dynamic_index_in_dim(blocks, (member + cols_on) % group, 1, False)
-            panels.append(to_panel(block, rows_on, cols_on) if rows_on + cols_on else block)
+    for gap in range(group):
+        block = lax.dynamic_index_in_dim(blocks, (member + gap) % group, 1, False)
+        panels.append(to_panel(block, 0, gap) if gap else block)
+    early = panels[1:]
+    panels = [lax.all_gather(panel, "tr") for panel in panels]
     extent = 2 * row_parts * cols
 
-    lefts, results, last, arrived, returned = [], [], (), (), ()
-    for at in range(len(sizes) + 1):
-        if at < len(sizes):
-            across, beside = sent[at]
-            if at + 1 < len(sizes):
-                fresh, across = pack(at + 1, across, (*arrived, *last))
-                pieces.append(fresh)
-                sent.append(forward(fresh))
-            else:
-                across = gate(across, (*arrived, *last))
-            gates = panels[1:group]
-            if at == 1:
-                right = call(
-                    functools.partial(right_kernel, row_parts, group),
-                    [bf16((extent, 2 * group * cols))] * 2,
-                    [IN_VMEM] * len(panels),
-                    [IN_VMEM] * 2,
-                    panels,
-                    (),
-                    across,
-                )
-                gates = right
-            here = [pieces[at][0], *across]
-            other = [beside, *(to_core(piece) for piece in across)]
-            sigmas = energy(at, here, other, gates)
-            owned = [sigmas[0]] + [to_chip(sigmas[gap], gap) for gap in range(1, chips)]
-            lefts.append([part for own in owned for part in [own] + [to_half(own, gap) for gap in range(1, row_parts)]])
-            returned = owned[1:2]
-            arrived = (*returned, *lefts[at][1:2])
-            if at == 0:
-                arrived += tuple(panels[group:])
-            last = sigmas[:1]
-        if at >= 1:
-            gates = (*last, *(returned if at + 1 == len(sizes) else ()), *(results[-1][1:] if results else ()))
-            results.append(product(at - 1, lefts[at - 1], gates))
-            last, returned = results[-1][:1], ()
+    lefts, results, returned, last = [], [], (), ()
+
+    def add_product(after):
+        at = len(results)
+        results.append(product(at, (*after, *(results[at - 2][1:] if at >= 2 else ()))))
+        return results[at][:1]
+
+    for at, step in enumerate(sizes):
+        across, beside = sent[at]
+        if at + 1 < len(sizes):
+            fresh, across = pack(at + 1, across, (*returned, *last, *(lefts[at - 1][1:] if at else ())))
+            pieces.append(fresh)
+            sent.append(forward(fresh))
+        else:
+            across = gate(across, (*returned, *last))
+        here = [pieces[at][0], *across]
+        other = [beside, *(to_core(piece) for piece in across)]
+        sigmas = energy(at, here, other, returned, () if at else early)
+        returned = [to_chip(sigmas[gap], gap) for gap in range(1, chips)]
+        lefts.append(sides(sigmas[0]))
+        last = sigmas[:1]
+        if at == min(1, len(sizes) - 1):
+            right = call(
+                functools.partial(right_kernel, group),
+                [bf16((extent, 2 * group * cols))] * 2,
+                [IN_VMEM] * len(panels),
+                [IN_VMEM] * 2,
+                panels,
+                (),
+                last,
+            )
+        if at >= 2:
+            last = add_product(last)
+    while len(results) < len(sizes):
+        last = add_product(last)
 
     return call(
         functools.partial(final_kernel, group, chips, sizes),

time: 129 us -> 137 us (1.062)
  local copies, waits for them, and re-layouts: 0.1 us -> 14.6 us
  between operations: 0.89 us -> 14.3 us
  Pallas kernels: 29.4 us -> 18.3 us
  starting transfers between devices: 32 us -> 22.3 us
    ppermute x7 -> x5, waiting for transfers between devices: 34.1 us -> 6.63 us  [to_panel(): return lax.ppermute(value, ('tr', 'tc'), moves)]
    ppermute x8, waiting for transfers between devices: 2.51 us -> 20.5 us  [to_chip(): return lax.ppermute(value, 'ka', moves)]
    unnamed x10 -> x54, local copies, waits for them, and re-layouts: 0.03 us -> 13.5 us
    pallas_call x15, Pallas kernels: 29.4 us -> 18.3 us  [call(): pl.pallas_call(ordered, out_shape=out_shapes, in_specs=in_specs + [ANYWHE...]
    ppermute x8 -> x5, waiting for transfers between devices: 26.2 us -> 34.4 us  [to_half(): lax.ppermute(value, 'tc', [(j, (j + group * gap) % col_parts) for j in ra...]
    ppermute x8 -> x5, starting transfers between devices: 13.6 us -> 8.32 us  [to_half(): lax.ppermute(value, 'tc', [(j, (j + group * gap) % col_parts) for j in ra...]
    ppermute x7 -> x5, starting transfers between devices: 9.12 us -> 5.19 us  [to_panel(): return lax.ppermute(value, ('tr', 'tc'), moves)]
    ppermute x8, waiting for transfers between devices: 3.23 us -> 5.01 us  [to_core(): lax.ppermute(value, 'ka', [(s, s + 1 - 2 * (s % CORES)) for s in range(mo...]
  transfers between devices with their start and end apart: 31 -> 28, of which waited for: 15 -> 17; matrix products, arithmetic and copies ran while one was open for 0% -> 1% of each run, Pallas kernels for 7% -> 11%
where the time goes in v6:
time: 137 us; the launch traced here: 136 us
  waiting for transfers between devices  66.5 us (49%)
  starting transfers between devices  22.3 us (16%)
  Pallas kernels  18.3 us (13%)
  local copies, waits for them, and re-layouts  14.6 us (11%)
  between operations  14.3 us (10%)
    ppermute x5, waiting for transfers between devices, to_half(): lax.ppermute(value, 'tc', [(j, (j + group * gap) % col_parts) for j in ra...  34.4 us
    ppermute x8, waiting for transfers between devices, to_chip(): return lax.ppermute(value, 'ka', moves)  20.5 us
    pallas_call x15, Pallas kernels, call(): pl.pallas_call(ordered, out_shape=out_shapes, in_specs=in_specs + [ANYWHE...  18.3 us
    unnamed x54, local copies, waits for them, and re-layouts  13.5 us
    ppermute x5, starting transfers between devices, to_half(): lax.ppermute(value, 'tc', [(j, (j + group * gap) % col_parts) for j in ra...  8.32 us
    ppermute x8, starting transfers between devices, to_chip(): return lax.ppermute(value, 'ka', moves)  8.14 us
    ppermute x5, waiting for transfers between devices, to_panel(): return lax.ppermute(value, ('tr', 'tc'), moves)  6.63 us
    ppermute x5, starting transfers between devices, to_panel(): return lax.ppermute(value, ('tr', 'tc'), moves)  5.19 us
  transfers between devices with their start and end apart: 28, of which 17 were waited for; matrix products, arithmetic and copies ran while one was open for 1% of the time, Pallas kernels for 11%

profile of v6, /device:TPU:0, one launch (start us, length us, event | category | flops | bytes accessed | tf_op | source)
XLA Modules:
  0.0 136.1 jit_solution(13030267578232331762)
XLA Ops:
  7.2 2.0 %shard_map.59 = (f32[3,2,40,256]{3,2,1,0:T(8,128)}, f32[3,2,40,256]{3,2,1,0:T(8,128)}) custom-call(f32[2,1,512,256]{3,2,1,0:T(8,128)} %refs_8_.1, f32[2,1,512,256]{3,2,1,0:T(8,128)} %refs_1_.7, f32[2,1,512,256]{3,2,1,0:T(8,128)} %refs_2_.7), custom_call_target="tpu_custom_call" | custom-call | flops 1 | bytes 1 | tf_op jit(solution)/shard_map/pallas_call | solution.py:221
  9.3 3.0 %collective-permute-start = (f32[3,2,40,256]{3,2,1,0:T(8,128)}, f32[3,2,40,256]{3,2,1,0:T(8,128)S(1)}, u32[]{:S(2)}, u32[]{:S(2)}) collective-permute-start(f32[3,2,40,256]{3,2,1,0:T(8,128)} %get-tuple-element.32), channel_id=1, source_target_pairs={{0,16},{8,24},{16,0},{24,8},{1,17},{9,25},{17,1},{25,9},{2,18},{10... | collective-permute-start | bytes 737288 | tf_op jit(solution)/shard_map/ppermute | solution.py:250
  13.4 1.6 %collective-permute-start.3 = (f32[2,256,256]{2,1,0:T(8,128)}, f32[2,256,256]{2,1,0:T(8,128)S(1)}, u32[]{:S(2)}, u32[]{:S(2)}) collective-permute-start(f32[2,256,256]{2,1,0:T(8,128)} %get-tuple-element.61), channel_id=1, source_target_pairs={{0,1},{1,0},{2,3},{3,2},{4,5},{5,4},{6,7},{7,6},{8,9},{9,8},{10,11... | collective-permute-start | bytes 1572872 | tf_op jit(solution)/shard_map/ppermute | solution.py:261
  15.0 3.4 %collective-permute-done.refs_3_ = f32[3,2,40,256]{3,2,1,0:T(8,128)S(1)} collective-permute-done((f32[3,2,40,256]{3,2,1,0:T(8,128)}, f32[3,2,40,256]{3,2,1,0:T(8,128)S(1)}, u32[]{:S(2)}, u32[]{:S(2)}) %collective-permute-start) | collective-permute-done | bytes 245792 | tf_op jit(solution)/shard_map/ppermute | solution.py:250
  20.4 1.7 %collective-permute-start.5 = (f32[3,2,80,256]{3,2,1,0:T(8,128)}, f32[3,2,80,256]{3,2,1,0:T(8,128)}, u32[]{:S(2)}, u32[]{:S(2)}) collective-permute-start(f32[3,2,80,256]{3,2,1,0:T(8,128)} %get-tuple-element.36), channel_id=1, source_target_pairs={{0,16},{8,24},{16,0},{24,8},{1,17},{9,25},{17,1},{25,9},{2,18},{10... | collective-permute-start | bytes 1474568 | tf_op jit(solution)/shard_map/ppermute | solution.py:250
  25.0 2.0 %collective-permute-done.3.refs_5_ = f32[2,256,256]{2,1,0:T(8,128)S(1)} collective-permute-done((f32[2,256,256]{2,1,0:T(8,128)}, f32[2,256,256]{2,1,0:T(8,128)S(1)}, u32[]{:S(2)}, u32[]{:S(2)}) %collective-permute-start.3) | collective-permute-done | bytes 524320 | tf_op jit(solution)/shard_map/ppermute | solution.py:261
  32.7 2.7 %collective-permute-start.4 = (f32[2,40,256]{2,1,0:T(8,128)S(1)}, f32[2,40,256]{2,1,0:T(8,128)S(1)}, u32[]{:S(2)}, u32[]{:S(2)}) collective-permute-start(f32[2,40,256]{2,1,0:T(8,128)S(1)} %get-tuple-element.34.refs_5_.refs_0_), channel_id=1, source_target_pairs={{0,2},{1,3},{2,0},{3,1},{4,6},{5,7},{6,4},{7,5},{8,10},{9,11},{10,... | collective-permute-start | bytes 245768 | tf_op jit(solution)/shard_map/ppermute | solution.py:264
  35.9 2.2 %collective-permute-done.4.refs_6_.refs_1_ = f32[2,40,256]{2,1,0:T(8,128)S(1)} collective-permute-done((f32[2,40,256]{2,1,0:T(8,128)S(1)}, f32[2,40,256]{2,1,0:T(8,128)S(1)}, u32[]{:S(2)}, u32[]{:S(2)}) %collective-permute-start.4) | collective-permute-done | bytes 81952 | tf_op jit(solution)/shard_map/ppermute | solution.py:264
  38.1 1.7 %collective-permute-done.6.refs_4_.refs_5_ = f32[2,40,256]{2,1,0:T(8,128)S(1)} collective-permute-done((f32[2,40,256]{2,1,0:T(8,128)S(1)}, f32[2,40,256]{2,1,0:T(8,128)S(1)}, u32[]{:S(2)}, u32[]{:S(2)}) %collective-permute-start.6) | collective-permute-done | bytes 81952 | tf_op jit(solution)/shard_map/ppermute | solution.py:250
  42.3 1.6 %collective-permute-done.8.refs_4_ = f32[3,2,80,256]{3,2,1,0:T(8,128)} collective-permute-done((f32[3,2,80,256]{3,2,1,0:T(8,128)}, f32[3,2,80,256]{3,2,1,0:T(8,128)}, u32[]{:S(2)}, u32[]{:S(2)}) %collective-permute-start.8) | collective-permute-done | bytes 491552 | tf_op jit(solution)/shard_map/ppermute | solution.py:253
  45.7 2.1 %shard_map.63 = (f32[2,120,256]{2,1,0:T(8,128)S(1)}, f32[2,80,256]{2,1,0:T(8,128)S(1)}) custom-call(f32[2,4]{1,0:T(2,128)S(1)} %copy-done.24, f32[3,2,80,256]{3,2,1,0:T(8,128)S(1)} %copy-done.12, f32[3,2,80,256]{3,2,1,0:T(8,128)} %get-tuple-element.38.refs_2_, f32[3,2,80,256]{3,2,1,0:T(8,128)} %collective-permute-done.7.refs_3_, ...), custom_call_target="tpu_custom_call" | custom-call | flops 1 | bytes 1 | tf_op jit(solution)/shard_map/pallas_call | solution.py:221
  49.4 7.7 %collective-permute-done.10.refs_3_ = f32[3,2,88,256]{3,2,1,0:T(8,128)} collective-permute-done((f32[3,2,88,256]{3,2,1,0:T(8,128)}, f32[3,2,88,256]{3,2,1,0:T(8,128)}, u32[]{:S(2)}, u32[]{:S(2)}) %collective-permute-start.10) | collective-permute-done | bytes 540704 | tf_op jit(solution)/shard_map/ppermute | solution.py:250
  57.1 3.0 %collective-permute-done.11.refs_4_.refs_5_ = f32[2,80,256]{2,1,0:T(8,128)S(1)} collective-permute-done((f32[2,80,256]{2,1,0:T(8,128)S(1)}, f32[2,80,256]{2,1,0:T(8,128)S(1)}, u32[]{:S(2)}, u32[]{:S(2)}) %collective-permute-start.11) | collective-permute-done | bytes 163872 | tf_op jit(solution)/shard_map/ppermute | solution.py:250
  60.2 1.8 %collective-permute-done.9.refs_6_.refs_3_.refs_1_ = f32[2,120,256]{2,1,0:T(8,128)S(1)} collective-permute-done((f32[2,120,256]{2,1,0:T(8,128)S(1)}, f32[2,120,256]{2,1,0:T(8,128)S(1)}, u32[]{:S(2)}, u32[]{:S(2)}) %collective-permute-start.9) | collective-permute-done | bytes 245792 | tf_op jit(solution)/shard_map/ppermute | solution.py:264
  63.6 1.5 %collective-permute-done.13.refs_4_ = f32[3,2,88,256]{3,2,1,0:T(8,128)S(1)} collective-permute-done((f32[3,2,88,256]{3,2,1,0:T(8,128)}, f32[3,2,88,256]{3,2,1,0:T(8,128)S(1)}, u32[]{:S(2)}, u32[]{:S(2)}) %collective-permute-start.13) | collective-permute-done | bytes 540704 | tf_op jit(solution)/shard_map/ppermute | solution.py:253
  65.1 1.8 %shard_map.66 = (f32[2,168,256]{2,1,0:T(8,128)S(1)}, f32[2,88,256]{2,1,0:T(8,128)S(1)}) custom-call(f32[2,4]{1,0:T(2,128)S(1)} %copy-done.25, f32[3,2,88,256]{3,2,1,0:T(8,128)S(1)} %copy-done.10, f32[3,2,88,256]{3,2,1,0:T(8,128)} %get-tuple-element.45.refs_2_, f32[3,2,88,256]{3,2,1,0:T(8,128)S(1)} %collective-permute-done.12.refs_3_, ...), custom_call_target="tpu_custom_call" | custom-call | flops 1 | bytes 1 | tf_op jit(solution)/shard_map/pallas_call | solution.py:221
  67.6 1.2 copy-done.7
  68.8 1.2 copy-done.8
  70.6 1.2 shard_map.67
  71.8 1.3 collective-permute-done.16.refs_0_
  73.1 3.4 %collective-permute-done.17.refs_1_.refs_5_ = f32[2,88,256]{2,1,0:T(8,128)S(1)} collective-permute-done((f32[2,88,256]{2,1,0:T(8,128)S(1)}, f32[2,88,256]{2,1,0:T(8,128)S(1)}, u32[]{:S(2)}, u32[]{:S(2)}) %collective-permute-start.17) | collective-permute-done | bytes 180256 | tf_op jit(solution)/shard_map/ppermute | solution.py:250
  79.0 1.4 %shard_map.69 = (f32[2,136,256]{2,1,0:T(8,128)S(1)}, f32[2,48,256]{2,1,0:T(8,128)S(1)}) custom-call(f32[2,4]{1,0:T(2,128)S(1)} %copy-done.26, f32[3,2,48,256]{3,2,1,0:T(8,128)} %get-tuple-element.49.refs_1_, f32[3,2,48,256]{3,2,1,0:T(8,128)S(1)} %shard_map.68.refs_2_, f32[3,2,48,256]{3,2,1,0:T(8,128)S(1)} %copy-done.16, ...), custom_call_target="tpu_custom_call" | custom-call | flops 1 | bytes 1 | tf_op jit(solution)/shard_map/pallas_call | solution.py:221
  80.5 2.1 %collective-permute-start.21 = (f32[2,136,256]{2,1,0:T(8,128)S(1)}, f32[2,136,256]{2,1,0:T(8,128)S(1)}, u32[]{:S(2)}, u32[]{:S(2)}) collective-permute-start(f32[2,136,256]{2,1,0:T(8,128)S(1)} %get-tuple-element.52.refs_6_.refs_2_.refs_0_), channel_id=1, source_target_pairs={{0,2},{1,3},{2,0},{3,1},{4,6},{5,7},{6,4},{7,5},{8,10},{9,11},{10,... | collective-permute-start | bytes 835592 | tf_op jit(solution)/shard_map/ppermute | solution.py:264
  83.1 17.5 %collective-permute-done.15.refs_3_.refs_1_ = f32[2,168,256]{2,1,0:T(8,128)S(1)} collective-permute-done((f32[2,168,256]{2,1,0:T(8,128)S(1)}, f32[2,168,256]{2,1,0:T(8,128)S(1)}, u32[]{:S(2)}, u32[]{:S(2)}) %collective-permute-start.15) | collective-permute-done | bytes 344096 | tf_op jit(solution)/shard_map/ppermute | solution.py:264
  100.6 1.2 shard_map.70
  102.4 4.2 %collective-permute-done.21.refs_3_.refs_1_ = f32[2,136,256]{2,1,0:T(8,128)S(1)} collective-permute-done((f32[2,136,256]{2,1,0:T(8,128)S(1)}, f32[2,136,256]{2,1,0:T(8,128)S(1)}, u32[]{:S(2)}, u32[]{:S(2)}) %collective-permute-start.21) | collective-permute-done | bytes 278560 | tf_op jit(solution)/shard_map/ppermute | solution.py:264
  106.6 1.3 shard_map.71
  108.0 2.4 %collective-permute-start.24 = (f32[2,48,256]{2,1,0:T(8,128)S(1)}, f32[2,48,256]{2,1,0:T(8,128)S(1)}, u32[]{:S(2)}, u32[]{:S(2)}) collective-permute-start(f32[2,48,256]{2,1,0:T(8,128)S(1)} %collective-permute-done.23.refs_2_), channel_id=1, source_target_pairs={{0,2},{1,3},{2,0},{3,1},{4,6},{5,7},{6,4},{7,5},{8,10},{9,11},{10,... | collective-permute-start | bytes 294920 | tf_op jit(solution)/shard_map/ppermute | solution.py:264
  110.4 8.7 %collective-permute-done.24.refs_3_ = f32[2,48,256]{2,1,0:T(8,128)S(1)} collective-permute-done((f32[2,48,256]{2,1,0:T(8,128)S(1)}, f32[2,48,256]{2,1,0:T(8,128)S(1)}, u32[]{:S(2)}, u32[]{:S(2)}) %collective-permute-start.24) | collective-permute-done | bytes 98336 | tf_op jit(solution)/shard_map/ppermute | solution.py:264
  120.2 2.9 %collective-permute-start.25 = (f32[2,96,256]{2,1,0:T(8,128)S(1)}, f32[2,96,256]{2,1,0:T(8,128)S(1)}, u32[]{:S(2)}, u32[]{:S(2)}) collective-permute-start(f32[2,96,256]{2,1,0:T(8,128)S(1)} %get-tuple-element.59), channel_id=1, source_target_pairs={{0,1},{1,0},{2,3},{3,2},{4,5},{5,4},{6,7},{7,6},{8,9},{9,8},{10,11... | collective-permute-start | bytes 589832 | tf_op jit(solution)/shard_map/ppermute | solution.py:261
  123.2 4.6 %collective-permute-done.25.refs_7_ = f32[2,96,256]{2,1,0:T(8,128)S(1)} collective-permute-done((f32[2,96,256]{2,1,0:T(8,128)S(1)}, f32[2,96,256]{2,1,0:T(8,128)S(1)}, u32[]{:S(2)}, u32[]{:S(2)}) %collective-permute-start.25) | collective-permute-done | bytes 196640 | tf_op jit(solution)/shard_map/ppermute | solution.py:261
  127.8 1.5 %shard_map.73 = (f32[2,1,512,256]{3,2,1,0:T(8,128)}, f32[2,1,512,256]{3,2,1,0:T(8,128)}) custom-call(f32[2,80,256]{2,1,0:T(8,128)S(1)} %get-tuple-element.47.refs_2_.refs_0_, f32[2,80,256]{2,1,0:T(8,128)S(1)} %collective-permute-done.14.refs_7_.refs_1_, f32[2,160,256]{2,1,0:T(8,128)S(1)} %get-tuple-element.53.refs_6_.refs_2_, ...), custom_call_target="tpu_custom_call" | custom-call | flops 1 | bytes 1 | tf_op jit(solution)/shard_map/pallas_call | solution.py:221
  (96 shorter events, 25.7 us)
Async XLA Ops:
  7.2 60.4 %all-gather.5.cloned.1.call-start = ((), (), s32[]{:S(2)}) async-start(), calls=%async_computation | async-start | bytes 1572864 | tf_op jit(solution)/shard_map/all_gather | solution.py:345
  9.2 9.2 %copy-start.1 = (f32[2,1,512,256]{3,2,1,0:T(8,128)S(1)}, f32[2,1,512,256]{3,2,1,0:T(8,128)}, u32[]{:S(2)}) copy-start(f32[2,1,512,256]{3,2,1,0:T(8,128)} %refs_1_.7) | copy-start | bytes 3145732
  9.3 9.2 %collective-permute-start = (f32[3,2,40,256]{3,2,1,0:T(8,128)}, f32[3,2,40,256]{3,2,1,0:T(8,128)S(1)}, u32[]{:S(2)}, u32[]{:S(2)}) collective-permute-start(f32[3,2,40,256]{3,2,1,0:T(8,128)} %get-tuple-element.32), channel_id=1, source_target_pairs={{0,16},{8,24},{16,0},{24,8},{1,17},{9,25},{17,1},{25,9},{2,18},{10... | collective-permute-start | bytes 737288 | tf_op jit(solution)/shard_map/ppermute | solution.py:250
  13.3 14.6 %copy-start.23 = (f32[2,4]{1,0:T(2,128)S(1)}, f32[2,4]{1,0:T(2,128)}, u32[]{:S(2)}) copy-start(f32[2,4]{1,0:T(2,128)} %constant.34.clone.refs_0_) | copy-start | bytes 100
  13.3 54.2 %all-gather.7.cloned.1.call-start = ((), (), s32[]{:S(2)}) async-start(), calls=%async_computation.1 | async-start | bytes 1572864 | tf_op jit(solution)/shard_map/all_gather | solution.py:345
  13.4 13.7 %collective-permute-start.3 = (f32[2,256,256]{2,1,0:T(8,128)}, f32[2,256,256]{2,1,0:T(8,128)S(1)}, u32[]{:S(2)}, u32[]{:S(2)}) collective-permute-start(f32[2,256,256]{2,1,0:T(8,128)} %get-tuple-element.61), channel_id=1, source_target_pairs={{0,1},{1,0},{2,3},{3,2},{4,5},{5,4},{6,7},{7,6},{8,9},{9,8},{10,11... | collective-permute-start | bytes 1572872 | tf_op jit(solution)/shard_map/ppermute | solution.py:261
  20.4 19.4 %collective-permute-start.5 = (f32[3,2,80,256]{3,2,1,0:T(8,128)}, f32[3,2,80,256]{3,2,1,0:T(8,128)}, u32[]{:S(2)}, u32[]{:S(2)}) collective-permute-start(f32[3,2,80,256]{3,2,1,0:T(8,128)} %get-tuple-element.36), channel_id=1, source_target_pairs={{0,16},{8,24},{16,0},{24,8},{1,17},{9,25},{17,1},{25,9},{2,18},{10... | collective-permute-start | bytes 1474568 | tf_op jit(solution)/shard_map/ppermute | solution.py:250
  22.1 1.5 %collective-permute-start.1 = (f32[3,2,40,256]{3,2,1,0:T(8,128)S(1)}, f32[3,2,40,256]{3,2,1,0:T(8,128)S(1)}, u32[]{:S(2)}, u32[]{:S(2)}) collective-permute-start(f32[3,2,40,256]{3,2,1,0:T(8,128)S(1)} %copy-done.17), channel_id=1, source_target_pairs={{0,8},{8,0},{16,24},{24,16},{1,9},{9,1},{17,25},{25,17},{2,10},{10... | collective-permute-start | bytes 737288 | tf_op jit(solution)/shard_map/ppermute | solution.py:253
  22.1 2.2 %collective-permute-start.2 = (f32[3,2,40,256]{3,2,1,0:T(8,128)S(1)}, f32[3,2,40,256]{3,2,1,0:T(8,128)S(1)}, u32[]{:S(2)}, u32[]{:S(2)}) collective-permute-start(f32[3,2,40,256]{3,2,1,0:T(8,128)S(1)} %get-tuple-element.33.refs_2_), channel_id=1, source_target_pairs={{0,8},{8,0},{16,24},{24,16},{1,9},{9,1},{17,25},{25,17},{2,10},{10... | collective-permute-start | bytes 737288 | tf_op jit(solution)/shard_map/ppermute | solution.py:253
  32.7 5.4 %collective-permute-start.4 = (f32[2,40,256]{2,1,0:T(8,128)S(1)}, f32[2,40,256]{2,1,0:T(8,128)S(1)}, u32[]{:S(2)}, u32[]{:S(2)}) collective-permute-start(f32[2,40,256]{2,1,0:T(8,128)S(1)} %get-tuple-element.34.refs_5_.refs_0_), channel_id=1, source_target_pairs={{0,2},{1,3},{2,0},{3,1},{4,6},{5,7},{6,4},{7,5},{8,10},{9,11},{10,... | collective-permute-start | bytes 245768 | tf_op jit(solution)/shard_map/ppermute | solution.py:264
  35.3 4.4 %collective-permute-start.6 = (f32[2,40,256]{2,1,0:T(8,128)S(1)}, f32[2,40,256]{2,1,0:T(8,128)S(1)}, u32[]{:S(2)}, u32[]{:S(2)}) collective-permute-start(f32[2,40,256]{2,1,0:T(8,128)S(1)} %get-tuple-element.37), channel_id=1, source_target_pairs={{0,16},{8,24},{16,0},{24,8},{1,17},{9,25},{17,1},{25,9},{2,18},{10... | collective-permute-start | bytes 245768 | tf_op jit(solution)/shard_map/ppermute | solution.py:250
  35.9 6.5 %collective-permute-start.7 = (f32[3,2,80,256]{3,2,1,0:T(8,128)}, f32[3,2,80,256]{3,2,1,0:T(8,128)}, u32[]{:S(2)}, u32[]{:S(2)}) collective-permute-start(f32[3,2,80,256]{3,2,1,0:T(8,128)} %copy-done.11), channel_id=1, source_target_pairs={{0,8},{8,0},{16,24},{24,16},{1,9},{9,1},{17,25},{25,17},{2,10},{10... | collective-permute-start | bytes 1474568 | tf_op jit(solution)/shard_map/ppermute | solution.py:253
  41.8 2.2 %collective-permute-start.8 = (f32[3,2,80,256]{3,2,1,0:T(8,128)}, f32[3,2,80,256]{3,2,1,0:T(8,128)}, u32[]{:S(2)}, u32[]{:S(2)}) collective-permute-start(f32[3,2,80,256]{3,2,1,0:T(8,128)} %get-tuple-element.38.refs_2_), channel_id=1, source_target_pairs={{0,8},{8,0},{16,24},{24,16},{1,9},{9,1},{17,25},{25,17},{2,10},{10... | collective-permute-start | bytes 1474568 | tf_op jit(solution)/shard_map/ppermute | solution.py:253
  41.8 15.4 %collective-permute-start.10 = (f32[3,2,88,256]{3,2,1,0:T(8,128)}, f32[3,2,88,256]{3,2,1,0:T(8,128)}, u32[]{:S(2)}, u32[]{:S(2)}) collective-permute-start(f32[3,2,88,256]{3,2,1,0:T(8,128)} %get-tuple-element.43), channel_id=1, source_target_pairs={{0,16},{8,24},{16,0},{24,8},{1,17},{9,25},{17,1},{25,9},{2,18},{10... | collective-permute-start | bytes 1622024 | tf_op jit(solution)/shard_map/ppermute | solution.py:250
  47.8 14.2 %collective-permute-start.9 = (f32[2,120,256]{2,1,0:T(8,128)S(1)}, f32[2,120,256]{2,1,0:T(8,128)S(1)}, u32[]{:S(2)}, u32[]{:S(2)}) collective-permute-start(f32[2,120,256]{2,1,0:T(8,128)S(1)} %get-tuple-element.39.refs_2_.refs_5_.refs_0_), channel_id=1, source_target_pairs={{0,2},{1,3},{2,0},{3,1},{4,6},{5,7},{6,4},{7,5},{8,10},{9,11},{10,... | collective-permute-start | bytes 737288 | tf_op jit(solution)/shard_map/ppermute | solution.py:264
  48.9 11.3 %collective-permute-start.11 = (f32[2,80,256]{2,1,0:T(8,128)S(1)}, f32[2,80,256]{2,1,0:T(8,128)S(1)}, u32[]{:S(2)}, u32[]{:S(2)}) collective-permute-start(f32[2,80,256]{2,1,0:T(8,128)S(1)} %get-tuple-element.44), channel_id=1, source_target_pairs={{0,16},{8,24},{16,0},{24,8},{1,17},{9,25},{17,1},{25,9},{2,18},{10... | collective-permute-start | bytes 491528 | tf_op jit(solution)/shard_map/ppermute | solution.py:250
  49.4 15.7 %copy-start.10 = (f32[3,2,88,256]{3,2,1,0:T(8,128)S(1)}, f32[3,2,88,256]{3,2,1,0:T(8,128)}, u32[]{:S(2)}) copy-start(f32[3,2,88,256]{3,2,1,0:T(8,128)} %copy-done.9) | copy-start | bytes 1622020
  49.4 15.7 %copy-start.25 = (f32[2,4]{1,0:T(2,128)S(1)}, f32[2,4]{1,0:T(2,128)}, u32[]{:S(2)}) copy-start(f32[2,4]{1,0:T(2,128)} %constant.34.clone.refs_0_) | copy-start | bytes 100
  49.4 14.2 %collective-permute-start.12 = (f32[3,2,88,256]{3,2,1,0:T(8,128)}, f32[3,2,88,256]{3,2,1,0:T(8,128)S(1)}, u32[]{:S(2)}, u32[]{:S(2)}) collective-permute-start(f32[3,2,88,256]{3,2,1,0:T(8,128)} %copy-done.9), channel_id=1, source_target_pairs={{0,8},{8,0},{16,24},{24,16},{1,9},{9,1},{17,25},{25,17},{2,10},{10... | collective-permute-start | bytes 1622024 | tf_op jit(solution)/shard_map/ppermute | solution.py:253
  62.9 2.2 %collective-permute-start.13 = (f32[3,2,88,256]{3,2,1,0:T(8,128)}, f32[3,2,88,256]{3,2,1,0:T(8,128)S(1)}, u32[]{:S(2)}, u32[]{:S(2)}) collective-permute-start(f32[3,2,88,256]{3,2,1,0:T(8,128)} %get-tuple-element.45.refs_2_), channel_id=1, source_target_pairs={{0,8},{8,0},{16,24},{24,16},{1,9},{9,1},{17,25},{25,17},{2,10},{10... | collective-permute-start | bytes 1622024 | tf_op jit(solution)/shard_map/ppermute | solution.py:253
  63.0 10.1 %collective-permute-start.16 = (f32[3,2,48,256]{3,2,1,0:T(8,128)}, f32[3,2,48,256]{3,2,1,0:T(8,128)S(1)}, u32[]{:S(2)}, u32[]{:S(2)}) collective-permute-start(f32[3,2,48,256]{3,2,1,0:T(8,128)} %get-tuple-element.50), channel_id=1, source_target_pairs={{0,16},{8,24},{16,0},{24,8},{1,17},{9,25},{17,1},{25,9},{2,18},{10... | collective-permute-start | bytes 884744 | tf_op jit(solution)/shard_map/ppermute | solution.py:250
  66.9 9.5 %collective-permute-start.17 = (f32[2,88,256]{2,1,0:T(8,128)S(1)}, f32[2,88,256]{2,1,0:T(8,128)S(1)}, u32[]{:S(2)}, u32[]{:S(2)}) collective-permute-start(f32[2,88,256]{2,1,0:T(8,128)S(1)} %get-tuple-element.51), channel_id=1, source_target_pairs={{0,16},{8,24},{16,0},{24,8},{1,17},{9,25},{17,1},{25,9},{2,18},{10... | collective-permute-start | bytes 540680 | tf_op jit(solution)/shard_map/ppermute | solution.py:250
  67.5 9.0 %collective-permute-start.18 = (f32[3,2,48,256]{3,2,1,0:T(8,128)}, f32[3,2,48,256]{3,2,1,0:T(8,128)S(1)}, u32[]{:S(2)}, u32[]{:S(2)}) collective-permute-start(f32[3,2,48,256]{3,2,1,0:T(8,128)} %get-tuple-element.49.refs_1_), channel_id=1, source_target_pairs={{0,8},{8,0},{16,24},{24,16},{1,9},{9,1},{17,25},{25,17},{2,10},{10... | collective-permute-start | bytes 884744 | tf_op jit(solution)/shard_map/ppermute | solution.py:253
  76.5 1.6 %collective-permute-start.19 = (f32[3,2,48,256]{3,2,1,0:T(8,128)S(1)}, f32[3,2,48,256]{3,2,1,0:T(8,128)S(1)}, u32[]{:S(2)}, u32[]{:S(2)}) collective-permute-start(f32[3,2,48,256]{3,2,1,0:T(8,128)S(1)} %shard_map.68.refs_2_), channel_id=1, source_target_pairs={{0,8},{8,0},{16,24},{24,16},{1,9},{9,1},{17,25},{25,17},{2,10},{10... | collective-permute-start | bytes 884744 | tf_op jit(solution)/shard_map/ppermute | solution.py:253
  76.5 24.1 %collective-permute-start.15 = (f32[2,168,256]{2,1,0:T(8,128)S(1)}, f32[2,168,256]{2,1,0:T(8,128)S(1)}, u32[]{:S(2)}, u32[]{:S(2)}) collective-permute-start(f32[2,168,256]{2,1,0:T(8,128)S(1)} %get-tuple-element.46.refs_6_.refs_2_.refs_0_), channel_id=1, source_target_pairs={{0,2},{1,3},{2,0},{3,1},{4,6},{5,7},{6,4},{7,5},{8,10},{9,11},{10,... | collective-permute-start | bytes 1032200 | tf_op jit(solution)/shard_map/ppermute | solution.py:264
  80.5 26.1 %collective-permute-start.21 = (f32[2,136,256]{2,1,0:T(8,128)S(1)}, f32[2,136,256]{2,1,0:T(8,128)S(1)}, u32[]{:S(2)}, u32[]{:S(2)}) collective-permute-start(f32[2,136,256]{2,1,0:T(8,128)S(1)} %get-tuple-element.52.refs_6_.refs_2_.refs_0_), channel_id=1, source_target_pairs={{0,2},{1,3},{2,0},{3,1},{4,6},{5,7},{6,4},{7,5},{8,10},{9,11},{10,... | collective-permute-start | bytes 835592 | tf_op jit(solution)/shard_map/ppermute | solution.py:264
  82.6 19.8 %collective-permute-start.14 = (f32[2,80,256]{2,1,0:T(8,128)S(1)}, f32[2,80,256]{2,1,0:T(8,128)S(1)}, u32[]{:S(2)}, u32[]{:S(2)}) collective-permute-start(f32[2,80,256]{2,1,0:T(8,128)S(1)} %get-tuple-element.48), channel_id=1, source_target_pairs={{0,1},{1,0},{2,3},{3,2},{4,5},{5,4},{6,7},{7,6},{8,9},{9,8},{10,11... | collective-permute-start | bytes 491528 | tf_op jit(solution)/shard_map/ppermute | solution.py:261
  101.8 17.3 %collective-permute-start.20 = (f32[2,160,256]{2,1,0:T(8,128)S(1)}, f32[2,160,256]{2,1,0:T(8,128)S(1)}, u32[]{:S(2)}, u32[]{:S(2)}) collective-permute-start(f32[2,160,256]{2,1,0:T(8,128)S(1)} %get-tuple-element.54), channel_id=1, source_target_pairs={{0,1},{1,0},{2,3},{3,2},{4,5},{5,4},{6,7},{7,6},{8,9},{9,8},{10,11... | collective-permute-start | bytes 983048 | tf_op jit(solution)/shard_map/ppermute | solution.py:261
  101.8 6.1 %collective-permute-start.23 = (f32[2,48,256]{2,1,0:T(8,128)S(1)}, f32[2,48,256]{2,1,0:T(8,128)S(1)}, u32[]{:S(2)}, u32[]{:S(2)}) collective-permute-start(f32[2,48,256]{2,1,0:T(8,128)S(1)} %get-tuple-element.57), channel_id=1, source_target_pairs={{0,16},{8,24},{16,0},{24,8},{1,17},{9,25},{17,1},{25,9},{2,18},{10... | collective-permute-start | bytes 294920 | tf_op jit(solution)/shard_map/ppermute | solution.py:250
  107.9 19.9 %collective-permute-start.22 = (f32[2,176,256]{2,1,0:T(8,128)S(1)}, f32[2,176,256]{2,1,0:T(8,128)S(1)}, u32[]{:S(2)}, u32[]{:S(2)}) collective-permute-start(f32[2,176,256]{2,1,0:T(8,128)S(1)} %get-tuple-element.56), channel_id=1, source_target_pairs={{0,1},{1,0},{2,3},{3,2},{4,5},{5,4},{6,7},{7,6},{8,9},{9,8},{10,11... | collective-permute-start | bytes 1081352 | tf_op jit(solution)/shard_map/ppermute | solution.py:261
  108.0 11.1 %collective-permute-start.24 = (f32[2,48,256]{2,1,0:T(8,128)S(1)}, f32[2,48,256]{2,1,0:T(8,128)S(1)}, u32[]{:S(2)}, u32[]{:S(2)}) collective-permute-start(f32[2,48,256]{2,1,0:T(8,128)S(1)} %collective-permute-done.23.refs_2_), channel_id=1, source_target_pairs={{0,2},{1,3},{2,0},{3,1},{4,6},{5,7},{6,4},{7,5},{8,10},{9,11},{10,... | collective-permute-start | bytes 294920 | tf_op jit(solution)/shard_map/ppermute | solution.py:264
  120.2 7.5 %collective-permute-start.25 = (f32[2,96,256]{2,1,0:T(8,128)S(1)}, f32[2,96,256]{2,1,0:T(8,128)S(1)}, u32[]{:S(2)}, u32[]{:S(2)}) collective-permute-start(f32[2,96,256]{2,1,0:T(8,128)S(1)} %get-tuple-element.59), channel_id=1, source_target_pairs={{0,1},{1,0},{2,3},{3,2},{4,5},{5,4},{6,7},{7,6},{8,9},{9,8},{10,11... | collective-permute-start | bytes 589832 | tf_op jit(solution)/shard_map/ppermute | solution.py:261
  (23 other events, 62.9 us)
Sparse Core Ops, SparseCore 0:
  13.5 21.6 all-gather.4
  42.4 21.7 all-gather.6

commit v7 on v6

--- a/solution.py
+++ b/solution.py
@@ -10,7 +10,7 @@
 from jax.sharding import PartitionSpec as P
 
 CORES = 2
-WEIGHTS = (5, 10, 11, 6)
+WEIGHTS = (10, 10, 8, 4)
 SUBLANES, LANES = 8, 128
 VMEM_LIMIT = 40 * 2**20
 FIRST_LIMIT = 56 * 2**20
@@ -155,23 +155,20 @@
     return high, (value - high.astype(jnp.float32)).astype(jnp.bfloat16)
 
 
-def right_kernel(group, *refs):
-    pieces, high, low = refs[:group], refs[-2], refs[-1]
-    half = lax.axis_index("tc") // group
-    row_parts, _, depth, cols = pieces[0].shape
-    for part in range(row_parts):
-        place = lax.rem(half - part + row_parts, row_parts) * depth
+def right_kernel(*refs):
+    panels, outs = refs[:-2], refs[-2:]
+    row_parts, (_, depth, width) = len(panels), panels[0].shape
+    shift = lax.axis_index("tc") // (lax.axis_size("tc") // row_parts) - lax.axis_index("tr")
+    first, second = pl.ds(0, width), pl.ds(width, width)
+    for part, panel in enumerate(panels):
+        place = lax.rem(shift + part + row_parts, row_parts) * depth
         upper = pl.ds(pl.multiple_of(place, depth), depth)
         lower = pl.ds(pl.multiple_of(place + row_parts * depth, depth), depth)
-        for gap, piece in enumerate(pieces):
-            first = pl.ds(gap * cols, cols)
-            second = pl.ds((group + gap) * cols, cols)
-            real, imag = split(piece[part, 0]), split(piece[part, 1])
-            for out, real_part, imag_part in zip((high, low), real, imag):
-                out[upper, first] = real_part
-                out[lower, second] = real_part
-                out[upper, second] = imag_part
-                out[lower, first] = -imag_part
+        for out, real, imag in zip(outs, split(panel[0]), split(panel[1])):
+            out[upper, first] = real
+            out[lower, second] = real
+            out[upper, second] = imag
+            out[lower, first] = -imag
 
 
 def product_kernel(group, spans, *refs):
@@ -342,7 +339,8 @@
         block = lax.dynamic_index_in_dim(blocks, (member + gap) % group, 1, False)
         panels.append(to_panel(block, 0, gap) if gap else block)
     early = panels[1:]
-    panels = [lax.all_gather(panel, "tr") for panel in panels]
+    panel = jnp.concatenate(panels, axis=2)
+    panels = [panel] + [to_panel(panel, gap, 0) for gap in range(1, row_parts)]
     extent = 2 * row_parts * cols
 
     lefts, results, returned, last = [], [], (), ()
@@ -354,21 +352,25 @@
 
     for at, step in enumerate(sizes):
         across, beside = sent[at]
+        sent_over = (*lefts[at - 1][1:], *(early if at == 1 else ())) if at else ()
         if at + 1 < len(sizes):
-            fresh, across = pack(at + 1, across, (*returned, *last, *(lefts[at - 1][1:] if at else ())))
+            fresh, across = pack(at + 1, across, (*returned, *last, *sent_over))
             pieces.append(fresh)
             sent.append(forward(fresh))
         else:
-            across = gate(across, (*returned, *last))
+            across = gate(across, (*returned, *last, *sent_over))
         here = [pieces[at][0], *across]
         other = [beside, *(to_core(piece) for piece in across)]
-        sigmas = energy(at, here, other, returned, () if at else early)
+        ending = at >= 2 and at + 1 == len(sizes)
+        if ending:
+            last = add_product(across[:1])
+        sigmas = energy(at, here, other, returned, last if ending else ())
         returned = [to_chip(sigmas[gap], gap) for gap in range(1, chips)]
         lefts.append(sides(sigmas[0]))
         last = sigmas[:1]
         if at == min(1, len(sizes) - 1):
             right = call(
-                functools.partial(right_kernel, group),
+                right_kernel,
                 [bf16((extent, 2 * group * cols))] * 2,
                 [IN_VMEM] * len(panels),
                 [IN_VMEM] * 2,
@@ -376,7 +378,7 @@
                 (),
                 last,
             )
-        if at >= 2:
+        if at >= 2 and not ending:
             last = add_product(last)
     while len(results) < len(sizes):
         last = add_product(last)

time: 137 us -> 119 us (0.87)
  local copies, waits for them, and re-layouts: 14.6 us -> 0.1 us
  between operations: 14.3 us -> 0.87 us
  waiting for transfers between devices: 66.5 us -> 73.1 us
  starting transfers between devices: 22.3 us -> 28.4 us
  Pallas kernels: 18.3 us -> 15.9 us
    ppermute x5 -> x6, waiting for transfers between devices: 6.63 us -> 22.3 us  [to_panel(): return lax.ppermute(value, ('tr', 'tc'), moves)]
    unnamed x54 -> x10, local copies, waits for them, and re-layouts: 13.5 us -> 0.02 us
    ppermute x5, waiting for transfers between devices: 34.4 us -> 23.7 us  [to_half(): lax.ppermute(value, 'tc', [(j, (j + group * gap) % col_parts) for j in ra...]
    ppermute x5 -> x6, starting transfers between devices: 5.19 us -> 11.6 us  [to_panel(): return lax.ppermute(value, ('tr', 'tc'), moves)]
    ppermute x8, waiting for transfers between devices: 20.5 us -> 25.4 us  [to_chip(): return lax.ppermute(value, 'ka', moves)]
    ppermute x8, waiting for transfers between devices: 5.01 us -> 1.72 us  [to_core(): lax.ppermute(value, 'ka', [(s, s + 1 - 2 * (s % CORES)) for s in range(mo...]
    pallas_call x15, Pallas kernels: 18.3 us -> 15.9 us  [call(): pl.pallas_call(ordered, out_shape=out_shapes, in_specs=in_specs + [ANYWHE...]
    ppermute x8, starting transfers between devices: 8.14 us -> 9.84 us  [to_chip(): return lax.ppermute(value, 'ka', moves)]
  transfers between devices with their start and end apart: 28 -> 27, of which waited for: 17 -> 14; matrix products, arithmetic and copies ran while one was open for 1% -> 0% of each run, Pallas kernels for 11% -> 10%
where the time goes in v7:
time: 119 us
  waiting for transfers between devices  73.1 us (61%)
  starting transfers between devices  28.4 us (24%)
  Pallas kernels  15.9 us (13%)
    ppermute x8, waiting for transfers between devices, to_chip(): return lax.ppermute(value, 'ka', moves)  25.4 us
    ppermute x5, waiting for transfers between devices, to_half(): lax.ppermute(value, 'tc', [(j, (j + group * gap) % col_parts) for j in ra...  23.7 us
    ppermute x6, waiting for transfers between devices, to_panel(): return lax.ppermute(value, ('tr', 'tc'), moves)  22.3 us
    pallas_call x15, Pallas kernels, call(): pl.pallas_call(ordered, out_shape=out_shapes, in_specs=in_specs + [ANYWHE...  15.9 us
    ppermute x6, starting transfers between devices, to_panel(): return lax.ppermute(value, ('tr', 'tc'), moves)  11.6 us
    ppermute x8, starting transfers between devices, to_chip(): return lax.ppermute(value, 'ka', moves)  9.84 us
    ppermute x5, starting transfers between devices, to_half(): lax.ppermute(value, 'tc', [(j, (j + group * gap) % col_parts) for j in ra...  6.7 us
  transfers between devices with their start and end apart: 27, of which 14 were waited for; matrix products, arithmetic and copies ran while one was open for 0% of the time, Pallas kernels for 10%

profile of v7, /device:TPU:0, one launch (start us, length us, event | category | flops | bytes accessed | tf_op | source)
XLA Modules:
  0.0 118.5 jit_solution(3467229303427819848)
XLA Ops:
  0.7 2.4 %shard_map.59 = (f32[3,2,80,256]{3,2,1,0:T(8,128)}, f32[3,2,80,256]{3,2,1,0:T(8,128)}) custom-call(f32[2,1,512,256]{3,2,1,0:T(8,128)} %refs_8_.1, f32[2,1,512,256]{3,2,1,0:T(8,128)} %refs_1_.7, f32[2,1,512,256]{3,2,1,0:T(8,128)} %refs_2_.7), custom_call_target="tpu_custom_call" | custom-call | flops 1 | bytes 1 | tf_op jit(solution)/shard_map/pallas_call | solution.py:218
  3.1 3.0 %collective-permute-start = (f32[3,2,80,256]{3,2,1,0:T(8,128)}, f32[3,2,80,256]{3,2,1,0:T(8,128)}, u32[]{:S(2)}, u32[]{:S(2)}) collective-permute-start(f32[3,2,80,256]{3,2,1,0:T(8,128)} %get-tuple-element.32), channel_id=1, source_target_pairs={{0,16},{8,24},{16,0},{24,8},{1,17},{9,25},{17,1},{25,9},{2,18},{10... | collective-permute-start | bytes 1474568 | tf_op jit(solution)/shard_map/ppermute | solution.py:247
  6.1 11.5 %collective-permute-done.refs_3_ = f32[3,2,80,256]{3,2,1,0:T(8,128)} collective-permute-done((f32[3,2,80,256]{3,2,1,0:T(8,128)}, f32[3,2,80,256]{3,2,1,0:T(8,128)}, u32[]{:S(2)}, u32[]{:S(2)}) %collective-permute-start) | collective-permute-done | bytes 491552 | tf_op jit(solution)/shard_map/ppermute | solution.py:247
  18.6 1.9 %collective-permute-start.6 = (f32[2,256,256]{2,1,0:T(8,128)S(1)}, f32[2,256,256]{2,1,0:T(8,128)S(1)}, u32[]{:S(2)}, u32[]{:S(2)}) collective-permute-start(f32[2,256,256]{2,1,0:T(8,128)S(1)} %get-tuple-element.61), channel_id=1, source_target_pairs={{0,1},{1,0},{2,3},{3,2},{4,5},{5,4},{6,7},{7,6},{8,9},{9,8},{10,11... | collective-permute-start | bytes 1572872 | tf_op jit(solution)/shard_map/ppermute | solution.py:258
  20.4 1.5 %collective-permute-start.4 = (f32[3,2,80,256]{3,2,1,0:T(8,128)S(1)}, f32[3,2,80,256]{3,2,1,0:T(8,128)S(1)}, u32[]{:S(2)}, u32[]{:S(2)}) collective-permute-start(f32[3,2,80,256]{3,2,1,0:T(8,128)S(1)} %get-tuple-element.36), channel_id=1, source_target_pairs={{0,16},{8,24},{16,0},{24,8},{1,17},{9,25},{17,1},{25,9},{2,18},{10... | collective-permute-start | bytes 1474568 | tf_op jit(solution)/shard_map/ppermute | solution.py:247
  22.0 1.9 %shard_map.61 = (f32[2,80,256]{2,1,0:T(8,128)S(1)}, f32[2,80,256]{2,1,0:T(8,128)S(1)}) custom-call(f32[2,4]{1,0:T(2,128)S(1)} %copy-done.4, f32[3,2,80,256]{3,2,1,0:T(8,128)S(1)} %copy-done.3, f32[3,2,80,256]{3,2,1,0:T(8,128)} %get-tuple-element.33.refs_2_, f32[3,2,80,256]{3,2,1,0:T(8,128)} %collective-permute-done.1.refs_3_, ...), custom_call_target="tpu_custom_call" | custom-call | flops 1 | bytes 1 | tf_op jit(solution)/shard_map/pallas_call | solution.py:218
  23.9 2.7 %collective-permute-start.3 = (f32[2,80,256]{2,1,0:T(8,128)S(1)}, f32[2,80,256]{2,1,0:T(8,128)S(1)}, u32[]{:S(2)}, u32[]{:S(2)}) collective-permute-start(f32[2,80,256]{2,1,0:T(8,128)S(1)} %get-tuple-element.34.refs_5_.refs_0_), channel_id=1, source_target_pairs={{0,2},{1,3},{2,0},{3,1},{4,6},{5,7},{6,4},{7,5},{8,10},{9,11},{10,... | collective-permute-start | bytes 491528 | tf_op jit(solution)/shard_map/ppermute | solution.py:261
  27.1 9.4 %collective-permute-done.6.refs_7_ = f32[2,256,256]{2,1,0:T(8,128)S(1)} collective-permute-done((f32[2,256,256]{2,1,0:T(8,128)S(1)}, f32[2,256,256]{2,1,0:T(8,128)S(1)}, u32[]{:S(2)}, u32[]{:S(2)}) %collective-permute-start.6) | collective-permute-done | bytes 524320 | tf_op jit(solution)/shard_map/ppermute | solution.py:258
  37.9 1.6 %collective-permute-start.11 = (f32[3,2,64,256]{3,2,1,0:T(8,128)S(1)}, f32[3,2,64,256]{3,2,1,0:T(8,128)S(1)}, u32[]{:S(2)}, u32[]{:S(2)}) collective-permute-start(f32[3,2,64,256]{3,2,1,0:T(8,128)S(1)} %get-tuple-element.43), channel_id=1, source_target_pairs={{0,16},{8,24},{16,0},{24,8},{1,17},{9,25},{17,1},{25,9},{2,18},{10... | collective-permute-start | bytes 1179656 | tf_op jit(solution)/shard_map/ppermute | solution.py:247
  39.6 1.6 %collective-permute-start.10 = (f32[2,256,512]{2,1,0:T(8,128)S(1)}, f32[2,256,512]{2,1,0:T(8,128)S(1)}, u32[]{:S(2)}, u32[]{:S(2)}) collective-permute-start(f32[2,256,512]{2,1,0:T(8,128)S(1)} %pad_maximum_fusion.refs_0_), channel_id=1, source_target_pairs={{0,4},{1,5},{2,6},{3,7},{4,0},{5,1},{6,2},{7,3},{8,12},{9,13},{10,... | collective-permute-start | bytes 3145736 | tf_op jit(solution)/shard_map/ppermute | solution.py:258
  41.2 1.3 %shard_map.63 = (f32[2,160,256]{2,1,0:T(8,128)S(1)}, f32[2,80,256]{2,1,0:T(8,128)S(1)}) custom-call(f32[2,4]{1,0:T(2,128)S(1)} %copy-done.4, f32[3,2,80,256]{3,2,1,0:T(8,128)S(1)} %get-tuple-element.35.refs_1_, f32[3,2,80,256]{3,2,1,0:T(8,128)S(1)} %get-tuple-element.38.refs_2_, f32[3,2,80,256]{3,2,1,0:T(8,128)S(1)} %collective-permute-done.7.refs_3_, ...), custom_call_target="tpu_custom_call" | custom-call | flops 1 | bytes 1 | tf_op jit(solution)/shard_map/pallas_call | solution.py:218
  42.5 2.7 %collective-permute-start.9 = (f32[2,160,256]{2,1,0:T(8,128)S(1)}, f32[2,160,256]{2,1,0:T(8,128)S(1)}, u32[]{:S(2)}, u32[]{:S(2)}) collective-permute-start(f32[2,160,256]{2,1,0:T(8,128)S(1)} %get-tuple-element.39.refs_2_.refs_5_.refs_0_), channel_id=1, source_target_pairs={{0,2},{1,3},{2,0},{3,1},{4,6},{5,7},{6,4},{7,5},{8,10},{9,11},{10,... | collective-permute-start | bytes 983048 | tf_op jit(solution)/shard_map/ppermute | solution.py:261
  45.7 4.2 %collective-permute-done.11.refs_3_ = f32[3,2,64,256]{3,2,1,0:T(8,128)S(1)} collective-permute-done((f32[3,2,64,256]{3,2,1,0:T(8,128)S(1)}, f32[3,2,64,256]{3,2,1,0:T(8,128)S(1)}, u32[]{:S(2)}, u32[]{:S(2)}) %collective-permute-start.11) | collective-permute-done | bytes 393248 | tf_op jit(solution)/shard_map/ppermute | solution.py:247
  49.9 3.1 %collective-permute-done.12.refs_4_.refs_5_ = f32[2,80,256]{2,1,0:T(8,128)S(1)} collective-permute-done((f32[2,80,256]{2,1,0:T(8,128)S(1)}, f32[2,80,256]{2,1,0:T(8,128)S(1)}, u32[]{:S(2)}, u32[]{:S(2)}) %collective-permute-start.12) | collective-permute-done | bytes 163872 | tf_op jit(solution)/shard_map/ppermute | solution.py:247
  53.0 7.1 %collective-permute-done.9.refs_6_.refs_3_.refs_1_ = f32[2,160,256]{2,1,0:T(8,128)S(1)} collective-permute-done((f32[2,160,256]{2,1,0:T(8,128)S(1)}, f32[2,160,256]{2,1,0:T(8,128)S(1)}, u32[]{:S(2)}, u32[]{:S(2)}) %collective-permute-start.9) | collective-permute-done | bytes 327712 | tf_op jit(solution)/shard_map/ppermute | solution.py:261
  60.4 1.7 %collective-permute-done.14.refs_4_ = f32[3,2,64,256]{3,2,1,0:T(8,128)S(1)} collective-permute-done((f32[3,2,64,256]{3,2,1,0:T(8,128)S(1)}, f32[3,2,64,256]{3,2,1,0:T(8,128)S(1)}, u32[]{:S(2)}, u32[]{:S(2)}) %collective-permute-start.14) | collective-permute-done | bytes 393248 | tf_op jit(solution)/shard_map/ppermute | solution.py:250
  64.0 1.5 %collective-permute-start.18 = (f32[2,64,256]{2,1,0:T(8,128)S(1)}, f32[2,64,256]{2,1,0:T(8,128)S(1)}, u32[]{:S(2)}, u32[]{:S(2)}) collective-permute-start(f32[2,64,256]{2,1,0:T(8,128)S(1)} %get-tuple-element.50), channel_id=1, source_target_pairs={{0,16},{8,24},{16,0},{24,8},{1,17},{9,25},{17,1},{25,9},{2,18},{10... | collective-permute-start | bytes 393224 | tf_op jit(solution)/shard_map/ppermute | solution.py:247
  66.1 1.2 %shard_map.67 = (f32[2,160,256]{2,1,0:T(8,128)S(1)}, f32[2,160,256]{2,1,0:T(8,128)S(1)}) custom-call(f32[2,80,256]{2,1,0:T(8,128)S(1)} %get-tuple-element.34.refs_5_.refs_0_, f32[2,80,256]{2,1,0:T(8,128)S(1)} %collective-permute-done.3.refs_6_.refs_1_, f32[2,160,256]{2,1,0:T(8,128)S(1)} %get-tuple-element.39.refs_2_.refs_5_.refs_0_, ...), custom_call_target="tpu_custom_call" | custom-call | flops 1 | bytes 1 | tf_op jit(solution)/shard_map/pallas_call | solution.py:218
  67.3 3.9 %collective-permute-done.17.refs_0_ = f32[3,2,32,256]{3,2,1,0:T(8,128)S(1)} collective-permute-done((f32[3,2,32,256]{3,2,1,0:T(8,128)S(1)}, f32[3,2,32,256]{3,2,1,0:T(8,128)S(1)}, u32[]{:S(2)}, u32[]{:S(2)}) %collective-permute-start.17) | collective-permute-done | bytes 196640 | tf_op jit(solution)/shard_map/ppermute | solution.py:247
  71.2 2.0 %collective-permute-done.18.refs_1_.refs_5_ = f32[2,64,256]{2,1,0:T(8,128)S(1)} collective-permute-done((f32[2,64,256]{2,1,0:T(8,128)S(1)}, f32[2,64,256]{2,1,0:T(8,128)S(1)}, u32[]{:S(2)}, u32[]{:S(2)}) %collective-permute-start.18) | collective-permute-done | bytes 131104 | tf_op jit(solution)/shard_map/ppermute | solution.py:247
  73.2 6.4 %collective-permute-done.16.refs_3_.refs_1_ = f32[2,144,256]{2,1,0:T(8,128)S(1)} collective-permute-done((f32[2,144,256]{2,1,0:T(8,128)S(1)}, f32[2,144,256]{2,1,0:T(8,128)S(1)}, u32[]{:S(2)}, u32[]{:S(2)}) %collective-permute-start.16) | collective-permute-done | bytes 294944 | tf_op jit(solution)/shard_map/ppermute | solution.py:261
  79.6 1.2 %shard_map.69 = (f32[2,160,256]{2,1,0:T(8,128)S(1)}, f32[2,160,256]{2,1,0:T(8,128)S(1)}) custom-call(f32[2,160,256]{2,1,0:T(8,128)S(1)} %get-tuple-element.39.refs_2_.refs_5_.refs_0_, f32[2,160,256]{2,1,0:T(8,128)S(1)} %collective-permute-done.9.refs_6_.refs_3_.refs_1_, f32[2,144,256]{2,1,0:T(8,128)S(1)} %get-tuple-element.46.refs_6_.refs_2_.refs_0_, ...), custom_call_target="tpu_custom_call" | custom-call | flops 1 | bytes 1 | tf_op jit(solution)/shard_map/pallas_call | solution.py:218
  80.8 2.1 %collective-permute-start.19 = (f32[2,160,256]{2,1,0:T(8,128)S(1)}, f32[2,160,256]{2,1,0:T(8,128)S(1)}, u32[]{:S(2)}, u32[]{:S(2)}) collective-permute-start(f32[2,160,256]{2,1,0:T(8,128)S(1)} %get-tuple-element.52), channel_id=1, source_target_pairs={{0,1},{1,0},{2,3},{3,2},{4,5},{5,4},{6,7},{7,6},{8,9},{9,8},{10,11... | collective-permute-start | bytes 983048 | tf_op jit(solution)/shard_map/ppermute | solution.py:258
  84.5 9.9 %collective-permute-done.15.refs_7_.refs_1_ = f32[2,160,256]{2,1,0:T(8,128)S(1)} collective-permute-done((f32[2,160,256]{2,1,0:T(8,128)S(1)}, f32[2,160,256]{2,1,0:T(8,128)S(1)}, u32[]{:S(2)}, u32[]{:S(2)}) %collective-permute-start.15) | collective-permute-done | bytes 327712 | tf_op jit(solution)/shard_map/ppermute | solution.py:258
  94.4 4.4 %collective-permute-done.22.refs_3_.refs_1_ = f32[2,96,256]{2,1,0:T(8,128)S(1)} collective-permute-done((f32[2,96,256]{2,1,0:T(8,128)S(1)}, f32[2,96,256]{2,1,0:T(8,128)S(1)}, u32[]{:S(2)}, u32[]{:S(2)}) %collective-permute-start.22) | collective-permute-done | bytes 196640 | tf_op jit(solution)/shard_map/ppermute | solution.py:261
  99.8 2.3 %collective-permute-start.23 = (f32[2,128,256]{2,1,0:T(8,128)S(1)}, f32[2,128,256]{2,1,0:T(8,128)S(1)}, u32[]{:S(2)}, u32[]{:S(2)}) collective-permute-start(f32[2,128,256]{2,1,0:T(8,128)S(1)} %get-tuple-element.56), channel_id=1, source_target_pairs={{0,1},{1,0},{2,3},{3,2},{4,5},{5,4},{6,7},{7,6},{8,9},{9,8},{10,11... | collective-permute-start | bytes 786440 | tf_op jit(solution)/shard_map/ppermute | solution.py:258
  102.1 1.3 %collective-permute-start.25 = (f32[2,32,256]{2,1,0:T(8,128)S(1)}, f32[2,32,256]{2,1,0:T(8,128)S(1)}, u32[]{:S(2)}, u32[]{:S(2)}) collective-permute-start(f32[2,32,256]{2,1,0:T(8,128)S(1)} %collective-permute-done.24.refs_2_), channel_id=1, source_target_pairs={{0,2},{1,3},{2,0},{3,1},{4,6},{5,7},{6,4},{7,5},{8,10},{9,11},{10,... | collective-permute-start | bytes 196616 | tf_op jit(solution)/shard_map/ppermute | solution.py:261
  103.3 5.8 %collective-permute-done.25.refs_3_ = f32[2,32,256]{2,1,0:T(8,128)S(1)} collective-permute-done((f32[2,32,256]{2,1,0:T(8,128)S(1)}, f32[2,32,256]{2,1,0:T(8,128)S(1)}, u32[]{:S(2)}, u32[]{:S(2)}) %collective-permute-start.25) | collective-permute-done | bytes 65568 | tf_op jit(solution)/shard_map/ppermute | solution.py:261
  109.1 1.2 %shard_map.72 = (f32[2,64,256]{2,1,0:T(8,128)S(1)}, f32[2,64,256]{2,1,0:T(8,128)S(1)}) custom-call(f32[2,96,256]{2,1,0:T(8,128)S(1)} %get-tuple-element.54.refs_2_.refs_6_.refs_0_, f32[2,96,256]{2,1,0:T(8,128)S(1)} %collective-permute-done.22.refs_3_.refs_1_, f32[2,32,256]{2,1,0:T(8,128)S(1)} %collective-permute-done.24.refs_2_, ...), custom_call_target="tpu_custom_call" | custom-call | flops 1 | bytes 1 | tf_op jit(solution)/shard_map/pallas_call | solution.py:218
  110.3 3.8 %collective-permute-start.26 = (f32[2,64,256]{2,1,0:T(8,128)S(1)}, f32[2,64,256]{2,1,0:T(8,128)S(1)}, u32[]{:S(2)}, u32[]{:S(2)}) collective-permute-start(f32[2,64,256]{2,1,0:T(8,128)S(1)} %get-tuple-element.59), channel_id=1, source_target_pairs={{0,1},{1,0},{2,3},{3,2},{4,5},{5,4},{6,7},{7,6},{8,9},{9,8},{10,11... | collective-permute-start | bytes 393224 | tf_op jit(solution)/shard_map/ppermute | solution.py:258
  114.1 2.9 %collective-permute-done.26.refs_7_ = f32[2,64,256]{2,1,0:T(8,128)S(1)} collective-permute-done((f32[2,64,256]{2,1,0:T(8,128)S(1)}, f32[2,64,256]{2,1,0:T(8,128)S(1)}, u32[]{:S(2)}, u32[]{:S(2)}) %collective-permute-start.26) | collective-permute-done | bytes 131104 | tf_op jit(solution)/shard_map/ppermute | solution.py:258
  117.0 1.5 %shard_map.73 = (f32[2,1,512,256]{3,2,1,0:T(8,128)}, f32[2,1,512,256]{3,2,1,0:T(8,128)}) custom-call(f32[2,160,256]{2,1,0:T(8,128)S(1)} %get-tuple-element.47.refs_2_.refs_0_, f32[2,160,256]{2,1,0:T(8,128)S(1)} %collective-permute-done.15.refs_7_.refs_1_, f32[2,160,256]{2,1,0:T(8,128)S(1)} %get-tuple-element.51.refs_6_.refs_2_, ...), custom_call_target="tpu_custom_call" | custom-call | flops 1 | bytes 1 | tf_op jit(solution)/shard_map/pallas_call | solution.py:218
  (49 shorter events, 8.8 us)
Async XLA Ops:
  0.6 17.0 %copy-start = (f32[2,1,512,256]{3,2,1,0:T(8,128)S(1)}, f32[2,1,512,256]{3,2,1,0:T(8,128)}, u32[]{:S(2)}) copy-start(f32[2,1,512,256]{3,2,1,0:T(8,128)} %refs_8_.1) | copy-start | bytes 3145732
  0.6 17.0 %copy-start.1 = (f32[2,1,512,256]{3,2,1,0:T(8,128)S(1)}, f32[2,1,512,256]{3,2,1,0:T(8,128)}, u32[]{:S(2)}) copy-start(f32[2,1,512,256]{3,2,1,0:T(8,128)} %refs_1_.7) | copy-start | bytes 3145732
  0.6 17.0 %copy-start.2 = (f32[2,1,512,256]{3,2,1,0:T(8,128)S(1)}, f32[2,1,512,256]{3,2,1,0:T(8,128)}, u32[]{:S(2)}) copy-start(f32[2,1,512,256]{3,2,1,0:T(8,128)} %refs_2_.7) | copy-start | bytes 3145732
  3.1 14.5 %collective-permute-start = (f32[3,2,80,256]{3,2,1,0:T(8,128)}, f32[3,2,80,256]{3,2,1,0:T(8,128)}, u32[]{:S(2)}, u32[]{:S(2)}) collective-permute-start(f32[3,2,80,256]{3,2,1,0:T(8,128)} %get-tuple-element.32), channel_id=1, source_target_pairs={{0,16},{8,24},{16,0},{24,8},{1,17},{9,25},{17,1},{25,9},{2,18},{10... | collective-permute-start | bytes 1474568 | tf_op jit(solution)/shard_map/ppermute | solution.py:247
  6.1 15.8 %collective-permute-start.1 = (f32[3,2,80,256]{3,2,1,0:T(8,128)}, f32[3,2,80,256]{3,2,1,0:T(8,128)}, u32[]{:S(2)}, u32[]{:S(2)}) collective-permute-start(f32[3,2,80,256]{3,2,1,0:T(8,128)} %get-tuple-element.31.refs_1_), channel_id=1, source_target_pairs={{0,8},{8,0},{16,24},{24,16},{1,9},{9,1},{17,25},{25,17},{2,10},{10... | collective-permute-start | bytes 1474568 | tf_op jit(solution)/shard_map/ppermute | solution.py:250
  6.1 15.8 %copy-start.3 = (f32[3,2,80,256]{3,2,1,0:T(8,128)S(1)}, f32[3,2,80,256]{3,2,1,0:T(8,128)}, u32[]{:S(2)}) copy-start(f32[3,2,80,256]{3,2,1,0:T(8,128)} %get-tuple-element.31.refs_1_) | copy-start | bytes 1474564
  6.1 15.8 %copy-start.4 = (f32[2,4]{1,0:T(2,128)S(1)}, f32[2,4]{1,0:T(2,128)}, u32[]{:S(2)}) copy-start(f32[2,4]{1,0:T(2,128)} %constant.34.clone.refs_0_) | copy-start | bytes 100
  18.4 3.6 %collective-permute-start.2 = (f32[3,2,80,256]{3,2,1,0:T(8,128)}, f32[3,2,80,256]{3,2,1,0:T(8,128)S(1)}, u32[]{:S(2)}, u32[]{:S(2)}) collective-permute-start(f32[3,2,80,256]{3,2,1,0:T(8,128)} %get-tuple-element.33.refs_2_), channel_id=1, source_target_pairs={{0,8},{8,0},{16,24},{24,16},{1,9},{9,1},{17,25},{25,17},{2,10},{10... | collective-permute-start | bytes 1474568 | tf_op jit(solution)/shard_map/ppermute | solution.py:250
  18.6 18.0 %collective-permute-start.6 = (f32[2,256,256]{2,1,0:T(8,128)S(1)}, f32[2,256,256]{2,1,0:T(8,128)S(1)}, u32[]{:S(2)}, u32[]{:S(2)}) collective-permute-start(f32[2,256,256]{2,1,0:T(8,128)S(1)} %get-tuple-element.61), channel_id=1, source_target_pairs={{0,1},{1,0},{2,3},{3,2},{4,5},{5,4},{6,7},{7,6},{8,9},{9,8},{10,11... | collective-permute-start | bytes 1572872 | tf_op jit(solution)/shard_map/ppermute | solution.py:258
  20.4 16.1 %collective-permute-start.4 = (f32[3,2,80,256]{3,2,1,0:T(8,128)S(1)}, f32[3,2,80,256]{3,2,1,0:T(8,128)S(1)}, u32[]{:S(2)}, u32[]{:S(2)}) collective-permute-start(f32[3,2,80,256]{3,2,1,0:T(8,128)S(1)} %get-tuple-element.36), channel_id=1, source_target_pairs={{0,16},{8,24},{16,0},{24,8},{1,17},{9,25},{17,1},{25,9},{2,18},{10... | collective-permute-start | bytes 1474568 | tf_op jit(solution)/shard_map/ppermute | solution.py:247
  23.9 12.6 %collective-permute-start.3 = (f32[2,80,256]{2,1,0:T(8,128)S(1)}, f32[2,80,256]{2,1,0:T(8,128)S(1)}, u32[]{:S(2)}, u32[]{:S(2)}) collective-permute-start(f32[2,80,256]{2,1,0:T(8,128)S(1)} %get-tuple-element.34.refs_5_.refs_0_), channel_id=1, source_target_pairs={{0,2},{1,3},{2,0},{3,1},{4,6},{5,7},{6,4},{7,5},{8,10},{9,11},{10,... | collective-permute-start | bytes 491528 | tf_op jit(solution)/shard_map/ppermute | solution.py:261
  26.6 10.7 %collective-permute-start.5 = (f32[2,80,256]{2,1,0:T(8,128)S(1)}, f32[2,80,256]{2,1,0:T(8,128)S(1)}, u32[]{:S(2)}, u32[]{:S(2)}) collective-permute-start(f32[2,80,256]{2,1,0:T(8,128)S(1)} %get-tuple-element.37), channel_id=1, source_target_pairs={{0,16},{8,24},{16,0},{24,8},{1,17},{9,25},{17,1},{25,9},{2,18},{10... | collective-permute-start | bytes 491528 | tf_op jit(solution)/shard_map/ppermute | solution.py:247
  27.1 14.1 %collective-permute-start.7 = (f32[3,2,80,256]{3,2,1,0:T(8,128)S(1)}, f32[3,2,80,256]{3,2,1,0:T(8,128)S(1)}, u32[]{:S(2)}, u32[]{:S(2)}) collective-permute-start(f32[3,2,80,256]{3,2,1,0:T(8,128)S(1)} %get-tuple-element.35.refs_1_), channel_id=1, source_target_pairs={{0,8},{8,0},{16,24},{24,16},{1,9},{9,1},{17,25},{25,17},{2,10},{10... | collective-permute-start | bytes 1474568 | tf_op jit(solution)/shard_map/ppermute | solution.py:250
  37.8 3.4 %collective-permute-start.8 = (f32[3,2,80,256]{3,2,1,0:T(8,128)S(1)}, f32[3,2,80,256]{3,2,1,0:T(8,128)S(1)}, u32[]{:S(2)}, u32[]{:S(2)}) collective-permute-start(f32[3,2,80,256]{3,2,1,0:T(8,128)S(1)} %get-tuple-element.38.refs_2_), channel_id=1, source_target_pairs={{0,8},{8,0},{16,24},{24,16},{1,9},{9,1},{17,25},{25,17},{2,10},{10... | collective-permute-start | bytes 1474568 | tf_op jit(solution)/shard_map/ppermute | solution.py:250
  37.9 12.0 %collective-permute-start.11 = (f32[3,2,64,256]{3,2,1,0:T(8,128)S(1)}, f32[3,2,64,256]{3,2,1,0:T(8,128)S(1)}, u32[]{:S(2)}, u32[]{:S(2)}) collective-permute-start(f32[3,2,64,256]{3,2,1,0:T(8,128)S(1)} %get-tuple-element.43), channel_id=1, source_target_pairs={{0,16},{8,24},{16,0},{24,8},{1,17},{9,25},{17,1},{25,9},{2,18},{10... | collective-permute-start | bytes 1179656 | tf_op jit(solution)/shard_map/ppermute | solution.py:247
  39.6 25.9 %collective-permute-start.10 = (f32[2,256,512]{2,1,0:T(8,128)S(1)}, f32[2,256,512]{2,1,0:T(8,128)S(1)}, u32[]{:S(2)}, u32[]{:S(2)}) collective-permute-start(f32[2,256,512]{2,1,0:T(8,128)S(1)} %pad_maximum_fusion.refs_0_), channel_id=1, source_target_pairs={{0,4},{1,5},{2,6},{3,7},{4,0},{5,1},{6,2},{7,3},{8,12},{9,13},{10,... | collective-permute-start | bytes 3145736 | tf_op jit(solution)/shard_map/ppermute | solution.py:258
  42.5 17.5 %collective-permute-start.9 = (f32[2,160,256]{2,1,0:T(8,128)S(1)}, f32[2,160,256]{2,1,0:T(8,128)S(1)}, u32[]{:S(2)}, u32[]{:S(2)}) collective-permute-start(f32[2,160,256]{2,1,0:T(8,128)S(1)} %get-tuple-element.39.refs_2_.refs_5_.refs_0_), channel_id=1, source_target_pairs={{0,2},{1,3},{2,0},{3,1},{4,6},{5,7},{6,4},{7,5},{8,10},{9,11},{10,... | collective-permute-start | bytes 983048 | tf_op jit(solution)/shard_map/ppermute | solution.py:261
  45.2 7.8 %collective-permute-start.12 = (f32[2,80,256]{2,1,0:T(8,128)S(1)}, f32[2,80,256]{2,1,0:T(8,128)S(1)}, u32[]{:S(2)}, u32[]{:S(2)}) collective-permute-start(f32[2,80,256]{2,1,0:T(8,128)S(1)} %get-tuple-element.44), channel_id=1, source_target_pairs={{0,16},{8,24},{16,0},{24,8},{1,17},{9,25},{17,1},{25,9},{2,18},{10... | collective-permute-start | bytes 491528 | tf_op jit(solution)/shard_map/ppermute | solution.py:247
  45.7 14.7 %collective-permute-start.13 = (f32[3,2,64,256]{3,2,1,0:T(8,128)S(1)}, f32[3,2,64,256]{3,2,1,0:T(8,128)S(1)}, u32[]{:S(2)}, u32[]{:S(2)}) collective-permute-start(f32[3,2,64,256]{3,2,1,0:T(8,128)S(1)} %get-tuple-element.42.refs_1_), channel_id=1, source_target_pairs={{0,8},{8,0},{16,24},{24,16},{1,9},{9,1},{17,25},{25,17},{2,10},{10... | collective-permute-start | bytes 1179656 | tf_op jit(solution)/shard_map/ppermute | solution.py:250
  60.3 1.8 %collective-permute-start.14 = (f32[3,2,64,256]{3,2,1,0:T(8,128)S(1)}, f32[3,2,64,256]{3,2,1,0:T(8,128)S(1)}, u32[]{:S(2)}, u32[]{:S(2)}) collective-permute-start(f32[3,2,64,256]{3,2,1,0:T(8,128)S(1)} %get-tuple-element.45.refs_2_), channel_id=1, source_target_pairs={{0,8},{8,0},{16,24},{24,16},{1,9},{9,1},{17,25},{25,17},{2,10},{10... | collective-permute-start | bytes 1179656 | tf_op jit(solution)/shard_map/ppermute | solution.py:250
  63.3 16.3 %collective-permute-start.16 = (f32[2,144,256]{2,1,0:T(8,128)S(1)}, f32[2,144,256]{2,1,0:T(8,128)S(1)}, u32[]{:S(2)}, u32[]{:S(2)}) collective-permute-start(f32[2,144,256]{2,1,0:T(8,128)S(1)} %get-tuple-element.46.refs_6_.refs_2_.refs_0_), channel_id=1, source_target_pairs={{0,2},{1,3},{2,0},{3,1},{4,6},{5,7},{6,4},{7,5},{8,10},{9,11},{10,... | collective-permute-start | bytes 884744 | tf_op jit(solution)/shard_map/ppermute | solution.py:261
  63.4 7.8 %collective-permute-start.17 = (f32[3,2,32,256]{3,2,1,0:T(8,128)S(1)}, f32[3,2,32,256]{3,2,1,0:T(8,128)S(1)}, u32[]{:S(2)}, u32[]{:S(2)}) collective-permute-start(f32[3,2,32,256]{3,2,1,0:T(8,128)S(1)} %get-tuple-element.49), channel_id=1, source_target_pairs={{0,16},{8,24},{16,0},{24,8},{1,17},{9,25},{17,1},{25,9},{2,18},{10... | collective-permute-start | bytes 589832 | tf_op jit(solution)/shard_map/ppermute | solution.py:247
  64.0 9.2 %collective-permute-start.18 = (f32[2,64,256]{2,1,0:T(8,128)S(1)}, f32[2,64,256]{2,1,0:T(8,128)S(1)}, u32[]{:S(2)}, u32[]{:S(2)}) collective-permute-start(f32[2,64,256]{2,1,0:T(8,128)S(1)} %get-tuple-element.50), channel_id=1, source_target_pairs={{0,16},{8,24},{16,0},{24,8},{1,17},{9,25},{17,1},{25,9},{2,18},{10... | collective-permute-start | bytes 393224 | tf_op jit(solution)/shard_map/ppermute | solution.py:247
  66.0 16.9 %collective-permute-start.20 = (f32[3,2,32,256]{3,2,1,0:T(8,128)S(1)}, f32[3,2,32,256]{3,2,1,0:T(8,128)S(1)}, u32[]{:S(2)}, u32[]{:S(2)}) collective-permute-start(f32[3,2,32,256]{3,2,1,0:T(8,128)S(1)} %get-tuple-element.53.refs_1_), channel_id=1, source_target_pairs={{0,8},{8,0},{16,24},{24,16},{1,9},{9,1},{17,25},{25,17},{2,10},{10... | collective-permute-start | bytes 589832 | tf_op jit(solution)/shard_map/ppermute | solution.py:250
  79.6 3.3 %collective-permute-start.21 = (f32[3,2,32,256]{3,2,1,0:T(8,128)S(1)}, f32[3,2,32,256]{3,2,1,0:T(8,128)S(1)}, u32[]{:S(2)}, u32[]{:S(2)}) collective-permute-start(f32[3,2,32,256]{3,2,1,0:T(8,128)S(1)} %shard_map.68.refs_6_.refs_2_), channel_id=1, source_target_pairs={{0,8},{8,0},{16,24},{24,16},{1,9},{9,1},{17,25},{25,17},{2,10},{10... | collective-permute-start | bytes 589832 | tf_op jit(solution)/shard_map/ppermute | solution.py:250
  79.6 14.7 %collective-permute-start.15 = (f32[2,160,256]{2,1,0:T(8,128)S(1)}, f32[2,160,256]{2,1,0:T(8,128)S(1)}, u32[]{:S(2)}, u32[]{:S(2)}) collective-permute-start(f32[2,160,256]{2,1,0:T(8,128)S(1)} %get-tuple-element.48), channel_id=1, source_target_pairs={{0,1},{1,0},{2,3},{3,2},{4,5},{5,4},{6,7},{7,6},{8,9},{9,8},{10,11... | collective-permute-start | bytes 983048 | tf_op jit(solution)/shard_map/ppermute | solution.py:258
  80.8 22.5 %collective-permute-start.19 = (f32[2,160,256]{2,1,0:T(8,128)S(1)}, f32[2,160,256]{2,1,0:T(8,128)S(1)}, u32[]{:S(2)}, u32[]{:S(2)}) collective-permute-start(f32[2,160,256]{2,1,0:T(8,128)S(1)} %get-tuple-element.52), channel_id=1, source_target_pairs={{0,1},{1,0},{2,3},{3,2},{4,5},{5,4},{6,7},{7,6},{8,9},{9,8},{10,11... | collective-permute-start | bytes 983048 | tf_op jit(solution)/shard_map/ppermute | solution.py:258
  83.8 15.0 %collective-permute-start.22 = (f32[2,96,256]{2,1,0:T(8,128)S(1)}, f32[2,96,256]{2,1,0:T(8,128)S(1)}, u32[]{:S(2)}, u32[]{:S(2)}) collective-permute-start(f32[2,96,256]{2,1,0:T(8,128)S(1)} %get-tuple-element.54.refs_2_.refs_6_.refs_0_), channel_id=1, source_target_pairs={{0,2},{1,3},{2,0},{3,1},{4,6},{5,7},{6,4},{7,5},{8,10},{9,11},{10,... | collective-permute-start | bytes 589832 | tf_op jit(solution)/shard_map/ppermute | solution.py:261
  83.9 18.2 %collective-permute-start.24 = (f32[2,32,256]{2,1,0:T(8,128)S(1)}, f32[2,32,256]{2,1,0:T(8,128)S(1)}, u32[]{:S(2)}, u32[]{:S(2)}) collective-permute-start(f32[2,32,256]{2,1,0:T(8,128)S(1)} %get-tuple-element.57), channel_id=1, source_target_pairs={{0,16},{8,24},{16,0},{24,8},{1,17},{9,25},{17,1},{25,9},{2,18},{10... | collective-permute-start | bytes 196616 | tf_op jit(solution)/shard_map/ppermute | solution.py:247
  99.8 17.2 %collective-permute-start.23 = (f32[2,128,256]{2,1,0:T(8,128)S(1)}, f32[2,128,256]{2,1,0:T(8,128)S(1)}, u32[]{:S(2)}, u32[]{:S(2)}) collective-permute-start(f32[2,128,256]{2,1,0:T(8,128)S(1)} %get-tuple-element.56), channel_id=1, source_target_pairs={{0,1},{1,0},{2,3},{3,2},{4,5},{5,4},{6,7},{7,6},{8,9},{9,8},{10,11... | collective-permute-start | bytes 786440 | tf_op jit(solution)/shard_map/ppermute | solution.py:258
  102.1 7.0 %collective-permute-start.25 = (f32[2,32,256]{2,1,0:T(8,128)S(1)}, f32[2,32,256]{2,1,0:T(8,128)S(1)}, u32[]{:S(2)}, u32[]{:S(2)}) collective-permute-start(f32[2,32,256]{2,1,0:T(8,128)S(1)} %collective-permute-done.24.refs_2_), channel_id=1, source_target_pairs={{0,2},{1,3},{2,0},{3,1},{4,6},{5,7},{6,4},{7,5},{8,10},{9,11},{10,... | collective-permute-start | bytes 196616 | tf_op jit(solution)/shard_map/ppermute | solution.py:261
  110.3 6.7 %collective-permute-start.26 = (f32[2,64,256]{2,1,0:T(8,128)S(1)}, f32[2,64,256]{2,1,0:T(8,128)S(1)}, u32[]{:S(2)}, u32[]{:S(2)}) collective-permute-start(f32[2,64,256]{2,1,0:T(8,128)S(1)} %get-tuple-element.59), channel_id=1, source_target_pairs={{0,1},{1,0},{2,3},{3,2},{4,5},{5,4},{6,7},{7,6},{8,9},{9,8},{10,11... | collective-permute-start | bytes 393224 | tf_op jit(solution)/shard_map/ppermute | solution.py:258

commit v8 on v5

--- a/solution.py
+++ b/solution.py
@@ -13,7 +13,7 @@
 WEIGHTS = (5, 10, 11, 6)
 SUBLANES, LANES = 8, 128
 VMEM_LIMIT = 40 * 2**20
-FIRST_LIMIT = 62 * 2**20
+FIRST_LIMIT = 56 * 2**20
 ANYWHERE = pl.BlockSpec(memory_space=pl.ANY)
 IN_VMEM = pl.BlockSpec(memory_space=pltpu.VMEM)
 IN_HBM = pl.BlockSpec(memory_space=pltpu.HBM)
@@ -266,7 +266,7 @@
             functools.partial(pack_kernel, chips, bases[at], step, count),
             [f32(value.shape) for value in passed] + [f32((3, 2, step, cols))] * chips,
             [IN_HBM] * 3 + [ANYWHERE] * count,
-            [ANYWHERE] * (count + chips),
+            [ANYWHERE] * count + [ANYWHERE if at else IN_VMEM] * chips,
             (*inputs, *passed),
             [pltpu.SemaphoreType.DMA((3 * chips,))],
             after,
@@ -334,7 +334,7 @@
                 pieces.append(fresh)
                 sent.append(forward(fresh))
             else:
-                across = gate(across, (*arrived, *last))
+                across = gate(across, (*arrived, *last, *(results[-2][1:] if len(results) > 1 else ())))
             gates = panels[1:group]
             if at == 1:
                 right = call(
@@ -358,7 +358,8 @@
                 arrived += tuple(panels[group:])
             last = sigmas[:1]
         if at >= 1:
-            gates = (*last, *(returned if at + 1 == len(sizes) else ()), *(results[-1][1:] if results else ()))
+            before = results[-2][1:] if len(results) > 1 else ()
+            gates = (*last, *(returned if at + 1 == len(sizes) else ()), *before)
             results.append(product(at - 1, lefts[at - 1], gates))
             last, returned = results[-1][:1], ()
 

time: 129 us -> 112 us (0.87)
  Pallas kernels: 29.4 us -> 15.5 us
  waiting for transfers between devices: 66 us -> 62.9 us
    ppermute x7, waiting for transfers between devices: 34.1 us -> 17.8 us  [to_panel(): return lax.ppermute(value, ('tr', 'tc'), moves)]
    pallas_call x15, Pallas kernels: 29.4 us -> 15.5 us  [call(): pl.pallas_call(ordered, out_shape=out_shapes, in_specs=in_specs + [ANYWHE...]
    ppermute x8, waiting for transfers between devices: 26.2 us -> 39.7 us  [to_half(): lax.ppermute(value, 'tc', [(j, (j + group * gap) % col_parts) for j in ra...]
    ppermute x8, starting transfers between devices: 13.6 us -> 11.6 us  [to_half(): lax.ppermute(value, 'tc', [(j, (j + group * gap) % col_parts) for j in ra...]
    ppermute x7, starting transfers between devices: 9.12 us -> 10.7 us  [to_panel(): return lax.ppermute(value, ('tr', 'tc'), moves)]
  transfers between devices with their start and end apart: 31 -> 31, of which waited for: 15 -> 13; matrix products, arithmetic and copies ran while one was open for 0% -> 0% of each run, Pallas kernels for 7% -> 11%
where the time goes in v8:
time: 112 us; the launch traced here: 111 us
  waiting for transfers between devices  62.9 us (56%)
  starting transfers between devices  32.1 us (29%)
  Pallas kernels  15.5 us (14%)
    ppermute x8, waiting for transfers between devices, to_half(): lax.ppermute(value, 'tc', [(j, (j + group * gap) % col_parts) for j in ra...  39.7 us
    ppermute x7, waiting for transfers between devices, to_panel(): return lax.ppermute(value, ('tr', 'tc'), moves)  17.8 us
    pallas_call x15, Pallas kernels, call(): pl.pallas_call(ordered, out_shape=out_shapes, in_specs=in_specs + [ANYWHE...  15.5 us
    ppermute x8, starting transfers between devices, to_half(): lax.ppermute(value, 'tc', [(j, (j + group * gap) % col_parts) for j in ra...  11.6 us
    ppermute x7, starting transfers between devices, to_panel(): return lax.ppermute(value, ('tr', 'tc'), moves)  10.7 us
    ppermute x8, starting transfers between devices, to_chip(): return lax.ppermute(value, 'ka', moves)  9.05 us
    ppermute x8, waiting for transfers between devices, to_core(): lax.ppermute(value, 'ka', [(s, s + 1 - 2 * (s % CORES)) for s in range(mo...  3.23 us
  transfers between devices with their start and end apart: 31, of which 13 were waited for; matrix products, arithmetic and copies ran while one was open for 0% of the time, Pallas kernels for 11%

profile of v8, /device:TPU:0, one launch (start us, length us, event | category | flops | bytes accessed | tf_op | source)
XLA Modules:
  0.0 111.5 jit_solution(6503775948689887660)
XLA Ops:
  0.7 2.1 %shard_map.59 = (f32[3,2,40,256]{3,2,1,0:T(8,128)}, f32[3,2,40,256]{3,2,1,0:T(8,128)}) custom-call(f32[2,1,512,256]{3,2,1,0:T(8,128)} %refs_8_.1, f32[2,1,512,256]{3,2,1,0:T(8,128)} %refs_1_.7, f32[2,1,512,256]{3,2,1,0:T(8,128)} %refs_2_.7), custom_call_target="tpu_custom_call" | custom-call | flops 1 | bytes 1 | tf_op jit(solution)/shard_map/pallas_call | solution.py:218
  2.7 3.0 %collective-permute-start = (f32[3,2,40,256]{3,2,1,0:T(8,128)}, f32[3,2,40,256]{3,2,1,0:T(8,128)S(1)}, u32[]{:S(2)}, u32[]{:S(2)}) collective-permute-start(f32[3,2,40,256]{3,2,1,0:T(8,128)} %get-tuple-element.32), channel_id=1, source_target_pairs={{0,16},{8,24},{16,0},{24,8},{1,17},{9,25},{17,1},{25,9},{2,18},{10... | collective-permute-start | bytes 737288 | tf_op jit(solution)/shard_map/ppermute | solution.py:247
  5.8 1.6 %collective-permute-start.3 = (f32[2,256,256]{2,1,0:T(8,128)S(1)}, f32[2,256,256]{2,1,0:T(8,128)S(1)}, u32[]{:S(2)}, u32[]{:S(2)}) collective-permute-start(f32[2,256,256]{2,1,0:T(8,128)S(1)} %get-tuple-element.61), channel_id=1, source_target_pairs={{0,1},{1,0},{2,3},{3,2},{4,5},{5,4},{6,7},{7,6},{8,9},{9,8},{10,11... | collective-permute-start | bytes 1572872 | tf_op jit(solution)/shard_map/ppermute | solution.py:258
  7.5 1.5 %collective-permute-start.7 = (f32[2,256,256]{2,1,0:T(8,128)S(1)}, f32[2,256,256]{2,1,0:T(8,128)S(1)}, u32[]{:S(2)}, u32[]{:S(2)}) collective-permute-start(f32[2,256,256]{2,1,0:T(8,128)S(1)} %get-tuple-element.60.refs_0_), channel_id=1, source_target_pairs={{0,4},{1,5},{2,6},{3,7},{4,0},{5,1},{6,2},{7,3},{8,12},{9,13},{10,... | collective-permute-start | bytes 1572872 | tf_op jit(solution)/shard_map/ppermute | solution.py:258
  9.7 2.2 %collective-permute-done.refs_3_ = f32[3,2,40,256]{3,2,1,0:T(8,128)S(1)} collective-permute-done((f32[3,2,40,256]{3,2,1,0:T(8,128)}, f32[3,2,40,256]{3,2,1,0:T(8,128)S(1)}, u32[]{:S(2)}, u32[]{:S(2)}) %collective-permute-start) | collective-permute-done | bytes 245792 | tf_op jit(solution)/shard_map/ppermute | solution.py:247
  12.6 1.8 %collective-permute-start.9 = (f32[3,2,80,256]{3,2,1,0:T(8,128)S(1)}, f32[3,2,80,256]{3,2,1,0:T(8,128)S(1)}, u32[]{:S(2)}, u32[]{:S(2)}) collective-permute-start(f32[3,2,80,256]{3,2,1,0:T(8,128)S(1)} %get-tuple-element.36), channel_id=1, source_target_pairs={{0,16},{8,24},{16,0},{24,8},{1,17},{9,25},{17,1},{25,9},{2,18},{10... | collective-permute-start | bytes 1474568 | tf_op jit(solution)/shard_map/ppermute | solution.py:247
  14.4 1.5 %collective-permute-done.2.refs_4_ = f32[3,2,40,256]{3,2,1,0:T(8,128)S(1)} collective-permute-done((f32[3,2,40,256]{3,2,1,0:T(8,128)S(1)}, f32[3,2,40,256]{3,2,1,0:T(8,128)S(1)}, u32[]{:S(2)}, u32[]{:S(2)}) %collective-permute-start.2) | collective-permute-done | bytes 245792 | tf_op jit(solution)/shard_map/ppermute | solution.py:250
  15.9 4.8 %collective-permute-done.3.refs_5_.refs_1_ = f32[2,256,256]{2,1,0:T(8,128)S(1)} collective-permute-done((f32[2,256,256]{2,1,0:T(8,128)S(1)}, f32[2,256,256]{2,1,0:T(8,128)S(1)}, u32[]{:S(2)}, u32[]{:S(2)}) %collective-permute-start.3) | collective-permute-done | bytes 524320 | tf_op jit(solution)/shard_map/ppermute | solution.py:258
  21.7 2.7 %collective-permute-start.4 = (f32[2,40,256]{2,1,0:T(8,128)S(1)}, f32[2,40,256]{2,1,0:T(8,128)S(1)}, u32[]{:S(2)}, u32[]{:S(2)}) collective-permute-start(f32[2,40,256]{2,1,0:T(8,128)S(1)} %get-tuple-element.34.refs_8_.refs_0_), channel_id=1, source_target_pairs={{0,2},{1,3},{2,0},{3,1},{4,6},{5,7},{6,4},{7,5},{8,10},{9,11},{10,... | collective-permute-start | bytes 245768 | tf_op jit(solution)/shard_map/ppermute | solution.py:261
  24.9 7.2 %collective-permute-done.7.refs_6_.refs_2_ = f32[2,256,256]{2,1,0:T(8,128)S(1)} collective-permute-done((f32[2,256,256]{2,1,0:T(8,128)S(1)}, f32[2,256,256]{2,1,0:T(8,128)S(1)}, u32[]{:S(2)}, u32[]{:S(2)}) %collective-permute-start.7) | collective-permute-done | bytes 524320 | tf_op jit(solution)/shard_map/ppermute | solution.py:258
  32.1 1.2 %collective-permute-done.8.refs_7_.refs_3_ = f32[2,256,256]{2,1,0:T(8,128)S(1)} collective-permute-done((f32[2,256,256]{2,1,0:T(8,128)S(1)}, f32[2,256,256]{2,1,0:T(8,128)S(1)}, u32[]{:S(2)}, u32[]{:S(2)}) %collective-permute-start.8) | collective-permute-done | bytes 524320 | tf_op jit(solution)/shard_map/ppermute | solution.py:258
  36.1 1.3 %shard_map.64 = (f32[2,80,256]{2,1,0:T(8,128)S(1)}, f32[2,80,256]{2,1,0:T(8,128)S(1)}) custom-call(f32[2,4]{1,0:T(2,128)S(1)} %copy-done.4, f32[3,2,80,256]{3,2,1,0:T(8,128)S(1)} %get-tuple-element.40.refs_1_, f32[3,2,80,256]{3,2,1,0:T(8,128)S(1)} %get-tuple-element.37.refs_4_.refs_2_, f32[3,2,80,256]{3,2,1,0:T(8,128)S(1)} %collective-permute-done.10.refs_3_, ...), custom_call_target="tpu_custom_call" | custom-call | flops 1 | bytes 1 | tf_op jit(solution)/shard_map/pallas_call | solution.py:218
  37.4 2.5 %collective-permute-start.13 = (f32[2,80,256]{2,1,0:T(8,128)S(1)}, f32[2,80,256]{2,1,0:T(8,128)S(1)}, u32[]{:S(2)}, u32[]{:S(2)}) collective-permute-start(f32[2,80,256]{2,1,0:T(8,128)S(1)} %get-tuple-element.41.refs_6_.refs_0_), channel_id=1, source_target_pairs={{0,2},{1,3},{2,0},{3,1},{4,6},{5,7},{6,4},{7,5},{8,10},{9,11},{10,... | collective-permute-start | bytes 491528 | tf_op jit(solution)/shard_map/ppermute | solution.py:261
  39.9 1.1 %collective-permute-start.14 = (f32[2,80,256]{2,1,0:T(8,128)S(1)}, f32[2,80,256]{2,1,0:T(8,128)S(1)}, u32[]{:S(2)}, u32[]{:S(2)}) collective-permute-start(f32[2,80,256]{2,1,0:T(8,128)S(1)} %get-tuple-element.44), channel_id=1, source_target_pairs={{0,16},{8,24},{16,0},{24,8},{1,17},{9,25},{17,1},{25,9},{2,18},{10... | collective-permute-start | bytes 491528 | tf_op jit(solution)/shard_map/ppermute | solution.py:247
  41.2 10.5 %collective-permute-done.6.refs_3_ = f32[2,40,256]{2,1,0:T(8,128)S(1)} collective-permute-done((f32[2,40,256]{2,1,0:T(8,128)S(1)}, f32[2,40,256]{2,1,0:T(8,128)S(1)}, u32[]{:S(2)}, u32[]{:S(2)}) %collective-permute-start.6) | collective-permute-done | bytes 81952 | tf_op jit(solution)/shard_map/ppermute | solution.py:261
  51.7 1.2 %shard_map.65 = (f32[2,80,256]{2,1,0:T(8,128)S(1)}, f32[2,80,256]{2,1,0:T(8,128)S(1)}) custom-call(f32[2,40,256]{2,1,0:T(8,128)S(1)} %get-tuple-element.34.refs_8_.refs_0_, f32[2,40,256]{2,1,0:T(8,128)S(1)} %collective-permute-done.4.refs_5_.refs_1_, f32[2,40,256]{2,1,0:T(8,128)S(1)} %collective-permute-done.5.refs_4_.refs_2_, ...), custom_call_target="tpu_custom_call" | custom-call | flops 1 | bytes 1 | tf_op jit(solution)/shard_map/pallas_call | solution.py:218
  55.4 1.3 %shard_map.67 = (f32[2,88,256]{2,1,0:T(8,128)S(1)}, f32[2,88,256]{2,1,0:T(8,128)S(1)}) custom-call(f32[2,4]{1,0:T(2,128)S(1)} %copy-done.4, f32[3,2,88,256]{3,2,1,0:T(8,128)S(1)} %get-tuple-element.45.refs_1_, f32[3,2,88,256]{3,2,1,0:T(8,128)S(1)} %get-tuple-element.47.refs_2_, f32[3,2,88,256]{3,2,1,0:T(8,128)S(1)} %collective-permute-done.17.refs_3_, ...), custom_call_target="tpu_custom_call" | custom-call | flops 1 | bytes 1 | tf_op jit(solution)/shard_map/pallas_call | solution.py:218
  56.7 1.9 %collective-permute-start.20 = (f32[2,88,256]{2,1,0:T(8,128)S(1)}, f32[2,88,256]{2,1,0:T(8,128)S(1)}, u32[]{:S(2)}, u32[]{:S(2)}) collective-permute-start(f32[2,88,256]{2,1,0:T(8,128)S(1)} %get-tuple-element.48.refs_6_.refs_0_), channel_id=1, source_target_pairs={{0,2},{1,3},{2,0},{3,1},{4,6},{5,7},{6,4},{7,5},{8,10},{9,11},{10,... | collective-permute-start | bytes 540680 | tf_op jit(solution)/shard_map/ppermute | solution.py:261
  59.1 1.3 %collective-permute-start.15 = (f32[2,80,256]{2,1,0:T(8,128)S(1)}, f32[2,80,256]{2,1,0:T(8,128)S(1)}, u32[]{:S(2)}, u32[]{:S(2)}) collective-permute-start(f32[2,80,256]{2,1,0:T(8,128)S(1)} %collective-permute-done.14.refs_4_.refs_2_), channel_id=1, source_target_pairs={{0,2},{1,3},{2,0},{3,1},{4,6},{5,7},{6,4},{7,5},{8,10},{9,11},{10,... | collective-permute-start | bytes 491528 | tf_op jit(solution)/shard_map/ppermute | solution.py:261
  61.5 13.6 %collective-permute-done.15.refs_3_ = f32[2,80,256]{2,1,0:T(8,128)S(1)} collective-permute-done((f32[2,80,256]{2,1,0:T(8,128)S(1)}, f32[2,80,256]{2,1,0:T(8,128)S(1)}, u32[]{:S(2)}, u32[]{:S(2)}) %collective-permute-start.15) | collective-permute-done | bytes 163872 | tf_op jit(solution)/shard_map/ppermute | solution.py:261
  75.1 1.2 %shard_map.68 = (f32[2,160,256]{2,1,0:T(8,128)S(1)}, f32[2,160,256]{2,1,0:T(8,128)S(1)}) custom-call(f32[2,80,256]{2,1,0:T(8,128)S(1)} %get-tuple-element.41.refs_6_.refs_0_, f32[2,80,256]{2,1,0:T(8,128)S(1)} %collective-permute-done.13.refs_5_.refs_1_, f32[2,80,256]{2,1,0:T(8,128)S(1)} %collective-permute-done.14.refs_4_.refs_2_, ...), custom_call_target="tpu_custom_call" | custom-call | flops 1 | bytes 1 | tf_op jit(solution)/shard_map/pallas_call | solution.py:218
  77.0 3.3 %collective-permute-start.19 = (f32[2,160,256]{2,1,0:T(8,128)S(1)}, f32[2,160,256]{2,1,0:T(8,128)S(1)}, u32[]{:S(2)}, u32[]{:S(2)}) collective-permute-start(f32[2,160,256]{2,1,0:T(8,128)S(1)} %get-tuple-element.50), channel_id=1, source_target_pairs={{0,1},{1,0},{2,3},{3,2},{4,5},{5,4},{6,7},{7,6},{8,9},{9,8},{10,11... | collective-permute-start | bytes 983048 | tf_op jit(solution)/shard_map/ppermute | solution.py:258
  81.9 6.5 %collective-permute-done.22.refs_3_ = f32[2,88,256]{2,1,0:T(8,128)S(1)} collective-permute-done((f32[2,88,256]{2,1,0:T(8,128)S(1)}, f32[2,88,256]{2,1,0:T(8,128)S(1)}, u32[]{:S(2)}, u32[]{:S(2)}) %collective-permute-start.22) | collective-permute-done | bytes 180256 | tf_op jit(solution)/shard_map/ppermute | solution.py:261
  88.4 1.3 %shard_map.71 = (f32[2,176,256]{2,1,0:T(8,128)S(1)}, f32[2,176,256]{2,1,0:T(8,128)S(1)}) custom-call(f32[2,88,256]{2,1,0:T(8,128)S(1)} %get-tuple-element.48.refs_6_.refs_0_, f32[2,88,256]{2,1,0:T(8,128)S(1)} %collective-permute-done.20.refs_2_.refs_1_, f32[2,88,256]{2,1,0:T(8,128)S(1)} %collective-permute-done.21.refs_1_.refs_2_, ...), custom_call_target="tpu_custom_call" | custom-call | flops 1 | bytes 1 | tf_op jit(solution)/shard_map/pallas_call | solution.py:218
  89.7 1.7 %collective-permute-start.28 = (f32[2,48,256]{2,1,0:T(8,128)S(1)}, f32[2,48,256]{2,1,0:T(8,128)S(1)}, u32[]{:S(2)}, u32[]{:S(2)}) collective-permute-start(f32[2,48,256]{2,1,0:T(8,128)S(1)} %get-tuple-element.54.refs_6_.refs_0_), channel_id=1, source_target_pairs={{0,2},{1,3},{2,0},{3,1},{4,6},{5,7},{6,4},{7,5},{8,10},{9,11},{10,... | collective-permute-start | bytes 294920 | tf_op jit(solution)/shard_map/ppermute | solution.py:261
  91.5 1.3 %collective-permute-start.29 = (f32[2,48,256]{2,1,0:T(8,128)S(1)}, f32[2,48,256]{2,1,0:T(8,128)S(1)}, u32[]{:S(2)}, u32[]{:S(2)}) collective-permute-start(f32[2,48,256]{2,1,0:T(8,128)S(1)} %collective-permute-done.26.refs_7_.refs_2_), channel_id=1, source_target_pairs={{0,2},{1,3},{2,0},{3,1},{4,6},{5,7},{6,4},{7,5},{8,10},{9,11},{10,... | collective-permute-start | bytes 294920 | tf_op jit(solution)/shard_map/ppermute | solution.py:261
  92.7 7.9 %collective-permute-done.28.refs_1_ = f32[2,48,256]{2,1,0:T(8,128)S(1)} collective-permute-done((f32[2,48,256]{2,1,0:T(8,128)S(1)}, f32[2,48,256]{2,1,0:T(8,128)S(1)}, u32[]{:S(2)}, u32[]{:S(2)}) %collective-permute-start.28) | collective-permute-done | bytes 98336 | tf_op jit(solution)/shard_map/ppermute | solution.py:261
  100.6 1.3 %collective-permute-done.29.refs_3_ = f32[2,48,256]{2,1,0:T(8,128)S(1)} collective-permute-done((f32[2,48,256]{2,1,0:T(8,128)S(1)}, f32[2,48,256]{2,1,0:T(8,128)S(1)}, u32[]{:S(2)}, u32[]{:S(2)}) %collective-permute-start.29) | collective-permute-done | bytes 98336 | tf_op jit(solution)/shard_map/ppermute | solution.py:261
  101.9 1.1 %shard_map.72 = (f32[2,96,256]{2,1,0:T(8,128)S(1)}, f32[2,96,256]{2,1,0:T(8,128)S(1)}) custom-call(f32[2,48,256]{2,1,0:T(8,128)S(1)} %get-tuple-element.54.refs_6_.refs_0_, f32[2,48,256]{2,1,0:T(8,128)S(1)} %collective-permute-done.28.refs_1_, f32[2,48,256]{2,1,0:T(8,128)S(1)} %collective-permute-done.26.refs_7_.refs_2_, ...), custom_call_target="tpu_custom_call" | custom-call | flops 1 | bytes 1 | tf_op jit(solution)/shard_map/pallas_call | solution.py:218
  103.0 2.4 %collective-permute-start.30 = (f32[2,96,256]{2,1,0:T(8,128)S(1)}, f32[2,96,256]{2,1,0:T(8,128)S(1)}, u32[]{:S(2)}, u32[]{:S(2)}) collective-permute-start(f32[2,96,256]{2,1,0:T(8,128)S(1)} %get-tuple-element.59), channel_id=1, source_target_pairs={{0,1},{1,0},{2,3},{3,2},{4,5},{5,4},{6,7},{7,6},{8,9},{9,8},{10,11... | collective-permute-start | bytes 589832 | tf_op jit(solution)/shard_map/ppermute | solution.py:258
  105.4 4.5 %collective-permute-done.30.refs_7_ = f32[2,96,256]{2,1,0:T(8,128)S(1)} collective-permute-done((f32[2,96,256]{2,1,0:T(8,128)S(1)}, f32[2,96,256]{2,1,0:T(8,128)S(1)}, u32[]{:S(2)}, u32[]{:S(2)}) %collective-permute-start.30) | collective-permute-done | bytes 196640 | tf_op jit(solution)/shard_map/ppermute | solution.py:258
  109.9 1.5 %shard_map.73 = (f32[2,1,512,256]{3,2,1,0:T(8,128)}, f32[2,1,512,256]{3,2,1,0:T(8,128)}) custom-call(f32[2,80,256]{2,1,0:T(8,128)S(1)} %get-tuple-element.42.refs_6_.refs_0_, f32[2,80,256]{2,1,0:T(8,128)S(1)} %collective-permute-done.12.refs_4_.refs_8_.refs_1_, f32[2,160,256]{2,1,0:T(8,128)S(1)} %get-tuple-element.49.refs_3_.refs_2_, ...), custom_call_target="tpu_custom_call" | custom-call | flops 1 | bytes 1 | tf_op jit(solution)/shard_map/pallas_call | solution.py:218
  (56 shorter events, 12.1 us)
Async XLA Ops:
  2.7 9.2 %collective-permute-start = (f32[3,2,40,256]{3,2,1,0:T(8,128)}, f32[3,2,40,256]{3,2,1,0:T(8,128)S(1)}, u32[]{:S(2)}, u32[]{:S(2)}) collective-permute-start(f32[3,2,40,256]{3,2,1,0:T(8,128)} %get-tuple-element.32), channel_id=1, source_target_pairs={{0,16},{8,24},{16,0},{24,8},{1,17},{9,25},{17,1},{25,9},{2,18},{10... | collective-permute-start | bytes 737288 | tf_op jit(solution)/shard_map/ppermute | solution.py:247
  5.8 14.9 %copy-start.4 = (f32[2,4]{1,0:T(2,128)S(1)}, f32[2,4]{1,0:T(2,128)}, u32[]{:S(2)}) copy-start(f32[2,4]{1,0:T(2,128)} %constant.42.clone.refs_0_) | copy-start | bytes 100
  5.8 14.9 %collective-permute-start.3 = (f32[2,256,256]{2,1,0:T(8,128)S(1)}, f32[2,256,256]{2,1,0:T(8,128)S(1)}, u32[]{:S(2)}, u32[]{:S(2)}) collective-permute-start(f32[2,256,256]{2,1,0:T(8,128)S(1)} %get-tuple-element.61), channel_id=1, source_target_pairs={{0,1},{1,0},{2,3},{3,2},{4,5},{5,4},{6,7},{7,6},{8,9},{9,8},{10,11... | collective-permute-start | bytes 1572872 | tf_op jit(solution)/shard_map/ppermute | solution.py:258
  7.5 6.9 %collective-permute-start.1 = (f32[3,2,40,256]{3,2,1,0:T(8,128)S(1)}, f32[3,2,40,256]{3,2,1,0:T(8,128)S(1)}, u32[]{:S(2)}, u32[]{:S(2)}) collective-permute-start(f32[3,2,40,256]{3,2,1,0:T(8,128)S(1)} %copy-done.3), channel_id=1, source_target_pairs={{0,8},{8,0},{16,24},{24,16},{1,9},{9,1},{17,25},{25,17},{2,10},{10... | collective-permute-start | bytes 737288 | tf_op jit(solution)/shard_map/ppermute | solution.py:250
  7.5 24.6 %collective-permute-start.7 = (f32[2,256,256]{2,1,0:T(8,128)S(1)}, f32[2,256,256]{2,1,0:T(8,128)S(1)}, u32[]{:S(2)}, u32[]{:S(2)}) collective-permute-start(f32[2,256,256]{2,1,0:T(8,128)S(1)} %get-tuple-element.60.refs_0_), channel_id=1, source_target_pairs={{0,4},{1,5},{2,6},{3,7},{4,0},{5,1},{6,2},{7,3},{8,12},{9,13},{10,... | collective-permute-start | bytes 1572872 | tf_op jit(solution)/shard_map/ppermute | solution.py:258
  9.0 24.3 %collective-permute-start.8 = (f32[2,256,256]{2,1,0:T(8,128)S(1)}, f32[2,256,256]{2,1,0:T(8,128)S(1)}, u32[]{:S(2)}, u32[]{:S(2)}) collective-permute-start(f32[2,256,256]{2,1,0:T(8,128)S(1)} %get-tuple-element.61), channel_id=1, source_target_pairs={{0,5},{1,4},{2,7},{3,6},{4,1},{5,0},{6,3},{7,2},{8,13},{9,12},{10,... | collective-permute-start | bytes 1572872 | tf_op jit(solution)/shard_map/ppermute | solution.py:258
  12.6 20.7 %collective-permute-start.9 = (f32[3,2,80,256]{3,2,1,0:T(8,128)S(1)}, f32[3,2,80,256]{3,2,1,0:T(8,128)S(1)}, u32[]{:S(2)}, u32[]{:S(2)}) collective-permute-start(f32[3,2,80,256]{3,2,1,0:T(8,128)S(1)} %get-tuple-element.36), channel_id=1, source_target_pairs={{0,16},{8,24},{16,0},{24,8},{1,17},{9,25},{17,1},{25,9},{2,18},{10... | collective-permute-start | bytes 1474568 | tf_op jit(solution)/shard_map/ppermute | solution.py:247
  14.4 1.5 %collective-permute-start.2 = (f32[3,2,40,256]{3,2,1,0:T(8,128)S(1)}, f32[3,2,40,256]{3,2,1,0:T(8,128)S(1)}, u32[]{:S(2)}, u32[]{:S(2)}) collective-permute-start(f32[3,2,40,256]{3,2,1,0:T(8,128)S(1)} %get-tuple-element.33.refs_2_), channel_id=1, source_target_pairs={{0,8},{8,0},{16,24},{24,16},{1,9},{9,1},{17,25},{25,17},{2,10},{10... | collective-permute-start | bytes 737288 | tf_op jit(solution)/shard_map/ppermute | solution.py:250
  21.7 11.7 %collective-permute-start.4 = (f32[2,40,256]{2,1,0:T(8,128)S(1)}, f32[2,40,256]{2,1,0:T(8,128)S(1)}, u32[]{:S(2)}, u32[]{:S(2)}) collective-permute-start(f32[2,40,256]{2,1,0:T(8,128)S(1)} %get-tuple-element.34.refs_8_.refs_0_), channel_id=1, source_target_pairs={{0,2},{1,3},{2,0},{3,1},{4,6},{5,7},{6,4},{7,5},{8,10},{9,11},{10,... | collective-permute-start | bytes 245768 | tf_op jit(solution)/shard_map/ppermute | solution.py:261
  24.3 9.0 %collective-permute-start.5 = (f32[2,40,256]{2,1,0:T(8,128)S(1)}, f32[2,40,256]{2,1,0:T(8,128)S(1)}, u32[]{:S(2)}, u32[]{:S(2)}) collective-permute-start(f32[2,40,256]{2,1,0:T(8,128)S(1)} %get-tuple-element.35), channel_id=1, source_target_pairs={{0,16},{8,24},{16,0},{24,8},{1,17},{9,25},{17,1},{25,9},{2,18},{10... | collective-permute-start | bytes 245768 | tf_op jit(solution)/shard_map/ppermute | solution.py:247
  32.1 3.3 %collective-permute-start.10 = (f32[3,2,80,256]{3,2,1,0:T(8,128)S(1)}, f32[3,2,80,256]{3,2,1,0:T(8,128)S(1)}, u32[]{:S(2)}, u32[]{:S(2)}) collective-permute-start(f32[3,2,80,256]{3,2,1,0:T(8,128)S(1)} %get-tuple-element.40.refs_1_), channel_id=1, source_target_pairs={{0,8},{8,0},{16,24},{24,16},{1,9},{9,1},{17,25},{25,17},{2,10},{10... | collective-permute-start | bytes 1474568 | tf_op jit(solution)/shard_map/ppermute | solution.py:250
  34.1 1.9 %collective-permute-start.11 = (f32[3,2,80,256]{3,2,1,0:T(8,128)S(1)}, f32[3,2,80,256]{3,2,1,0:T(8,128)S(1)}, u32[]{:S(2)}, u32[]{:S(2)}) collective-permute-start(f32[3,2,80,256]{3,2,1,0:T(8,128)S(1)} %get-tuple-element.37.refs_4_.refs_2_), channel_id=1, source_target_pairs={{0,8},{8,0},{16,24},{24,16},{1,9},{9,1},{17,25},{25,17},{2,10},{10... | collective-permute-start | bytes 1474568 | tf_op jit(solution)/shard_map/ppermute | solution.py:250
  34.2 18.7 %collective-permute-start.16 = (f32[3,2,88,256]{3,2,1,0:T(8,128)S(1)}, f32[3,2,88,256]{3,2,1,0:T(8,128)S(1)}, u32[]{:S(2)}, u32[]{:S(2)}) collective-permute-start(f32[3,2,88,256]{3,2,1,0:T(8,128)S(1)} %get-tuple-element.46), channel_id=1, source_target_pairs={{0,16},{8,24},{16,0},{24,8},{1,17},{9,25},{17,1},{25,9},{2,18},{10... | collective-permute-start | bytes 1622024 | tf_op jit(solution)/shard_map/ppermute | solution.py:247
  37.4 15.5 %collective-permute-start.13 = (f32[2,80,256]{2,1,0:T(8,128)S(1)}, f32[2,80,256]{2,1,0:T(8,128)S(1)}, u32[]{:S(2)}, u32[]{:S(2)}) collective-permute-start(f32[2,80,256]{2,1,0:T(8,128)S(1)} %get-tuple-element.41.refs_6_.refs_0_), channel_id=1, source_target_pairs={{0,2},{1,3},{2,0},{3,1},{4,6},{5,7},{6,4},{7,5},{8,10},{9,11},{10,... | collective-permute-start | bytes 491528 | tf_op jit(solution)/shard_map/ppermute | solution.py:261
  39.9 13.0 %collective-permute-start.14 = (f32[2,80,256]{2,1,0:T(8,128)S(1)}, f32[2,80,256]{2,1,0:T(8,128)S(1)}, u32[]{:S(2)}, u32[]{:S(2)}) collective-permute-start(f32[2,80,256]{2,1,0:T(8,128)S(1)} %get-tuple-element.44), channel_id=1, source_target_pairs={{0,16},{8,24},{16,0},{24,8},{1,17},{9,25},{17,1},{25,9},{2,18},{10... | collective-permute-start | bytes 491528 | tf_op jit(solution)/shard_map/ppermute | solution.py:247
  41.0 10.6 %collective-permute-start.6 = (f32[2,40,256]{2,1,0:T(8,128)S(1)}, f32[2,40,256]{2,1,0:T(8,128)S(1)}, u32[]{:S(2)}, u32[]{:S(2)}) collective-permute-start(f32[2,40,256]{2,1,0:T(8,128)S(1)} %collective-permute-done.5.refs_4_.refs_2_), channel_id=1, source_target_pairs={{0,2},{1,3},{2,0},{3,1},{4,6},{5,7},{6,4},{7,5},{8,10},{9,11},{10,... | collective-permute-start | bytes 245768 | tf_op jit(solution)/shard_map/ppermute | solution.py:261
  41.2 13.1 %collective-permute-start.17 = (f32[3,2,88,256]{3,2,1,0:T(8,128)S(1)}, f32[3,2,88,256]{3,2,1,0:T(8,128)S(1)}, u32[]{:S(2)}, u32[]{:S(2)}) collective-permute-start(f32[3,2,88,256]{3,2,1,0:T(8,128)S(1)} %get-tuple-element.45.refs_1_), channel_id=1, source_target_pairs={{0,8},{8,0},{16,24},{24,16},{1,9},{9,1},{17,25},{25,17},{2,10},{10... | collective-permute-start | bytes 1622024 | tf_op jit(solution)/shard_map/ppermute | solution.py:250
  53.4 2.0 %collective-permute-start.18 = (f32[3,2,88,256]{3,2,1,0:T(8,128)S(1)}, f32[3,2,88,256]{3,2,1,0:T(8,128)S(1)}, u32[]{:S(2)}, u32[]{:S(2)}) collective-permute-start(f32[3,2,88,256]{3,2,1,0:T(8,128)S(1)} %get-tuple-element.47.refs_2_), channel_id=1, source_target_pairs={{0,8},{8,0},{16,24},{24,16},{1,9},{9,1},{17,25},{25,17},{2,10},{10... | collective-permute-start | bytes 1622024 | tf_op jit(solution)/shard_map/ppermute | solution.py:250
  53.5 22.9 %collective-permute-start.23 = (f32[3,2,48,256]{3,2,1,0:T(8,128)S(1)}, f32[3,2,48,256]{3,2,1,0:T(8,128)S(1)}, u32[]{:S(2)}, u32[]{:S(2)}) collective-permute-start(f32[3,2,48,256]{3,2,1,0:T(8,128)S(1)} %get-tuple-element.53), channel_id=1, source_target_pairs={{0,16},{8,24},{16,0},{24,8},{1,17},{9,25},{17,1},{25,9},{2,18},{10... | collective-permute-start | bytes 884744 | tf_op jit(solution)/shard_map/ppermute | solution.py:247
  56.7 19.7 %collective-permute-start.20 = (f32[2,88,256]{2,1,0:T(8,128)S(1)}, f32[2,88,256]{2,1,0:T(8,128)S(1)}, u32[]{:S(2)}, u32[]{:S(2)}) collective-permute-start(f32[2,88,256]{2,1,0:T(8,128)S(1)} %get-tuple-element.48.refs_6_.refs_0_), channel_id=1, source_target_pairs={{0,2},{1,3},{2,0},{3,1},{4,6},{5,7},{6,4},{7,5},{8,10},{9,11},{10,... | collective-permute-start | bytes 540680 | tf_op jit(solution)/shard_map/ppermute | solution.py:261
  58.6 17.8 %collective-permute-start.21 = (f32[2,88,256]{2,1,0:T(8,128)S(1)}, f32[2,88,256]{2,1,0:T(8,128)S(1)}, u32[]{:S(2)}, u32[]{:S(2)}) collective-permute-start(f32[2,88,256]{2,1,0:T(8,128)S(1)} %get-tuple-element.51), channel_id=1, source_target_pairs={{0,16},{8,24},{16,0},{24,8},{1,17},{9,25},{17,1},{25,9},{2,18},{10... | collective-permute-start | bytes 540680 | tf_op jit(solution)/shard_map/ppermute | solution.py:247
  59.1 16.0 %collective-permute-start.15 = (f32[2,80,256]{2,1,0:T(8,128)S(1)}, f32[2,80,256]{2,1,0:T(8,128)S(1)}, u32[]{:S(2)}, u32[]{:S(2)}) collective-permute-start(f32[2,80,256]{2,1,0:T(8,128)S(1)} %collective-permute-done.14.refs_4_.refs_2_), channel_id=1, source_target_pairs={{0,2},{1,3},{2,0},{3,1},{4,6},{5,7},{6,4},{7,5},{8,10},{9,11},{10,... | collective-permute-start | bytes 491528 | tf_op jit(solution)/shard_map/ppermute | solution.py:261
  60.5 15.9 %collective-permute-start.12 = (f32[2,80,256]{2,1,0:T(8,128)S(1)}, f32[2,80,256]{2,1,0:T(8,128)S(1)}, u32[]{:S(2)}, u32[]{:S(2)}) collective-permute-start(f32[2,80,256]{2,1,0:T(8,128)S(1)} %get-tuple-element.43), channel_id=1, source_target_pairs={{0,1},{1,0},{2,3},{3,2},{4,5},{5,4},{6,7},{7,6},{8,9},{9,8},{10,11... | collective-permute-start | bytes 491528 | tf_op jit(solution)/shard_map/ppermute | solution.py:258
  75.1 5.2 %collective-permute-start.24 = (f32[3,2,48,256]{3,2,1,0:T(8,128)S(1)}, f32[3,2,48,256]{3,2,1,0:T(8,128)S(1)}, u32[]{:S(2)}, u32[]{:S(2)}) collective-permute-start(f32[3,2,48,256]{3,2,1,0:T(8,128)S(1)} %get-tuple-element.52.refs_1_), channel_id=1, source_target_pairs={{0,8},{8,0},{16,24},{24,16},{1,9},{9,1},{17,25},{25,17},{2,10},{10... | collective-permute-start | bytes 884744 | tf_op jit(solution)/shard_map/ppermute | solution.py:250
  76.4 3.9 %collective-permute-start.25 = (f32[3,2,48,256]{3,2,1,0:T(8,128)S(1)}, f32[3,2,48,256]{3,2,1,0:T(8,128)S(1)}, u32[]{:S(2)}, u32[]{:S(2)}) collective-permute-start(f32[3,2,48,256]{3,2,1,0:T(8,128)S(1)} %shard_map.69.refs_2_), channel_id=1, source_target_pairs={{0,8},{8,0},{16,24},{24,16},{1,9},{9,1},{17,25},{25,17},{2,10},{10... | collective-permute-start | bytes 884744 | tf_op jit(solution)/shard_map/ppermute | solution.py:250
  77.0 11.4 %collective-permute-start.22 = (f32[2,88,256]{2,1,0:T(8,128)S(1)}, f32[2,88,256]{2,1,0:T(8,128)S(1)}, u32[]{:S(2)}, u32[]{:S(2)}) collective-permute-start(f32[2,88,256]{2,1,0:T(8,128)S(1)} %collective-permute-done.21.refs_1_.refs_2_), channel_id=1, source_target_pairs={{0,2},{1,3},{2,0},{3,1},{4,6},{5,7},{6,4},{7,5},{8,10},{9,11},{10,... | collective-permute-start | bytes 540680 | tf_op jit(solution)/shard_map/ppermute | solution.py:261
  77.0 15.8 %collective-permute-start.19 = (f32[2,160,256]{2,1,0:T(8,128)S(1)}, f32[2,160,256]{2,1,0:T(8,128)S(1)}, u32[]{:S(2)}, u32[]{:S(2)}) collective-permute-start(f32[2,160,256]{2,1,0:T(8,128)S(1)} %get-tuple-element.50), channel_id=1, source_target_pairs={{0,1},{1,0},{2,3},{3,2},{4,5},{5,4},{6,7},{7,6},{8,9},{9,8},{10,11... | collective-permute-start | bytes 983048 | tf_op jit(solution)/shard_map/ppermute | solution.py:258
  81.3 7.0 %collective-permute-start.26 = (f32[2,48,256]{2,1,0:T(8,128)S(1)}, f32[2,48,256]{2,1,0:T(8,128)S(1)}, u32[]{:S(2)}, u32[]{:S(2)}) collective-permute-start(f32[2,48,256]{2,1,0:T(8,128)S(1)} %get-tuple-element.55), channel_id=1, source_target_pairs={{0,16},{8,24},{16,0},{24,8},{1,17},{9,25},{17,1},{25,9},{2,18},{10... | collective-permute-start | bytes 294920 | tf_op jit(solution)/shard_map/ppermute | solution.py:247
  89.7 20.3 %collective-permute-start.27 = (f32[2,176,256]{2,1,0:T(8,128)S(1)}, f32[2,176,256]{2,1,0:T(8,128)S(1)}, u32[]{:S(2)}, u32[]{:S(2)}) collective-permute-start(f32[2,176,256]{2,1,0:T(8,128)S(1)} %get-tuple-element.57), channel_id=1, source_target_pairs={{0,1},{1,0},{2,3},{3,2},{4,5},{5,4},{6,7},{7,6},{8,9},{9,8},{10,11... | collective-permute-start | bytes 1081352 | tf_op jit(solution)/shard_map/ppermute | solution.py:258
  89.7 10.9 %collective-permute-start.28 = (f32[2,48,256]{2,1,0:T(8,128)S(1)}, f32[2,48,256]{2,1,0:T(8,128)S(1)}, u32[]{:S(2)}, u32[]{:S(2)}) collective-permute-start(f32[2,48,256]{2,1,0:T(8,128)S(1)} %get-tuple-element.54.refs_6_.refs_0_), channel_id=1, source_target_pairs={{0,2},{1,3},{2,0},{3,1},{4,6},{5,7},{6,4},{7,5},{8,10},{9,11},{10,... | collective-permute-start | bytes 294920 | tf_op jit(solution)/shard_map/ppermute | solution.py:261
  91.5 10.4 %collective-permute-start.29 = (f32[2,48,256]{2,1,0:T(8,128)S(1)}, f32[2,48,256]{2,1,0:T(8,128)S(1)}, u32[]{:S(2)}, u32[]{:S(2)}) collective-permute-start(f32[2,48,256]{2,1,0:T(8,128)S(1)} %collective-permute-done.26.refs_7_.refs_2_), channel_id=1, source_target_pairs={{0,2},{1,3},{2,0},{3,1},{4,6},{5,7},{6,4},{7,5},{8,10},{9,11},{10,... | collective-permute-start | bytes 294920 | tf_op jit(solution)/shard_map/ppermute | solution.py:261
  103.0 6.9 %collective-permute-start.30 = (f32[2,96,256]{2,1,0:T(8,128)S(1)}, f32[2,96,256]{2,1,0:T(8,128)S(1)}, u32[]{:S(2)}, u32[]{:S(2)}) collective-permute-start(f32[2,96,256]{2,1,0:T(8,128)S(1)} %get-tuple-element.59), channel_id=1, source_target_pairs={{0,1},{1,0},{2,3},{3,2},{4,5},{5,4},{6,7},{7,6},{8,9},{9,8},{10,11... | collective-permute-start | bytes 589832 | tf_op jit(solution)/shard_map/ppermute | solution.py:258
  (4 other events, 29.4 us)

commit v9 on v8

--- a/solution.py
+++ b/solution.py
@@ -10,7 +10,7 @@
 from jax.sharding import PartitionSpec as P
 
 CORES = 2
-WEIGHTS = (5, 10, 11, 6)
+WEIGHTS = (8, 11, 8, 5)
 SUBLANES, LANES = 8, 128
 VMEM_LIMIT = 40 * 2**20
 FIRST_LIMIT = 56 * 2**20

time: 112 us -> 119 us (1.062)
  starting transfers between devices: 32.1 us -> 37.4 us
  waiting for transfers between devices: 62.9 us -> 64.7 us
    ppermute x8, waiting for transfers between devices: 39.7 us -> 34.2 us  [to_half(): lax.ppermute(value, 'tc', [(j, (j + group * gap) % col_parts) for j in ra...]
    ppermute x8, waiting for transfers between devices: 2.2 us -> 7.6 us  [to_chip(): return lax.ppermute(value, 'ka', moves)]
    ppermute x7, waiting for transfers between devices: 17.8 us -> 22.3 us  [to_panel(): return lax.ppermute(value, ('tr', 'tc'), moves)]
    ppermute x8, starting transfers between devices: 11.6 us -> 14.9 us  [to_half(): lax.ppermute(value, 'tc', [(j, (j + group * gap) % col_parts) for j in ra...]
    ppermute x8, waiting for transfers between devices: 3.23 us -> 0.68 us  [to_core(): lax.ppermute(value, 'ka', [(s, s + 1 - 2 * (s % CORES)) for s in range(mo...]
    ppermute x8, starting transfers between devices: 9.05 us -> 10.3 us  [to_chip(): return lax.ppermute(value, 'ka', moves)]
  transfers between devices with their start and end apart: 31 -> 31, of which waited for: 13 -> 11; matrix products, arithmetic and copies ran while one was open for 0% -> 0% of each run, Pallas kernels for 11% -> 10%
where the time goes in v9:
time: 119 us
  waiting for transfers between devices  64.7 us (54%)
  starting transfers between devices  37.4 us (31%)
  Pallas kernels  15.6 us (13%)
    ppermute x8, waiting for transfers between devices, to_half(): lax.ppermute(value, 'tc', [(j, (j + group * gap) % col_parts) for j in ra...  34.2 us
    ppermute x7, waiting for transfers between devices, to_panel(): return lax.ppermute(value, ('tr', 'tc'), moves)  22.3 us
    pallas_call x15, Pallas kernels, call(): pl.pallas_call(ordered, out_shape=out_shapes, in_specs=in_specs + [ANYWHE...  15.6 us
    ppermute x8, starting transfers between devices, to_half(): lax.ppermute(value, 'tc', [(j, (j + group * gap) % col_parts) for j in ra...  14.9 us
    ppermute x7, starting transfers between devices, to_panel(): return lax.ppermute(value, ('tr', 'tc'), moves)  11.5 us
    ppermute x8, starting transfers between devices, to_chip(): return lax.ppermute(value, 'ka', moves)  10.3 us
    ppermute x8, waiting for transfers between devices, to_chip(): return lax.ppermute(value, 'ka', moves)  7.6 us
  transfers between devices with their start and end apart: 31, of which 11 were waited for; matrix products, arithmetic and copies ran while one was open for 0% of the time, Pallas kernels for 10%

profile of v9, /device:TPU:0, one launch (start us, length us, event | category | flops | bytes accessed | tf_op | source)
XLA Modules:
  0.0 118.7 jit_solution(4037739897137622415)
XLA Ops:
  0.7 2.3 %shard_map.59 = (f32[3,2,64,256]{3,2,1,0:T(8,128)}, f32[3,2,64,256]{3,2,1,0:T(8,128)}) custom-call(f32[2,1,512,256]{3,2,1,0:T(8,128)} %refs_8_.1, f32[2,1,512,256]{3,2,1,0:T(8,128)} %refs_1_.7, f32[2,1,512,256]{3,2,1,0:T(8,128)} %refs_2_.7), custom_call_target="tpu_custom_call" | custom-call | flops 1 | bytes 1 | tf_op jit(solution)/shard_map/pallas_call | solution.py:218
  3.0 3.0 %collective-permute-start = (f32[3,2,64,256]{3,2,1,0:T(8,128)}, f32[3,2,64,256]{3,2,1,0:T(8,128)S(1)}, u32[]{:S(2)}, u32[]{:S(2)}) collective-permute-start(f32[3,2,64,256]{3,2,1,0:T(8,128)} %get-tuple-element.32), channel_id=1, source_target_pairs={{0,16},{8,24},{16,0},{24,8},{1,17},{9,25},{17,1},{25,9},{2,18},{10... | collective-permute-start | bytes 1179656 | tf_op jit(solution)/shard_map/ppermute | solution.py:247
  6.1 1.6 %collective-permute-start.3 = (f32[2,256,256]{2,1,0:T(8,128)S(1)}, f32[2,256,256]{2,1,0:T(8,128)S(1)}, u32[]{:S(2)}, u32[]{:S(2)}) collective-permute-start(f32[2,256,256]{2,1,0:T(8,128)S(1)} %get-tuple-element.61), channel_id=1, source_target_pairs={{0,1},{1,0},{2,3},{3,2},{4,5},{5,4},{6,7},{7,6},{8,9},{9,8},{10,11... | collective-permute-start | bytes 1572872 | tf_op jit(solution)/shard_map/ppermute | solution.py:258
  7.7 7.6 %collective-permute-done.refs_3_ = f32[3,2,64,256]{3,2,1,0:T(8,128)S(1)} collective-permute-done((f32[3,2,64,256]{3,2,1,0:T(8,128)}, f32[3,2,64,256]{3,2,1,0:T(8,128)S(1)}, u32[]{:S(2)}, u32[]{:S(2)}) %collective-permute-start) | collective-permute-done | bytes 393248 | tf_op jit(solution)/shard_map/ppermute | solution.py:247
  16.1 1.8 %collective-permute-start.9 = (f32[3,2,88,256]{3,2,1,0:T(8,128)S(1)}, f32[3,2,88,256]{3,2,1,0:T(8,128)S(1)}, u32[]{:S(2)}, u32[]{:S(2)}) collective-permute-start(f32[3,2,88,256]{3,2,1,0:T(8,128)S(1)} %get-tuple-element.36), channel_id=1, source_target_pairs={{0,16},{8,24},{16,0},{24,8},{1,17},{9,25},{17,1},{25,9},{2,18},{10... | collective-permute-start | bytes 1622024 | tf_op jit(solution)/shard_map/ppermute | solution.py:247
  17.9 1.5 %collective-permute-start.7 = (f32[2,256,256]{2,1,0:T(8,128)S(1)}, f32[2,256,256]{2,1,0:T(8,128)S(1)}, u32[]{:S(2)}, u32[]{:S(2)}) collective-permute-start(f32[2,256,256]{2,1,0:T(8,128)S(1)} %get-tuple-element.60.refs_0_), channel_id=1, source_target_pairs={{0,4},{1,5},{2,6},{3,7},{4,0},{5,1},{6,2},{7,3},{8,12},{9,13},{10,... | collective-permute-start | bytes 1572872 | tf_op jit(solution)/shard_map/ppermute | solution.py:258
  19.4 1.5 %collective-permute-start.8 = (f32[2,256,256]{2,1,0:T(8,128)S(1)}, f32[2,256,256]{2,1,0:T(8,128)S(1)}, u32[]{:S(2)}, u32[]{:S(2)}) collective-permute-start(f32[2,256,256]{2,1,0:T(8,128)S(1)} %get-tuple-element.61), channel_id=1, source_target_pairs={{0,5},{1,4},{2,7},{3,6},{4,1},{5,0},{6,3},{7,2},{8,13},{9,12},{10,... | collective-permute-start | bytes 1572872 | tf_op jit(solution)/shard_map/ppermute | solution.py:258
  20.9 1.6 %shard_map.61 = (f32[2,64,256]{2,1,0:T(8,128)S(1)}, f32[2,64,256]{2,1,0:T(8,128)S(1)}) custom-call(f32[2,4]{1,0:T(2,128)S(1)} %copy-done.4, f32[3,2,64,256]{3,2,1,0:T(8,128)S(1)} %copy-done.3, f32[3,2,64,256]{3,2,1,0:T(8,128)S(1)} %get-tuple-element.33.refs_2_, f32[3,2,64,256]{3,2,1,0:T(8,128)} %collective-permute-done.1.refs_3_, ...), custom_call_target="tpu_custom_call" | custom-call | flops 1 | bytes 1 | tf_op jit(solution)/shard_map/pallas_call | solution.py:218
  22.5 2.7 %collective-permute-start.4 = (f32[2,64,256]{2,1,0:T(8,128)S(1)}, f32[2,64,256]{2,1,0:T(8,128)S(1)}, u32[]{:S(2)}, u32[]{:S(2)}) collective-permute-start(f32[2,64,256]{2,1,0:T(8,128)S(1)} %get-tuple-element.34.refs_8_.refs_0_), channel_id=1, source_target_pairs={{0,2},{1,3},{2,0},{3,1},{4,6},{5,7},{6,4},{7,5},{8,10},{9,11},{10,... | collective-permute-start | bytes 393224 | tf_op jit(solution)/shard_map/ppermute | solution.py:261
  25.7 17.7 %collective-permute-done.7.refs_6_.refs_2_ = f32[2,256,256]{2,1,0:T(8,128)S(1)} collective-permute-done((f32[2,256,256]{2,1,0:T(8,128)S(1)}, f32[2,256,256]{2,1,0:T(8,128)S(1)}, u32[]{:S(2)}, u32[]{:S(2)}) %collective-permute-start.7) | collective-permute-done | bytes 524320 | tf_op jit(solution)/shard_map/ppermute | solution.py:258
  46.2 1.3 %shard_map.64 = (f32[2,88,256]{2,1,0:T(8,128)S(1)}, f32[2,88,256]{2,1,0:T(8,128)S(1)}) custom-call(f32[2,4]{1,0:T(2,128)S(1)} %copy-done.4, f32[3,2,88,256]{3,2,1,0:T(8,128)S(1)} %get-tuple-element.40.refs_1_, f32[3,2,88,256]{3,2,1,0:T(8,128)S(1)} %get-tuple-element.37.refs_4_.refs_2_, f32[3,2,88,256]{3,2,1,0:T(8,128)S(1)} %collective-permute-done.10.refs_3_, ...), custom_call_target="tpu_custom_call" | custom-call | flops 1 | bytes 1 | tf_op jit(solution)/shard_map/pallas_call | solution.py:218
  47.5 2.7 %collective-permute-start.13 = (f32[2,88,256]{2,1,0:T(8,128)S(1)}, f32[2,88,256]{2,1,0:T(8,128)S(1)}, u32[]{:S(2)}, u32[]{:S(2)}) collective-permute-start(f32[2,88,256]{2,1,0:T(8,128)S(1)} %get-tuple-element.41.refs_6_.refs_0_), channel_id=1, source_target_pairs={{0,2},{1,3},{2,0},{3,1},{4,6},{5,7},{6,4},{7,5},{8,10},{9,11},{10,... | collective-permute-start | bytes 540680 | tf_op jit(solution)/shard_map/ppermute | solution.py:261
  50.2 1.1 collective-permute-start.14
  51.6 13.2 %collective-permute-done.6.refs_3_ = f32[2,64,256]{2,1,0:T(8,128)S(1)} collective-permute-done((f32[2,64,256]{2,1,0:T(8,128)S(1)}, f32[2,64,256]{2,1,0:T(8,128)S(1)}, u32[]{:S(2)}, u32[]{:S(2)}) %collective-permute-start.6) | collective-permute-done | bytes 131104 | tf_op jit(solution)/shard_map/ppermute | solution.py:261
  64.8 1.0 shard_map.65
  67.6 3.4 %collective-permute-start.15 = (f32[2,88,256]{2,1,0:T(8,128)S(1)}, f32[2,88,256]{2,1,0:T(8,128)S(1)}, u32[]{:S(2)}, u32[]{:S(2)}) collective-permute-start(f32[2,88,256]{2,1,0:T(8,128)S(1)} %collective-permute-done.14.refs_4_.refs_2_), channel_id=1, source_target_pairs={{0,2},{1,3},{2,0},{3,1},{4,6},{5,7},{6,4},{7,5},{8,10},{9,11},{10,... | collective-permute-start | bytes 540680 | tf_op jit(solution)/shard_map/ppermute | solution.py:261
  70.9 1.2 shard_map.67
  72.2 1.6 %collective-permute-start.21 = (f32[2,64,256]{2,1,0:T(8,128)S(1)}, f32[2,64,256]{2,1,0:T(8,128)S(1)}, u32[]{:S(2)}, u32[]{:S(2)}) collective-permute-start(f32[2,64,256]{2,1,0:T(8,128)S(1)} %get-tuple-element.51), channel_id=1, source_target_pairs={{0,16},{8,24},{16,0},{24,8},{1,17},{9,25},{17,1},{25,9},{2,18},{10... | collective-permute-start | bytes 393224 | tf_op jit(solution)/shard_map/ppermute | solution.py:247
  73.7 3.8 %collective-permute-done.15.refs_3_ = f32[2,88,256]{2,1,0:T(8,128)S(1)} collective-permute-done((f32[2,88,256]{2,1,0:T(8,128)S(1)}, f32[2,88,256]{2,1,0:T(8,128)S(1)}, u32[]{:S(2)}, u32[]{:S(2)}) %collective-permute-start.15) | collective-permute-done | bytes 180256 | tf_op jit(solution)/shard_map/ppermute | solution.py:261
  77.6 1.3 %shard_map.68 = (f32[2,176,256]{2,1,0:T(8,128)S(1)}, f32[2,176,256]{2,1,0:T(8,128)S(1)}) custom-call(f32[2,88,256]{2,1,0:T(8,128)S(1)} %get-tuple-element.41.refs_6_.refs_0_, f32[2,88,256]{2,1,0:T(8,128)S(1)} %collective-permute-done.13.refs_5_.refs_1_, f32[2,88,256]{2,1,0:T(8,128)S(1)} %collective-permute-done.14.refs_4_.refs_2_, ...), custom_call_target="tpu_custom_call" | custom-call | flops 1 | bytes 1 | tf_op jit(solution)/shard_map/pallas_call | solution.py:218
  78.9 1.2 %collective-permute-done.12.refs_4_.refs_8_.refs_1_ = f32[2,128,256]{2,1,0:T(8,128)S(1)} collective-permute-done((f32[2,128,256]{2,1,0:T(8,128)S(1)}, f32[2,128,256]{2,1,0:T(8,128)S(1)}, u32[]{:S(2)}, u32[]{:S(2)}) %collective-permute-start.12) | collective-permute-done | bytes 262176 | tf_op jit(solution)/shard_map/ppermute | solution.py:258
  80.1 4.9 %collective-permute-done.20.refs_2_.refs_1_ = f32[2,64,256]{2,1,0:T(8,128)S(1)} collective-permute-done((f32[2,64,256]{2,1,0:T(8,128)S(1)}, f32[2,64,256]{2,1,0:T(8,128)S(1)}, u32[]{:S(2)}, u32[]{:S(2)}) %collective-permute-start.20) | collective-permute-done | bytes 131104 | tf_op jit(solution)/shard_map/ppermute | solution.py:261
  85.1 2.9 %collective-permute-start.22 = (f32[2,64,256]{2,1,0:T(8,128)S(1)}, f32[2,64,256]{2,1,0:T(8,128)S(1)}, u32[]{:S(2)}, u32[]{:S(2)}) collective-permute-start(f32[2,64,256]{2,1,0:T(8,128)S(1)} %collective-permute-done.21.refs_1_.refs_2_), channel_id=1, source_target_pairs={{0,2},{1,3},{2,0},{3,1},{4,6},{5,7},{6,4},{7,5},{8,10},{9,11},{10,... | collective-permute-start | bytes 393224 | tf_op jit(solution)/shard_map/ppermute | solution.py:261
  89.0 1.6 %collective-permute-start.26 = (f32[2,40,256]{2,1,0:T(8,128)S(1)}, f32[2,40,256]{2,1,0:T(8,128)S(1)}, u32[]{:S(2)}, u32[]{:S(2)}) collective-permute-start(f32[2,40,256]{2,1,0:T(8,128)S(1)} %get-tuple-element.55), channel_id=1, source_target_pairs={{0,16},{8,24},{16,0},{24,8},{1,17},{9,25},{17,1},{25,9},{2,18},{10... | collective-permute-start | bytes 245768 | tf_op jit(solution)/shard_map/ppermute | solution.py:247
  90.5 6.0 %collective-permute-done.22.refs_3_ = f32[2,64,256]{2,1,0:T(8,128)S(1)} collective-permute-done((f32[2,64,256]{2,1,0:T(8,128)S(1)}, f32[2,64,256]{2,1,0:T(8,128)S(1)}, u32[]{:S(2)}, u32[]{:S(2)}) %collective-permute-start.22) | collective-permute-done | bytes 131104 | tf_op jit(solution)/shard_map/ppermute | solution.py:261
  97.5 3.4 %collective-permute-start.27 = (f32[2,128,256]{2,1,0:T(8,128)S(1)}, f32[2,128,256]{2,1,0:T(8,128)S(1)}, u32[]{:S(2)}, u32[]{:S(2)}) collective-permute-start(f32[2,128,256]{2,1,0:T(8,128)S(1)} %get-tuple-element.57), channel_id=1, source_target_pairs={{0,1},{1,0},{2,3},{3,2},{4,5},{5,4},{6,7},{7,6},{8,9},{9,8},{10,11... | collective-permute-start | bytes 786440 | tf_op jit(solution)/shard_map/ppermute | solution.py:258
  101.0 2.8 %collective-permute-start.29 = (f32[2,40,256]{2,1,0:T(8,128)S(1)}, f32[2,40,256]{2,1,0:T(8,128)S(1)}, u32[]{:S(2)}, u32[]{:S(2)}) collective-permute-start(f32[2,40,256]{2,1,0:T(8,128)S(1)} %collective-permute-done.26.refs_7_.refs_2_), channel_id=1, source_target_pairs={{0,2},{1,3},{2,0},{3,1},{4,6},{5,7},{6,4},{7,5},{8,10},{9,11},{10,... | collective-permute-start | bytes 245768 | tf_op jit(solution)/shard_map/ppermute | solution.py:261
  103.9 5.3 %collective-permute-done.28.refs_1_ = f32[2,40,256]{2,1,0:T(8,128)S(1)} collective-permute-done((f32[2,40,256]{2,1,0:T(8,128)S(1)}, f32[2,40,256]{2,1,0:T(8,128)S(1)}, u32[]{:S(2)}, u32[]{:S(2)}) %collective-permute-start.28) | collective-permute-done | bytes 81952 | tf_op jit(solution)/shard_map/ppermute | solution.py:261
  110.1 1.2 %shard_map.72 = (f32[2,80,256]{2,1,0:T(8,128)S(1)}, f32[2,80,256]{2,1,0:T(8,128)S(1)}) custom-call(f32[2,40,256]{2,1,0:T(8,128)S(1)} %get-tuple-element.54.refs_6_.refs_0_, f32[2,40,256]{2,1,0:T(8,128)S(1)} %collective-permute-done.28.refs_1_, f32[2,40,256]{2,1,0:T(8,128)S(1)} %collective-permute-done.26.refs_7_.refs_2_, ...), custom_call_target="tpu_custom_call" | custom-call | flops 1 | bytes 1 | tf_op jit(solution)/shard_map/pallas_call | solution.py:218
  111.3 2.6 %collective-permute-start.30 = (f32[2,80,256]{2,1,0:T(8,128)S(1)}, f32[2,80,256]{2,1,0:T(8,128)S(1)}, u32[]{:S(2)}, u32[]{:S(2)}) collective-permute-start(f32[2,80,256]{2,1,0:T(8,128)S(1)} %get-tuple-element.59), channel_id=1, source_target_pairs={{0,1},{1,0},{2,3},{3,2},{4,5},{5,4},{6,7},{7,6},{8,9},{9,8},{10,11... | collective-permute-start | bytes 491528 | tf_op jit(solution)/shard_map/ppermute | solution.py:258
  113.8 3.4 %collective-permute-done.30.refs_7_ = f32[2,80,256]{2,1,0:T(8,128)S(1)} collective-permute-done((f32[2,80,256]{2,1,0:T(8,128)S(1)}, f32[2,80,256]{2,1,0:T(8,128)S(1)}, u32[]{:S(2)}, u32[]{:S(2)}) %collective-permute-start.30) | collective-permute-done | bytes 163872 | tf_op jit(solution)/shard_map/ppermute | solution.py:258
  117.2 1.5 %shard_map.73 = (f32[2,1,512,256]{3,2,1,0:T(8,128)}, f32[2,1,512,256]{3,2,1,0:T(8,128)}) custom-call(f32[2,128,256]{2,1,0:T(8,128)S(1)} %get-tuple-element.42.refs_6_.refs_0_, f32[2,128,256]{2,1,0:T(8,128)S(1)} %collective-permute-done.12.refs_4_.refs_8_.refs_1_, f32[2,176,256]{2,1,0:T(8,128)S(1)} %get-tuple-element.49.refs_3_.refs_2_, ...), custom_call_target="tpu_custom_call" | custom-call | flops 1 | bytes 1 | tf_op jit(solution)/shard_map/pallas_call | solution.py:218
  (56 shorter events, 9.2 us)
Async XLA Ops:
  3.0 12.3 %collective-permute-start = (f32[3,2,64,256]{3,2,1,0:T(8,128)}, f32[3,2,64,256]{3,2,1,0:T(8,128)S(1)}, u32[]{:S(2)}, u32[]{:S(2)}) collective-permute-start(f32[3,2,64,256]{3,2,1,0:T(8,128)} %get-tuple-element.32), channel_id=1, source_target_pairs={{0,16},{8,24},{16,0},{24,8},{1,17},{9,25},{17,1},{25,9},{2,18},{10... | collective-permute-start | bytes 1179656 | tf_op jit(solution)/shard_map/ppermute | solution.py:247
  6.0 13.4 %collective-permute-start.1 = (f32[3,2,64,256]{3,2,1,0:T(8,128)}, f32[3,2,64,256]{3,2,1,0:T(8,128)}, u32[]{:S(2)}, u32[]{:S(2)}) collective-permute-start(f32[3,2,64,256]{3,2,1,0:T(8,128)} %get-tuple-element.31.refs_1_), channel_id=1, source_target_pairs={{0,8},{8,0},{16,24},{24,16},{1,9},{9,1},{17,25},{25,17},{2,10},{10... | collective-permute-start | bytes 1179656 | tf_op jit(solution)/shard_map/ppermute | solution.py:250
  6.0 14.9 %copy-start.3 = (f32[3,2,64,256]{3,2,1,0:T(8,128)S(1)}, f32[3,2,64,256]{3,2,1,0:T(8,128)}, u32[]{:S(2)}) copy-start(f32[3,2,64,256]{3,2,1,0:T(8,128)} %get-tuple-element.31.refs_1_) | copy-start | bytes 1179652
  6.1 14.8 %collective-permute-start.3 = (f32[2,256,256]{2,1,0:T(8,128)S(1)}, f32[2,256,256]{2,1,0:T(8,128)S(1)}, u32[]{:S(2)}, u32[]{:S(2)}) collective-permute-start(f32[2,256,256]{2,1,0:T(8,128)S(1)} %get-tuple-element.61), channel_id=1, source_target_pairs={{0,1},{1,0},{2,3},{3,2},{4,5},{5,4},{6,7},{7,6},{8,9},{9,8},{10,11... | collective-permute-start | bytes 1572872 | tf_op jit(solution)/shard_map/ppermute | solution.py:258
  16.1 27.4 %collective-permute-start.9 = (f32[3,2,88,256]{3,2,1,0:T(8,128)S(1)}, f32[3,2,88,256]{3,2,1,0:T(8,128)S(1)}, u32[]{:S(2)}, u32[]{:S(2)}) collective-permute-start(f32[3,2,88,256]{3,2,1,0:T(8,128)S(1)} %get-tuple-element.36), channel_id=1, source_target_pairs={{0,16},{8,24},{16,0},{24,8},{1,17},{9,25},{17,1},{25,9},{2,18},{10... | collective-permute-start | bytes 1622024 | tf_op jit(solution)/shard_map/ppermute | solution.py:247
  17.9 3.1 %collective-permute-start.2 = (f32[3,2,64,256]{3,2,1,0:T(8,128)S(1)}, f32[3,2,64,256]{3,2,1,0:T(8,128)S(1)}, u32[]{:S(2)}, u32[]{:S(2)}) collective-permute-start(f32[3,2,64,256]{3,2,1,0:T(8,128)S(1)} %get-tuple-element.33.refs_2_), channel_id=1, source_target_pairs={{0,8},{8,0},{16,24},{24,16},{1,9},{9,1},{17,25},{25,17},{2,10},{10... | collective-permute-start | bytes 1179656 | tf_op jit(solution)/shard_map/ppermute | solution.py:250
  17.9 25.6 %collective-permute-start.7 = (f32[2,256,256]{2,1,0:T(8,128)S(1)}, f32[2,256,256]{2,1,0:T(8,128)S(1)}, u32[]{:S(2)}, u32[]{:S(2)}) collective-permute-start(f32[2,256,256]{2,1,0:T(8,128)S(1)} %get-tuple-element.60.refs_0_), channel_id=1, source_target_pairs={{0,4},{1,5},{2,6},{3,7},{4,0},{5,1},{6,2},{7,3},{8,12},{9,13},{10,... | collective-permute-start | bytes 1572872 | tf_op jit(solution)/shard_map/ppermute | solution.py:258
  19.4 24.1 %collective-permute-start.8 = (f32[2,256,256]{2,1,0:T(8,128)S(1)}, f32[2,256,256]{2,1,0:T(8,128)S(1)}, u32[]{:S(2)}, u32[]{:S(2)}) collective-permute-start(f32[2,256,256]{2,1,0:T(8,128)S(1)} %get-tuple-element.61), channel_id=1, source_target_pairs={{0,5},{1,4},{2,7},{3,6},{4,1},{5,0},{6,3},{7,2},{8,13},{9,12},{10,... | collective-permute-start | bytes 1572872 | tf_op jit(solution)/shard_map/ppermute | solution.py:258
  22.5 20.9 %collective-permute-start.4 = (f32[2,64,256]{2,1,0:T(8,128)S(1)}, f32[2,64,256]{2,1,0:T(8,128)S(1)}, u32[]{:S(2)}, u32[]{:S(2)}) collective-permute-start(f32[2,64,256]{2,1,0:T(8,128)S(1)} %get-tuple-element.34.refs_8_.refs_0_), channel_id=1, source_target_pairs={{0,2},{1,3},{2,0},{3,1},{4,6},{5,7},{6,4},{7,5},{8,10},{9,11},{10,... | collective-permute-start | bytes 393224 | tf_op jit(solution)/shard_map/ppermute | solution.py:261
  25.2 18.2 %collective-permute-start.5 = (f32[2,64,256]{2,1,0:T(8,128)S(1)}, f32[2,64,256]{2,1,0:T(8,128)S(1)}, u32[]{:S(2)}, u32[]{:S(2)}) collective-permute-start(f32[2,64,256]{2,1,0:T(8,128)S(1)} %get-tuple-element.35), channel_id=1, source_target_pairs={{0,16},{8,24},{16,0},{24,8},{1,17},{9,25},{17,1},{25,9},{2,18},{10... | collective-permute-start | bytes 393224 | tf_op jit(solution)/shard_map/ppermute | solution.py:247
  43.4 2.1 %collective-permute-start.10 = (f32[3,2,88,256]{3,2,1,0:T(8,128)S(1)}, f32[3,2,88,256]{3,2,1,0:T(8,128)S(1)}, u32[]{:S(2)}, u32[]{:S(2)}) collective-permute-start(f32[3,2,88,256]{3,2,1,0:T(8,128)S(1)} %get-tuple-element.40.refs_1_), channel_id=1, source_target_pairs={{0,8},{8,0},{16,24},{24,16},{1,9},{9,1},{17,25},{25,17},{2,10},{10... | collective-permute-start | bytes 1622024 | tf_op jit(solution)/shard_map/ppermute | solution.py:250
  44.1 2.1 %collective-permute-start.11 = (f32[3,2,88,256]{3,2,1,0:T(8,128)S(1)}, f32[3,2,88,256]{3,2,1,0:T(8,128)S(1)}, u32[]{:S(2)}, u32[]{:S(2)}) collective-permute-start(f32[3,2,88,256]{3,2,1,0:T(8,128)S(1)} %get-tuple-element.37.refs_4_.refs_2_), channel_id=1, source_target_pairs={{0,8},{8,0},{16,24},{24,16},{1,9},{9,1},{17,25},{25,17},{2,10},{10... | collective-permute-start | bytes 1622024 | tf_op jit(solution)/shard_map/ppermute | solution.py:250
  44.6 21.1 %collective-permute-start.16 = (f32[3,2,64,256]{3,2,1,0:T(8,128)S(1)}, f32[3,2,64,256]{3,2,1,0:T(8,128)S(1)}, u32[]{:S(2)}, u32[]{:S(2)}) collective-permute-start(f32[3,2,64,256]{3,2,1,0:T(8,128)S(1)} %get-tuple-element.46), channel_id=1, source_target_pairs={{0,16},{8,24},{16,0},{24,8},{1,17},{9,25},{17,1},{25,9},{2,18},{10... | collective-permute-start | bytes 1179656 | tf_op jit(solution)/shard_map/ppermute | solution.py:247
  47.5 18.3 %collective-permute-start.13 = (f32[2,88,256]{2,1,0:T(8,128)S(1)}, f32[2,88,256]{2,1,0:T(8,128)S(1)}, u32[]{:S(2)}, u32[]{:S(2)}) collective-permute-start(f32[2,88,256]{2,1,0:T(8,128)S(1)} %get-tuple-element.41.refs_6_.refs_0_), channel_id=1, source_target_pairs={{0,2},{1,3},{2,0},{3,1},{4,6},{5,7},{6,4},{7,5},{8,10},{9,11},{10,... | collective-permute-start | bytes 540680 | tf_op jit(solution)/shard_map/ppermute | solution.py:261
  50.2 15.6 %collective-permute-start.14 = (f32[2,88,256]{2,1,0:T(8,128)S(1)}, f32[2,88,256]{2,1,0:T(8,128)S(1)}, u32[]{:S(2)}, u32[]{:S(2)}) collective-permute-start(f32[2,88,256]{2,1,0:T(8,128)S(1)} %get-tuple-element.44), channel_id=1, source_target_pairs={{0,16},{8,24},{16,0},{24,8},{1,17},{9,25},{17,1},{25,9},{2,18},{10... | collective-permute-start | bytes 540680 | tf_op jit(solution)/shard_map/ppermute | solution.py:247
  51.2 13.6 %collective-permute-start.6 = (f32[2,64,256]{2,1,0:T(8,128)S(1)}, f32[2,64,256]{2,1,0:T(8,128)S(1)}, u32[]{:S(2)}, u32[]{:S(2)}) collective-permute-start(f32[2,64,256]{2,1,0:T(8,128)S(1)} %collective-permute-done.5.refs_4_.refs_2_), channel_id=1, source_target_pairs={{0,2},{1,3},{2,0},{3,1},{4,6},{5,7},{6,4},{7,5},{8,10},{9,11},{10,... | collective-permute-start | bytes 393224 | tf_op jit(solution)/shard_map/ppermute | solution.py:261
  51.6 19.4 %collective-permute-start.17 = (f32[3,2,64,256]{3,2,1,0:T(8,128)S(1)}, f32[3,2,64,256]{3,2,1,0:T(8,128)S(1)}, u32[]{:S(2)}, u32[]{:S(2)}) collective-permute-start(f32[3,2,64,256]{3,2,1,0:T(8,128)S(1)} %get-tuple-element.45.refs_1_), channel_id=1, source_target_pairs={{0,8},{8,0},{16,24},{24,16},{1,9},{9,1},{17,25},{25,17},{2,10},{10... | collective-permute-start | bytes 1179656 | tf_op jit(solution)/shard_map/ppermute | solution.py:250
  66.2 4.7 %collective-permute-start.18 = (f32[3,2,64,256]{3,2,1,0:T(8,128)S(1)}, f32[3,2,64,256]{3,2,1,0:T(8,128)S(1)}, u32[]{:S(2)}, u32[]{:S(2)}) collective-permute-start(f32[3,2,64,256]{3,2,1,0:T(8,128)S(1)} %get-tuple-element.47.refs_2_), channel_id=1, source_target_pairs={{0,8},{8,0},{16,24},{24,16},{1,9},{9,1},{17,25},{25,17},{2,10},{10... | collective-permute-start | bytes 1179656 | tf_op jit(solution)/shard_map/ppermute | solution.py:250
  66.3 13.8 %collective-permute-start.12 = (f32[2,128,256]{2,1,0:T(8,128)S(1)}, f32[2,128,256]{2,1,0:T(8,128)S(1)}, u32[]{:S(2)}, u32[]{:S(2)}) collective-permute-start(f32[2,128,256]{2,1,0:T(8,128)S(1)} %get-tuple-element.43), channel_id=1, source_target_pairs={{0,1},{1,0},{2,3},{3,2},{4,5},{5,4},{6,7},{7,6},{8,9},{9,8},{10,11... | collective-permute-start | bytes 786440 | tf_op jit(solution)/shard_map/ppermute | solution.py:258
  67.0 13.1 %collective-permute-start.23 = (f32[3,2,40,256]{3,2,1,0:T(8,128)S(1)}, f32[3,2,40,256]{3,2,1,0:T(8,128)S(1)}, u32[]{:S(2)}, u32[]{:S(2)}) collective-permute-start(f32[3,2,40,256]{3,2,1,0:T(8,128)S(1)} %get-tuple-element.53), channel_id=1, source_target_pairs={{0,16},{8,24},{16,0},{24,8},{1,17},{9,25},{17,1},{25,9},{2,18},{10... | collective-permute-start | bytes 737288 | tf_op jit(solution)/shard_map/ppermute | solution.py:247
  67.6 10.0 %collective-permute-start.15 = (f32[2,88,256]{2,1,0:T(8,128)S(1)}, f32[2,88,256]{2,1,0:T(8,128)S(1)}, u32[]{:S(2)}, u32[]{:S(2)}) collective-permute-start(f32[2,88,256]{2,1,0:T(8,128)S(1)} %collective-permute-done.14.refs_4_.refs_2_), channel_id=1, source_target_pairs={{0,2},{1,3},{2,0},{3,1},{4,6},{5,7},{6,4},{7,5},{8,10},{9,11},{10,... | collective-permute-start | bytes 540680 | tf_op jit(solution)/shard_map/ppermute | solution.py:261
  72.1 13.0 %collective-permute-start.20 = (f32[2,64,256]{2,1,0:T(8,128)S(1)}, f32[2,64,256]{2,1,0:T(8,128)S(1)}, u32[]{:S(2)}, u32[]{:S(2)}) collective-permute-start(f32[2,64,256]{2,1,0:T(8,128)S(1)} %get-tuple-element.48.refs_6_.refs_0_), channel_id=1, source_target_pairs={{0,2},{1,3},{2,0},{3,1},{4,6},{5,7},{6,4},{7,5},{8,10},{9,11},{10,... | collective-permute-start | bytes 393224 | tf_op jit(solution)/shard_map/ppermute | solution.py:261
  72.2 12.9 %collective-permute-start.21 = (f32[2,64,256]{2,1,0:T(8,128)S(1)}, f32[2,64,256]{2,1,0:T(8,128)S(1)}, u32[]{:S(2)}, u32[]{:S(2)}) collective-permute-start(f32[2,64,256]{2,1,0:T(8,128)S(1)} %get-tuple-element.51), channel_id=1, source_target_pairs={{0,16},{8,24},{16,0},{24,8},{1,17},{9,25},{17,1},{25,9},{2,18},{10... | collective-permute-start | bytes 393224 | tf_op jit(solution)/shard_map/ppermute | solution.py:247
  77.6 10.5 %collective-permute-start.24 = (f32[3,2,40,256]{3,2,1,0:T(8,128)S(1)}, f32[3,2,40,256]{3,2,1,0:T(8,128)S(1)}, u32[]{:S(2)}, u32[]{:S(2)}) collective-permute-start(f32[3,2,40,256]{3,2,1,0:T(8,128)S(1)} %get-tuple-element.52.refs_1_), channel_id=1, source_target_pairs={{0,8},{8,0},{16,24},{24,16},{1,9},{9,1},{17,25},{25,17},{2,10},{10... | collective-permute-start | bytes 737288 | tf_op jit(solution)/shard_map/ppermute | solution.py:250
  85.1 3.0 %collective-permute-start.25 = (f32[3,2,40,256]{3,2,1,0:T(8,128)S(1)}, f32[3,2,40,256]{3,2,1,0:T(8,128)S(1)}, u32[]{:S(2)}, u32[]{:S(2)}) collective-permute-start(f32[3,2,40,256]{3,2,1,0:T(8,128)S(1)} %shard_map.69.refs_2_), channel_id=1, source_target_pairs={{0,8},{8,0},{16,24},{24,16},{1,9},{9,1},{17,25},{25,17},{2,10},{10... | collective-permute-start | bytes 737288 | tf_op jit(solution)/shard_map/ppermute | solution.py:250
  85.1 18.8 %collective-permute-start.19 = (f32[2,176,256]{2,1,0:T(8,128)S(1)}, f32[2,176,256]{2,1,0:T(8,128)S(1)}, u32[]{:S(2)}, u32[]{:S(2)}) collective-permute-start(f32[2,176,256]{2,1,0:T(8,128)S(1)} %get-tuple-element.50), channel_id=1, source_target_pairs={{0,1},{1,0},{2,3},{3,2},{4,5},{5,4},{6,7},{7,6},{8,9},{9,8},{10,11... | collective-permute-start | bytes 1081352 | tf_op jit(solution)/shard_map/ppermute | solution.py:258
  85.1 11.4 %collective-permute-start.22 = (f32[2,64,256]{2,1,0:T(8,128)S(1)}, f32[2,64,256]{2,1,0:T(8,128)S(1)}, u32[]{:S(2)}, u32[]{:S(2)}) collective-permute-start(f32[2,64,256]{2,1,0:T(8,128)S(1)} %collective-permute-done.21.refs_1_.refs_2_), channel_id=1, source_target_pairs={{0,2},{1,3},{2,0},{3,1},{4,6},{5,7},{6,4},{7,5},{8,10},{9,11},{10,... | collective-permute-start | bytes 393224 | tf_op jit(solution)/shard_map/ppermute | solution.py:261
  89.0 7.6 %collective-permute-start.26 = (f32[2,40,256]{2,1,0:T(8,128)S(1)}, f32[2,40,256]{2,1,0:T(8,128)S(1)}, u32[]{:S(2)}, u32[]{:S(2)}) collective-permute-start(f32[2,40,256]{2,1,0:T(8,128)S(1)} %get-tuple-element.55), channel_id=1, source_target_pairs={{0,16},{8,24},{16,0},{24,8},{1,17},{9,25},{17,1},{25,9},{2,18},{10... | collective-permute-start | bytes 245768 | tf_op jit(solution)/shard_map/ppermute | solution.py:247
  97.5 19.7 %collective-permute-start.27 = (f32[2,128,256]{2,1,0:T(8,128)S(1)}, f32[2,128,256]{2,1,0:T(8,128)S(1)}, u32[]{:S(2)}, u32[]{:S(2)}) collective-permute-start(f32[2,128,256]{2,1,0:T(8,128)S(1)} %get-tuple-element.57), channel_id=1, source_target_pairs={{0,1},{1,0},{2,3},{3,2},{4,5},{5,4},{6,7},{7,6},{8,9},{9,8},{10,11... | collective-permute-start | bytes 786440 | tf_op jit(solution)/shard_map/ppermute | solution.py:258
  101.0 8.2 %collective-permute-start.28 = (f32[2,40,256]{2,1,0:T(8,128)S(1)}, f32[2,40,256]{2,1,0:T(8,128)S(1)}, u32[]{:S(2)}, u32[]{:S(2)}) collective-permute-start(f32[2,40,256]{2,1,0:T(8,128)S(1)} %get-tuple-element.54.refs_6_.refs_0_), channel_id=1, source_target_pairs={{0,2},{1,3},{2,0},{3,1},{4,6},{5,7},{6,4},{7,5},{8,10},{9,11},{10,... | collective-permute-start | bytes 245768 | tf_op jit(solution)/shard_map/ppermute | solution.py:261
  101.0 9.0 %collective-permute-start.29 = (f32[2,40,256]{2,1,0:T(8,128)S(1)}, f32[2,40,256]{2,1,0:T(8,128)S(1)}, u32[]{:S(2)}, u32[]{:S(2)}) collective-permute-start(f32[2,40,256]{2,1,0:T(8,128)S(1)} %collective-permute-done.26.refs_7_.refs_2_), channel_id=1, source_target_pairs={{0,2},{1,3},{2,0},{3,1},{4,6},{5,7},{6,4},{7,5},{8,10},{9,11},{10,... | collective-permute-start | bytes 245768 | tf_op jit(solution)/shard_map/ppermute | solution.py:261
  111.3 5.9 %collective-permute-start.30 = (f32[2,80,256]{2,1,0:T(8,128)S(1)}, f32[2,80,256]{2,1,0:T(8,128)S(1)}, u32[]{:S(2)}, u32[]{:S(2)}) collective-permute-start(f32[2,80,256]{2,1,0:T(8,128)S(1)} %get-tuple-element.59), channel_id=1, source_target_pairs={{0,1},{1,0},{2,3},{3,2},{4,5},{5,4},{6,7},{7,6},{8,9},{9,8},{10,11... | collective-permute-start | bytes 491528 | tf_op jit(solution)/shard_map/ppermute | solution.py:258
  (4 other events, 49.5 us)

commit v10 on v9

--- a/solution.py
+++ b/solution.py
@@ -335,7 +335,7 @@
                 sent.append(forward(fresh))
             else:
                 across = gate(across, (*arrived, *last, *(results[-2][1:] if len(results) > 1 else ())))
-            gates = panels[1:group]
+            gates = () if at else panels[1 : group + 1]
             if at == 1:
                 right = call(
                     functools.partial(right_kernel, row_parts, group),
@@ -355,7 +355,7 @@
             returned = owned[1:2]
             arrived = (*returned, *lefts[at][1:2])
             if at == 0:
-                arrived += tuple(panels[group:])
+                arrived += tuple(panels[group + 1 :])
             last = sigmas[:1]
         if at >= 1:
             before = results[-2][1:] if len(results) > 1 else ()

time: 119 us -> 111 us (0.933)
  waiting for transfers between devices: 64.7 us -> 57 us
    ppermute x7, waiting for transfers between devices: 22.3 us -> 15.1 us  [to_panel(): return lax.ppermute(value, ('tr', 'tc'), moves)]
    ppermute x8, waiting for transfers between devices: 7.6 us -> 6.07 us  [to_chip(): return lax.ppermute(value, 'ka', moves)]
  transfers between devices with their start and end apart: 31 -> 31, of which waited for: 11 -> 13; matrix products, arithmetic and copies ran while one was open for 0% -> 0% of each run, Pallas kernels for 10% -> 11%
where the time goes in v10:
time: 111 us
  waiting for transfers between devices  57 us (51%)
  starting transfers between devices  37.5 us (34%)
  Pallas kernels  15.5 us (14%)
    ppermute x8, waiting for transfers between devices, to_half(): lax.ppermute(value, 'tc', [(j, (j + group * gap) % col_parts) for j in ra...  34.9 us
    pallas_call x15, Pallas kernels, call(): pl.pallas_call(ordered, out_shape=out_shapes, in_specs=in_specs + [ANYWHE...  15.5 us
    ppermute x7, waiting for transfers between devices, to_panel(): return lax.ppermute(value, ('tr', 'tc'), moves)  15.1 us
    ppermute x8, starting transfers between devices, to_half(): lax.ppermute(value, 'tc', [(j, (j + group * gap) % col_parts) for j in ra...  14.9 us
    ppermute x7, starting transfers between devices, to_panel(): return lax.ppermute(value, ('tr', 'tc'), moves)  12.4 us
    ppermute x8, starting transfers between devices, to_chip(): return lax.ppermute(value, 'ka', moves)  10 us
    ppermute x8, waiting for transfers between devices, to_chip(): return lax.ppermute(value, 'ka', moves)  6.07 us
  transfers between devices with their start and end apart: 31, of which 13 were waited for; matrix products, arithmetic and copies ran while one was open for 0% of the time, Pallas kernels for 11%

profile of v10, /device:TPU:0, one launch (start us, length us, event | category | flops | bytes accessed | tf_op | source)
XLA Modules:
  0.0 111.0 jit_solution(14798794315815209513)
XLA Ops:
  0.7 2.3 %shard_map.59 = (f32[3,2,64,256]{3,2,1,0:T(8,128)}, f32[3,2,64,256]{3,2,1,0:T(8,128)}) custom-call(f32[2,1,512,256]{3,2,1,0:T(8,128)} %refs_8_.1, f32[2,1,512,256]{3,2,1,0:T(8,128)} %refs_1_.7, f32[2,1,512,256]{3,2,1,0:T(8,128)} %refs_2_.7), custom_call_target="tpu_custom_call" | custom-call | flops 1 | bytes 1 | tf_op jit(solution)/shard_map/pallas_call | solution.py:218
  3.0 3.0 %collective-permute-start = (f32[3,2,64,256]{3,2,1,0:T(8,128)}, f32[3,2,64,256]{3,2,1,0:T(8,128)S(1)}, u32[]{:S(2)}, u32[]{:S(2)}) collective-permute-start(f32[3,2,64,256]{3,2,1,0:T(8,128)} %get-tuple-element.32), channel_id=1, source_target_pairs={{0,16},{8,24},{16,0},{24,8},{1,17},{9,25},{17,1},{25,9},{2,18},{10... | collective-permute-start | bytes 1179656 | tf_op jit(solution)/shard_map/ppermute | solution.py:247
  6.1 1.6 %collective-permute-start.3 = (f32[2,256,256]{2,1,0:T(8,128)S(1)}, f32[2,256,256]{2,1,0:T(8,128)S(1)}, u32[]{:S(2)}, u32[]{:S(2)}) collective-permute-start(f32[2,256,256]{2,1,0:T(8,128)S(1)} %get-tuple-element.61), channel_id=1, source_target_pairs={{0,1},{1,0},{2,3},{3,2},{4,5},{5,4},{6,7},{7,6},{8,9},{9,8},{10,11... | collective-permute-start | bytes 1572872 | tf_op jit(solution)/shard_map/ppermute | solution.py:258
  7.7 1.5 %collective-permute-start.4 = (f32[2,256,256]{2,1,0:T(8,128)S(1)}, f32[2,256,256]{2,1,0:T(8,128)S(1)}, u32[]{:S(2)}, u32[]{:S(2)}) collective-permute-start(f32[2,256,256]{2,1,0:T(8,128)S(1)} %get-tuple-element.60.refs_0_), channel_id=1, source_target_pairs={{0,4},{1,5},{2,6},{3,7},{4,0},{5,1},{6,2},{7,3},{8,12},{9,13},{10,... | collective-permute-start | bytes 1572872 | tf_op jit(solution)/shard_map/ppermute | solution.py:258
  9.2 6.1 %collective-permute-done.refs_3_ = f32[3,2,64,256]{3,2,1,0:T(8,128)S(1)} collective-permute-done((f32[3,2,64,256]{3,2,1,0:T(8,128)}, f32[3,2,64,256]{3,2,1,0:T(8,128)S(1)}, u32[]{:S(2)}, u32[]{:S(2)}) %collective-permute-start) | collective-permute-done | bytes 393248 | tf_op jit(solution)/shard_map/ppermute | solution.py:247
  16.1 1.8 %collective-permute-start.9 = (f32[3,2,88,256]{3,2,1,0:T(8,128)S(1)}, f32[3,2,88,256]{3,2,1,0:T(8,128)S(1)}, u32[]{:S(2)}, u32[]{:S(2)}) collective-permute-start(f32[3,2,88,256]{3,2,1,0:T(8,128)S(1)} %get-tuple-element.36), channel_id=1, source_target_pairs={{0,16},{8,24},{16,0},{24,8},{1,17},{9,25},{17,1},{25,9},{2,18},{10... | collective-permute-start | bytes 1622024 | tf_op jit(solution)/shard_map/ppermute | solution.py:247
  17.9 2.5 %collective-permute-start.8 = (f32[2,256,256]{2,1,0:T(8,128)S(1)}, f32[2,256,256]{2,1,0:T(8,128)S(1)}, u32[]{:S(2)}, u32[]{:S(2)}) collective-permute-start(f32[2,256,256]{2,1,0:T(8,128)S(1)} %get-tuple-element.61), channel_id=1, source_target_pairs={{0,5},{1,4},{2,7},{3,6},{4,1},{5,0},{6,3},{7,2},{8,13},{9,12},{10,... | collective-permute-start | bytes 1572872 | tf_op jit(solution)/shard_map/ppermute | solution.py:258
  20.5 1.3 %collective-permute-done.4.refs_6_.refs_2_ = f32[2,256,256]{2,1,0:T(8,128)S(1)} collective-permute-done((f32[2,256,256]{2,1,0:T(8,128)S(1)}, f32[2,256,256]{2,1,0:T(8,128)S(1)}, u32[]{:S(2)}, u32[]{:S(2)}) %collective-permute-start.4) | collective-permute-done | bytes 524320 | tf_op jit(solution)/shard_map/ppermute | solution.py:258
  21.8 1.6 %shard_map.61 = (f32[2,64,256]{2,1,0:T(8,128)S(1)}, f32[2,64,256]{2,1,0:T(8,128)S(1)}) custom-call(f32[2,4]{1,0:T(2,128)S(1)} %copy-done.4, f32[3,2,64,256]{3,2,1,0:T(8,128)S(1)} %copy-done.3, f32[3,2,64,256]{3,2,1,0:T(8,128)S(1)} %get-tuple-element.33.refs_2_, f32[3,2,64,256]{3,2,1,0:T(8,128)} %collective-permute-done.1.refs_3_, ...), custom_call_target="tpu_custom_call" | custom-call | flops 1 | bytes 1 | tf_op jit(solution)/shard_map/pallas_call | solution.py:218
  23.4 2.7 %collective-permute-start.5 = (f32[2,64,256]{2,1,0:T(8,128)S(1)}, f32[2,64,256]{2,1,0:T(8,128)S(1)}, u32[]{:S(2)}, u32[]{:S(2)}) collective-permute-start(f32[2,64,256]{2,1,0:T(8,128)S(1)} %get-tuple-element.34.refs_7_.refs_0_), channel_id=1, source_target_pairs={{0,2},{1,3},{2,0},{3,1},{4,6},{5,7},{6,4},{7,5},{8,10},{9,11},{10,... | collective-permute-start | bytes 393224 | tf_op jit(solution)/shard_map/ppermute | solution.py:261
  26.6 9.3 %collective-permute-done.8.refs_6_.refs_3_ = f32[2,256,256]{2,1,0:T(8,128)S(1)} collective-permute-done((f32[2,256,256]{2,1,0:T(8,128)S(1)}, f32[2,256,256]{2,1,0:T(8,128)S(1)}, u32[]{:S(2)}, u32[]{:S(2)}) %collective-permute-start.8) | collective-permute-done | bytes 524320 | tf_op jit(solution)/shard_map/ppermute | solution.py:258
  38.5 1.3 %shard_map.64 = (f32[2,88,256]{2,1,0:T(8,128)S(1)}, f32[2,88,256]{2,1,0:T(8,128)S(1)}) custom-call(f32[2,4]{1,0:T(2,128)S(1)} %copy-done.4, f32[3,2,88,256]{3,2,1,0:T(8,128)S(1)} %get-tuple-element.40.refs_1_, f32[3,2,88,256]{3,2,1,0:T(8,128)S(1)} %get-tuple-element.37.refs_4_.refs_2_, f32[3,2,88,256]{3,2,1,0:T(8,128)S(1)} %collective-permute-done.10.refs_3_, ...), custom_call_target="tpu_custom_call" | custom-call | flops 1 | bytes 1 | tf_op jit(solution)/shard_map/pallas_call | solution.py:218
  39.8 2.6 %collective-permute-start.13 = (f32[2,88,256]{2,1,0:T(8,128)S(1)}, f32[2,88,256]{2,1,0:T(8,128)S(1)}, u32[]{:S(2)}, u32[]{:S(2)}) collective-permute-start(f32[2,88,256]{2,1,0:T(8,128)S(1)} %get-tuple-element.41.refs_6_.refs_0_), channel_id=1, source_target_pairs={{0,2},{1,3},{2,0},{3,1},{4,6},{5,7},{6,4},{7,5},{8,10},{9,11},{10,... | collective-permute-start | bytes 540680 | tf_op jit(solution)/shard_map/ppermute | solution.py:261
  43.6 13.3 %collective-permute-done.7.refs_3_ = f32[2,64,256]{2,1,0:T(8,128)S(1)} collective-permute-done((f32[2,64,256]{2,1,0:T(8,128)S(1)}, f32[2,64,256]{2,1,0:T(8,128)S(1)}, u32[]{:S(2)}, u32[]{:S(2)}) %collective-permute-start.7) | collective-permute-done | bytes 131104 | tf_op jit(solution)/shard_map/ppermute | solution.py:261
  56.9 1.0 shard_map.65
  59.9 3.4 %collective-permute-start.15 = (f32[2,88,256]{2,1,0:T(8,128)S(1)}, f32[2,88,256]{2,1,0:T(8,128)S(1)}, u32[]{:S(2)}, u32[]{:S(2)}) collective-permute-start(f32[2,88,256]{2,1,0:T(8,128)S(1)} %collective-permute-done.14.refs_4_.refs_2_), channel_id=1, source_target_pairs={{0,2},{1,3},{2,0},{3,1},{4,6},{5,7},{6,4},{7,5},{8,10},{9,11},{10,... | collective-permute-start | bytes 540680 | tf_op jit(solution)/shard_map/ppermute | solution.py:261
  63.2 1.2 %shard_map.67 = (f32[2,64,256]{2,1,0:T(8,128)S(1)}, f32[2,64,256]{2,1,0:T(8,128)S(1)}) custom-call(f32[2,4]{1,0:T(2,128)S(1)} %copy-done.4, f32[3,2,64,256]{3,2,1,0:T(8,128)S(1)} %get-tuple-element.45.refs_1_, f32[3,2,64,256]{3,2,1,0:T(8,128)S(1)} %get-tuple-element.47.refs_2_, f32[3,2,64,256]{3,2,1,0:T(8,128)S(1)} %collective-permute-done.17.refs_3_, ...), custom_call_target="tpu_custom_call" | custom-call | flops 1 | bytes 1 | tf_op jit(solution)/shard_map/pallas_call | solution.py:218
  64.5 1.3 %collective-permute-start.21 = (f32[2,64,256]{2,1,0:T(8,128)S(1)}, f32[2,64,256]{2,1,0:T(8,128)S(1)}, u32[]{:S(2)}, u32[]{:S(2)}) collective-permute-start(f32[2,64,256]{2,1,0:T(8,128)S(1)} %get-tuple-element.51), channel_id=1, source_target_pairs={{0,16},{8,24},{16,0},{24,8},{1,17},{9,25},{17,1},{25,9},{2,18},{10... | collective-permute-start | bytes 393224 | tf_op jit(solution)/shard_map/ppermute | solution.py:247
  65.7 3.8 %collective-permute-done.15.refs_3_ = f32[2,88,256]{2,1,0:T(8,128)S(1)} collective-permute-done((f32[2,88,256]{2,1,0:T(8,128)S(1)}, f32[2,88,256]{2,1,0:T(8,128)S(1)}, u32[]{:S(2)}, u32[]{:S(2)}) %collective-permute-start.15) | collective-permute-done | bytes 180256 | tf_op jit(solution)/shard_map/ppermute | solution.py:261
  69.6 1.3 %shard_map.68 = (f32[2,176,256]{2,1,0:T(8,128)S(1)}, f32[2,176,256]{2,1,0:T(8,128)S(1)}) custom-call(f32[2,88,256]{2,1,0:T(8,128)S(1)} %get-tuple-element.41.refs_6_.refs_0_, f32[2,88,256]{2,1,0:T(8,128)S(1)} %collective-permute-done.13.refs_5_.refs_1_, f32[2,88,256]{2,1,0:T(8,128)S(1)} %collective-permute-done.14.refs_4_.refs_2_, ...), custom_call_target="tpu_custom_call" | custom-call | flops 1 | bytes 1 | tf_op jit(solution)/shard_map/pallas_call | solution.py:218
  70.9 1.1 collective-permute-done.12.refs_4_.refs_8_.refs_1_
  72.0 5.4 %collective-permute-done.20.refs_2_.refs_1_ = f32[2,64,256]{2,1,0:T(8,128)S(1)} collective-permute-done((f32[2,64,256]{2,1,0:T(8,128)S(1)}, f32[2,64,256]{2,1,0:T(8,128)S(1)}, u32[]{:S(2)}, u32[]{:S(2)}) %collective-permute-start.20) | collective-permute-done | bytes 131104 | tf_op jit(solution)/shard_map/ppermute | solution.py:261
  77.4 2.9 %collective-permute-start.22 = (f32[2,64,256]{2,1,0:T(8,128)S(1)}, f32[2,64,256]{2,1,0:T(8,128)S(1)}, u32[]{:S(2)}, u32[]{:S(2)}) collective-permute-start(f32[2,64,256]{2,1,0:T(8,128)S(1)} %collective-permute-done.21.refs_1_.refs_2_), channel_id=1, source_target_pairs={{0,2},{1,3},{2,0},{3,1},{4,6},{5,7},{6,4},{7,5},{8,10},{9,11},{10,... | collective-permute-start | bytes 393224 | tf_op jit(solution)/shard_map/ppermute | solution.py:261
  81.2 1.3 %collective-permute-start.26 = (f32[2,40,256]{2,1,0:T(8,128)S(1)}, f32[2,40,256]{2,1,0:T(8,128)S(1)}, u32[]{:S(2)}, u32[]{:S(2)}) collective-permute-start(f32[2,40,256]{2,1,0:T(8,128)S(1)} %get-tuple-element.55), channel_id=1, source_target_pairs={{0,16},{8,24},{16,0},{24,8},{1,17},{9,25},{17,1},{25,9},{2,18},{10... | collective-permute-start | bytes 245768 | tf_op jit(solution)/shard_map/ppermute | solution.py:247
  82.5 6.3 %collective-permute-done.22.refs_3_ = f32[2,64,256]{2,1,0:T(8,128)S(1)} collective-permute-done((f32[2,64,256]{2,1,0:T(8,128)S(1)}, f32[2,64,256]{2,1,0:T(8,128)S(1)}, u32[]{:S(2)}, u32[]{:S(2)}) %collective-permute-start.22) | collective-permute-done | bytes 131104 | tf_op jit(solution)/shard_map/ppermute | solution.py:261
  89.8 3.4 %collective-permute-start.27 = (f32[2,128,256]{2,1,0:T(8,128)S(1)}, f32[2,128,256]{2,1,0:T(8,128)S(1)}, u32[]{:S(2)}, u32[]{:S(2)}) collective-permute-start(f32[2,128,256]{2,1,0:T(8,128)S(1)} %get-tuple-element.57), channel_id=1, source_target_pairs={{0,1},{1,0},{2,3},{3,2},{4,5},{5,4},{6,7},{7,6},{8,9},{9,8},{10,11... | collective-permute-start | bytes 786440 | tf_op jit(solution)/shard_map/ppermute | solution.py:258
  93.3 2.8 %collective-permute-start.29 = (f32[2,40,256]{2,1,0:T(8,128)S(1)}, f32[2,40,256]{2,1,0:T(8,128)S(1)}, u32[]{:S(2)}, u32[]{:S(2)}) collective-permute-start(f32[2,40,256]{2,1,0:T(8,128)S(1)} %collective-permute-done.26.refs_7_.refs_2_), channel_id=1, source_target_pairs={{0,2},{1,3},{2,0},{3,1},{4,6},{5,7},{6,4},{7,5},{8,10},{9,11},{10,... | collective-permute-start | bytes 245768 | tf_op jit(solution)/shard_map/ppermute | solution.py:261
  96.1 5.3 %collective-permute-done.28.refs_1_ = f32[2,40,256]{2,1,0:T(8,128)S(1)} collective-permute-done((f32[2,40,256]{2,1,0:T(8,128)S(1)}, f32[2,40,256]{2,1,0:T(8,128)S(1)}, u32[]{:S(2)}, u32[]{:S(2)}) %collective-permute-start.28) | collective-permute-done | bytes 81952 | tf_op jit(solution)/shard_map/ppermute | solution.py:261
  102.3 1.2 %shard_map.72 = (f32[2,80,256]{2,1,0:T(8,128)S(1)}, f32[2,80,256]{2,1,0:T(8,128)S(1)}) custom-call(f32[2,40,256]{2,1,0:T(8,128)S(1)} %get-tuple-element.54.refs_6_.refs_0_, f32[2,40,256]{2,1,0:T(8,128)S(1)} %collective-permute-done.28.refs_1_, f32[2,40,256]{2,1,0:T(8,128)S(1)} %collective-permute-done.26.refs_7_.refs_2_, ...), custom_call_target="tpu_custom_call" | custom-call | flops 1 | bytes 1 | tf_op jit(solution)/shard_map/pallas_call | solution.py:218
  103.5 2.6 %collective-permute-start.30 = (f32[2,80,256]{2,1,0:T(8,128)S(1)}, f32[2,80,256]{2,1,0:T(8,128)S(1)}, u32[]{:S(2)}, u32[]{:S(2)}) collective-permute-start(f32[2,80,256]{2,1,0:T(8,128)S(1)} %get-tuple-element.59), channel_id=1, source_target_pairs={{0,1},{1,0},{2,3},{3,2},{4,5},{5,4},{6,7},{7,6},{8,9},{9,8},{10,11... | collective-permute-start | bytes 491528 | tf_op jit(solution)/shard_map/ppermute | solution.py:258
  106.1 3.4 %collective-permute-done.30.refs_7_ = f32[2,80,256]{2,1,0:T(8,128)S(1)} collective-permute-done((f32[2,80,256]{2,1,0:T(8,128)S(1)}, f32[2,80,256]{2,1,0:T(8,128)S(1)}, u32[]{:S(2)}, u32[]{:S(2)}) %collective-permute-start.30) | collective-permute-done | bytes 163872 | tf_op jit(solution)/shard_map/ppermute | solution.py:258
  109.5 1.5 %shard_map.73 = (f32[2,1,512,256]{3,2,1,0:T(8,128)}, f32[2,1,512,256]{3,2,1,0:T(8,128)}) custom-call(f32[2,128,256]{2,1,0:T(8,128)S(1)} %get-tuple-element.42.refs_6_.refs_0_, f32[2,128,256]{2,1,0:T(8,128)S(1)} %collective-permute-done.12.refs_4_.refs_8_.refs_1_, f32[2,176,256]{2,1,0:T(8,128)S(1)} %get-tuple-element.49.refs_3_.refs_2_, ...), custom_call_target="tpu_custom_call" | custom-call | flops 1 | bytes 1 | tf_op jit(solution)/shard_map/pallas_call | solution.py:218
  (56 shorter events, 10.2 us)
Async XLA Ops:
  3.0 12.3 %collective-permute-start = (f32[3,2,64,256]{3,2,1,0:T(8,128)}, f32[3,2,64,256]{3,2,1,0:T(8,128)S(1)}, u32[]{:S(2)}, u32[]{:S(2)}) collective-permute-start(f32[3,2,64,256]{3,2,1,0:T(8,128)} %get-tuple-element.32), channel_id=1, source_target_pairs={{0,16},{8,24},{16,0},{24,8},{1,17},{9,25},{17,1},{25,9},{2,18},{10... | collective-permute-start | bytes 1179656 | tf_op jit(solution)/shard_map/ppermute | solution.py:247
  6.0 11.9 %collective-permute-start.1 = (f32[3,2,64,256]{3,2,1,0:T(8,128)}, f32[3,2,64,256]{3,2,1,0:T(8,128)}, u32[]{:S(2)}, u32[]{:S(2)}) collective-permute-start(f32[3,2,64,256]{3,2,1,0:T(8,128)} %get-tuple-element.31.refs_1_), channel_id=1, source_target_pairs={{0,8},{8,0},{16,24},{24,16},{1,9},{9,1},{17,25},{25,17},{2,10},{10... | collective-permute-start | bytes 1179656 | tf_op jit(solution)/shard_map/ppermute | solution.py:250
  6.0 15.7 %copy-start.3 = (f32[3,2,64,256]{3,2,1,0:T(8,128)S(1)}, f32[3,2,64,256]{3,2,1,0:T(8,128)}, u32[]{:S(2)}) copy-start(f32[3,2,64,256]{3,2,1,0:T(8,128)} %get-tuple-element.31.refs_1_) | copy-start | bytes 1179652
  6.1 14.4 %collective-permute-start.3 = (f32[2,256,256]{2,1,0:T(8,128)S(1)}, f32[2,256,256]{2,1,0:T(8,128)S(1)}, u32[]{:S(2)}, u32[]{:S(2)}) collective-permute-start(f32[2,256,256]{2,1,0:T(8,128)S(1)} %get-tuple-element.61), channel_id=1, source_target_pairs={{0,1},{1,0},{2,3},{3,2},{4,5},{5,4},{6,7},{7,6},{8,9},{9,8},{10,11... | collective-permute-start | bytes 1572872 | tf_op jit(solution)/shard_map/ppermute | solution.py:258
  7.7 14.1 %collective-permute-start.4 = (f32[2,256,256]{2,1,0:T(8,128)S(1)}, f32[2,256,256]{2,1,0:T(8,128)S(1)}, u32[]{:S(2)}, u32[]{:S(2)}) collective-permute-start(f32[2,256,256]{2,1,0:T(8,128)S(1)} %get-tuple-element.60.refs_0_), channel_id=1, source_target_pairs={{0,4},{1,5},{2,6},{3,7},{4,0},{5,1},{6,2},{7,3},{8,12},{9,13},{10,... | collective-permute-start | bytes 1572872 | tf_op jit(solution)/shard_map/ppermute | solution.py:258
  16.1 19.9 %collective-permute-start.9 = (f32[3,2,88,256]{3,2,1,0:T(8,128)S(1)}, f32[3,2,88,256]{3,2,1,0:T(8,128)S(1)}, u32[]{:S(2)}, u32[]{:S(2)}) collective-permute-start(f32[3,2,88,256]{3,2,1,0:T(8,128)S(1)} %get-tuple-element.36), channel_id=1, source_target_pairs={{0,16},{8,24},{16,0},{24,8},{1,17},{9,25},{17,1},{25,9},{2,18},{10... | collective-permute-start | bytes 1622024 | tf_op jit(solution)/shard_map/ppermute | solution.py:247
  17.9 3.9 %collective-permute-start.2 = (f32[3,2,64,256]{3,2,1,0:T(8,128)S(1)}, f32[3,2,64,256]{3,2,1,0:T(8,128)S(1)}, u32[]{:S(2)}, u32[]{:S(2)}) collective-permute-start(f32[3,2,64,256]{3,2,1,0:T(8,128)S(1)} %get-tuple-element.33.refs_2_), channel_id=1, source_target_pairs={{0,8},{8,0},{16,24},{24,16},{1,9},{9,1},{17,25},{25,17},{2,10},{10... | collective-permute-start | bytes 1179656 | tf_op jit(solution)/shard_map/ppermute | solution.py:250
  17.9 18.0 %collective-permute-start.8 = (f32[2,256,256]{2,1,0:T(8,128)S(1)}, f32[2,256,256]{2,1,0:T(8,128)S(1)}, u32[]{:S(2)}, u32[]{:S(2)}) collective-permute-start(f32[2,256,256]{2,1,0:T(8,128)S(1)} %get-tuple-element.61), channel_id=1, source_target_pairs={{0,5},{1,4},{2,7},{3,6},{4,1},{5,0},{6,3},{7,2},{8,13},{9,12},{10,... | collective-permute-start | bytes 1572872 | tf_op jit(solution)/shard_map/ppermute | solution.py:258
  23.4 12.5 %collective-permute-start.5 = (f32[2,64,256]{2,1,0:T(8,128)S(1)}, f32[2,64,256]{2,1,0:T(8,128)S(1)}, u32[]{:S(2)}, u32[]{:S(2)}) collective-permute-start(f32[2,64,256]{2,1,0:T(8,128)S(1)} %get-tuple-element.34.refs_7_.refs_0_), channel_id=1, source_target_pairs={{0,2},{1,3},{2,0},{3,1},{4,6},{5,7},{6,4},{7,5},{8,10},{9,11},{10,... | collective-permute-start | bytes 393224 | tf_op jit(solution)/shard_map/ppermute | solution.py:261
  26.1 9.9 %collective-permute-start.6 = (f32[2,64,256]{2,1,0:T(8,128)S(1)}, f32[2,64,256]{2,1,0:T(8,128)S(1)}, u32[]{:S(2)}, u32[]{:S(2)}) collective-permute-start(f32[2,64,256]{2,1,0:T(8,128)S(1)} %get-tuple-element.35), channel_id=1, source_target_pairs={{0,16},{8,24},{16,0},{24,8},{1,17},{9,25},{17,1},{25,9},{2,18},{10... | collective-permute-start | bytes 393224 | tf_op jit(solution)/shard_map/ppermute | solution.py:247
  26.6 11.1 %collective-permute-start.10 = (f32[3,2,88,256]{3,2,1,0:T(8,128)S(1)}, f32[3,2,88,256]{3,2,1,0:T(8,128)S(1)}, u32[]{:S(2)}, u32[]{:S(2)}) collective-permute-start(f32[3,2,88,256]{3,2,1,0:T(8,128)S(1)} %get-tuple-element.40.refs_1_), channel_id=1, source_target_pairs={{0,8},{8,0},{16,24},{24,16},{1,9},{9,1},{17,25},{25,17},{2,10},{10... | collective-permute-start | bytes 1622024 | tf_op jit(solution)/shard_map/ppermute | solution.py:250
  36.5 2.0 %collective-permute-start.11 = (f32[3,2,88,256]{3,2,1,0:T(8,128)S(1)}, f32[3,2,88,256]{3,2,1,0:T(8,128)S(1)}, u32[]{:S(2)}, u32[]{:S(2)}) collective-permute-start(f32[3,2,88,256]{3,2,1,0:T(8,128)S(1)} %get-tuple-element.37.refs_4_.refs_2_), channel_id=1, source_target_pairs={{0,8},{8,0},{16,24},{24,16},{1,9},{9,1},{17,25},{25,17},{2,10},{10... | collective-permute-start | bytes 1622024 | tf_op jit(solution)/shard_map/ppermute | solution.py:250
  36.6 21.3 %collective-permute-start.16 = (f32[3,2,64,256]{3,2,1,0:T(8,128)S(1)}, f32[3,2,64,256]{3,2,1,0:T(8,128)S(1)}, u32[]{:S(2)}, u32[]{:S(2)}) collective-permute-start(f32[3,2,64,256]{3,2,1,0:T(8,128)S(1)} %get-tuple-element.46), channel_id=1, source_target_pairs={{0,16},{8,24},{16,0},{24,8},{1,17},{9,25},{17,1},{25,9},{2,18},{10... | collective-permute-start | bytes 1179656 | tf_op jit(solution)/shard_map/ppermute | solution.py:247
  39.8 18.1 %collective-permute-start.13 = (f32[2,88,256]{2,1,0:T(8,128)S(1)}, f32[2,88,256]{2,1,0:T(8,128)S(1)}, u32[]{:S(2)}, u32[]{:S(2)}) collective-permute-start(f32[2,88,256]{2,1,0:T(8,128)S(1)} %get-tuple-element.41.refs_6_.refs_0_), channel_id=1, source_target_pairs={{0,2},{1,3},{2,0},{3,1},{4,6},{5,7},{6,4},{7,5},{8,10},{9,11},{10,... | collective-permute-start | bytes 540680 | tf_op jit(solution)/shard_map/ppermute | solution.py:261
  42.4 15.5 %collective-permute-start.14 = (f32[2,88,256]{2,1,0:T(8,128)S(1)}, f32[2,88,256]{2,1,0:T(8,128)S(1)}, u32[]{:S(2)}, u32[]{:S(2)}) collective-permute-start(f32[2,88,256]{2,1,0:T(8,128)S(1)} %get-tuple-element.44), channel_id=1, source_target_pairs={{0,16},{8,24},{16,0},{24,8},{1,17},{9,25},{17,1},{25,9},{2,18},{10... | collective-permute-start | bytes 540680 | tf_op jit(solution)/shard_map/ppermute | solution.py:247
  43.2 13.7 %collective-permute-start.7 = (f32[2,64,256]{2,1,0:T(8,128)S(1)}, f32[2,64,256]{2,1,0:T(8,128)S(1)}, u32[]{:S(2)}, u32[]{:S(2)}) collective-permute-start(f32[2,64,256]{2,1,0:T(8,128)S(1)} %collective-permute-done.6.refs_4_.refs_2_), channel_id=1, source_target_pairs={{0,2},{1,3},{2,0},{3,1},{4,6},{5,7},{6,4},{7,5},{8,10},{9,11},{10,... | collective-permute-start | bytes 393224 | tf_op jit(solution)/shard_map/ppermute | solution.py:261
  43.6 19.6 %collective-permute-start.17 = (f32[3,2,64,256]{3,2,1,0:T(8,128)S(1)}, f32[3,2,64,256]{3,2,1,0:T(8,128)S(1)}, u32[]{:S(2)}, u32[]{:S(2)}) collective-permute-start(f32[3,2,64,256]{3,2,1,0:T(8,128)S(1)} %get-tuple-element.45.refs_1_), channel_id=1, source_target_pairs={{0,8},{8,0},{16,24},{24,16},{1,9},{9,1},{17,25},{25,17},{2,10},{10... | collective-permute-start | bytes 1179656 | tf_op jit(solution)/shard_map/ppermute | solution.py:250
  58.3 4.9 %collective-permute-start.18 = (f32[3,2,64,256]{3,2,1,0:T(8,128)S(1)}, f32[3,2,64,256]{3,2,1,0:T(8,128)S(1)}, u32[]{:S(2)}, u32[]{:S(2)}) collective-permute-start(f32[3,2,64,256]{3,2,1,0:T(8,128)S(1)} %get-tuple-element.47.refs_2_), channel_id=1, source_target_pairs={{0,8},{8,0},{16,24},{24,16},{1,9},{9,1},{17,25},{25,17},{2,10},{10... | collective-permute-start | bytes 1179656 | tf_op jit(solution)/shard_map/ppermute | solution.py:250
  58.4 13.6 %collective-permute-start.12 = (f32[2,128,256]{2,1,0:T(8,128)S(1)}, f32[2,128,256]{2,1,0:T(8,128)S(1)}, u32[]{:S(2)}, u32[]{:S(2)}) collective-permute-start(f32[2,128,256]{2,1,0:T(8,128)S(1)} %get-tuple-element.43), channel_id=1, source_target_pairs={{0,1},{1,0},{2,3},{3,2},{4,5},{5,4},{6,7},{7,6},{8,9},{9,8},{10,11... | collective-permute-start | bytes 786440 | tf_op jit(solution)/shard_map/ppermute | solution.py:258
  59.0 12.9 %collective-permute-start.23 = (f32[3,2,40,256]{3,2,1,0:T(8,128)S(1)}, f32[3,2,40,256]{3,2,1,0:T(8,128)S(1)}, u32[]{:S(2)}, u32[]{:S(2)}) collective-permute-start(f32[3,2,40,256]{3,2,1,0:T(8,128)S(1)} %get-tuple-element.53), channel_id=1, source_target_pairs={{0,16},{8,24},{16,0},{24,8},{1,17},{9,25},{17,1},{25,9},{2,18},{10... | collective-permute-start | bytes 737288 | tf_op jit(solution)/shard_map/ppermute | solution.py:247
  59.9 9.7 %collective-permute-start.15 = (f32[2,88,256]{2,1,0:T(8,128)S(1)}, f32[2,88,256]{2,1,0:T(8,128)S(1)}, u32[]{:S(2)}, u32[]{:S(2)}) collective-permute-start(f32[2,88,256]{2,1,0:T(8,128)S(1)} %collective-permute-done.14.refs_4_.refs_2_), channel_id=1, source_target_pairs={{0,2},{1,3},{2,0},{3,1},{4,6},{5,7},{6,4},{7,5},{8,10},{9,11},{10,... | collective-permute-start | bytes 540680 | tf_op jit(solution)/shard_map/ppermute | solution.py:261
  64.4 13.0 %collective-permute-start.20 = (f32[2,64,256]{2,1,0:T(8,128)S(1)}, f32[2,64,256]{2,1,0:T(8,128)S(1)}, u32[]{:S(2)}, u32[]{:S(2)}) collective-permute-start(f32[2,64,256]{2,1,0:T(8,128)S(1)} %get-tuple-element.48.refs_6_.refs_0_), channel_id=1, source_target_pairs={{0,2},{1,3},{2,0},{3,1},{4,6},{5,7},{6,4},{7,5},{8,10},{9,11},{10,... | collective-permute-start | bytes 393224 | tf_op jit(solution)/shard_map/ppermute | solution.py:261
  64.5 12.9 %collective-permute-start.21 = (f32[2,64,256]{2,1,0:T(8,128)S(1)}, f32[2,64,256]{2,1,0:T(8,128)S(1)}, u32[]{:S(2)}, u32[]{:S(2)}) collective-permute-start(f32[2,64,256]{2,1,0:T(8,128)S(1)} %get-tuple-element.51), channel_id=1, source_target_pairs={{0,16},{8,24},{16,0},{24,8},{1,17},{9,25},{17,1},{25,9},{2,18},{10... | collective-permute-start | bytes 393224 | tf_op jit(solution)/shard_map/ppermute | solution.py:247
  69.6 10.8 %collective-permute-start.24 = (f32[3,2,40,256]{3,2,1,0:T(8,128)S(1)}, f32[3,2,40,256]{3,2,1,0:T(8,128)S(1)}, u32[]{:S(2)}, u32[]{:S(2)}) collective-permute-start(f32[3,2,40,256]{3,2,1,0:T(8,128)S(1)} %get-tuple-element.52.refs_1_), channel_id=1, source_target_pairs={{0,8},{8,0},{16,24},{24,16},{1,9},{9,1},{17,25},{25,17},{2,10},{10... | collective-permute-start | bytes 737288 | tf_op jit(solution)/shard_map/ppermute | solution.py:250
  77.3 3.0 %collective-permute-start.25 = (f32[3,2,40,256]{3,2,1,0:T(8,128)S(1)}, f32[3,2,40,256]{3,2,1,0:T(8,128)S(1)}, u32[]{:S(2)}, u32[]{:S(2)}) collective-permute-start(f32[3,2,40,256]{3,2,1,0:T(8,128)S(1)} %shard_map.69.refs_2_), channel_id=1, source_target_pairs={{0,8},{8,0},{16,24},{24,16},{1,9},{9,1},{17,25},{25,17},{2,10},{10... | collective-permute-start | bytes 737288 | tf_op jit(solution)/shard_map/ppermute | solution.py:250
  77.3 18.8 %collective-permute-start.19 = (f32[2,176,256]{2,1,0:T(8,128)S(1)}, f32[2,176,256]{2,1,0:T(8,128)S(1)}, u32[]{:S(2)}, u32[]{:S(2)}) collective-permute-start(f32[2,176,256]{2,1,0:T(8,128)S(1)} %get-tuple-element.50), channel_id=1, source_target_pairs={{0,1},{1,0},{2,3},{3,2},{4,5},{5,4},{6,7},{7,6},{8,9},{9,8},{10,11... | collective-permute-start | bytes 1081352 | tf_op jit(solution)/shard_map/ppermute | solution.py:258
  77.4 11.4 %collective-permute-start.22 = (f32[2,64,256]{2,1,0:T(8,128)S(1)}, f32[2,64,256]{2,1,0:T(8,128)S(1)}, u32[]{:S(2)}, u32[]{:S(2)}) collective-permute-start(f32[2,64,256]{2,1,0:T(8,128)S(1)} %collective-permute-done.21.refs_1_.refs_2_), channel_id=1, source_target_pairs={{0,2},{1,3},{2,0},{3,1},{4,6},{5,7},{6,4},{7,5},{8,10},{9,11},{10,... | collective-permute-start | bytes 393224 | tf_op jit(solution)/shard_map/ppermute | solution.py:261
  81.2 7.6 %collective-permute-start.26 = (f32[2,40,256]{2,1,0:T(8,128)S(1)}, f32[2,40,256]{2,1,0:T(8,128)S(1)}, u32[]{:S(2)}, u32[]{:S(2)}) collective-permute-start(f32[2,40,256]{2,1,0:T(8,128)S(1)} %get-tuple-element.55), channel_id=1, source_target_pairs={{0,16},{8,24},{16,0},{24,8},{1,17},{9,25},{17,1},{25,9},{2,18},{10... | collective-permute-start | bytes 245768 | tf_op jit(solution)/shard_map/ppermute | solution.py:247
  89.8 19.7 %collective-permute-start.27 = (f32[2,128,256]{2,1,0:T(8,128)S(1)}, f32[2,128,256]{2,1,0:T(8,128)S(1)}, u32[]{:S(2)}, u32[]{:S(2)}) collective-permute-start(f32[2,128,256]{2,1,0:T(8,128)S(1)} %get-tuple-element.57), channel_id=1, source_target_pairs={{0,1},{1,0},{2,3},{3,2},{4,5},{5,4},{6,7},{7,6},{8,9},{9,8},{10,11... | collective-permute-start | bytes 786440 | tf_op jit(solution)/shard_map/ppermute | solution.py:258
  93.2 8.2 %collective-permute-start.28 = (f32[2,40,256]{2,1,0:T(8,128)S(1)}, f32[2,40,256]{2,1,0:T(8,128)S(1)}, u32[]{:S(2)}, u32[]{:S(2)}) collective-permute-start(f32[2,40,256]{2,1,0:T(8,128)S(1)} %get-tuple-element.54.refs_6_.refs_0_), channel_id=1, source_target_pairs={{0,2},{1,3},{2,0},{3,1},{4,6},{5,7},{6,4},{7,5},{8,10},{9,11},{10,... | collective-permute-start | bytes 245768 | tf_op jit(solution)/shard_map/ppermute | solution.py:261
  93.3 9.0 %collective-permute-start.29 = (f32[2,40,256]{2,1,0:T(8,128)S(1)}, f32[2,40,256]{2,1,0:T(8,128)S(1)}, u32[]{:S(2)}, u32[]{:S(2)}) collective-permute-start(f32[2,40,256]{2,1,0:T(8,128)S(1)} %collective-permute-done.26.refs_7_.refs_2_), channel_id=1, source_target_pairs={{0,2},{1,3},{2,0},{3,1},{4,6},{5,7},{6,4},{7,5},{8,10},{9,11},{10,... | collective-permute-start | bytes 245768 | tf_op jit(solution)/shard_map/ppermute | solution.py:261
  103.5 5.9 %collective-permute-start.30 = (f32[2,80,256]{2,1,0:T(8,128)S(1)}, f32[2,80,256]{2,1,0:T(8,128)S(1)}, u32[]{:S(2)}, u32[]{:S(2)}) collective-permute-start(f32[2,80,256]{2,1,0:T(8,128)S(1)} %get-tuple-element.59), channel_id=1, source_target_pairs={{0,1},{1,0},{2,3},{3,2},{4,5},{5,4},{6,7},{7,6},{8,9},{9,8},{10,11... | collective-permute-start | bytes 491528 | tf_op jit(solution)/shard_map/ppermute | solution.py:258
  (4 other events, 50.4 us)

commit v11 on v10

--- a/solution.py
+++ b/solution.py
@@ -359,7 +359,7 @@
             last = sigmas[:1]
         if at >= 1:
             before = results[-2][1:] if len(results) > 1 else ()
-            gates = (*last, *(returned if at + 1 == len(sizes) else ()), *before)
+            gates = (*last, *((*returned, *lefts[at][1:2]) if at + 1 == len(sizes) else ()), *before)
             results.append(product(at - 1, lefts[at - 1], gates))
             last, returned = results[-1][:1], ()
 

time: 111 us -> 111 us (level)
  starting transfers between devices: 37.5 us -> 34.7 us
  waiting for transfers between devices: 57 us -> 59.6 us
    ppermute x8, starting transfers between devices: 14.9 us -> 12.2 us  [to_half(): lax.ppermute(value, 'tc', [(j, (j + group * gap) % col_parts) for j in ra...]
    ppermute x8, waiting for transfers between devices: 34.9 us -> 37.6 us  [to_half(): lax.ppermute(value, 'tc', [(j, (j + group * gap) % col_parts) for j in ra...]
where the time goes in v11:
time: 111 us
  waiting for transfers between devices  59.6 us (54%)
  starting transfers between devices  34.7 us (31%)
  Pallas kernels  15.6 us (14%)
    ppermute x8, waiting for transfers between devices, to_half(): lax.ppermute(value, 'tc', [(j, (j + group * gap) % col_parts) for j in ra...  37.6 us
    pallas_call x15, Pallas kernels, call(): pl.pallas_call(ordered, out_shape=out_shapes, in_specs=in_specs + [ANYWHE...  15.6 us
    ppermute x7, waiting for transfers between devices, to_panel(): return lax.ppermute(value, ('tr', 'tc'), moves)  15.1 us
    ppermute x7, starting transfers between devices, to_panel(): return lax.ppermute(value, ('tr', 'tc'), moves)  12.4 us
    ppermute x8, starting transfers between devices, to_half(): lax.ppermute(value, 'tc', [(j, (j + group * gap) % col_parts) for j in ra...  12.2 us
    ppermute x8, starting transfers between devices, to_chip(): return lax.ppermute(value, 'ka', moves)  10 us
    ppermute x8, waiting for transfers between devices, to_chip(): return lax.ppermute(value, 'ka', moves)  6.07 us
  transfers between devices with their start and end apart: 31, of which 13 were waited for; matrix products, arithmetic and copies ran while one was open for 0% of the time, Pallas kernels for 11%

profile of v11, /device:TPU:0, one launch (start us, length us, event | category | flops | bytes accessed | tf_op | source)
XLA Modules:
  0.0 110.9 jit_solution(12297165000130828926)
XLA Ops:
  0.7 2.3 %shard_map.59 = (f32[3,2,64,256]{3,2,1,0:T(8,128)}, f32[3,2,64,256]{3,2,1,0:T(8,128)}) custom-call(f32[2,1,512,256]{3,2,1,0:T(8,128)} %refs_8_.1, f32[2,1,512,256]{3,2,1,0:T(8,128)} %refs_1_.7, f32[2,1,512,256]{3,2,1,0:T(8,128)} %refs_2_.7), custom_call_target="tpu_custom_call" | custom-call | flops 1 | bytes 1 | tf_op jit(solution)/shard_map/pallas_call | solution.py:218
  3.0 3.0 %collective-permute-start = (f32[3,2,64,256]{3,2,1,0:T(8,128)}, f32[3,2,64,256]{3,2,1,0:T(8,128)S(1)}, u32[]{:S(2)}, u32[]{:S(2)}) collective-permute-start(f32[3,2,64,256]{3,2,1,0:T(8,128)} %get-tuple-element.32), channel_id=1, source_target_pairs={{0,16},{8,24},{16,0},{24,8},{1,17},{9,25},{17,1},{25,9},{2,18},{10... | collective-permute-start | bytes 1179656 | tf_op jit(solution)/shard_map/ppermute | solution.py:247
  6.1 1.6 %collective-permute-start.3 = (f32[2,256,256]{2,1,0:T(8,128)S(1)}, f32[2,256,256]{2,1,0:T(8,128)S(1)}, u32[]{:S(2)}, u32[]{:S(2)}) collective-permute-start(f32[2,256,256]{2,1,0:T(8,128)S(1)} %get-tuple-element.61), channel_id=1, source_target_pairs={{0,1},{1,0},{2,3},{3,2},{4,5},{5,4},{6,7},{7,6},{8,9},{9,8},{10,11... | collective-permute-start | bytes 1572872 | tf_op jit(solution)/shard_map/ppermute | solution.py:258
  7.7 1.5 %collective-permute-start.4 = (f32[2,256,256]{2,1,0:T(8,128)S(1)}, f32[2,256,256]{2,1,0:T(8,128)S(1)}, u32[]{:S(2)}, u32[]{:S(2)}) collective-permute-start(f32[2,256,256]{2,1,0:T(8,128)S(1)} %get-tuple-element.60.refs_0_), channel_id=1, source_target_pairs={{0,4},{1,5},{2,6},{3,7},{4,0},{5,1},{6,2},{7,3},{8,12},{9,13},{10,... | collective-permute-start | bytes 1572872 | tf_op jit(solution)/shard_map/ppermute | solution.py:258
  9.2 6.1 %collective-permute-done.refs_3_ = f32[3,2,64,256]{3,2,1,0:T(8,128)S(1)} collective-permute-done((f32[3,2,64,256]{3,2,1,0:T(8,128)}, f32[3,2,64,256]{3,2,1,0:T(8,128)S(1)}, u32[]{:S(2)}, u32[]{:S(2)}) %collective-permute-start) | collective-permute-done | bytes 393248 | tf_op jit(solution)/shard_map/ppermute | solution.py:247
  16.1 1.8 %collective-permute-start.9 = (f32[3,2,88,256]{3,2,1,0:T(8,128)S(1)}, f32[3,2,88,256]{3,2,1,0:T(8,128)S(1)}, u32[]{:S(2)}, u32[]{:S(2)}) collective-permute-start(f32[3,2,88,256]{3,2,1,0:T(8,128)S(1)} %get-tuple-element.36), channel_id=1, source_target_pairs={{0,16},{8,24},{16,0},{24,8},{1,17},{9,25},{17,1},{25,9},{2,18},{10... | collective-permute-start | bytes 1622024 | tf_op jit(solution)/shard_map/ppermute | solution.py:247
  17.9 2.5 %collective-permute-start.8 = (f32[2,256,256]{2,1,0:T(8,128)S(1)}, f32[2,256,256]{2,1,0:T(8,128)S(1)}, u32[]{:S(2)}, u32[]{:S(2)}) collective-permute-start(f32[2,256,256]{2,1,0:T(8,128)S(1)} %get-tuple-element.61), channel_id=1, source_target_pairs={{0,5},{1,4},{2,7},{3,6},{4,1},{5,0},{6,3},{7,2},{8,13},{9,12},{10,... | collective-permute-start | bytes 1572872 | tf_op jit(solution)/shard_map/ppermute | solution.py:258
  20.5 1.3 %collective-permute-done.4.refs_6_.refs_2_ = f32[2,256,256]{2,1,0:T(8,128)S(1)} collective-permute-done((f32[2,256,256]{2,1,0:T(8,128)S(1)}, f32[2,256,256]{2,1,0:T(8,128)S(1)}, u32[]{:S(2)}, u32[]{:S(2)}) %collective-permute-start.4) | collective-permute-done | bytes 524320 | tf_op jit(solution)/shard_map/ppermute | solution.py:258
  21.8 1.6 %shard_map.61 = (f32[2,64,256]{2,1,0:T(8,128)S(1)}, f32[2,64,256]{2,1,0:T(8,128)S(1)}) custom-call(f32[2,4]{1,0:T(2,128)S(1)} %copy-done.4, f32[3,2,64,256]{3,2,1,0:T(8,128)S(1)} %copy-done.3, f32[3,2,64,256]{3,2,1,0:T(8,128)S(1)} %get-tuple-element.33.refs_2_, f32[3,2,64,256]{3,2,1,0:T(8,128)} %collective-permute-done.1.refs_3_, ...), custom_call_target="tpu_custom_call" | custom-call | flops 1 | bytes 1 | tf_op jit(solution)/shard_map/pallas_call | solution.py:218
  23.4 2.7 %collective-permute-start.5 = (f32[2,64,256]{2,1,0:T(8,128)S(1)}, f32[2,64,256]{2,1,0:T(8,128)S(1)}, u32[]{:S(2)}, u32[]{:S(2)}) collective-permute-start(f32[2,64,256]{2,1,0:T(8,128)S(1)} %get-tuple-element.34.refs_7_.refs_0_), channel_id=1, source_target_pairs={{0,2},{1,3},{2,0},{3,1},{4,6},{5,7},{6,4},{7,5},{8,10},{9,11},{10,... | collective-permute-start | bytes 393224 | tf_op jit(solution)/shard_map/ppermute | solution.py:261
  26.6 9.3 %collective-permute-done.8.refs_6_.refs_3_ = f32[2,256,256]{2,1,0:T(8,128)S(1)} collective-permute-done((f32[2,256,256]{2,1,0:T(8,128)S(1)}, f32[2,256,256]{2,1,0:T(8,128)S(1)}, u32[]{:S(2)}, u32[]{:S(2)}) %collective-permute-start.8) | collective-permute-done | bytes 524320 | tf_op jit(solution)/shard_map/ppermute | solution.py:258
  38.5 1.3 %shard_map.64 = (f32[2,88,256]{2,1,0:T(8,128)S(1)}, f32[2,88,256]{2,1,0:T(8,128)S(1)}) custom-call(f32[2,4]{1,0:T(2,128)S(1)} %copy-done.4, f32[3,2,88,256]{3,2,1,0:T(8,128)S(1)} %get-tuple-element.40.refs_1_, f32[3,2,88,256]{3,2,1,0:T(8,128)S(1)} %get-tuple-element.37.refs_4_.refs_2_, f32[3,2,88,256]{3,2,1,0:T(8,128)S(1)} %collective-permute-done.10.refs_3_, ...), custom_call_target="tpu_custom_call" | custom-call | flops 1 | bytes 1 | tf_op jit(solution)/shard_map/pallas_call | solution.py:218
  39.8 2.6 %collective-permute-start.13 = (f32[2,88,256]{2,1,0:T(8,128)S(1)}, f32[2,88,256]{2,1,0:T(8,128)S(1)}, u32[]{:S(2)}, u32[]{:S(2)}) collective-permute-start(f32[2,88,256]{2,1,0:T(8,128)S(1)} %get-tuple-element.41.refs_6_.refs_0_), channel_id=1, source_target_pairs={{0,2},{1,3},{2,0},{3,1},{4,6},{5,7},{6,4},{7,5},{8,10},{9,11},{10,... | collective-permute-start | bytes 540680 | tf_op jit(solution)/shard_map/ppermute | solution.py:261
  43.6 13.3 %collective-permute-done.7.refs_3_ = f32[2,64,256]{2,1,0:T(8,128)S(1)} collective-permute-done((f32[2,64,256]{2,1,0:T(8,128)S(1)}, f32[2,64,256]{2,1,0:T(8,128)S(1)}, u32[]{:S(2)}, u32[]{:S(2)}) %collective-permute-start.7) | collective-permute-done | bytes 131104 | tf_op jit(solution)/shard_map/ppermute | solution.py:261
  56.9 1.0 shard_map.65
  59.9 3.4 %collective-permute-start.15 = (f32[2,88,256]{2,1,0:T(8,128)S(1)}, f32[2,88,256]{2,1,0:T(8,128)S(1)}, u32[]{:S(2)}, u32[]{:S(2)}) collective-permute-start(f32[2,88,256]{2,1,0:T(8,128)S(1)} %collective-permute-done.14.refs_4_.refs_2_), channel_id=1, source_target_pairs={{0,2},{1,3},{2,0},{3,1},{4,6},{5,7},{6,4},{7,5},{8,10},{9,11},{10,... | collective-permute-start | bytes 540680 | tf_op jit(solution)/shard_map/ppermute | solution.py:261
  63.2 1.2 %shard_map.67 = (f32[2,64,256]{2,1,0:T(8,128)S(1)}, f32[2,64,256]{2,1,0:T(8,128)S(1)}) custom-call(f32[2,4]{1,0:T(2,128)S(1)} %copy-done.4, f32[3,2,64,256]{3,2,1,0:T(8,128)S(1)} %get-tuple-element.45.refs_1_, f32[3,2,64,256]{3,2,1,0:T(8,128)S(1)} %get-tuple-element.47.refs_2_, f32[3,2,64,256]{3,2,1,0:T(8,128)S(1)} %collective-permute-done.17.refs_3_, ...), custom_call_target="tpu_custom_call" | custom-call | flops 1 | bytes 1 | tf_op jit(solution)/shard_map/pallas_call | solution.py:218
  64.5 1.3 %collective-permute-start.21 = (f32[2,64,256]{2,1,0:T(8,128)S(1)}, f32[2,64,256]{2,1,0:T(8,128)S(1)}, u32[]{:S(2)}, u32[]{:S(2)}) collective-permute-start(f32[2,64,256]{2,1,0:T(8,128)S(1)} %get-tuple-element.51), channel_id=1, source_target_pairs={{0,16},{8,24},{16,0},{24,8},{1,17},{9,25},{17,1},{25,9},{2,18},{10... | collective-permute-start | bytes 393224 | tf_op jit(solution)/shard_map/ppermute | solution.py:247
  65.7 3.8 %collective-permute-done.15.refs_3_ = f32[2,88,256]{2,1,0:T(8,128)S(1)} collective-permute-done((f32[2,88,256]{2,1,0:T(8,128)S(1)}, f32[2,88,256]{2,1,0:T(8,128)S(1)}, u32[]{:S(2)}, u32[]{:S(2)}) %collective-permute-start.15) | collective-permute-done | bytes 180256 | tf_op jit(solution)/shard_map/ppermute | solution.py:261
  69.6 1.3 %shard_map.68 = (f32[2,176,256]{2,1,0:T(8,128)S(1)}, f32[2,176,256]{2,1,0:T(8,128)S(1)}) custom-call(f32[2,88,256]{2,1,0:T(8,128)S(1)} %get-tuple-element.41.refs_6_.refs_0_, f32[2,88,256]{2,1,0:T(8,128)S(1)} %collective-permute-done.13.refs_5_.refs_1_, f32[2,88,256]{2,1,0:T(8,128)S(1)} %collective-permute-done.14.refs_4_.refs_2_, ...), custom_call_target="tpu_custom_call" | custom-call | flops 1 | bytes 1 | tf_op jit(solution)/shard_map/pallas_call | solution.py:218
  70.9 1.1 collective-permute-done.12.refs_4_.refs_9_.refs_1_
  72.0 5.4 %collective-permute-done.20.refs_2_.refs_1_ = f32[2,64,256]{2,1,0:T(8,128)S(1)} collective-permute-done((f32[2,64,256]{2,1,0:T(8,128)S(1)}, f32[2,64,256]{2,1,0:T(8,128)S(1)}, u32[]{:S(2)}, u32[]{:S(2)}) %collective-permute-start.20) | collective-permute-done | bytes 131104 | tf_op jit(solution)/shard_map/ppermute | solution.py:261
  77.4 2.9 %collective-permute-start.22 = (f32[2,64,256]{2,1,0:T(8,128)S(1)}, f32[2,64,256]{2,1,0:T(8,128)S(1)}, u32[]{:S(2)}, u32[]{:S(2)}) collective-permute-start(f32[2,64,256]{2,1,0:T(8,128)S(1)} %collective-permute-done.21.refs_1_.refs_2_), channel_id=1, source_target_pairs={{0,2},{1,3},{2,0},{3,1},{4,6},{5,7},{6,4},{7,5},{8,10},{9,11},{10,... | collective-permute-start | bytes 393224 | tf_op jit(solution)/shard_map/ppermute | solution.py:261
  81.2 1.3 %collective-permute-start.26 = (f32[2,40,256]{2,1,0:T(8,128)S(1)}, f32[2,40,256]{2,1,0:T(8,128)S(1)}, u32[]{:S(2)}, u32[]{:S(2)}) collective-permute-start(f32[2,40,256]{2,1,0:T(8,128)S(1)} %get-tuple-element.55), channel_id=1, source_target_pairs={{0,16},{8,24},{16,0},{24,8},{1,17},{9,25},{17,1},{25,9},{2,18},{10... | collective-permute-start | bytes 245768 | tf_op jit(solution)/shard_map/ppermute | solution.py:247
  82.6 6.4 %collective-permute-done.22.refs_3_ = f32[2,64,256]{2,1,0:T(8,128)S(1)} collective-permute-done((f32[2,64,256]{2,1,0:T(8,128)S(1)}, f32[2,64,256]{2,1,0:T(8,128)S(1)}, u32[]{:S(2)}, u32[]{:S(2)}) %collective-permute-start.22) | collective-permute-done | bytes 131104 | tf_op jit(solution)/shard_map/ppermute | solution.py:261
  89.0 1.5 %collective-permute-done.27.refs_8_.refs_1_ = f32[2,40,256]{2,1,0:T(8,128)S(1)} collective-permute-done((f32[2,40,256]{2,1,0:T(8,128)S(1)}, f32[2,40,256]{2,1,0:T(8,128)S(1)}, u32[]{:S(2)}, u32[]{:S(2)}) %collective-permute-start.27) | collective-permute-done | bytes 81952 | tf_op jit(solution)/shard_map/ppermute | solution.py:261
  91.5 3.4 %collective-permute-start.28 = (f32[2,128,256]{2,1,0:T(8,128)S(1)}, f32[2,128,256]{2,1,0:T(8,128)S(1)}, u32[]{:S(2)}, u32[]{:S(2)}) collective-permute-start(f32[2,128,256]{2,1,0:T(8,128)S(1)} %get-tuple-element.57), channel_id=1, source_target_pairs={{0,1},{1,0},{2,3},{3,2},{4,5},{5,4},{6,7},{7,6},{8,9},{9,8},{10,11... | collective-permute-start | bytes 786440 | tf_op jit(solution)/shard_map/ppermute | solution.py:258
  95.1 7.3 %collective-permute-done.29.refs_3_ = f32[2,40,256]{2,1,0:T(8,128)S(1)} collective-permute-done((f32[2,40,256]{2,1,0:T(8,128)S(1)}, f32[2,40,256]{2,1,0:T(8,128)S(1)}, u32[]{:S(2)}, u32[]{:S(2)}) %collective-permute-start.29) | collective-permute-done | bytes 81952 | tf_op jit(solution)/shard_map/ppermute | solution.py:261
  102.3 1.2 %shard_map.72 = (f32[2,80,256]{2,1,0:T(8,128)S(1)}, f32[2,80,256]{2,1,0:T(8,128)S(1)}) custom-call(f32[2,40,256]{2,1,0:T(8,128)S(1)} %get-tuple-element.54.refs_6_.refs_0_, f32[2,40,256]{2,1,0:T(8,128)S(1)} %collective-permute-done.27.refs_8_.refs_1_, f32[2,40,256]{2,1,0:T(8,128)S(1)} %collective-permute-done.26.refs_7_.refs_2_, ...), custom_call_target="tpu_custom_call" | custom-call | flops 1 | bytes 1 | tf_op jit(solution)/shard_map/pallas_call | solution.py:218
  103.5 2.6 %collective-permute-start.30 = (f32[2,80,256]{2,1,0:T(8,128)S(1)}, f32[2,80,256]{2,1,0:T(8,128)S(1)}, u32[]{:S(2)}, u32[]{:S(2)}) collective-permute-start(f32[2,80,256]{2,1,0:T(8,128)S(1)} %get-tuple-element.59), channel_id=1, source_target_pairs={{0,1},{1,0},{2,3},{3,2},{4,5},{5,4},{6,7},{7,6},{8,9},{9,8},{10,11... | collective-permute-start | bytes 491528 | tf_op jit(solution)/shard_map/ppermute | solution.py:258
  106.1 3.3 %collective-permute-done.30.refs_7_ = f32[2,80,256]{2,1,0:T(8,128)S(1)} collective-permute-done((f32[2,80,256]{2,1,0:T(8,128)S(1)}, f32[2,80,256]{2,1,0:T(8,128)S(1)}, u32[]{:S(2)}, u32[]{:S(2)}) %collective-permute-start.30) | collective-permute-done | bytes 163872 | tf_op jit(solution)/shard_map/ppermute | solution.py:258
  109.4 1.5 %shard_map.73 = (f32[2,1,512,256]{3,2,1,0:T(8,128)}, f32[2,1,512,256]{3,2,1,0:T(8,128)}) custom-call(f32[2,128,256]{2,1,0:T(8,128)S(1)} %get-tuple-element.42.refs_6_.refs_0_, f32[2,128,256]{2,1,0:T(8,128)S(1)} %collective-permute-done.12.refs_4_.refs_9_.refs_1_, f32[2,176,256]{2,1,0:T(8,128)S(1)} %get-tuple-element.49.refs_3_.refs_2_, ...), custom_call_target="tpu_custom_call" | custom-call | flops 1 | bytes 1 | tf_op jit(solution)/shard_map/pallas_call | solution.py:218
  (56 shorter events, 9.5 us)
Async XLA Ops:
  3.0 12.3 %collective-permute-start = (f32[3,2,64,256]{3,2,1,0:T(8,128)}, f32[3,2,64,256]{3,2,1,0:T(8,128)S(1)}, u32[]{:S(2)}, u32[]{:S(2)}) collective-permute-start(f32[3,2,64,256]{3,2,1,0:T(8,128)} %get-tuple-element.32), channel_id=1, source_target_pairs={{0,16},{8,24},{16,0},{24,8},{1,17},{9,25},{17,1},{25,9},{2,18},{10... | collective-permute-start | bytes 1179656 | tf_op jit(solution)/shard_map/ppermute | solution.py:247
  6.0 11.9 %collective-permute-start.1 = (f32[3,2,64,256]{3,2,1,0:T(8,128)}, f32[3,2,64,256]{3,2,1,0:T(8,128)}, u32[]{:S(2)}, u32[]{:S(2)}) collective-permute-start(f32[3,2,64,256]{3,2,1,0:T(8,128)} %get-tuple-element.31.refs_1_), channel_id=1, source_target_pairs={{0,8},{8,0},{16,24},{24,16},{1,9},{9,1},{17,25},{25,17},{2,10},{10... | collective-permute-start | bytes 1179656 | tf_op jit(solution)/shard_map/ppermute | solution.py:250
  6.0 15.7 %copy-start.3 = (f32[3,2,64,256]{3,2,1,0:T(8,128)S(1)}, f32[3,2,64,256]{3,2,1,0:T(8,128)}, u32[]{:S(2)}) copy-start(f32[3,2,64,256]{3,2,1,0:T(8,128)} %get-tuple-element.31.refs_1_) | copy-start | bytes 1179652
  6.1 14.4 %collective-permute-start.3 = (f32[2,256,256]{2,1,0:T(8,128)S(1)}, f32[2,256,256]{2,1,0:T(8,128)S(1)}, u32[]{:S(2)}, u32[]{:S(2)}) collective-permute-start(f32[2,256,256]{2,1,0:T(8,128)S(1)} %get-tuple-element.61), channel_id=1, source_target_pairs={{0,1},{1,0},{2,3},{3,2},{4,5},{5,4},{6,7},{7,6},{8,9},{9,8},{10,11... | collective-permute-start | bytes 1572872 | tf_op jit(solution)/shard_map/ppermute | solution.py:258
  7.7 14.1 %collective-permute-start.4 = (f32[2,256,256]{2,1,0:T(8,128)S(1)}, f32[2,256,256]{2,1,0:T(8,128)S(1)}, u32[]{:S(2)}, u32[]{:S(2)}) collective-permute-start(f32[2,256,256]{2,1,0:T(8,128)S(1)} %get-tuple-element.60.refs_0_), channel_id=1, source_target_pairs={{0,4},{1,5},{2,6},{3,7},{4,0},{5,1},{6,2},{7,3},{8,12},{9,13},{10,... | collective-permute-start | bytes 1572872 | tf_op jit(solution)/shard_map/ppermute | solution.py:258
  16.1 19.9 %collective-permute-start.9 = (f32[3,2,88,256]{3,2,1,0:T(8,128)S(1)}, f32[3,2,88,256]{3,2,1,0:T(8,128)S(1)}, u32[]{:S(2)}, u32[]{:S(2)}) collective-permute-start(f32[3,2,88,256]{3,2,1,0:T(8,128)S(1)} %get-tuple-element.36), channel_id=1, source_target_pairs={{0,16},{8,24},{16,0},{24,8},{1,17},{9,25},{17,1},{25,9},{2,18},{10... | collective-permute-start | bytes 1622024 | tf_op jit(solution)/shard_map/ppermute | solution.py:247
  17.9 3.9 %collective-permute-start.2 = (f32[3,2,64,256]{3,2,1,0:T(8,128)S(1)}, f32[3,2,64,256]{3,2,1,0:T(8,128)S(1)}, u32[]{:S(2)}, u32[]{:S(2)}) collective-permute-start(f32[3,2,64,256]{3,2,1,0:T(8,128)S(1)} %get-tuple-element.33.refs_2_), channel_id=1, source_target_pairs={{0,8},{8,0},{16,24},{24,16},{1,9},{9,1},{17,25},{25,17},{2,10},{10... | collective-permute-start | bytes 1179656 | tf_op jit(solution)/shard_map/ppermute | solution.py:250
  17.9 18.0 %collective-permute-start.8 = (f32[2,256,256]{2,1,0:T(8,128)S(1)}, f32[2,256,256]{2,1,0:T(8,128)S(1)}, u32[]{:S(2)}, u32[]{:S(2)}) collective-permute-start(f32[2,256,256]{2,1,0:T(8,128)S(1)} %get-tuple-element.61), channel_id=1, source_target_pairs={{0,5},{1,4},{2,7},{3,6},{4,1},{5,0},{6,3},{7,2},{8,13},{9,12},{10,... | collective-permute-start | bytes 1572872 | tf_op jit(solution)/shard_map/ppermute | solution.py:258
  23.4 12.5 %collective-permute-start.5 = (f32[2,64,256]{2,1,0:T(8,128)S(1)}, f32[2,64,256]{2,1,0:T(8,128)S(1)}, u32[]{:S(2)}, u32[]{:S(2)}) collective-permute-start(f32[2,64,256]{2,1,0:T(8,128)S(1)} %get-tuple-element.34.refs_7_.refs_0_), channel_id=1, source_target_pairs={{0,2},{1,3},{2,0},{3,1},{4,6},{5,7},{6,4},{7,5},{8,10},{9,11},{10,... | collective-permute-start | bytes 393224 | tf_op jit(solution)/shard_map/ppermute | solution.py:261
  26.1 9.9 %collective-permute-start.6 = (f32[2,64,256]{2,1,0:T(8,128)S(1)}, f32[2,64,256]{2,1,0:T(8,128)S(1)}, u32[]{:S(2)}, u32[]{:S(2)}) collective-permute-start(f32[2,64,256]{2,1,0:T(8,128)S(1)} %get-tuple-element.35), channel_id=1, source_target_pairs={{0,16},{8,24},{16,0},{24,8},{1,17},{9,25},{17,1},{25,9},{2,18},{10... | collective-permute-start | bytes 393224 | tf_op jit(solution)/shard_map/ppermute | solution.py:247
  26.6 11.1 %collective-permute-start.10 = (f32[3,2,88,256]{3,2,1,0:T(8,128)S(1)}, f32[3,2,88,256]{3,2,1,0:T(8,128)S(1)}, u32[]{:S(2)}, u32[]{:S(2)}) collective-permute-start(f32[3,2,88,256]{3,2,1,0:T(8,128)S(1)} %get-tuple-element.40.refs_1_), channel_id=1, source_target_pairs={{0,8},{8,0},{16,24},{24,16},{1,9},{9,1},{17,25},{25,17},{2,10},{10... | collective-permute-start | bytes 1622024 | tf_op jit(solution)/shard_map/ppermute | solution.py:250
  36.5 2.0 %collective-permute-start.11 = (f32[3,2,88,256]{3,2,1,0:T(8,128)S(1)}, f32[3,2,88,256]{3,2,1,0:T(8,128)S(1)}, u32[]{:S(2)}, u32[]{:S(2)}) collective-permute-start(f32[3,2,88,256]{3,2,1,0:T(8,128)S(1)} %get-tuple-element.37.refs_4_.refs_2_), channel_id=1, source_target_pairs={{0,8},{8,0},{16,24},{24,16},{1,9},{9,1},{17,25},{25,17},{2,10},{10... | collective-permute-start | bytes 1622024 | tf_op jit(solution)/shard_map/ppermute | solution.py:250
  36.6 21.3 %collective-permute-start.16 = (f32[3,2,64,256]{3,2,1,0:T(8,128)S(1)}, f32[3,2,64,256]{3,2,1,0:T(8,128)S(1)}, u32[]{:S(2)}, u32[]{:S(2)}) collective-permute-start(f32[3,2,64,256]{3,2,1,0:T(8,128)S(1)} %get-tuple-element.46), channel_id=1, source_target_pairs={{0,16},{8,24},{16,0},{24,8},{1,17},{9,25},{17,1},{25,9},{2,18},{10... | collective-permute-start | bytes 1179656 | tf_op jit(solution)/shard_map/ppermute | solution.py:247
  39.8 18.1 %collective-permute-start.13 = (f32[2,88,256]{2,1,0:T(8,128)S(1)}, f32[2,88,256]{2,1,0:T(8,128)S(1)}, u32[]{:S(2)}, u32[]{:S(2)}) collective-permute-start(f32[2,88,256]{2,1,0:T(8,128)S(1)} %get-tuple-element.41.refs_6_.refs_0_), channel_id=1, source_target_pairs={{0,2},{1,3},{2,0},{3,1},{4,6},{5,7},{6,4},{7,5},{8,10},{9,11},{10,... | collective-permute-start | bytes 540680 | tf_op jit(solution)/shard_map/ppermute | solution.py:261
  42.4 15.5 %collective-permute-start.14 = (f32[2,88,256]{2,1,0:T(8,128)S(1)}, f32[2,88,256]{2,1,0:T(8,128)S(1)}, u32[]{:S(2)}, u32[]{:S(2)}) collective-permute-start(f32[2,88,256]{2,1,0:T(8,128)S(1)} %get-tuple-element.44), channel_id=1, source_target_pairs={{0,16},{8,24},{16,0},{24,8},{1,17},{9,25},{17,1},{25,9},{2,18},{10... | collective-permute-start | bytes 540680 | tf_op jit(solution)/shard_map/ppermute | solution.py:247
  43.2 13.7 %collective-permute-start.7 = (f32[2,64,256]{2,1,0:T(8,128)S(1)}, f32[2,64,256]{2,1,0:T(8,128)S(1)}, u32[]{:S(2)}, u32[]{:S(2)}) collective-permute-start(f32[2,64,256]{2,1,0:T(8,128)S(1)} %collective-permute-done.6.refs_4_.refs_2_), channel_id=1, source_target_pairs={{0,2},{1,3},{2,0},{3,1},{4,6},{5,7},{6,4},{7,5},{8,10},{9,11},{10,... | collective-permute-start | bytes 393224 | tf_op jit(solution)/shard_map/ppermute | solution.py:261
  43.6 19.6 %collective-permute-start.17 = (f32[3,2,64,256]{3,2,1,0:T(8,128)S(1)}, f32[3,2,64,256]{3,2,1,0:T(8,128)S(1)}, u32[]{:S(2)}, u32[]{:S(2)}) collective-permute-start(f32[3,2,64,256]{3,2,1,0:T(8,128)S(1)} %get-tuple-element.45.refs_1_), channel_id=1, source_target_pairs={{0,8},{8,0},{16,24},{24,16},{1,9},{9,1},{17,25},{25,17},{2,10},{10... | collective-permute-start | bytes 1179656 | tf_op jit(solution)/shard_map/ppermute | solution.py:250
  58.3 4.9 %collective-permute-start.18 = (f32[3,2,64,256]{3,2,1,0:T(8,128)S(1)}, f32[3,2,64,256]{3,2,1,0:T(8,128)S(1)}, u32[]{:S(2)}, u32[]{:S(2)}) collective-permute-start(f32[3,2,64,256]{3,2,1,0:T(8,128)S(1)} %get-tuple-element.47.refs_2_), channel_id=1, source_target_pairs={{0,8},{8,0},{16,24},{24,16},{1,9},{9,1},{17,25},{25,17},{2,10},{10... | collective-permute-start | bytes 1179656 | tf_op jit(solution)/shard_map/ppermute | solution.py:250
  58.4 13.6 %collective-permute-start.12 = (f32[2,128,256]{2,1,0:T(8,128)S(1)}, f32[2,128,256]{2,1,0:T(8,128)S(1)}, u32[]{:S(2)}, u32[]{:S(2)}) collective-permute-start(f32[2,128,256]{2,1,0:T(8,128)S(1)} %get-tuple-element.43), channel_id=1, source_target_pairs={{0,1},{1,0},{2,3},{3,2},{4,5},{5,4},{6,7},{7,6},{8,9},{9,8},{10,11... | collective-permute-start | bytes 786440 | tf_op jit(solution)/shard_map/ppermute | solution.py:258
  59.0 12.9 %collective-permute-start.23 = (f32[3,2,40,256]{3,2,1,0:T(8,128)S(1)}, f32[3,2,40,256]{3,2,1,0:T(8,128)S(1)}, u32[]{:S(2)}, u32[]{:S(2)}) collective-permute-start(f32[3,2,40,256]{3,2,1,0:T(8,128)S(1)} %get-tuple-element.53), channel_id=1, source_target_pairs={{0,16},{8,24},{16,0},{24,8},{1,17},{9,25},{17,1},{25,9},{2,18},{10... | collective-permute-start | bytes 737288 | tf_op jit(solution)/shard_map/ppermute | solution.py:247
  59.9 9.7 %collective-permute-start.15 = (f32[2,88,256]{2,1,0:T(8,128)S(1)}, f32[2,88,256]{2,1,0:T(8,128)S(1)}, u32[]{:S(2)}, u32[]{:S(2)}) collective-permute-start(f32[2,88,256]{2,1,0:T(8,128)S(1)} %collective-permute-done.14.refs_4_.refs_2_), channel_id=1, source_target_pairs={{0,2},{1,3},{2,0},{3,1},{4,6},{5,7},{6,4},{7,5},{8,10},{9,11},{10,... | collective-permute-start | bytes 540680 | tf_op jit(solution)/shard_map/ppermute | solution.py:261
  64.4 13.0 %collective-permute-start.20 = (f32[2,64,256]{2,1,0:T(8,128)S(1)}, f32[2,64,256]{2,1,0:T(8,128)S(1)}, u32[]{:S(2)}, u32[]{:S(2)}) collective-permute-start(f32[2,64,256]{2,1,0:T(8,128)S(1)} %get-tuple-element.48.refs_6_.refs_0_), channel_id=1, source_target_pairs={{0,2},{1,3},{2,0},{3,1},{4,6},{5,7},{6,4},{7,5},{8,10},{9,11},{10,... | collective-permute-start | bytes 393224 | tf_op jit(solution)/shard_map/ppermute | solution.py:261
  64.5 12.9 %collective-permute-start.21 = (f32[2,64,256]{2,1,0:T(8,128)S(1)}, f32[2,64,256]{2,1,0:T(8,128)S(1)}, u32[]{:S(2)}, u32[]{:S(2)}) collective-permute-start(f32[2,64,256]{2,1,0:T(8,128)S(1)} %get-tuple-element.51), channel_id=1, source_target_pairs={{0,16},{8,24},{16,0},{24,8},{1,17},{9,25},{17,1},{25,9},{2,18},{10... | collective-permute-start | bytes 393224 | tf_op jit(solution)/shard_map/ppermute | solution.py:247
  69.6 10.8 %collective-permute-start.24 = (f32[3,2,40,256]{3,2,1,0:T(8,128)S(1)}, f32[3,2,40,256]{3,2,1,0:T(8,128)S(1)}, u32[]{:S(2)}, u32[]{:S(2)}) collective-permute-start(f32[3,2,40,256]{3,2,1,0:T(8,128)S(1)} %get-tuple-element.52.refs_1_), channel_id=1, source_target_pairs={{0,8},{8,0},{16,24},{24,16},{1,9},{9,1},{17,25},{25,17},{2,10},{10... | collective-permute-start | bytes 737288 | tf_op jit(solution)/shard_map/ppermute | solution.py:250
  77.3 3.0 %collective-permute-start.25 = (f32[3,2,40,256]{3,2,1,0:T(8,128)S(1)}, f32[3,2,40,256]{3,2,1,0:T(8,128)S(1)}, u32[]{:S(2)}, u32[]{:S(2)}) collective-permute-start(f32[3,2,40,256]{3,2,1,0:T(8,128)S(1)} %shard_map.69.refs_2_), channel_id=1, source_target_pairs={{0,8},{8,0},{16,24},{24,16},{1,9},{9,1},{17,25},{25,17},{2,10},{10... | collective-permute-start | bytes 737288 | tf_op jit(solution)/shard_map/ppermute | solution.py:250
  77.3 17.7 %collective-permute-start.19 = (f32[2,176,256]{2,1,0:T(8,128)S(1)}, f32[2,176,256]{2,1,0:T(8,128)S(1)}, u32[]{:S(2)}, u32[]{:S(2)}) collective-permute-start(f32[2,176,256]{2,1,0:T(8,128)S(1)} %get-tuple-element.50), channel_id=1, source_target_pairs={{0,1},{1,0},{2,3},{3,2},{4,5},{5,4},{6,7},{7,6},{8,9},{9,8},{10,11... | collective-permute-start | bytes 1081352 | tf_op jit(solution)/shard_map/ppermute | solution.py:258
  77.4 11.6 %collective-permute-start.22 = (f32[2,64,256]{2,1,0:T(8,128)S(1)}, f32[2,64,256]{2,1,0:T(8,128)S(1)}, u32[]{:S(2)}, u32[]{:S(2)}) collective-permute-start(f32[2,64,256]{2,1,0:T(8,128)S(1)} %collective-permute-done.21.refs_1_.refs_2_), channel_id=1, source_target_pairs={{0,2},{1,3},{2,0},{3,1},{4,6},{5,7},{6,4},{7,5},{8,10},{9,11},{10,... | collective-permute-start | bytes 393224 | tf_op jit(solution)/shard_map/ppermute | solution.py:261
  81.2 7.8 %collective-permute-start.26 = (f32[2,40,256]{2,1,0:T(8,128)S(1)}, f32[2,40,256]{2,1,0:T(8,128)S(1)}, u32[]{:S(2)}, u32[]{:S(2)}) collective-permute-start(f32[2,40,256]{2,1,0:T(8,128)S(1)} %get-tuple-element.55), channel_id=1, source_target_pairs={{0,16},{8,24},{16,0},{24,8},{1,17},{9,25},{17,1},{25,9},{2,18},{10... | collective-permute-start | bytes 245768 | tf_op jit(solution)/shard_map/ppermute | solution.py:247
  82.5 8.0 %collective-permute-start.27 = (f32[2,40,256]{2,1,0:T(8,128)S(1)}, f32[2,40,256]{2,1,0:T(8,128)S(1)}, u32[]{:S(2)}, u32[]{:S(2)}) collective-permute-start(f32[2,40,256]{2,1,0:T(8,128)S(1)} %get-tuple-element.54.refs_6_.refs_0_), channel_id=1, source_target_pairs={{0,2},{1,3},{2,0},{3,1},{4,6},{5,7},{6,4},{7,5},{8,10},{9,11},{10,... | collective-permute-start | bytes 245768 | tf_op jit(solution)/shard_map/ppermute | solution.py:261
  91.5 17.9 %collective-permute-start.28 = (f32[2,128,256]{2,1,0:T(8,128)S(1)}, f32[2,128,256]{2,1,0:T(8,128)S(1)}, u32[]{:S(2)}, u32[]{:S(2)}) collective-permute-start(f32[2,128,256]{2,1,0:T(8,128)S(1)} %get-tuple-element.57), channel_id=1, source_target_pairs={{0,1},{1,0},{2,3},{3,2},{4,5},{5,4},{6,7},{7,6},{8,9},{9,8},{10,11... | collective-permute-start | bytes 786440 | tf_op jit(solution)/shard_map/ppermute | solution.py:258
  95.0 7.4 %collective-permute-start.29 = (f32[2,40,256]{2,1,0:T(8,128)S(1)}, f32[2,40,256]{2,1,0:T(8,128)S(1)}, u32[]{:S(2)}, u32[]{:S(2)}) collective-permute-start(f32[2,40,256]{2,1,0:T(8,128)S(1)} %collective-permute-done.26.refs_7_.refs_2_), channel_id=1, source_target_pairs={{0,2},{1,3},{2,0},{3,1},{4,6},{5,7},{6,4},{7,5},{8,10},{9,11},{10,... | collective-permute-start | bytes 245768 | tf_op jit(solution)/shard_map/ppermute | solution.py:261
  103.5 5.9 %collective-permute-start.30 = (f32[2,80,256]{2,1,0:T(8,128)S(1)}, f32[2,80,256]{2,1,0:T(8,128)S(1)}, u32[]{:S(2)}, u32[]{:S(2)}) collective-permute-start(f32[2,80,256]{2,1,0:T(8,128)S(1)} %get-tuple-element.59), channel_id=1, source_target_pairs={{0,1},{1,0},{2,3},{3,2},{4,5},{5,4},{6,7},{7,6},{8,9},{9,8},{10,11... | collective-permute-start | bytes 491528 | tf_op jit(solution)/shard_map/ppermute | solution.py:258
  (4 other events, 50.4 us)

commit v12 on v11

--- a/solution.py
+++ b/solution.py
@@ -355,7 +355,7 @@
             returned = owned[1:2]
             arrived = (*returned, *lefts[at][1:2])
             if at == 0:
-                arrived += tuple(panels[group + 1 :])
+                arrived += (*panels[group + 1 :], *lefts[at][row_parts + 1 : 2 * row_parts])
             last = sigmas[:1]
         if at >= 1:
             before = results[-2][1:] if len(results) > 1 else ()

time: 111 us -> 114 us (1.027)
  starting transfers between devices: 34.7 us -> 44.1 us
  waiting for transfers between devices: 59.6 us -> 53 us
    ppermute x8, waiting for transfers between devices: 37.6 us -> 24.7 us  [to_half(): lax.ppermute(value, 'tc', [(j, (j + group * gap) % col_parts) for j in ra...]
    ppermute x8, starting transfers between devices: 12.2 us -> 20.4 us  [to_half(): lax.ppermute(value, 'tc', [(j, (j + group * gap) % col_parts) for j in ra...]
    ppermute x8, waiting for transfers between devices: 6.07 us -> 13 us  [to_chip(): return lax.ppermute(value, 'ka', moves)]
  transfers between devices with their start and end apart: 31 -> 31, of which waited for: 13 -> 15; matrix products, arithmetic and copies ran while one was open for 0% -> 0% of each run, Pallas kernels for 11% -> 10%
where the time goes in v12:
time: 114 us; the launch traced here: 113 us
  waiting for transfers between devices  53 us (46%)
  starting transfers between devices  44.1 us (39%)
  Pallas kernels  15.5 us (14%)
    ppermute x8, waiting for transfers between devices, to_half(): lax.ppermute(value, 'tc', [(j, (j + group * gap) % col_parts) for j in ra...  24.7 us
    ppermute x8, starting transfers between devices, to_half(): lax.ppermute(value, 'tc', [(j, (j + group * gap) % col_parts) for j in ra...  20.4 us
    pallas_call x15, Pallas kernels, call(): pl.pallas_call(ordered, out_shape=out_shapes, in_specs=in_specs + [ANYWHE...  15.5 us
    ppermute x7, waiting for transfers between devices, to_panel(): return lax.ppermute(value, ('tr', 'tc'), moves)  14.5 us
    ppermute x8, waiting for transfers between devices, to_chip(): return lax.ppermute(value, 'ka', moves)  13 us
    ppermute x7, starting transfers between devices, to_panel(): return lax.ppermute(value, ('tr', 'tc'), moves)  12.7 us
    ppermute x8, starting transfers between devices, to_chip(): return lax.ppermute(value, 'ka', moves)  10.7 us
  transfers between devices with their start and end apart: 31, of which 15 were waited for; matrix products, arithmetic and copies ran while one was open for 0% of the time, Pallas kernels for 10%

profile of v12, /device:TPU:0, one launch (start us, length us, event | category | flops | bytes accessed | tf_op | source)
XLA Modules:
  0.0 113.4 jit_solution(9171414645093701029)
XLA Ops:
  0.7 2.3 %shard_map.59 = (f32[3,2,64,256]{3,2,1,0:T(8,128)}, f32[3,2,64,256]{3,2,1,0:T(8,128)}) custom-call(f32[2,1,512,256]{3,2,1,0:T(8,128)} %refs_8_.1, f32[2,1,512,256]{3,2,1,0:T(8,128)} %refs_1_.7, f32[2,1,512,256]{3,2,1,0:T(8,128)} %refs_2_.7), custom_call_target="tpu_custom_call" | custom-call | flops 1 | bytes 1 | tf_op jit(solution)/shard_map/pallas_call | solution.py:218
  3.0 3.0 %collective-permute-start = (f32[3,2,64,256]{3,2,1,0:T(8,128)}, f32[3,2,64,256]{3,2,1,0:T(8,128)S(1)}, u32[]{:S(2)}, u32[]{:S(2)}) collective-permute-start(f32[3,2,64,256]{3,2,1,0:T(8,128)} %get-tuple-element.32), channel_id=1, source_target_pairs={{0,16},{8,24},{16,0},{24,8},{1,17},{9,25},{17,1},{25,9},{2,18},{10... | collective-permute-start | bytes 1179656 | tf_op jit(solution)/shard_map/ppermute | solution.py:247
  6.1 1.6 %collective-permute-start.3 = (f32[2,256,256]{2,1,0:T(8,128)S(1)}, f32[2,256,256]{2,1,0:T(8,128)S(1)}, u32[]{:S(2)}, u32[]{:S(2)}) collective-permute-start(f32[2,256,256]{2,1,0:T(8,128)S(1)} %get-tuple-element.61), channel_id=1, source_target_pairs={{0,1},{1,0},{2,3},{3,2},{4,5},{5,4},{6,7},{7,6},{8,9},{9,8},{10,11... | collective-permute-start | bytes 1572872 | tf_op jit(solution)/shard_map/ppermute | solution.py:258
  7.7 1.5 %collective-permute-start.4 = (f32[2,256,256]{2,1,0:T(8,128)S(1)}, f32[2,256,256]{2,1,0:T(8,128)S(1)}, u32[]{:S(2)}, u32[]{:S(2)}) collective-permute-start(f32[2,256,256]{2,1,0:T(8,128)S(1)} %get-tuple-element.60.refs_0_), channel_id=1, source_target_pairs={{0,4},{1,5},{2,6},{3,7},{4,0},{5,1},{6,2},{7,3},{8,12},{9,13},{10,... | collective-permute-start | bytes 1572872 | tf_op jit(solution)/shard_map/ppermute | solution.py:258
  9.2 6.1 %collective-permute-done.refs_3_ = f32[3,2,64,256]{3,2,1,0:T(8,128)S(1)} collective-permute-done((f32[3,2,64,256]{3,2,1,0:T(8,128)}, f32[3,2,64,256]{3,2,1,0:T(8,128)S(1)}, u32[]{:S(2)}, u32[]{:S(2)}) %collective-permute-start) | collective-permute-done | bytes 393248 | tf_op jit(solution)/shard_map/ppermute | solution.py:247
  16.1 1.8 %collective-permute-start.9 = (f32[3,2,88,256]{3,2,1,0:T(8,128)S(1)}, f32[3,2,88,256]{3,2,1,0:T(8,128)S(1)}, u32[]{:S(2)}, u32[]{:S(2)}) collective-permute-start(f32[3,2,88,256]{3,2,1,0:T(8,128)S(1)} %get-tuple-element.36), channel_id=1, source_target_pairs={{0,16},{8,24},{16,0},{24,8},{1,17},{9,25},{17,1},{25,9},{2,18},{10... | collective-permute-start | bytes 1622024 | tf_op jit(solution)/shard_map/ppermute | solution.py:247
  17.9 2.5 %collective-permute-start.8 = (f32[2,256,256]{2,1,0:T(8,128)S(1)}, f32[2,256,256]{2,1,0:T(8,128)S(1)}, u32[]{:S(2)}, u32[]{:S(2)}) collective-permute-start(f32[2,256,256]{2,1,0:T(8,128)S(1)} %get-tuple-element.61), channel_id=1, source_target_pairs={{0,5},{1,4},{2,7},{3,6},{4,1},{5,0},{6,3},{7,2},{8,13},{9,12},{10,... | collective-permute-start | bytes 1572872 | tf_op jit(solution)/shard_map/ppermute | solution.py:258
  20.5 7.3 %collective-permute-done.4.refs_6_.refs_2_ = f32[2,256,256]{2,1,0:T(8,128)S(1)} collective-permute-done((f32[2,256,256]{2,1,0:T(8,128)S(1)}, f32[2,256,256]{2,1,0:T(8,128)S(1)}, u32[]{:S(2)}, u32[]{:S(2)}) %collective-permute-start.4) | collective-permute-done | bytes 524320 | tf_op jit(solution)/shard_map/ppermute | solution.py:258
  27.8 1.6 %shard_map.61 = (f32[2,64,256]{2,1,0:T(8,128)S(1)}, f32[2,64,256]{2,1,0:T(8,128)S(1)}) custom-call(f32[2,4]{1,0:T(2,128)S(1)} %copy-done.4, f32[3,2,64,256]{3,2,1,0:T(8,128)S(1)} %copy-done.3, f32[3,2,64,256]{3,2,1,0:T(8,128)S(1)} %get-tuple-element.33.refs_2_, f32[3,2,64,256]{3,2,1,0:T(8,128)} %collective-permute-done.1.refs_3_, ...), custom_call_target="tpu_custom_call" | custom-call | flops 1 | bytes 1 | tf_op jit(solution)/shard_map/pallas_call | solution.py:218
  29.4 1.7 %collective-permute-start.6 = (f32[2,64,256]{2,1,0:T(8,128)S(1)}, f32[2,64,256]{2,1,0:T(8,128)S(1)}, u32[]{:S(2)}, u32[]{:S(2)}) collective-permute-start(f32[2,64,256]{2,1,0:T(8,128)S(1)} %get-tuple-element.35), channel_id=1, source_target_pairs={{0,16},{8,24},{16,0},{24,8},{1,17},{9,25},{17,1},{25,9},{2,18},{10... | collective-permute-start | bytes 393224 | tf_op jit(solution)/shard_map/ppermute | solution.py:247
  31.1 6.1 %collective-permute-start.5 = (f32[2,64,256]{2,1,0:T(8,128)S(1)}, f32[2,64,256]{2,1,0:T(8,128)S(1)}, u32[]{:S(2)}, u32[]{:S(2)}) collective-permute-start(f32[2,64,256]{2,1,0:T(8,128)S(1)} %get-tuple-element.34.refs_8_.refs_0_), channel_id=1, source_target_pairs={{0,2},{1,3},{2,0},{3,1},{4,6},{5,7},{6,4},{7,5},{8,10},{9,11},{10,... | collective-permute-start | bytes 393224 | tf_op jit(solution)/shard_map/ppermute | solution.py:261
  37.2 4.4 %collective-permute-start.7 = (f32[2,64,256]{2,1,0:T(8,128)S(1)}, f32[2,64,256]{2,1,0:T(8,128)S(1)}, u32[]{:S(2)}, u32[]{:S(2)}) collective-permute-start(f32[2,64,256]{2,1,0:T(8,128)S(1)} %collective-permute-done.6.refs_4_.refs_2_), channel_id=1, source_target_pairs={{0,2},{1,3},{2,0},{3,1},{4,6},{5,7},{6,4},{7,5},{8,10},{9,11},{10,... | collective-permute-start | bytes 393224 | tf_op jit(solution)/shard_map/ppermute | solution.py:261
  41.6 1.8 %collective-permute-done.5.refs_5_.refs_1_ = f32[2,64,256]{2,1,0:T(8,128)S(1)} collective-permute-done((f32[2,64,256]{2,1,0:T(8,128)S(1)}, f32[2,64,256]{2,1,0:T(8,128)S(1)}, u32[]{:S(2)}, u32[]{:S(2)}) %collective-permute-start.5) | collective-permute-done | bytes 131104 | tf_op jit(solution)/shard_map/ppermute | solution.py:261
  43.4 1.4 %collective-permute-done.7.refs_7_.refs_3_ = f32[2,64,256]{2,1,0:T(8,128)S(1)} collective-permute-done((f32[2,64,256]{2,1,0:T(8,128)S(1)}, f32[2,64,256]{2,1,0:T(8,128)S(1)}, u32[]{:S(2)}, u32[]{:S(2)}) %collective-permute-start.7) | collective-permute-done | bytes 131104 | tf_op jit(solution)/shard_map/ppermute | solution.py:261
  47.4 1.3 %shard_map.64 = (f32[2,88,256]{2,1,0:T(8,128)S(1)}, f32[2,88,256]{2,1,0:T(8,128)S(1)}) custom-call(f32[2,4]{1,0:T(2,128)S(1)} %copy-done.4, f32[3,2,88,256]{3,2,1,0:T(8,128)S(1)} %get-tuple-element.40.refs_1_, f32[3,2,88,256]{3,2,1,0:T(8,128)S(1)} %get-tuple-element.37.refs_4_.refs_2_, f32[3,2,88,256]{3,2,1,0:T(8,128)S(1)} %collective-permute-done.10.refs_3_, ...), custom_call_target="tpu_custom_call" | custom-call | flops 1 | bytes 1 | tf_op jit(solution)/shard_map/pallas_call | solution.py:218
  48.7 2.7 %collective-permute-start.13 = (f32[2,88,256]{2,1,0:T(8,128)S(1)}, f32[2,88,256]{2,1,0:T(8,128)S(1)}, u32[]{:S(2)}, u32[]{:S(2)}) collective-permute-start(f32[2,88,256]{2,1,0:T(8,128)S(1)} %get-tuple-element.41.refs_6_.refs_0_), channel_id=1, source_target_pairs={{0,2},{1,3},{2,0},{3,1},{4,6},{5,7},{6,4},{7,5},{8,10},{9,11},{10,... | collective-permute-start | bytes 540680 | tf_op jit(solution)/shard_map/ppermute | solution.py:261
  53.2 4.2 %collective-permute-done.16.refs_3_ = f32[3,2,64,256]{3,2,1,0:T(8,128)S(1)} collective-permute-done((f32[3,2,64,256]{3,2,1,0:T(8,128)S(1)}, f32[3,2,64,256]{3,2,1,0:T(8,128)S(1)}, u32[]{:S(2)}, u32[]{:S(2)}) %collective-permute-start.16) | collective-permute-done | bytes 393248 | tf_op jit(solution)/shard_map/ppermute | solution.py:247
  58.1 2.7 %collective-permute-done.14.refs_4_.refs_2_ = f32[2,88,256]{2,1,0:T(8,128)S(1)} collective-permute-done((f32[2,88,256]{2,1,0:T(8,128)S(1)}, f32[2,88,256]{2,1,0:T(8,128)S(1)}, u32[]{:S(2)}, u32[]{:S(2)}) %collective-permute-start.14) | collective-permute-done | bytes 180256 | tf_op jit(solution)/shard_map/ppermute | solution.py:247
  62.0 2.7 %collective-permute-start.15 = (f32[2,88,256]{2,1,0:T(8,128)S(1)}, f32[2,88,256]{2,1,0:T(8,128)S(1)}, u32[]{:S(2)}, u32[]{:S(2)}) collective-permute-start(f32[2,88,256]{2,1,0:T(8,128)S(1)} %collective-permute-done.14.refs_4_.refs_2_), channel_id=1, source_target_pairs={{0,2},{1,3},{2,0},{3,1},{4,6},{5,7},{6,4},{7,5},{8,10},{9,11},{10,... | collective-permute-start | bytes 540680 | tf_op jit(solution)/shard_map/ppermute | solution.py:261
  67.6 4.3 %collective-permute-done.15.refs_3_ = f32[2,88,256]{2,1,0:T(8,128)S(1)} collective-permute-done((f32[2,88,256]{2,1,0:T(8,128)S(1)}, f32[2,88,256]{2,1,0:T(8,128)S(1)}, u32[]{:S(2)}, u32[]{:S(2)}) %collective-permute-start.15) | collective-permute-done | bytes 180256 | tf_op jit(solution)/shard_map/ppermute | solution.py:261
  72.0 1.3 %shard_map.68 = (f32[2,176,256]{2,1,0:T(8,128)S(1)}, f32[2,176,256]{2,1,0:T(8,128)S(1)}) custom-call(f32[2,88,256]{2,1,0:T(8,128)S(1)} %get-tuple-element.41.refs_6_.refs_0_, f32[2,88,256]{2,1,0:T(8,128)S(1)} %collective-permute-done.13.refs_5_.refs_1_, f32[2,88,256]{2,1,0:T(8,128)S(1)} %collective-permute-done.14.refs_4_.refs_2_, ...), custom_call_target="tpu_custom_call" | custom-call | flops 1 | bytes 1 | tf_op jit(solution)/shard_map/pallas_call | solution.py:218
  73.3 3.4 %collective-permute-done.12.refs_4_.refs_9_.refs_1_ = f32[2,128,256]{2,1,0:T(8,128)S(1)} collective-permute-done((f32[2,128,256]{2,1,0:T(8,128)S(1)}, f32[2,128,256]{2,1,0:T(8,128)S(1)}, u32[]{:S(2)}, u32[]{:S(2)}) %collective-permute-start.12) | collective-permute-done | bytes 262176 | tf_op jit(solution)/shard_map/ppermute | solution.py:258
  76.6 2.3 %collective-permute-done.20.refs_2_.refs_1_ = f32[2,64,256]{2,1,0:T(8,128)S(1)} collective-permute-done((f32[2,64,256]{2,1,0:T(8,128)S(1)}, f32[2,64,256]{2,1,0:T(8,128)S(1)}, u32[]{:S(2)}, u32[]{:S(2)}) %collective-permute-start.20) | collective-permute-done | bytes 131104 | tf_op jit(solution)/shard_map/ppermute | solution.py:261
  80.1 3.4 %collective-permute-start.22 = (f32[2,64,256]{2,1,0:T(8,128)S(1)}, f32[2,64,256]{2,1,0:T(8,128)S(1)}, u32[]{:S(2)}, u32[]{:S(2)}) collective-permute-start(f32[2,64,256]{2,1,0:T(8,128)S(1)} %collective-permute-done.21.refs_1_.refs_2_), channel_id=1, source_target_pairs={{0,2},{1,3},{2,0},{3,1},{4,6},{5,7},{6,4},{7,5},{8,10},{9,11},{10,... | collective-permute-start | bytes 393224 | tf_op jit(solution)/shard_map/ppermute | solution.py:261
  84.4 1.6 %collective-permute-start.26 = (f32[2,40,256]{2,1,0:T(8,128)S(1)}, f32[2,40,256]{2,1,0:T(8,128)S(1)}, u32[]{:S(2)}, u32[]{:S(2)}) collective-permute-start(f32[2,40,256]{2,1,0:T(8,128)S(1)} %get-tuple-element.55), channel_id=1, source_target_pairs={{0,16},{8,24},{16,0},{24,8},{1,17},{9,25},{17,1},{25,9},{2,18},{10... | collective-permute-start | bytes 245768 | tf_op jit(solution)/shard_map/ppermute | solution.py:247
  86.0 5.7 %collective-permute-done.22.refs_3_ = f32[2,64,256]{2,1,0:T(8,128)S(1)} collective-permute-done((f32[2,64,256]{2,1,0:T(8,128)S(1)}, f32[2,64,256]{2,1,0:T(8,128)S(1)}, u32[]{:S(2)}, u32[]{:S(2)}) %collective-permute-start.22) | collective-permute-done | bytes 131104 | tf_op jit(solution)/shard_map/ppermute | solution.py:261
  93.9 4.2 %collective-permute-start.28 = (f32[2,128,256]{2,1,0:T(8,128)S(1)}, f32[2,128,256]{2,1,0:T(8,128)S(1)}, u32[]{:S(2)}, u32[]{:S(2)}) collective-permute-start(f32[2,128,256]{2,1,0:T(8,128)S(1)} %get-tuple-element.57), channel_id=1, source_target_pairs={{0,1},{1,0},{2,3},{3,2},{4,5},{5,4},{6,7},{7,6},{8,9},{9,8},{10,11... | collective-permute-start | bytes 786440 | tf_op jit(solution)/shard_map/ppermute | solution.py:258
  98.1 7.2 %collective-permute-done.29.refs_3_ = f32[2,40,256]{2,1,0:T(8,128)S(1)} collective-permute-done((f32[2,40,256]{2,1,0:T(8,128)S(1)}, f32[2,40,256]{2,1,0:T(8,128)S(1)}, u32[]{:S(2)}, u32[]{:S(2)}) %collective-permute-start.29) | collective-permute-done | bytes 81952 | tf_op jit(solution)/shard_map/ppermute | solution.py:261
  105.3 1.2 %shard_map.72 = (f32[2,80,256]{2,1,0:T(8,128)S(1)}, f32[2,80,256]{2,1,0:T(8,128)S(1)}) custom-call(f32[2,40,256]{2,1,0:T(8,128)S(1)} %get-tuple-element.54.refs_6_.refs_0_, f32[2,40,256]{2,1,0:T(8,128)S(1)} %collective-permute-done.27.refs_8_.refs_1_, f32[2,40,256]{2,1,0:T(8,128)S(1)} %collective-permute-done.26.refs_7_.refs_2_, ...), custom_call_target="tpu_custom_call" | custom-call | flops 1 | bytes 1 | tf_op jit(solution)/shard_map/pallas_call | solution.py:218
  106.5 1.6 %collective-permute-start.30 = (f32[2,80,256]{2,1,0:T(8,128)S(1)}, f32[2,80,256]{2,1,0:T(8,128)S(1)}, u32[]{:S(2)}, u32[]{:S(2)}) collective-permute-start(f32[2,80,256]{2,1,0:T(8,128)S(1)} %get-tuple-element.59), channel_id=1, source_target_pairs={{0,1},{1,0},{2,3},{3,2},{4,5},{5,4},{6,7},{7,6},{8,9},{9,8},{10,11... | collective-permute-start | bytes 491528 | tf_op jit(solution)/shard_map/ppermute | solution.py:258
  108.1 3.8 %collective-permute-done.30.refs_7_ = f32[2,80,256]{2,1,0:T(8,128)S(1)} collective-permute-done((f32[2,80,256]{2,1,0:T(8,128)S(1)}, f32[2,80,256]{2,1,0:T(8,128)S(1)}, u32[]{:S(2)}, u32[]{:S(2)}) %collective-permute-start.30) | collective-permute-done | bytes 163872 | tf_op jit(solution)/shard_map/ppermute | solution.py:258
  111.9 1.5 %shard_map.73 = (f32[2,1,512,256]{3,2,1,0:T(8,128)}, f32[2,1,512,256]{3,2,1,0:T(8,128)}) custom-call(f32[2,128,256]{2,1,0:T(8,128)S(1)} %get-tuple-element.42.refs_6_.refs_0_, f32[2,128,256]{2,1,0:T(8,128)S(1)} %collective-permute-done.12.refs_4_.refs_9_.refs_1_, f32[2,176,256]{2,1,0:T(8,128)S(1)} %get-tuple-element.49.refs_3_.refs_2_, ...), custom_call_target="tpu_custom_call" | custom-call | flops 1 | bytes 1 | tf_op jit(solution)/shard_map/pallas_call | solution.py:218
  (56 shorter events, 14.3 us)
Async XLA Ops:
  3.0 12.3 %collective-permute-start = (f32[3,2,64,256]{3,2,1,0:T(8,128)}, f32[3,2,64,256]{3,2,1,0:T(8,128)S(1)}, u32[]{:S(2)}, u32[]{:S(2)}) collective-permute-start(f32[3,2,64,256]{3,2,1,0:T(8,128)} %get-tuple-element.32), channel_id=1, source_target_pairs={{0,16},{8,24},{16,0},{24,8},{1,17},{9,25},{17,1},{25,9},{2,18},{10... | collective-permute-start | bytes 1179656 | tf_op jit(solution)/shard_map/ppermute | solution.py:247
  6.0 12.0 %collective-permute-start.1 = (f32[3,2,64,256]{3,2,1,0:T(8,128)}, f32[3,2,64,256]{3,2,1,0:T(8,128)}, u32[]{:S(2)}, u32[]{:S(2)}) collective-permute-start(f32[3,2,64,256]{3,2,1,0:T(8,128)} %get-tuple-element.31.refs_1_), channel_id=1, source_target_pairs={{0,8},{8,0},{16,24},{24,16},{1,9},{9,1},{17,25},{25,17},{2,10},{10... | collective-permute-start | bytes 1179656 | tf_op jit(solution)/shard_map/ppermute | solution.py:250
  6.0 21.8 %copy-start.3 = (f32[3,2,64,256]{3,2,1,0:T(8,128)S(1)}, f32[3,2,64,256]{3,2,1,0:T(8,128)}, u32[]{:S(2)}) copy-start(f32[3,2,64,256]{3,2,1,0:T(8,128)} %get-tuple-element.31.refs_1_) | copy-start | bytes 1179652
  6.1 14.4 %collective-permute-start.3 = (f32[2,256,256]{2,1,0:T(8,128)S(1)}, f32[2,256,256]{2,1,0:T(8,128)S(1)}, u32[]{:S(2)}, u32[]{:S(2)}) collective-permute-start(f32[2,256,256]{2,1,0:T(8,128)S(1)} %get-tuple-element.61), channel_id=1, source_target_pairs={{0,1},{1,0},{2,3},{3,2},{4,5},{5,4},{6,7},{7,6},{8,9},{9,8},{10,11... | collective-permute-start | bytes 1572872 | tf_op jit(solution)/shard_map/ppermute | solution.py:258
  7.7 20.1 %collective-permute-start.4 = (f32[2,256,256]{2,1,0:T(8,128)S(1)}, f32[2,256,256]{2,1,0:T(8,128)S(1)}, u32[]{:S(2)}, u32[]{:S(2)}) collective-permute-start(f32[2,256,256]{2,1,0:T(8,128)S(1)} %get-tuple-element.60.refs_0_), channel_id=1, source_target_pairs={{0,4},{1,5},{2,6},{3,7},{4,0},{5,1},{6,2},{7,3},{8,12},{9,13},{10,... | collective-permute-start | bytes 1572872 | tf_op jit(solution)/shard_map/ppermute | solution.py:258
  16.1 11.8 %collective-permute-start.2 = (f32[3,2,64,256]{3,2,1,0:T(8,128)S(1)}, f32[3,2,64,256]{3,2,1,0:T(8,128)S(1)}, u32[]{:S(2)}, u32[]{:S(2)}) collective-permute-start(f32[3,2,64,256]{3,2,1,0:T(8,128)S(1)} %get-tuple-element.33.refs_2_), channel_id=1, source_target_pairs={{0,8},{8,0},{16,24},{24,16},{1,9},{9,1},{17,25},{25,17},{2,10},{10... | collective-permute-start | bytes 1179656 | tf_op jit(solution)/shard_map/ppermute | solution.py:250
  16.1 27.3 %collective-permute-start.9 = (f32[3,2,88,256]{3,2,1,0:T(8,128)S(1)}, f32[3,2,88,256]{3,2,1,0:T(8,128)S(1)}, u32[]{:S(2)}, u32[]{:S(2)}) collective-permute-start(f32[3,2,88,256]{3,2,1,0:T(8,128)S(1)} %get-tuple-element.36), channel_id=1, source_target_pairs={{0,16},{8,24},{16,0},{24,8},{1,17},{9,25},{17,1},{25,9},{2,18},{10... | collective-permute-start | bytes 1622024 | tf_op jit(solution)/shard_map/ppermute | solution.py:247
  17.9 23.7 %collective-permute-start.8 = (f32[2,256,256]{2,1,0:T(8,128)S(1)}, f32[2,256,256]{2,1,0:T(8,128)S(1)}, u32[]{:S(2)}, u32[]{:S(2)}) collective-permute-start(f32[2,256,256]{2,1,0:T(8,128)S(1)} %get-tuple-element.61), channel_id=1, source_target_pairs={{0,5},{1,4},{2,7},{3,6},{4,1},{5,0},{6,3},{7,2},{8,13},{9,12},{10,... | collective-permute-start | bytes 1572872 | tf_op jit(solution)/shard_map/ppermute | solution.py:258
  29.4 7.7 %collective-permute-start.6 = (f32[2,64,256]{2,1,0:T(8,128)S(1)}, f32[2,64,256]{2,1,0:T(8,128)S(1)}, u32[]{:S(2)}, u32[]{:S(2)}) collective-permute-start(f32[2,64,256]{2,1,0:T(8,128)S(1)} %get-tuple-element.35), channel_id=1, source_target_pairs={{0,16},{8,24},{16,0},{24,8},{1,17},{9,25},{17,1},{25,9},{2,18},{10... | collective-permute-start | bytes 393224 | tf_op jit(solution)/shard_map/ppermute | solution.py:247
  31.1 12.3 %collective-permute-start.5 = (f32[2,64,256]{2,1,0:T(8,128)S(1)}, f32[2,64,256]{2,1,0:T(8,128)S(1)}, u32[]{:S(2)}, u32[]{:S(2)}) collective-permute-start(f32[2,64,256]{2,1,0:T(8,128)S(1)} %get-tuple-element.34.refs_8_.refs_0_), channel_id=1, source_target_pairs={{0,2},{1,3},{2,0},{3,1},{4,6},{5,7},{6,4},{7,5},{8,10},{9,11},{10,... | collective-permute-start | bytes 393224 | tf_op jit(solution)/shard_map/ppermute | solution.py:261
  37.2 7.6 %collective-permute-start.7 = (f32[2,64,256]{2,1,0:T(8,128)S(1)}, f32[2,64,256]{2,1,0:T(8,128)S(1)}, u32[]{:S(2)}, u32[]{:S(2)}) collective-permute-start(f32[2,64,256]{2,1,0:T(8,128)S(1)} %collective-permute-done.6.refs_4_.refs_2_), channel_id=1, source_target_pairs={{0,2},{1,3},{2,0},{3,1},{4,6},{5,7},{6,4},{7,5},{8,10},{9,11},{10,... | collective-permute-start | bytes 393224 | tf_op jit(solution)/shard_map/ppermute | solution.py:261
  41.6 5.0 %collective-permute-start.10 = (f32[3,2,88,256]{3,2,1,0:T(8,128)S(1)}, f32[3,2,88,256]{3,2,1,0:T(8,128)S(1)}, u32[]{:S(2)}, u32[]{:S(2)}) collective-permute-start(f32[3,2,88,256]{3,2,1,0:T(8,128)S(1)} %get-tuple-element.40.refs_1_), channel_id=1, source_target_pairs={{0,8},{8,0},{16,24},{24,16},{1,9},{9,1},{17,25},{25,17},{2,10},{10... | collective-permute-start | bytes 1622024 | tf_op jit(solution)/shard_map/ppermute | solution.py:250
  45.4 2.0 %collective-permute-start.11 = (f32[3,2,88,256]{3,2,1,0:T(8,128)S(1)}, f32[3,2,88,256]{3,2,1,0:T(8,128)S(1)}, u32[]{:S(2)}, u32[]{:S(2)}) collective-permute-start(f32[3,2,88,256]{3,2,1,0:T(8,128)S(1)} %get-tuple-element.37.refs_4_.refs_2_), channel_id=1, source_target_pairs={{0,8},{8,0},{16,24},{24,16},{1,9},{9,1},{17,25},{25,17},{2,10},{10... | collective-permute-start | bytes 1622024 | tf_op jit(solution)/shard_map/ppermute | solution.py:250
  45.4 12.0 %collective-permute-start.16 = (f32[3,2,64,256]{3,2,1,0:T(8,128)S(1)}, f32[3,2,64,256]{3,2,1,0:T(8,128)S(1)}, u32[]{:S(2)}, u32[]{:S(2)}) collective-permute-start(f32[3,2,64,256]{3,2,1,0:T(8,128)S(1)} %get-tuple-element.46), channel_id=1, source_target_pairs={{0,16},{8,24},{16,0},{24,8},{1,17},{9,25},{17,1},{25,9},{2,18},{10... | collective-permute-start | bytes 1179656 | tf_op jit(solution)/shard_map/ppermute | solution.py:247
  48.7 9.4 %collective-permute-start.13 = (f32[2,88,256]{2,1,0:T(8,128)S(1)}, f32[2,88,256]{2,1,0:T(8,128)S(1)}, u32[]{:S(2)}, u32[]{:S(2)}) collective-permute-start(f32[2,88,256]{2,1,0:T(8,128)S(1)} %get-tuple-element.41.refs_6_.refs_0_), channel_id=1, source_target_pairs={{0,2},{1,3},{2,0},{3,1},{4,6},{5,7},{6,4},{7,5},{8,10},{9,11},{10,... | collective-permute-start | bytes 540680 | tf_op jit(solution)/shard_map/ppermute | solution.py:261
  51.4 9.4 %collective-permute-start.14 = (f32[2,88,256]{2,1,0:T(8,128)S(1)}, f32[2,88,256]{2,1,0:T(8,128)S(1)}, u32[]{:S(2)}, u32[]{:S(2)}) collective-permute-start(f32[2,88,256]{2,1,0:T(8,128)S(1)} %get-tuple-element.44), channel_id=1, source_target_pairs={{0,16},{8,24},{16,0},{24,8},{1,17},{9,25},{17,1},{25,9},{2,18},{10... | collective-permute-start | bytes 540680 | tf_op jit(solution)/shard_map/ppermute | solution.py:247
  52.2 12.5 %collective-permute-start.17 = (f32[3,2,64,256]{3,2,1,0:T(8,128)S(1)}, f32[3,2,64,256]{3,2,1,0:T(8,128)S(1)}, u32[]{:S(2)}, u32[]{:S(2)}) collective-permute-start(f32[3,2,64,256]{3,2,1,0:T(8,128)S(1)} %get-tuple-element.45.refs_1_), channel_id=1, source_target_pairs={{0,8},{8,0},{16,24},{24,16},{1,9},{9,1},{17,25},{25,17},{2,10},{10... | collective-permute-start | bytes 1179656 | tf_op jit(solution)/shard_map/ppermute | solution.py:250
  61.2 3.4 %collective-permute-start.18 = (f32[3,2,64,256]{3,2,1,0:T(8,128)S(1)}, f32[3,2,64,256]{3,2,1,0:T(8,128)S(1)}, u32[]{:S(2)}, u32[]{:S(2)}) collective-permute-start(f32[3,2,64,256]{3,2,1,0:T(8,128)S(1)} %get-tuple-element.47.refs_2_), channel_id=1, source_target_pairs={{0,8},{8,0},{16,24},{24,16},{1,9},{9,1},{17,25},{25,17},{2,10},{10... | collective-permute-start | bytes 1179656 | tf_op jit(solution)/shard_map/ppermute | solution.py:250
  61.3 15.3 %collective-permute-start.12 = (f32[2,128,256]{2,1,0:T(8,128)S(1)}, f32[2,128,256]{2,1,0:T(8,128)S(1)}, u32[]{:S(2)}, u32[]{:S(2)}) collective-permute-start(f32[2,128,256]{2,1,0:T(8,128)S(1)} %get-tuple-element.43), channel_id=1, source_target_pairs={{0,1},{1,0},{2,3},{3,2},{4,5},{5,4},{6,7},{7,6},{8,9},{9,8},{10,11... | collective-permute-start | bytes 786440 | tf_op jit(solution)/shard_map/ppermute | solution.py:258
  61.4 15.3 %collective-permute-start.23 = (f32[3,2,40,256]{3,2,1,0:T(8,128)S(1)}, f32[3,2,40,256]{3,2,1,0:T(8,128)S(1)}, u32[]{:S(2)}, u32[]{:S(2)}) collective-permute-start(f32[3,2,40,256]{3,2,1,0:T(8,128)S(1)} %get-tuple-element.53), channel_id=1, source_target_pairs={{0,16},{8,24},{16,0},{24,8},{1,17},{9,25},{17,1},{25,9},{2,18},{10... | collective-permute-start | bytes 737288 | tf_op jit(solution)/shard_map/ppermute | solution.py:247
  62.0 10.0 %collective-permute-start.15 = (f32[2,88,256]{2,1,0:T(8,128)S(1)}, f32[2,88,256]{2,1,0:T(8,128)S(1)}, u32[]{:S(2)}, u32[]{:S(2)}) collective-permute-start(f32[2,88,256]{2,1,0:T(8,128)S(1)} %collective-permute-done.14.refs_4_.refs_2_), channel_id=1, source_target_pairs={{0,2},{1,3},{2,0},{3,1},{4,6},{5,7},{6,4},{7,5},{8,10},{9,11},{10,... | collective-permute-start | bytes 540680 | tf_op jit(solution)/shard_map/ppermute | solution.py:261
  65.8 13.1 %collective-permute-start.20 = (f32[2,64,256]{2,1,0:T(8,128)S(1)}, f32[2,64,256]{2,1,0:T(8,128)S(1)}, u32[]{:S(2)}, u32[]{:S(2)}) collective-permute-start(f32[2,64,256]{2,1,0:T(8,128)S(1)} %get-tuple-element.48.refs_6_.refs_0_), channel_id=1, source_target_pairs={{0,2},{1,3},{2,0},{3,1},{4,6},{5,7},{6,4},{7,5},{8,10},{9,11},{10,... | collective-permute-start | bytes 393224 | tf_op jit(solution)/shard_map/ppermute | solution.py:261
  66.9 12.1 %collective-permute-start.21 = (f32[2,64,256]{2,1,0:T(8,128)S(1)}, f32[2,64,256]{2,1,0:T(8,128)S(1)}, u32[]{:S(2)}, u32[]{:S(2)}) collective-permute-start(f32[2,64,256]{2,1,0:T(8,128)S(1)} %get-tuple-element.51), channel_id=1, source_target_pairs={{0,16},{8,24},{16,0},{24,8},{1,17},{9,25},{17,1},{25,9},{2,18},{10... | collective-permute-start | bytes 393224 | tf_op jit(solution)/shard_map/ppermute | solution.py:247
  72.0 11.6 %collective-permute-start.24 = (f32[3,2,40,256]{3,2,1,0:T(8,128)S(1)}, f32[3,2,40,256]{3,2,1,0:T(8,128)S(1)}, u32[]{:S(2)}, u32[]{:S(2)}) collective-permute-start(f32[3,2,40,256]{3,2,1,0:T(8,128)S(1)} %get-tuple-element.52.refs_1_), channel_id=1, source_target_pairs={{0,8},{8,0},{16,24},{24,16},{1,9},{9,1},{17,25},{25,17},{2,10},{10... | collective-permute-start | bytes 737288 | tf_op jit(solution)/shard_map/ppermute | solution.py:250
  79.0 4.6 %collective-permute-start.25 = (f32[3,2,40,256]{3,2,1,0:T(8,128)S(1)}, f32[3,2,40,256]{3,2,1,0:T(8,128)S(1)}, u32[]{:S(2)}, u32[]{:S(2)}) collective-permute-start(f32[3,2,40,256]{3,2,1,0:T(8,128)S(1)} %shard_map.69.refs_2_), channel_id=1, source_target_pairs={{0,8},{8,0},{16,24},{24,16},{1,9},{9,1},{17,25},{25,17},{2,10},{10... | collective-permute-start | bytes 737288 | tf_op jit(solution)/shard_map/ppermute | solution.py:250
  79.0 19.1 %collective-permute-start.19 = (f32[2,176,256]{2,1,0:T(8,128)S(1)}, f32[2,176,256]{2,1,0:T(8,128)S(1)}, u32[]{:S(2)}, u32[]{:S(2)}) collective-permute-start(f32[2,176,256]{2,1,0:T(8,128)S(1)} %get-tuple-element.50), channel_id=1, source_target_pairs={{0,1},{1,0},{2,3},{3,2},{4,5},{5,4},{6,7},{7,6},{8,9},{9,8},{10,11... | collective-permute-start | bytes 1081352 | tf_op jit(solution)/shard_map/ppermute | solution.py:258
  80.1 11.6 %collective-permute-start.22 = (f32[2,64,256]{2,1,0:T(8,128)S(1)}, f32[2,64,256]{2,1,0:T(8,128)S(1)}, u32[]{:S(2)}, u32[]{:S(2)}) collective-permute-start(f32[2,64,256]{2,1,0:T(8,128)S(1)} %collective-permute-done.21.refs_1_.refs_2_), channel_id=1, source_target_pairs={{0,2},{1,3},{2,0},{3,1},{4,6},{5,7},{6,4},{7,5},{8,10},{9,11},{10,... | collective-permute-start | bytes 393224 | tf_op jit(solution)/shard_map/ppermute | solution.py:261
  84.4 7.3 %collective-permute-start.26 = (f32[2,40,256]{2,1,0:T(8,128)S(1)}, f32[2,40,256]{2,1,0:T(8,128)S(1)}, u32[]{:S(2)}, u32[]{:S(2)}) collective-permute-start(f32[2,40,256]{2,1,0:T(8,128)S(1)} %get-tuple-element.55), channel_id=1, source_target_pairs={{0,16},{8,24},{16,0},{24,8},{1,17},{9,25},{17,1},{25,9},{2,18},{10... | collective-permute-start | bytes 245768 | tf_op jit(solution)/shard_map/ppermute | solution.py:247
  86.0 6.9 %collective-permute-start.27 = (f32[2,40,256]{2,1,0:T(8,128)S(1)}, f32[2,40,256]{2,1,0:T(8,128)S(1)}, u32[]{:S(2)}, u32[]{:S(2)}) collective-permute-start(f32[2,40,256]{2,1,0:T(8,128)S(1)} %get-tuple-element.54.refs_6_.refs_0_), channel_id=1, source_target_pairs={{0,2},{1,3},{2,0},{3,1},{4,6},{5,7},{6,4},{7,5},{8,10},{9,11},{10,... | collective-permute-start | bytes 245768 | tf_op jit(solution)/shard_map/ppermute | solution.py:261
  93.9 18.0 %collective-permute-start.28 = (f32[2,128,256]{2,1,0:T(8,128)S(1)}, f32[2,128,256]{2,1,0:T(8,128)S(1)}, u32[]{:S(2)}, u32[]{:S(2)}) collective-permute-start(f32[2,128,256]{2,1,0:T(8,128)S(1)} %get-tuple-element.57), channel_id=1, source_target_pairs={{0,1},{1,0},{2,3},{3,2},{4,5},{5,4},{6,7},{7,6},{8,9},{9,8},{10,11... | collective-permute-start | bytes 786440 | tf_op jit(solution)/shard_map/ppermute | solution.py:258
  98.1 7.3 %collective-permute-start.29 = (f32[2,40,256]{2,1,0:T(8,128)S(1)}, f32[2,40,256]{2,1,0:T(8,128)S(1)}, u32[]{:S(2)}, u32[]{:S(2)}) collective-permute-start(f32[2,40,256]{2,1,0:T(8,128)S(1)} %collective-permute-done.26.refs_7_.refs_2_), channel_id=1, source_target_pairs={{0,2},{1,3},{2,0},{3,1},{4,6},{5,7},{6,4},{7,5},{8,10},{9,11},{10,... | collective-permute-start | bytes 245768 | tf_op jit(solution)/shard_map/ppermute | solution.py:261
  106.5 5.4 %collective-permute-start.30 = (f32[2,80,256]{2,1,0:T(8,128)S(1)}, f32[2,80,256]{2,1,0:T(8,128)S(1)}, u32[]{:S(2)}, u32[]{:S(2)}) collective-permute-start(f32[2,80,256]{2,1,0:T(8,128)S(1)} %get-tuple-element.59), channel_id=1, source_target_pairs={{0,1},{1,0},{2,3},{3,2},{4,5},{5,4},{6,7},{7,6},{8,9},{9,8},{10,11... | collective-permute-start | bytes 491528 | tf_op jit(solution)/shard_map/ppermute | solution.py:258
  (4 other events, 56.4 us)
